TPU v7x, 32 devices: a whole 2x2x4 slice. The times are simulated.
32 devices in a mesh: req: 2 (over y), ctx: 8 (over z, x), tp: 2 (over core).
Axes of the slice: x: 2, y: 2, z: 4, core: 2. Of those that a mesh axis runs over, the one named last changes fastest.
Arguments:
- hidden: bfloat16 [2048, 8192], P(('req', 'ctx')), parts along dimension 0, may hold values from -6 to 6
- suffix_hidden: bfloat16 [32, 8192], P(('req', 'ctx')), parts along dimension 0, may hold values from -6 to 6
- norm_gain: float32 [8192], replicated, may hold values from 0.1 to 1.9
- key_matrix: bfloat16 [8192, 512], P('ctx', 'tp'), may hold values from -0.0625 to 0.0625
- value_matrix: bfloat16 [8192, 512], P('ctx', 'tp'), may hold values from -0.0625 to 0.0625
- key_offset_bias: float32 [512], P('tp'), may hold values from -4 to 4
- value_offset_bias: float32 [512], P('tp'), may hold values from -4 to 4
- suffix_query_rows: bfloat16 [32, 4096], P(('req', 'ctx'), 'tp'), parts along dimension 0, may hold values from -100 to 100
- slot_keys: bfloat16 [64, 128, 512], P(('req', 'ctx'), None, 'tp'), parts along dimension 0, may hold values from -4 to 4
- slot_values: bfloat16 [64, 128, 512], P(('req', 'ctx'), None, 'tp'), parts along dimension 0, may hold values from -4 to 4
- page_slot_table: int32 [32], P('req'), parts along dimension 0, may hold values from 0 to 31, as said below
- split_page: int32 [2], P('req'), parts along dimension 0, may hold values from 4 to 8
Outputs:
- front_keys: bfloat16 [2048, 512], P(('req', 'ctx'), 'tp'), parts along dimension 0
- front_values: bfloat16 [2048, 512], P(('req', 'ctx'), 'tp'), parts along dimension 0
- attended: bfloat16 [32, 4096], P(('req', 'ctx'), 'tp'), parts along dimension 0
There are 2 independent parts, one for each index of `req`. A program takes and returns all parts, laid end to end along the dimension named above; an argument that names none is the same for every part. Nothing has to cross between parts.
Inputs may be any that keep to these rules, and one draw needn't show every extreme that they name: `page_slot_table`: distinct storage slots; slot s lies on ctx device s // 4; no device holds more than 4 pages of a group, and some device holds exactly 4.
All inputs are finite; a program needn't handle non-finite values.
Results may differ from a plain program's by a relative error of at most 0.0063.
Values may be sent and summed in bfloat16 or wider, within the bound.
No kernel may reach another device: no remote copies, remote signals or barrier semaphores. Data moves between devices by JAX's collectives and lax.ppermute only.
A program may use at most 64 MiB of HBM per device.

v0:
```python
import functools
import math

import jax
import jax.numpy as jnp
from jax import lax
from jax.experimental import pallas as pl
from jax.experimental.pallas import tpu as pltpu
from jax.sharding import PartitionSpec as P

QUERY_HEADS = 32
KEY_VALUE_HEADS = 4
HEAD_SIZE = 128


epsilon = 1e-06
rope_base = 1000000.0
masked_score = -1e30


def rms_rows(matrix, norm_gain):
    widened = matrix.astype(jnp.float32)
    inverse = lax.rsqrt(jnp.mean(widened * widened, axis=-1, keepdims=True) + epsilon)
    return (widened * inverse * norm_gain).astype(jnp.bfloat16)


def rotate(key_rows, positions, head_dim):
    row_count = key_rows.shape[0]
    split_heads = key_rows.reshape(row_count, -1, head_dim)
    half_dim = head_dim // 2
    inverse_freq = rope_base ** (-(jnp.arange(half_dim, dtype=jnp.float32) * (2.0 / head_dim)))
    angles = positions.astype(jnp.float32)[:, None] * inverse_freq[None, :]
    cosine = jnp.concatenate([jnp.cos(angles), jnp.cos(angles)], -1)[:, None, :]
    sine = jnp.concatenate([jnp.sin(angles), jnp.sin(angles)], -1)[:, None, :]
    turned = jnp.concatenate([-split_heads[..., half_dim:], split_heads[..., :half_dim]], -1)
    return (split_heads * cosine + turned * sine).reshape(row_count, -1)


def gathered_plan(
    hidden,
    suffix_hidden,
    norm_gain,
    key_matrix,
    value_matrix,
    key_offset_bias,
    value_offset_bias,
    suffix_query_rows,
    slot_keys,
    slot_values,
    page_slot_table,
    split_page,
):
    ctx_index = lax.axis_index("ctx")
    queries = lax.all_gather(suffix_query_rows, "ctx", axis=0, tiled=True)
    front_rows = hidden.shape[0]
    suffix_rows = suffix_hidden.shape[0]
    page_size = slot_keys.shape[1]
    slot_count = slot_keys.shape[0]
    total_pages = page_slot_table.shape[0]
    prefix_len = total_pages * page_size
    normed = rms_rows(jnp.concatenate([hidden, suffix_hidden], 0), norm_gain)
    col_width = key_matrix.shape[1]

    def accumulate(block_rows):
        return jnp.dot(normed, block_rows, preferred_element_type=jnp.float32)

    key_acc = accumulate(lax.all_gather(key_matrix, "ctx", axis=0, tiled=True))
    value_acc = accumulate(lax.all_gather(value_matrix, "ctx", axis=0, tiled=True))
    front_pos = ctx_index * front_rows + jnp.arange(front_rows, dtype=jnp.int32)
    suffix_pos = prefix_len + ctx_index * suffix_rows + jnp.arange(suffix_rows, dtype=jnp.int32)
    new_keys = rotate(
        key_acc + key_offset_bias, jnp.concatenate([front_pos, suffix_pos], 0), HEAD_SIZE
    ).astype(jnp.bfloat16)
    new_values = (value_acc + value_offset_bias).astype(jnp.bfloat16)
    cut_pos = split_page[0] * page_size
    global_slot = ctx_index * slot_count + jnp.arange(slot_count, dtype=jnp.int32)
    page_index = jnp.arange(total_pages, dtype=jnp.int32)
    slot_hits = (page_slot_table[None, :] == global_slot[:, None]) & (
        page_index[None, :] >= split_page[0]
    )
    slot_live = jnp.max(slot_hits.astype(jnp.int32), axis=1) > 0
    every_key = jnp.concatenate(
        [new_keys[:front_rows], slot_keys.reshape(-1, col_width), new_keys[front_rows:]], 0
    )
    every_value = jnp.concatenate(
        [new_values[:front_rows], slot_values.reshape(-1, col_width), new_values[front_rows:]], 0
    )
    query_count = queries.shape[0]
    query_pos = prefix_len + jnp.arange(query_count, dtype=jnp.int32)
    prefix_seen = jnp.concatenate([front_pos < cut_pos, jnp.repeat(slot_live, page_size)], 0)
    suffix_seen = suffix_pos[None, :] <= query_pos[:, None]
    visible = jnp.concatenate(
        [jnp.broadcast_to(prefix_seen[None, :], (query_count, prefix_seen.shape[0])), suffix_seen],
        1,
    )
    visible_wide = visible[:, None, :]
    sharing_count = QUERY_HEADS // KEY_VALUE_HEADS
    local_heads = col_width // HEAD_SIZE
    grouped_heads = queries.reshape(query_count, local_heads, sharing_count, HEAD_SIZE)
    top_list = []
    total_list = []
    numer_list = []
    for current_head in range(local_heads):
        head_keys = every_key[:, current_head * HEAD_SIZE : (current_head + 1) * HEAD_SIZE]
        head_values = every_value[:, current_head * HEAD_SIZE : (current_head + 1) * HEAD_SIZE]
        scores = jnp.einsum(
            "qgd,ld->qgl",
            grouped_heads[:, current_head],
            head_keys,
            preferred_element_type=jnp.float32,
        ) * (1.0 / math.sqrt(HEAD_SIZE))
        scores = jnp.where(visible_wide, scores, masked_score)
        row_top = jnp.max(scores, axis=-1)
        expos = jnp.where(visible_wide, jnp.exp(scores - row_top[..., None]), 0.0)
        total_list.append(jnp.sum(expos, axis=-1))
        top_list.append(row_top)
        numer_list.append(
            jnp.einsum(
                "qgl,ld->qgd",
                expos.astype(jnp.bfloat16),
                head_values,
                preferred_element_type=jnp.float32,
            )
        )
    row_top = jnp.stack(top_list, 1)
    weight_total = jnp.stack(total_list, 1)
    numer = jnp.stack(numer_list, 1)
    global_top = lax.pmax(row_top, "ctx")
    factor = jnp.exp(row_top - global_top)
    own_total, own_numer = (
        lax.psum_scatter(
            (weight_total * factor).reshape(query_count, -1), "ctx", scatter_dimension=0, tiled=True
        ),
        lax.psum_scatter(
            (numer * factor[..., None]).reshape(query_count, -1),
            "ctx",
            scatter_dimension=0,
            tiled=True,
        ),
    )
    own_total = own_total.reshape(suffix_rows, local_heads, sharing_count)
    own_numer = own_numer.reshape(suffix_rows, local_heads, sharing_count, HEAD_SIZE)
    attended = (own_numer / own_total[..., None]).reshape(suffix_rows, -1).astype(jnp.bfloat16)
    return (new_keys[:front_rows], new_values[:front_rows], attended)

GROUPS = 4
PAIR = 2
LANES = 128
SCALE = 1.0 / math.sqrt(HEAD_SIZE)


def row_scale(values):
    mean = jnp.sum(values * values, axis=-1, keepdims=True) * (1.0 / values.shape[-1])
    return lax.rsqrt(mean + epsilon)


CHUNKS = 4


def far_first():
    return sorted(range(1, GROUPS), key=lambda s: s < GROUPS // 2)


def norm_kernel(query_any, hidden_any, suffix_any, gain_any, key_any, value_any, *rest):
    blocks_any, packed_any, own_any = rest[:GROUPS], rest[GROUPS], rest[GROUPS + 1]
    hidden_ref, suffix_ref, gain_ref, query_ref, packed_ref, tail_ref = rest[GROUPS + 2 : GROUPS + 8]
    outs, (sems, out_sems) = rest[GROUPS + 8 : -2], rest[-2:]
    depth = key_any.shape[0]
    packing = [
        pltpu.make_async_copy(key_any, packed_ref.at[:depth], sems.at[CHUNKS + 3]),
        pltpu.make_async_copy(value_any, packed_ref.at[depth:], sems.at[CHUNKS + 4]),
    ]
    unpacking = pltpu.make_async_copy(packed_ref, packed_any, sems.at[CHUNKS + 5])
    core, ctx = lax.axis_index("tp"), lax.axis_index("ctx")
    z, x = ctx // PAIR, ctx % PAIR
    half_rows, features = hidden_ref.shape
    rows = half_rows // CHUNKS
    block = features // (GROUPS * PAIR)
    per_block = block // LANES
    pieces = PAIR * per_block
    copies = [
        pltpu.make_async_copy(gain_any, gain_ref, sems.at[CHUNKS]),
        pltpu.make_async_copy(suffix_any, suffix_ref, sems.at[CHUNKS + 1]),
        pltpu.make_async_copy(query_any, query_ref, sems.at[CHUNKS + 2]),
    ]
    for i in range(CHUNKS):
        start = pl.multiple_of(core * half_rows + i * rows, rows)
        copies.append(
            pltpu.make_async_copy(
                hidden_any.at[pl.ds(start, rows)], hidden_ref.at[i * rows : (i + 1) * rows], sems.at[i]
            )
        )
    for copy in copies + packing:
        copy.start()

    def offset(shift, side, j):
        owner = (z ^ shift) * PAIR + (x ^ side)
        return pl.multiple_of(owner * block + j * LANES, LANES)

    copies[0].wait()
    copies[1].wait()
    copies[2].wait()
    query_rows = query_ref[...].astype(jnp.float32)
    lines = query_rows.shape[1] // LANES
    for r in range(query_rows.shape[0]):
        tile = [query_rows[r : r + 1, j * LANES : (j + 1) * LANES] for j in range(lines)]
        tile = jnp.concatenate(tile, 0).astype(jnp.bfloat16)
        start = pieces * half_rows + pieces + r * lines
        for out in outs:
            out[start : start + lines, :] = tile

    both = suffix_ref[...].astype(jnp.float32)
    normed = both * row_scale(both) * gain_ref[...]
    tail_ref[...] = jnp.where(core == 0, normed[0:1], normed[1:2])
    for shift in range(GROUPS):
        ends = [
            tail_ref[:, pl.ds(offset(shift, side, j), LANES)]
            for side in range(PAIR)
            for j in range(per_block)
        ]
        start = pieces * half_rows
        outs[shift][start : start + pieces, :] = jnp.concatenate(ends, 0).astype(jnp.bfloat16)
    inverses = []
    for i in range(CHUNKS):
        copies[3 + i].wait()
        inverses.append(row_scale(hidden_ref[i * rows : (i + 1) * rows, :].astype(jnp.float32)))
    for copy in packing:
        copy.wait()
    unpacking.start()
    leaving = []
    for shift in far_first() + [0]:
        for side in range(PAIR):
            for j in range(per_block):
                columns = pl.ds(offset(shift, side, j), LANES)
                for i in range(CHUNKS):
                    piece = hidden_ref[i * rows : (i + 1) * rows, columns].astype(jnp.float32)
                    piece = piece * inverses[i] * gain_ref[:, columns]
                    start = (side * per_block + j) * half_rows + i * rows
                    outs[shift][start : start + rows, :] = piece.astype(jnp.bfloat16)
        leaving.append(pltpu.make_async_copy(outs[shift], blocks_any[shift], out_sems.at[shift]))
        leaving[-1].start()
    leaving.append(pltpu.make_async_copy(outs[0], own_any, out_sems.at[GROUPS]))
    leaving[-1].start()
    for copy in leaving:
        copy.wait()
    unpacking.wait()


def fetch_kernel(from_any, to_ref, sem):
    copy = pltpu.make_async_copy(from_any, to_ref, sem)
    copy.start()
    copy.wait()


def project_kernel(*refs):
    blocks = refs[: 2 * GROUPS]
    near_key, near_value, far = refs[2 * GROUPS : 2 * GROUPS + 3]
    outs = refs[2 * GROUPS + 3 : 3 * GROUPS + 3]
    query_ref, lhs_ref = refs[3 * GROUPS + 3 :]
    depth = near_key.shape[0]
    pieces = 2 * depth // LANES
    half_rows = (lhs_ref.shape[0] - 16) // (2 * GROUPS)
    rows = 2 * half_rows
    tails = [None] * len(blocks)
    for i, block in enumerate(blocks):
        for j in range(pieces):
            lhs_ref[i * half_rows : (i + 1) * half_rows, j * LANES : (j + 1) * LANES] = block[
                j * half_rows : (j + 1) * half_rows, :
            ]
        tail = block[pieces * half_rows : pieces * half_rows + pieces, :].astype(jnp.float32)
        tails[i] = jnp.concatenate([tail[j : j + 1] for j in range(pieces)], 1)
    tails.append(jnp.zeros((16 - len(tails), 2 * depth), jnp.float32))
    lines = query_ref.shape[0] // GROUPS
    for group in range(GROUPS):
        block = blocks[2 * group]
        query_ref[group * lines : (group + 1) * lines, :] = block[block.shape[0] - lines :, :]
    total = GROUPS * rows
    lhs_ref[total : total + 16, :] = jnp.concatenate(tails, 0).astype(jnp.bfloat16)

    def product(near, at):
        return jnp.dot(
            lhs_ref[:, :depth], near[...], preferred_element_type=jnp.float32
        ) + jnp.dot(lhs_ref[:, depth:], far[at, :], preferred_element_type=jnp.float32)

    keys = product(near_key, slice(0, depth))
    values = product(near_value, slice(depth, 2 * depth))
    high = keys.astype(jnp.bfloat16).astype(jnp.float32)
    low = keys - high
    columns = []
    for array in (high, low, values):
        for j in range(array.shape[1] // LANES):
            columns.append(array[:, j * LANES : (j + 1) * LANES])
    for group in range(GROUPS):
        for t, column in enumerate(columns):
            outs[group][t * rows : (t + 1) * rows, :] = column[
                group * rows : (group + 1) * rows
            ].astype(jnp.bfloat16)
        ends = [c[total + 2 * group : total + 2 * group + 2] for c in columns]
        ends.append(jnp.zeros((16 - 2 * len(columns), LANES), jnp.float32))
        outs[group][len(columns) * rows :, :] = jnp.concatenate(ends, 0).astype(jnp.bfloat16)


def head_queries(parts, head, width):
    sharing = QUERY_HEADS // KEY_VALUE_HEADS
    lines = sharing * width // HEAD_SIZE
    each = parts[0].shape[0] // GROUPS
    found = []
    for group in range(GROUPS):
        for part in parts:
            tiles = part[group * each : (group + 1) * each, :].astype(jnp.float32)
            for start in range(head * sharing, each, lines):
                found.append(tiles[start : start + sharing])
    return jnp.concatenate(found, 0).astype(jnp.bfloat16)


def times_transposed(a, b):
    return lax.dot_general(a, b, (((1,), (1,)), ((), ())), preferred_element_type=jnp.float32)


def loaded_kernel(place_ref, table_ref, split_ref, *refs):
    parts = refs[:PAIR]
    key_ref, value_ref, top_ref, total_ref, numer_ref, query_ref = refs[PAIR:]
    ctx = place_ref[1]
    slots, page, width = key_ref.shape
    heads = width // HEAD_SIZE
    split = split_ref[0]
    live = []
    for s in range(slots):
        hit = jnp.int32(0)
        for p in range(table_ref.shape[0]):
            hit = hit | ((table_ref[p] == ctx * slots + s) & (p >= split)).astype(jnp.int32)
        live.append(hit)
    for head in range(heads):
        columns = slice(head * HEAD_SIZE, (head + 1) * HEAD_SIZE)
        queries = head_queries(parts, head, width)
        count = queries.shape[0]
        query_ref[head * count : (head + 1) * count, :] = queries
        scores = [
            jnp.where(live[s] > 0, times_transposed(queries, key_ref[s, :, columns]) * SCALE, masked_score)
            for s in range(slots)
        ]
        top = scores[0].max(-1, keepdims=True)
        for s in range(1, slots):
            top = jnp.maximum(top, scores[s].max(-1, keepdims=True))
        total = jnp.zeros((count, 1), jnp.float32)
        numer = jnp.zeros((count, HEAD_SIZE), jnp.float32)
        for s in range(slots):
            expos = jnp.where(live[s] > 0, jnp.exp(scores[s] - top), 0.0)
            total += expos.sum(-1, keepdims=True)
            numer += jnp.dot(
                expos.astype(jnp.bfloat16), value_ref[s, :, columns], preferred_element_type=jnp.float32
            )
        rows = slice(head * count, (head + 1) * count)
        top_ref[rows, :] = jnp.broadcast_to(top, (count, LANES))
        total_ref[rows, :] = jnp.broadcast_to(total, (count, LANES))
        numer_ref[rows, :] = numer


def front_kernel(
    place_ref, split_ref, own, *refs
):
    received = refs[: GROUPS - 1]
    (key_bias, value_bias, cosine_ref, sine_ref, query_ref, top_ref, total_ref, numer_ref) = refs[
        GROUPS - 1 : GROUPS + 7
    ]
    front_key, front_value = refs[GROUPS + 7 : GROUPS + 9]
    outs = refs[GROUPS + 9 :]
    core, ctx = place_ref[0], place_ref[1]
    rows, width = front_key.shape
    half_rows = rows // 2
    heads = width // HEAD_SIZE
    sharing = QUERY_HEADS // KEY_VALUE_HEADS
    count = query_ref.shape[0] // heads
    own_queries = count // sharing // (GROUPS * PAIR)
    visible = ctx < split_ref[0]

    def summed(start, size):
        value = own[start : start + size, :].astype(jnp.float32)
        for ref in received:
            value += ref[start : start + size, :].astype(jnp.float32)
        return value

    ends = summed(3 * heads * rows, 16)
    row_query = lax.broadcasted_iota(jnp.int32, (count, 16), 0) // sharing
    query_position = (ctx ^ (row_query // own_queries)) * own_queries + row_query % own_queries
    end_column = lax.broadcasted_iota(jnp.int32, (count, 16), 1)
    end_position = ctx * 2 + jnp.where(end_column == 0, core, 1 - core)
    end_seen = (end_column < 2) & (end_position <= query_position)
    pad = jnp.zeros((14, HEAD_SIZE), jnp.float32)
    for head in range(heads):
        columns = slice(head * HEAD_SIZE, (head + 1) * HEAD_SIZE)
        raw = summed(head * rows, rows) + summed((heads + head) * rows, rows)
        value = (summed((2 * heads + head) * rows, rows) + value_bias[:, columns]).astype(jnp.bfloat16)
        end_raw = ends[2 * head : 2 * head + 2] + ends[2 * (heads + head) : 2 * (heads + head) + 2]
        end_value = ends[2 * (2 * heads + head) : 2 * (2 * heads + head) + 2] + value_bias[:, columns]
        end_raw = jnp.concatenate([end_raw + key_bias[:, columns], pad], 0)
        end_value = jnp.concatenate([end_value, pad], 0).astype(jnp.bfloat16)
        raw = raw + key_bias[:, columns]

        def rotated(k, part):
            turned = pltpu.roll(k, HEAD_SIZE // 2, 1)
            return (k * cosine_ref[part, :] + turned * sine_ref[part, :]).astype(jnp.bfloat16)

        key = rotated(raw, slice(0, rows))
        end_key = rotated(end_raw, slice(rows, rows + 16))
        for half in range(2):
            to = pl.ds(pl.multiple_of(lax.rem(core + half, 2) * half_rows, half_rows), half_rows)
            front_key[to, columns] = key[half * half_rows : (half + 1) * half_rows]
            front_value[to, columns] = value[half * half_rows : (half + 1) * half_rows]
        part = slice(head * count, (head + 1) * count)
        queries = query_ref[part, :]
        scores = jnp.where(visible, times_transposed(queries, key) * SCALE, masked_score)
        end_scores = jnp.where(end_seen, times_transposed(queries, end_key) * SCALE, masked_score)
        old_top = top_ref[part, :]
        top = jnp.maximum(scores.max(-1, keepdims=True), end_scores.max(-1, keepdims=True))
        top = jnp.maximum(old_top, top)
        factor = jnp.exp(old_top - top)
        expos = jnp.where(visible, jnp.exp(scores - top), 0.0)
        end_expos = jnp.where(end_seen, jnp.exp(end_scores - top[:, :16]), 0.0)
        total = total_ref[part, :] * factor + (
            expos.sum(-1, keepdims=True) + end_expos.sum(-1, keepdims=True)
        )
        numer = (
            numer_ref[part, :] * factor
            + jnp.dot(expos.astype(jnp.bfloat16), value, preferred_element_type=jnp.float32)
            + jnp.dot(end_expos.astype(jnp.bfloat16), end_value, preferred_element_type=jnp.float32)
        )
        stats = (kept_stats(top[:, 0:1], total[:, 0:1]), sent_stats(top[:, 0:1], total[:, 0:1]))
        each = own_queries * sharing
        for slot in range(GROUPS * PAIR):
            start = (slot // PAIR * 2 * heads + head) * each
            at = slice(slot * each, (slot + 1) * each)
            out = outs[slot % PAIR]
            out[start : start + each, :] = numer[at].astype(out.dtype)
            out[start + heads * each : start + (heads + 1) * each, :] = stats[slot % PAIR][at]


def kept_stats(top, total):
    lane = lax.broadcasted_iota(jnp.int32, (top.shape[0], LANES), 1)
    return jnp.where(lane < LANES // 2, top, total)


def sent_stats(top, total):
    terms = []
    for rest, count in ((top, 3), (total, 2)):
        for _ in range(count):
            term = rest.astype(jnp.bfloat16).astype(jnp.float32)
            terms.append(term)
            rest = rest - term
    part = lax.broadcasted_iota(jnp.int32, (top.shape[0], LANES), 1) // 16
    stats = jnp.broadcast_to(terms[-1], part.shape)
    for i, term in enumerate(terms[:-1]):
        stats = jnp.where(part == i, term, stats)
    return stats.astype(jnp.bfloat16)


def merged(kept, others, start, rows):
    half = LANES // 2
    stats = kept[start + rows : start + 2 * rows, :]
    tops, totals = [stats[:, 0:1]], [stats[:, half : half + 1]]
    numers = [kept[start : start + rows, :]]
    for other in others:
        terms = other[start + rows : start + 2 * rows, :].astype(jnp.float32)
        tops.append((terms[:, 0:1] + terms[:, 16:17]) + terms[:, 32:33])
        totals.append(terms[:, 48:49] + terms[:, 64:65])
        numers.append(other[start : start + rows, :].astype(jnp.float32))
    top = functools.reduce(jnp.maximum, tops)
    factors = [jnp.exp(t - top) for t in tops]
    total = sum(f * t for f, t in zip(factors, totals))
    numer = sum(f * n for f, n in zip(factors, numers))
    return numer, top, total


def merge_kernel(kept, other, keep_ref, *send_refs):
    each = keep_ref.shape[0]
    rows = each // 2
    for slot in range(GROUPS):
        numer, top, total = merged(kept, [other], slot * each, rows)
        if slot == 0:
            keep_ref[:rows, :] = numer
            keep_ref[rows:, :] = kept_stats(top, total)
        else:
            send_refs[slot - 1][:rows, :] = numer.astype(jnp.bfloat16)
            send_refs[slot - 1][rows:, :] = sent_stats(top, total)


def last_kernel(kept, *refs):
    others, out_ref = refs[:-1], refs[-1]
    numer, _, total = merged(kept, others, 0, kept.shape[0] // 2)
    result = numer / total
    queries, width = out_ref.shape
    sharing = QUERY_HEADS // KEY_VALUE_HEADS
    heads = width // HEAD_SIZE // sharing
    lines = []
    for i in range(queries):
        starts = [(h * queries + i) * sharing + g for h in range(heads) for g in range(sharing)]
        lines.append(jnp.concatenate([result[s : s + 1] for s in starts], 1))
    out_ref[...] = jnp.concatenate(lines, 0).astype(jnp.bfloat16)


def exchange_plan(
    hidden,
    suffix_hidden,
    norm_gain,
    key_matrix,
    value_matrix,
    key_offset_bias,
    value_offset_bias,
    suffix_query_rows,
    slot_keys,
    slot_values,
    page_slot_table,
    split_page,
):
    n_ctx = GROUPS * PAIR
    ctx = lax.axis_index("ctx").astype(jnp.int32)
    core = lax.axis_index("tp").astype(jnp.int32)
    place = jnp.stack([core, ctx])
    rows, features = hidden.shape
    half_rows = rows // 2
    width = key_matrix.shape[1]
    query_width = suffix_query_rows.shape[1]
    prefix_len = page_slot_table.shape[0] * slot_keys.shape[1]
    smem = pl.BlockSpec(memory_space=pltpu.SMEM)
    vmem = pl.BlockSpec(memory_space=pltpu.VMEM)
    params = pltpu.CompilerParams(vmem_limit_bytes=48 * 1024 * 1024)

    def move(array, target):
        pairs = []
        for c in range(n_ctx):
            for t in range(2):
                to_c, to_t = target(c, t)
                pairs.append((c * 2 + t, to_c * 2 + to_t))
        return lax.ppermute(array, ("ctx", "tp"), pairs)

    def along(shift):
        return lambda c, t: ((c // PAIR ^ shift) * PAIR + c % PAIR, t)

    def beside(c, t):
        return (c ^ 1, t)

    def sibling(c, t):
        return (c, 1 - t)

    hbm = pl.BlockSpec(memory_space=pltpu.HBM)
    pieces = features // GROUPS // LANES
    own_queries = suffix_query_rows.shape[0]
    lines = query_width // LANES
    block_rows = pieces * half_rows + pieces + own_queries * lines
    *blocks, packed, own = pl.pallas_call(
        norm_kernel,
        in_specs=[hbm] * 6,
        out_specs=[hbm] * (GROUPS + 2),
        out_shape=[jax.ShapeDtypeStruct((block_rows, LANES), jnp.bfloat16)] * GROUPS
        + [
            jax.ShapeDtypeStruct((2 * key_matrix.shape[0], width), jnp.bfloat16),
            jax.ShapeDtypeStruct((block_rows, LANES), jnp.bfloat16),
        ],
        scratch_shapes=[
            pltpu.VMEM((half_rows, features), jnp.bfloat16),
            pltpu.VMEM(suffix_hidden.shape, jnp.bfloat16),
            pltpu.VMEM((1, features), jnp.float32),
            pltpu.VMEM(suffix_query_rows.shape, jnp.bfloat16),
            pltpu.VMEM((2 * key_matrix.shape[0], width), jnp.bfloat16),
            pltpu.VMEM((1, features), jnp.float32),
        ]
        + [pltpu.VMEM((block_rows, LANES), jnp.bfloat16)] * GROUPS
        + [
            pltpu.SemaphoreType.DMA((CHUNKS + 6,)),
            pltpu.SemaphoreType.DMA((GROUPS + 1,)),
        ],
        compiler_params=pltpu.CompilerParams(vmem_limit_bytes=60 * 1024 * 1024),
        cost_estimate=pl.CostEstimate(
            flops=4 * half_rows * features, bytes_accessed=4 * half_rows * features, transcendentals=0
        ),
        name="norm_rows",
    )(
        suffix_query_rows,
        hidden,
        suffix_hidden,
        norm_gain.reshape(1, features),
        key_matrix,
        value_matrix,
    )
    far = move(packed, beside)

    mine = {s: move(blocks[s], along(s)) for s in far_first()}
    theirs = {s: move(mine.get(s, blocks[0]), sibling) for s in [0] + far_first()}
    mine[0] = pl.pallas_call(
        fetch_kernel,
        in_specs=[hbm],
        out_specs=vmem,
        out_shape=jax.ShapeDtypeStruct(own.shape, own.dtype),
        scratch_shapes=[pltpu.SemaphoreType.DMA],
        compiler_params=params,
        cost_estimate=pl.CostEstimate(flops=0, bytes_accessed=16 * 1024 * 1024, transcendentals=0),
        name="fetch_own",
    )(own)
    lhs = [part[s] for s in range(GROUPS) for part in (mine, theirs)]

    inverse_freq = rope_base ** (
        -(jnp.arange(HEAD_SIZE // 2, dtype=jnp.float32) * (2.0 / HEAD_SIZE))
    )
    row = jnp.arange(rows + 16, dtype=jnp.int32)
    front_position = ctx * rows + (row + core * half_rows) % rows
    end_position = prefix_len + ctx * 2 + jnp.where(row == rows, core, 1 - core)
    position = jnp.where(row < rows, front_position, end_position)
    angles = position.astype(jnp.float32)[:, None] * inverse_freq[None, :]
    cosine, sine = jnp.cos(angles), jnp.sin(angles)
    cosine = jnp.concatenate([cosine, cosine], 1)
    sine = jnp.concatenate([-sine, sine], 1)

    part_rows = 3 * (width // LANES) * rows + 16
    *partials, own_tiles = pl.pallas_call(
        project_kernel,
        in_specs=[vmem] * (2 * GROUPS + 3),
        out_specs=[vmem] * (GROUPS + 1),
        out_shape=[jax.ShapeDtypeStruct((part_rows, LANES), jnp.bfloat16)] * GROUPS
        + [jax.ShapeDtypeStruct((GROUPS * own_queries * lines, LANES), jnp.bfloat16)],
        scratch_shapes=[pltpu.VMEM((GROUPS * rows + 16, PAIR * features // n_ctx), jnp.bfloat16)],
        compiler_params=params,
        cost_estimate=pl.CostEstimate(flops=2 * GROUPS * rows * 2 * width * features // GROUPS, bytes_accessed=6 * 1024 * 1024, transcendentals=0),
        name="project",
    )(*lhs, key_matrix, value_matrix, far)
    received = [move(partials[s], along(s)) for s in far_first()[1:] + far_first()[:1]]
    beside_tiles = move(own_tiles, beside)

    states = n_ctx * own_queries * query_width // HEAD_SIZE
    state = jax.ShapeDtypeStruct((states, LANES), jnp.float32)
    top, total, numer, queries = pl.pallas_call(
        loaded_kernel,
        in_specs=[smem, smem, smem] + [vmem] * (PAIR + 2),
        out_specs=[vmem] * 4,
        out_shape=[state] * 3 + [jax.ShapeDtypeStruct((states, LANES), jnp.bfloat16)],
        compiler_params=params,
        cost_estimate=pl.CostEstimate(
            flops=4 * states * slot_keys.shape[0] * slot_keys.shape[1] * HEAD_SIZE,
            bytes_accessed=4 * slot_keys.size,
            transcendentals=states * slot_keys.shape[0] * slot_keys.shape[1],
        ),
        name="loaded_attention",
    )(place, page_slot_table, split_page, own_tiles, beside_tiles, slot_keys, slot_values)


    def payloads(size):
        return [jax.ShapeDtypeStruct((size, LANES), kind) for kind in (jnp.float32, jnp.bfloat16)]

    row_shape = jax.ShapeDtypeStruct((rows, width), jnp.bfloat16)
    front_key, front_value, kept, sent = pl.pallas_call(
        front_kernel,
        in_specs=[smem, smem] + [vmem] * (GROUPS + 8),
        out_specs=[vmem] * 4,
        out_shape=[row_shape] * 2 + payloads(states),
        compiler_params=params,
        cost_estimate=pl.CostEstimate(flops=4 * states * rows * HEAD_SIZE, bytes_accessed=2 * 1024 * 1024, transcendentals=states * rows),
        name="front_attention",
    )(
        place,
        split_page,
        partials[0],
        *received,
        key_offset_bias.reshape(1, width),
        value_offset_bias.reshape(1, width),
        cosine,
        sine,
        queries,
        top,
        total,
        numer,
    )
    kept, *sent = pl.pallas_call(
        merge_kernel,
        in_specs=[vmem] * 2,
        out_specs=[vmem] * GROUPS,
        out_shape=payloads(states // GROUPS) + payloads(states // GROUPS)[1:] * (GROUPS - 2),
        compiler_params=params,
        name="merge",
    )(kept, move(sent, beside))
    attended = pl.pallas_call(
        last_kernel,
        in_specs=[vmem] * GROUPS,
        out_specs=vmem,
        out_shape=jax.ShapeDtypeStruct((own_queries, query_width), jnp.bfloat16),
        compiler_params=params,
        name="finish",
    )(kept, *[move(sent[s - 1], along(s)) for s in range(1, GROUPS)])
    return (front_key, front_value, attended)


def solution(mesh):
    per_device = exchange_plan if mesh.shape["ctx"] == GROUPS * PAIR else gathered_plan
    return jax.shard_map(
        per_device,
        mesh=mesh,
        in_specs=(
            P(("req", "ctx"), None),
            P(("req", "ctx"), None),
            P(),
            P("ctx", "tp"),
            P("ctx", "tp"),
            P("tp"),
            P("tp"),
            P(("req", "ctx"), "tp"),
            P(("req", "ctx"), None, "tp"),
            P(("req", "ctx"), None, "tp"),
            P("req"),
            P("req"),
        ),
        out_specs=(P(("req", "ctx"), "tp"), P(("req", "ctx"), "tp"), P(("req", "ctx"), "tp")),
        check_vma=False,
    )
```

profile of v0, /device:TPU:0, one launch (start us, length us, event | category | flops | bytes accessed | tf_op | source)
XLA Modules:
  0.0 72.0 jit_solution(8830614358803929693)
XLA Ops:
  0.7 3.4 %norm_rows.1 = (bf16[1072,128]{1,0:T(8,128)(2,1)}, bf16[1072,128]{1,0:T(8,128)(2,1)}, bf16[1072,128]{1,0:T(8,128)(2,1)}, bf16[1072,128]{1,0:T(8,128)(2,1)}, bf16...) custom-call(bf16[2,2048]{1,0:T(2,128)(2,1)} %query_any.1, bf16[128,8192]{1,0:T(8,128)(2,1)} %hidden_any.1, ...), custom_call_target="tpu_custom_call" | custom-call | flops 2097152 | bytes 2097152 | tf_op jit(solution)/shard_map/norm_rows/pallas_call | solution.py:550
  4.1 3.0 %collective-permute-start.7 = (bf16[2048,256]{1,0:T(8,128)(2,1)}, bf16[2048,256]{1,0:T(8,128)(2,1)S(1)}, u32[]{:S(2)}, u32[]{:S(2)}) collective-permute-start(bf16[2048,256]{1,0:T(8,128)(2,1)} %get-tuple-element.31), channel_id=1, source_target_pairs={{0,2},{1,3},{2,0},{3,1},{4,6},{5,7},{6,4},{7,5},{8,10},{9,11},{10,... | collective-permute-start | bytes 3145736 | tf_op jit(solution)/shard_map/ppermute | solution.py:534
  7.1 1.6 %collective-permute-start.1 = (bf16[1072,128]{1,0:T(8,128)(2,1)}, bf16[1072,128]{1,0:T(8,128)(2,1)S(1)}, u32[]{:S(2)}, u32[]{:S(2)}) collective-permute-start(bf16[1072,128]{1,0:T(8,128)(2,1)} %get-tuple-element.28), channel_id=1, source_target_pairs={{0,4},{1,5},{2,6},{3,7},{4,0},{5,1},{6,2},{7,3},{8,12},{9,13},{10,... | collective-permute-start | bytes 823304 | tf_op jit(solution)/shard_map/ppermute | solution.py:534
  8.7 2.6 %collective-permute-start.3 = (bf16[1072,128]{1,0:T(8,128)(2,1)}, bf16[1072,128]{1,0:T(8,128)(2,1)S(1)}, u32[]{:S(2)}, u32[]{:S(2)}) collective-permute-start(bf16[1072,128]{1,0:T(8,128)(2,1)} %get-tuple-element.29), channel_id=1, source_target_pairs={{0,8},{1,9},{2,10},{3,11},{4,12},{5,13},{6,14},{7,15},{8,0},{9,1},... | collective-permute-start | bytes 823304 | tf_op jit(solution)/shard_map/ppermute | solution.py:534
  11.5 8.8 %collective-permute-done.1.refs_2_ = bf16[1072,128]{1,0:T(8,128)(2,1)S(1)} collective-permute-done((bf16[1072,128]{1,0:T(8,128)(2,1)}, bf16[1072,128]{1,0:T(8,128)(2,1)S(1)}, u32[]{:S(2)}, u32[]{:S(2)}) %collective-permute-start.1) | collective-permute-done | bytes 274464 | tf_op jit(solution)/shard_map/ppermute | solution.py:534
  20.3 10.7 %collective-permute-done.3.refs_4_ = bf16[1072,128]{1,0:T(8,128)(2,1)S(1)} collective-permute-done((bf16[1072,128]{1,0:T(8,128)(2,1)}, bf16[1072,128]{1,0:T(8,128)(2,1)S(1)}, u32[]{:S(2)}, u32[]{:S(2)}) %collective-permute-start.3) | collective-permute-done | bytes 274464 | tf_op jit(solution)/shard_map/ppermute | solution.py:534
  31.0 0.5 collective-permute-start.6
  31.6 1.0 %copy-done.2 = bf16[1072,128]{1,0:T(8,128)(2,1)S(1)} copy-done((bf16[1072,128]{1,0:T(8,128)(2,1)S(1)}, bf16[1072,128]{1,0:T(8,128)(2,1)}, u32[]{:S(2)}) %copy-start.2) | copy-done | bytes 274456
  33.0 1.4 %project.1 = (bf16[784,128]{1,0:T(8,128)(2,1)S(1)}, bf16[784,128]{1,0:T(8,128)(2,1)S(1)}, bf16[784,128]{1,0:T(8,128)(2,1)S(1)}, bf16[784,128]{1,0:T(8,128)(2,1)S(1)}, bf16[128,128]{1,0:T(8,128)(2,1)S(1)}) custom-call(bf16[1072,128]{1,0:T(8,128)(2,1)S(1)} %fetch_own.1.refs_0_, bf16[1072,128]{1,0:T(8,128)(2,1)S(1)} %collective-permute-done.refs_1_, ...), custom_call_target="tpu_custom_call" | custom-call | flops 1073741824 | bytes 6291456 | tf_op jit(solution)/shard_map/project/pallas_call | solution.py:614
  34.4 5.4 %collective-permute-start.10 = (bf16[784,128]{1,0:T(8,128)(2,1)S(1)}, bf16[784,128]{1,0:T(8,128)(2,1)S(1)}, u32[]{:S(2)}, u32[]{:S(2)}) collective-permute-start(bf16[784,128]{1,0:T(8,128)(2,1)S(1)} %get-tuple-element.35), channel_id=1, source_target_pairs={{0,8},{1,9},{2,10},{3,11},{4,12},{5,13},{6,14},{7,15},{8,0},{9,1},... | collective-permute-start | bytes 602120 | tf_op jit(solution)/shard_map/ppermute | solution.py:534
  39.8 1.4 %collective-permute-start.8 = (bf16[784,128]{1,0:T(8,128)(2,1)S(1)}, bf16[784,128]{1,0:T(8,128)(2,1)S(1)}, u32[]{:S(2)}, u32[]{:S(2)}) collective-permute-start(bf16[784,128]{1,0:T(8,128)(2,1)S(1)} %get-tuple-element.33), channel_id=1, source_target_pairs={{0,12},{1,13},{2,14},{3,15},{4,8},{5,9},{6,10},{7,11},{8,4},{9,5},... | collective-permute-start | bytes 602120 | tf_op jit(solution)/shard_map/ppermute | solution.py:534
  41.2 0.6 collective-permute-start.11
  42.6 2.7 %collective-permute-done.11.refs_1_ = bf16[128,128]{1,0:T(8,128)(2,1)S(1)} collective-permute-done((bf16[128,128]{1,0:T(8,128)(2,1)S(1)}, bf16[128,128]{1,0:T(8,128)(2,1)S(1)}, u32[]{:S(2)}, u32[]{:S(2)}) %collective-permute-start.11) | collective-permute-done | bytes 32800 | tf_op jit(solution)/shard_map/ppermute | solution.py:534
  45.2 1.4 %loaded_attention.1 = (f32[256,128]{1,0:T(8,128)S(1)}, f32[256,128]{1,0:T(8,128)S(1)}, f32[256,128]{1,0:T(8,128)S(1)}, bf16[256,128]{1,0:T(8,128)(2,1)S(1)}) custom-call(s32[2]{0:T(128)S(1)} %pad_add_fusion.place_ref, s32[16]{0:T(128)S(1)} %copy-done.7, s32[1]{0:T(128)S(6)} %copy.15.split_ref, bf16[128,128]{1,0:T(8,128)(2,1)S(1)} %get-tuple-element.36.refs_0_, ...), custom_call_target="tpu_custom_call" | custom-call | flops 67108864 | bytes 524288 | tf_op jit(solution)/shard_map/loaded_attention/pallas_call | solution.py:630
  46.6 7.7 %collective-permute-done.10.refs_2_ = bf16[784,128]{1,0:T(8,128)(2,1)S(1)} collective-permute-done((bf16[784,128]{1,0:T(8,128)(2,1)S(1)}, bf16[784,128]{1,0:T(8,128)(2,1)S(1)}, u32[]{:S(2)}, u32[]{:S(2)}) %collective-permute-start.10) | collective-permute-done | bytes 200736 | tf_op jit(solution)/shard_map/ppermute | solution.py:534
  54.3 1.1 %collective-permute-done.9.refs_1_ = bf16[784,128]{1,0:T(8,128)(2,1)S(1)} collective-permute-done((bf16[784,128]{1,0:T(8,128)(2,1)S(1)}, bf16[784,128]{1,0:T(8,128)(2,1)S(1)}, u32[]{:S(2)}, u32[]{:S(2)}) %collective-permute-start.9) | collective-permute-done | bytes 200736 | tf_op jit(solution)/shard_map/ppermute | solution.py:534
  55.3 2.1 %front_attention.1 = (bf16[128,256]{1,0:T(8,128)(2,1)}, bf16[128,256]{1,0:T(8,128)(2,1)}, f32[256,128]{1,0:T(8,128)S(1)}, bf16[256,128]{1,0:T(8,128)(2,1)S(1)}) custom-call(s32[2]{0:T(128)S(1)} %pad_add_fusion.place_ref, s32[1]{0:T(128)S(6)} %copy.15.split_ref, bf16[784,128]{1,0:T(8,128)(2,1)S(1)} %get-tuple-element.32.own, ...), custom_call_target="tpu_custom_call" | custom-call | flops 16777216 | bytes 2097152 | tf_op jit(solution)/shard_map/front_attention/pallas_call | solution.py:649
  57.4 0.5 collective-permute-start.12
  57.9 3.7 %collective-permute-done.12.other = bf16[256,128]{1,0:T(8,128)(2,1)S(1)} collective-permute-done((bf16[256,128]{1,0:T(8,128)(2,1)S(1)}, bf16[256,128]{1,0:T(8,128)(2,1)S(1)}, u32[]{:S(2)}, u32[]{:S(2)}) %collective-permute-start.12) | collective-permute-done | bytes 65568 | tf_op jit(solution)/shard_map/ppermute | solution.py:534
  62.0 3.6 %collective-permute-start.13 = (bf16[64,128]{1,0:T(8,128)(2,1)S(1)}, bf16[64,128]{1,0:T(8,128)(2,1)S(1)}, u32[]{:S(2)}, u32[]{:S(2)}) collective-permute-start(bf16[64,128]{1,0:T(8,128)(2,1)S(1)} %get-tuple-element.46), channel_id=1, source_target_pairs={{0,4},{1,5},{2,6},{3,7},{4,0},{5,1},{6,2},{7,3},{8,12},{9,13},{10,... | collective-permute-start | bytes 49160 | tf_op jit(solution)/shard_map/ppermute | solution.py:534
  65.6 2.4 %collective-permute-start.15 = (bf16[64,128]{1,0:T(8,128)(2,1)S(1)}, bf16[64,128]{1,0:T(8,128)(2,1)S(1)}, u32[]{:S(2)}, u32[]{:S(2)}) collective-permute-start(bf16[64,128]{1,0:T(8,128)(2,1)S(1)} %get-tuple-element.48), channel_id=1, source_target_pairs={{0,12},{1,13},{2,14},{3,15},{4,8},{5,9},{6,10},{7,11},{8,4},{9,5},... | collective-permute-start | bytes 49160 | tf_op jit(solution)/shard_map/ppermute | solution.py:534
  68.1 2.2 %collective-permute-done.14.refs_1_ = bf16[64,128]{1,0:T(8,128)(2,1)S(1)} collective-permute-done((bf16[64,128]{1,0:T(8,128)(2,1)S(1)}, bf16[64,128]{1,0:T(8,128)(2,1)S(1)}, u32[]{:S(2)}, u32[]{:S(2)}) %collective-permute-start.14) | collective-permute-done | bytes 16416 | tf_op jit(solution)/shard_map/ppermute | solution.py:534
  70.3 0.9 %collective-permute-done.15.refs_2_ = bf16[64,128]{1,0:T(8,128)(2,1)S(1)} collective-permute-done((bf16[64,128]{1,0:T(8,128)(2,1)S(1)}, bf16[64,128]{1,0:T(8,128)(2,1)S(1)}, u32[]{:S(2)}, u32[]{:S(2)}) %collective-permute-start.15) | collective-permute-done | bytes 16416 | tf_op jit(solution)/shard_map/ppermute | solution.py:534
  71.2 0.8 %finish.1 = bf16[2,2048]{1,0:T(2,128)(2,1)} custom-call(f32[64,128]{1,0:T(8,128)S(1)} %get-tuple-element.45.kept, bf16[64,128]{1,0:T(8,128)(2,1)S(1)} %collective-permute-done.13.refs_0_, bf16[64,128]{1,0:T(8,128)(2,1)S(1)} %collective-permute-done.14.refs_1_, bf16[64,128]{1,0:T(8,128)(2,1)S(1)} %collective-permute-done.15.refs_2_), custom_call_target="tpu_custom_call" | custom-call | tf_op jit(solution)/shard_map/finish/pallas_call | solution.py:679
  (36 shorter events, 1.2 us)
Async XLA Ops:
  0.6 32.4 %copy-start = (bf16[1024,256]{1,0:T(8,128)(2,1)S(1)}, bf16[1024,256]{1,0:T(8,128)(2,1)}, u32[]{:S(2)}) copy-start(bf16[1024,256]{1,0:T(8,128)(2,1)} %refs_8_.1) | copy-start | bytes 1572868
  0.6 32.4 %copy-start.1 = (bf16[1024,256]{1,0:T(8,128)(2,1)S(1)}, bf16[1024,256]{1,0:T(8,128)(2,1)}, u32[]{:S(2)}) copy-start(bf16[1024,256]{1,0:T(8,128)(2,1)} %refs_9_.1) | copy-start | bytes 1572868
  4.1 28.9 %collective-permute-start.7 = (bf16[2048,256]{1,0:T(8,128)(2,1)}, bf16[2048,256]{1,0:T(8,128)(2,1)S(1)}, u32[]{:S(2)}, u32[]{:S(2)}) collective-permute-start(bf16[2048,256]{1,0:T(8,128)(2,1)} %get-tuple-element.31), channel_id=1, source_target_pairs={{0,2},{1,3},{2,0},{3,1},{4,6},{5,7},{6,4},{7,5},{8,10},{9,11},{10,... | collective-permute-start | bytes 3145736 | tf_op jit(solution)/shard_map/ppermute | solution.py:534
  7.1 13.2 %collective-permute-start.1 = (bf16[1072,128]{1,0:T(8,128)(2,1)}, bf16[1072,128]{1,0:T(8,128)(2,1)S(1)}, u32[]{:S(2)}, u32[]{:S(2)}) collective-permute-start(bf16[1072,128]{1,0:T(8,128)(2,1)} %get-tuple-element.28), channel_id=1, source_target_pairs={{0,4},{1,5},{2,6},{3,7},{4,0},{5,1},{6,2},{7,3},{8,12},{9,13},{10,... | collective-permute-start | bytes 823304 | tf_op jit(solution)/shard_map/ppermute | solution.py:534
  8.7 22.4 %collective-permute-start.3 = (bf16[1072,128]{1,0:T(8,128)(2,1)}, bf16[1072,128]{1,0:T(8,128)(2,1)S(1)}, u32[]{:S(2)}, u32[]{:S(2)}) collective-permute-start(bf16[1072,128]{1,0:T(8,128)(2,1)} %get-tuple-element.29), channel_id=1, source_target_pairs={{0,8},{1,9},{2,10},{3,11},{4,12},{5,13},{6,14},{7,15},{8,0},{9,1},... | collective-permute-start | bytes 823304 | tf_op jit(solution)/shard_map/ppermute | solution.py:534
  11.2 19.8 %collective-permute-start.5 = (bf16[1072,128]{1,0:T(8,128)(2,1)}, bf16[1072,128]{1,0:T(8,128)(2,1)S(1)}, u32[]{:S(2)}, u32[]{:S(2)}) collective-permute-start(bf16[1072,128]{1,0:T(8,128)(2,1)} %get-tuple-element.30), channel_id=1, source_target_pairs={{0,12},{1,13},{2,14},{3,15},{4,8},{5,9},{6,10},{7,11},{8,4},{9,5},... | collective-permute-start | bytes 823304 | tf_op jit(solution)/shard_map/ppermute | solution.py:534
  11.5 21.5 %collective-permute-start = (bf16[1072,128]{1,0:T(8,128)(2,1)}, bf16[1072,128]{1,0:T(8,128)(2,1)S(1)}, u32[]{:S(2)}, u32[]{:S(2)}) collective-permute-start(bf16[1072,128]{1,0:T(8,128)(2,1)} %get-tuple-element.27), channel_id=1, source_target_pairs={{0,1},{1,0},{2,3},{3,2},{4,5},{5,4},{6,7},{7,6},{8,9},{9,8},{10,11... | collective-permute-start | bytes 823304 | tf_op jit(solution)/shard_map/ppermute | solution.py:534
  20.3 12.7 %collective-permute-start.2 = (bf16[1072,128]{1,0:T(8,128)(2,1)S(1)}, bf16[1072,128]{1,0:T(8,128)(2,1)S(1)}, u32[]{:S(2)}, u32[]{:S(2)}) collective-permute-start(bf16[1072,128]{1,0:T(8,128)(2,1)S(1)} %collective-permute-done.1.refs_2_), channel_id=1, source_target_pairs={{0,1},{1,0},{2,3},{3,2},{4,5},{5,4},{6,7},{7,6},{8,9},{9,8},{10,11... | collective-permute-start | bytes 823304 | tf_op jit(solution)/shard_map/ppermute | solution.py:534
  31.0 2.0 %collective-permute-start.4 = (bf16[1072,128]{1,0:T(8,128)(2,1)S(1)}, bf16[1072,128]{1,0:T(8,128)(2,1)S(1)}, u32[]{:S(2)}, u32[]{:S(2)}) collective-permute-start(bf16[1072,128]{1,0:T(8,128)(2,1)S(1)} %collective-permute-done.3.refs_4_), channel_id=1, source_target_pairs={{0,1},{1,0},{2,3},{3,2},{4,5},{5,4},{6,7},{7,6},{8,9},{9,8},{10,11... | collective-permute-start | bytes 823304 | tf_op jit(solution)/shard_map/ppermute | solution.py:534
  31.0 2.0 %collective-permute-start.6 = (bf16[1072,128]{1,0:T(8,128)(2,1)S(1)}, bf16[1072,128]{1,0:T(8,128)(2,1)S(1)}, u32[]{:S(2)}, u32[]{:S(2)}) collective-permute-start(bf16[1072,128]{1,0:T(8,128)(2,1)S(1)} %collective-permute-done.5.refs_6_), channel_id=1, source_target_pairs={{0,1},{1,0},{2,3},{3,2},{4,5},{5,4},{6,7},{7,6},{8,9},{9,8},{10,11... | collective-permute-start | bytes 823304 | tf_op jit(solution)/shard_map/ppermute | solution.py:534
  31.6 1.0 %copy-start.2 = (bf16[1072,128]{1,0:T(8,128)(2,1)S(1)}, bf16[1072,128]{1,0:T(8,128)(2,1)}, u32[]{:S(2)}) copy-start(bf16[1072,128]{1,0:T(8,128)(2,1)} %get-tuple-element.26.from_any) | copy-start | bytes 823300
  32.9 12.3 %copy-start.3 = (bf16[4,128,256]{2,1,0:T(8,128)(2,1)S(1)}, bf16[4,128,256]{2,1,0:T(8,128)(2,1)}, u32[]{:S(2)}) copy-start(bf16[4,128,256]{2,1,0:T(8,128)(2,1)} %refs_2_.1) | copy-start | bytes 786436
  32.9 12.3 %copy-start.4 = (bf16[4,128,256]{2,1,0:T(8,128)(2,1)S(1)}, bf16[4,128,256]{2,1,0:T(8,128)(2,1)}, u32[]{:S(2)}) copy-start(bf16[4,128,256]{2,1,0:T(8,128)(2,1)} %refs_3_.1) | copy-start | bytes 786436
  32.9 12.3 %copy-start.7 = (s32[16]{0:T(128)S(1)}, s32[16]{0:T(128)}, u32[]{:S(2)}) copy-start(s32[16]{0:T(128)} %table_ref.1) | copy-start | bytes 196
  32.9 22.4 %copy-start.5 = (f32[256]{0:T(256)S(1)}, f32[256]{0:T(256)}, u32[]{:S(2)}) copy-start(f32[256]{0:T(256)} %param.17) | copy-start | bytes 3076
  33.0 22.4 %copy-start.6 = (f32[256]{0:T(256)S(1)}, f32[256]{0:T(256)}, u32[]{:S(2)}) copy-start(f32[256]{0:T(256)} %param.18) | copy-start | bytes 3076
  34.4 19.9 %collective-permute-start.10 = (bf16[784,128]{1,0:T(8,128)(2,1)S(1)}, bf16[784,128]{1,0:T(8,128)(2,1)S(1)}, u32[]{:S(2)}, u32[]{:S(2)}) collective-permute-start(bf16[784,128]{1,0:T(8,128)(2,1)S(1)} %get-tuple-element.35), channel_id=1, source_target_pairs={{0,8},{1,9},{2,10},{3,11},{4,12},{5,13},{6,14},{7,15},{8,0},{9,1},... | collective-permute-start | bytes 602120 | tf_op jit(solution)/shard_map/ppermute | solution.py:534
  39.8 14.5 %collective-permute-start.8 = (bf16[784,128]{1,0:T(8,128)(2,1)S(1)}, bf16[784,128]{1,0:T(8,128)(2,1)S(1)}, u32[]{:S(2)}, u32[]{:S(2)}) collective-permute-start(bf16[784,128]{1,0:T(8,128)(2,1)S(1)} %get-tuple-element.33), channel_id=1, source_target_pairs={{0,12},{1,13},{2,14},{3,15},{4,8},{5,9},{6,10},{7,11},{8,4},{9,5},... | collective-permute-start | bytes 602120 | tf_op jit(solution)/shard_map/ppermute | solution.py:534
  41.1 14.2 %collective-permute-start.9 = (bf16[784,128]{1,0:T(8,128)(2,1)S(1)}, bf16[784,128]{1,0:T(8,128)(2,1)S(1)}, u32[]{:S(2)}, u32[]{:S(2)}) collective-permute-start(bf16[784,128]{1,0:T(8,128)(2,1)S(1)} %get-tuple-element.34), channel_id=1, source_target_pairs={{0,4},{1,5},{2,6},{3,7},{4,0},{5,1},{6,2},{7,3},{8,12},{9,13},{10,... | collective-permute-start | bytes 602120 | tf_op jit(solution)/shard_map/ppermute | solution.py:534
  41.2 4.0 %collective-permute-start.11 = (bf16[128,128]{1,0:T(8,128)(2,1)S(1)}, bf16[128,128]{1,0:T(8,128)(2,1)S(1)}, u32[]{:S(2)}, u32[]{:S(2)}) collective-permute-start(bf16[128,128]{1,0:T(8,128)(2,1)S(1)} %get-tuple-element.36.refs_0_), channel_id=1, source_target_pairs={{0,2},{1,3},{2,0},{3,1},{4,6},{5,7},{6,4},{7,5},{8,10},{9,11},{10,... | collective-permute-start | bytes 98312 | tf_op jit(solution)/shard_map/ppermute | solution.py:534
  57.4 4.3 %collective-permute-start.12 = (bf16[256,128]{1,0:T(8,128)(2,1)S(1)}, bf16[256,128]{1,0:T(8,128)(2,1)S(1)}, u32[]{:S(2)}, u32[]{:S(2)}) collective-permute-start(bf16[256,128]{1,0:T(8,128)(2,1)S(1)} %get-tuple-element.44), channel_id=1, source_target_pairs={{0,2},{1,3},{2,0},{3,1},{4,6},{5,7},{6,4},{7,5},{8,10},{9,11},{10,... | collective-permute-start | bytes 196616 | tf_op jit(solution)/shard_map/ppermute | solution.py:534
  62.0 6.1 %collective-permute-start.13 = (bf16[64,128]{1,0:T(8,128)(2,1)S(1)}, bf16[64,128]{1,0:T(8,128)(2,1)S(1)}, u32[]{:S(2)}, u32[]{:S(2)}) collective-permute-start(bf16[64,128]{1,0:T(8,128)(2,1)S(1)} %get-tuple-element.46), channel_id=1, source_target_pairs={{0,4},{1,5},{2,6},{3,7},{4,0},{5,1},{6,2},{7,3},{8,12},{9,13},{10,... | collective-permute-start | bytes 49160 | tf_op jit(solution)/shard_map/ppermute | solution.py:534
  65.6 4.6 %collective-permute-start.14 = (bf16[64,128]{1,0:T(8,128)(2,1)S(1)}, bf16[64,128]{1,0:T(8,128)(2,1)S(1)}, u32[]{:S(2)}, u32[]{:S(2)}) collective-permute-start(bf16[64,128]{1,0:T(8,128)(2,1)S(1)} %get-tuple-element.47), channel_id=1, source_target_pairs={{0,8},{1,9},{2,10},{3,11},{4,12},{5,13},{6,14},{7,15},{8,0},{9,1},... | collective-permute-start | bytes 49160 | tf_op jit(solution)/shard_map/ppermute | solution.py:534
  65.6 5.5 %collective-permute-start.15 = (bf16[64,128]{1,0:T(8,128)(2,1)S(1)}, bf16[64,128]{1,0:T(8,128)(2,1)S(1)}, u32[]{:S(2)}, u32[]{:S(2)}) collective-permute-start(bf16[64,128]{1,0:T(8,128)(2,1)S(1)} %get-tuple-element.48), channel_id=1, source_target_pairs={{0,12},{1,13},{2,14},{3,15},{4,8},{5,9},{6,10},{7,11},{8,4},{9,5},... | collective-permute-start | bytes 49160 | tf_op jit(solution)/shard_map/ppermute | solution.py:534
where the time goes:
time: 72.2 us; the launch traced here: 72 us
  waiting for transfers between devices  37.8 us (52%)
  starting transfers between devices  21.8 us (30%)
  Pallas kernels  9.38 us (13%)
  between operations  1.47 us (2%)
  local copies, waits for them, and re-layouts  1 us (1%)
    ppermute x16, waiting for transfers between devices, move(): return lax.ppermute(array, ('ctx', 'tp'), pairs)  37.8 us
    ppermute x16, starting transfers between devices, move(): return lax.ppermute(array, ('ctx', 'tp'), pairs)  21.8 us
    pallas_call x1, Pallas kernels, exchange_plan(): pl.pallas_call(norm_kernel, in_specs=[hbm] * 6, out_specs=[hbm] * (GROUPS...  3.41 us
    pallas_call x1, Pallas kernels, exchange_plan(): pl.pallas_call(front_kernel, in_specs=[smem, smem] + [vmem] * (GROUPS + 8...  2.08 us
  transfers between devices with their start and end apart: 16, of which 8 were waited for; matrix products, arithmetic and copies ran while one was open for 1% of the time, Pallas kernels for 2%

commit v1 on v0

--- a/solution.py
+++ b/solution.py
@@ -158,7 +158,7 @@
 
 
 def far_first():
-    return sorted(range(1, GROUPS), key=lambda s: s < GROUPS // 2)
+    return list(range(GROUPS - 1, 0, -1))
 
 
 def norm_kernel(query_any, hidden_any, suffix_any, gain_any, key_any, value_any, *rest):
@@ -271,8 +271,8 @@
         tails[i] = jnp.concatenate([tail[j : j + 1] for j in range(pieces)], 1)
     tails.append(jnp.zeros((16 - len(tails), 2 * depth), jnp.float32))
     lines = query_ref.shape[0] // GROUPS
-    for group in range(GROUPS):
-        block = blocks[2 * group]
+    for place, group in enumerate([0] + far_first()):
+        block = blocks[2 * place]
         query_ref[group * lines : (group + 1) * lines, :] = block[block.shape[0] - lines :, :]
     total = GROUPS * rows
     lhs_ref[total : total + 16, :] = jnp.concatenate(tails, 0).astype(jnp.bfloat16)
@@ -585,7 +585,18 @@
     far = move(packed, beside)
 
     mine = {s: move(blocks[s], along(s)) for s in far_first()}
-    theirs = {s: move(mine.get(s, blocks[0]), sibling) for s in [0] + far_first()}
+    inverse_freq = rope_base ** (
+        -(jnp.arange(HEAD_SIZE // 2, dtype=jnp.float32) * (2.0 / HEAD_SIZE))
+    )
+    row = jnp.arange(rows + 16, dtype=jnp.int32)
+    front_position = ctx * rows + (row + core * half_rows) % rows
+    end_position = prefix_len + ctx * 2 + jnp.where(row == rows, core, 1 - core)
+    position = jnp.where(row < rows, front_position, end_position)
+    angles = position.astype(jnp.float32)[:, None] * inverse_freq[None, :]
+    cosine, sine = jnp.cos(angles), jnp.sin(angles)
+    cosine = jnp.concatenate([cosine, cosine], 1)
+    sine = jnp.concatenate([-sine, sine], 1)
+
     mine[0] = pl.pallas_call(
         fetch_kernel,
         in_specs=[hbm],
@@ -596,19 +607,12 @@
         cost_estimate=pl.CostEstimate(flops=0, bytes_accessed=16 * 1024 * 1024, transcendentals=0),
         name="fetch_own",
     )(own)
-    lhs = [part[s] for s in range(GROUPS) for part in (mine, theirs)]
-
-    inverse_freq = rope_base ** (
-        -(jnp.arange(HEAD_SIZE // 2, dtype=jnp.float32) * (2.0 / HEAD_SIZE))
-    )
-    row = jnp.arange(rows + 16, dtype=jnp.int32)
-    front_position = ctx * rows + (row + core * half_rows) % rows
-    end_position = prefix_len + ctx * 2 + jnp.where(row == rows, core, 1 - core)
-    position = jnp.where(row < rows, front_position, end_position)
-    angles = position.astype(jnp.float32)[:, None] * inverse_freq[None, :]
-    cosine, sine = jnp.cos(angles), jnp.sin(angles)
-    cosine = jnp.concatenate([cosine, cosine], 1)
-    sine = jnp.concatenate([-sine, sine], 1)
+    first = far_first()[0]
+    mine[first], mine[0], cosine, sine = lax.optimization_barrier(
+        (mine[first], mine[0], cosine, sine)
+    )
+    theirs = {s: move(blocks[0] if s == 0 else mine[s], sibling) for s in [0] + far_first()}
+    lhs = [part[s] for s in [0] + far_first() for part in (mine, theirs)]
 
     part_rows = 3 * (width // LANES) * rows + 16
     *partials, own_tiles = pl.pallas_call(
@@ -622,7 +626,7 @@
         cost_estimate=pl.CostEstimate(flops=2 * GROUPS * rows * 2 * width * features // GROUPS, bytes_accessed=6 * 1024 * 1024, transcendentals=0),
         name="project",
     )(*lhs, key_matrix, value_matrix, far)
-    received = [move(partials[s], along(s)) for s in far_first()[1:] + far_first()[:1]]
+    received = [move(partials[1 + i], along(s)) for i, s in enumerate(far_first())]
     beside_tiles = move(own_tiles, beside)
 
     states = n_ctx * own_queries * query_width // HEAD_SIZE
@@ -683,7 +687,7 @@
         out_shape=jax.ShapeDtypeStruct((own_queries, query_width), jnp.bfloat16),
         compiler_params=params,
         name="finish",
-    )(kept, *[move(sent[s - 1], along(s)) for s in range(1, GROUPS)])
+    )(kept, *[move(sent[s - 1], along(s)) for s in far_first()])
     return (front_key, front_value, attended)
 
 

time: 72.2 us -> 70.4 us (0.975)
  starting transfers between devices: 21.8 us -> 18 us
  waiting for transfers between devices: 37.8 us -> 39.9 us
    ppermute x16, starting transfers between devices: 21.8 us -> 18 us  [move(): return lax.ppermute(array, ('ctx', 'tp'), pairs)]
    ppermute x16, waiting for transfers between devices: 37.8 us -> 39.9 us  [move(): return lax.ppermute(array, ('ctx', 'tp'), pairs)]
  transfers between devices with their start and end apart: 16 -> 16, of which waited for: 8 -> 11; matrix products, arithmetic and copies ran while one was open for 1% -> 1% of each run, Pallas kernels for 2% -> 2%
where the time goes in v1:
time: 70.4 us; the launch traced here: 70.3 us
  waiting for transfers between devices  39.9 us (57%)
  starting transfers between devices  18 us (26%)
  Pallas kernels  9.43 us (13%)
  between operations  1.41 us (2%)
  local copies, waits for them, and re-layouts  0.98 us (1%)
    ppermute x16, waiting for transfers between devices, move(): return lax.ppermute(array, ('ctx', 'tp'), pairs)  39.9 us
    ppermute x16, starting transfers between devices, move(): return lax.ppermute(array, ('ctx', 'tp'), pairs)  18 us
    pallas_call x1, Pallas kernels, exchange_plan(): pl.pallas_call(norm_kernel, in_specs=[hbm] * 6, out_specs=[hbm] * (GROUPS...  3.45 us
    pallas_call x1, Pallas kernels, exchange_plan(): pl.pallas_call(front_kernel, in_specs=[smem, smem] + [vmem] * (GROUPS + 8...  2.08 us
  transfers between devices with their start and end apart: 16, of which 11 were waited for; matrix products, arithmetic and copies ran while one was open for 1% of the time, Pallas kernels for 2%

profile of v1, /device:TPU:0, one launch (start us, length us, event | category | flops | bytes accessed | tf_op | source)
XLA Modules:
  0.0 70.3 jit_solution(18055403534902454149)
XLA Ops:
  0.7 3.4 %norm_rows.1 = (bf16[1072,128]{1,0:T(8,128)(2,1)}, bf16[1072,128]{1,0:T(8,128)(2,1)}, bf16[1072,128]{1,0:T(8,128)(2,1)}, bf16[1072,128]{1,0:T(8,128)(2,1)}, bf16...) custom-call(bf16[2,2048]{1,0:T(2,128)(2,1)} %query_any.1, bf16[128,8192]{1,0:T(8,128)(2,1)} %hidden_any.1, ...), custom_call_target="tpu_custom_call" | custom-call | flops 2097152 | bytes 2097152 | tf_op jit(solution)/shard_map/norm_rows/pallas_call | solution.py:550
  4.1 3.0 %collective-permute-start.7 = (bf16[2048,256]{1,0:T(8,128)(2,1)}, bf16[2048,256]{1,0:T(8,128)(2,1)S(1)}, u32[]{:S(2)}, u32[]{:S(2)}) collective-permute-start(bf16[2048,256]{1,0:T(8,128)(2,1)} %get-tuple-element.37), channel_id=1, source_target_pairs={{0,2},{1,3},{2,0},{3,1},{4,6},{5,7},{6,4},{7,5},{8,10},{9,11},{10,... | collective-permute-start | bytes 3145736 | tf_op jit(solution)/shard_map/ppermute | solution.py:534
  7.1 3.6 %collective-permute-start = (bf16[1072,128]{1,0:T(8,128)(2,1)}, bf16[1072,128]{1,0:T(8,128)(2,1)S(1)}, u32[]{:S(2)}, u32[]{:S(2)}) collective-permute-start(bf16[1072,128]{1,0:T(8,128)(2,1)} %get-tuple-element.30), channel_id=1, source_target_pairs={{0,12},{1,13},{2,14},{3,15},{4,8},{5,9},{6,10},{7,11},{8,4},{9,5},... | collective-permute-start | bytes 823304 | tf_op jit(solution)/shard_map/ppermute | solution.py:534
  10.7 0.8 %collective-permute-start.5 = (bf16[1072,128]{1,0:T(8,128)(2,1)}, bf16[1072,128]{1,0:T(8,128)(2,1)S(1)}, u32[]{:S(2)}, u32[]{:S(2)}) collective-permute-start(bf16[1072,128]{1,0:T(8,128)(2,1)} %get-tuple-element.36), channel_id=1, source_target_pairs={{0,4},{1,5},{2,6},{3,7},{4,0},{5,1},{6,2},{7,3},{8,12},{9,13},{10,... | collective-permute-start | bytes 823304 | tf_op jit(solution)/shard_map/ppermute | solution.py:534
  11.5 1.0 %copy-done.2 = bf16[1072,128]{1,0:T(8,128)(2,1)S(1)} copy-done((bf16[1072,128]{1,0:T(8,128)(2,1)S(1)}, bf16[1072,128]{1,0:T(8,128)(2,1)}, u32[]{:S(2)}) %copy-start.2) | copy-done | bytes 274456
  13.0 5.7 %collective-permute-done.refs_2_ = bf16[1072,128]{1,0:T(8,128)(2,1)S(1)} collective-permute-done((bf16[1072,128]{1,0:T(8,128)(2,1)}, bf16[1072,128]{1,0:T(8,128)(2,1)S(1)}, u32[]{:S(2)}, u32[]{:S(2)}) %collective-permute-start) | collective-permute-done | bytes 274464 | tf_op jit(solution)/shard_map/ppermute | solution.py:534
  18.8 15.2 %collective-permute-done.3.refs_4_ = bf16[1072,128]{1,0:T(8,128)(2,1)S(1)} collective-permute-done((bf16[1072,128]{1,0:T(8,128)(2,1)}, bf16[1072,128]{1,0:T(8,128)(2,1)S(1)}, u32[]{:S(2)}, u32[]{:S(2)}) %collective-permute-start.3) | collective-permute-done | bytes 274464 | tf_op jit(solution)/shard_map/ppermute | solution.py:534
  34.0 0.5 collective-permute-start.6
  34.5 1.0 %collective-permute-done.4.refs_5_ = bf16[1072,128]{1,0:T(8,128)(2,1)S(1)} collective-permute-done((bf16[1072,128]{1,0:T(8,128)(2,1)S(1)}, bf16[1072,128]{1,0:T(8,128)(2,1)S(1)}, u32[]{:S(2)}, u32[]{:S(2)}) %collective-permute-start.4) | collective-permute-done | bytes 274464 | tf_op jit(solution)/shard_map/ppermute | solution.py:534
  36.0 1.4 %project.1 = (bf16[784,128]{1,0:T(8,128)(2,1)S(1)}, bf16[784,128]{1,0:T(8,128)(2,1)S(1)}, bf16[784,128]{1,0:T(8,128)(2,1)S(1)}, bf16[784,128]{1,0:T(8,128)(2,1)S(1)}, bf16[128,128]{1,0:T(8,128)(2,1)S(1)}) custom-call(bf16[1072,128]{1,0:T(8,128)(2,1)S(1)} %fetch_own.1.refs_0_, bf16[1072,128]{1,0:T(8,128)(2,1)S(1)} %collective-permute-done.1.refs_1_, ...), custom_call_target="tpu_custom_call" | custom-call | flops 1073741824 | bytes 6291456 | tf_op jit(solution)/shard_map/project/pallas_call | solution.py:618
  37.3 2.5 %collective-permute-start.8 = (bf16[784,128]{1,0:T(8,128)(2,1)S(1)}, bf16[784,128]{1,0:T(8,128)(2,1)S(1)}, u32[]{:S(2)}, u32[]{:S(2)}) collective-permute-start(bf16[784,128]{1,0:T(8,128)(2,1)S(1)} %get-tuple-element.39), channel_id=1, source_target_pairs={{0,12},{1,13},{2,14},{3,15},{4,8},{5,9},{6,10},{7,11},{8,4},{9,5},... | collective-permute-start | bytes 602120 | tf_op jit(solution)/shard_map/ppermute | solution.py:534
  39.9 1.9 %collective-permute-start.10 = (bf16[784,128]{1,0:T(8,128)(2,1)S(1)}, bf16[784,128]{1,0:T(8,128)(2,1)S(1)}, u32[]{:S(2)}, u32[]{:S(2)}) collective-permute-start(bf16[784,128]{1,0:T(8,128)(2,1)S(1)} %get-tuple-element.41), channel_id=1, source_target_pairs={{0,4},{1,5},{2,6},{3,7},{4,0},{5,1},{6,2},{7,3},{8,12},{9,13},{10,... | collective-permute-start | bytes 602120 | tf_op jit(solution)/shard_map/ppermute | solution.py:534
  41.8 0.5 collective-permute-start.11
  43.0 2.7 %collective-permute-done.11.refs_1_ = bf16[128,128]{1,0:T(8,128)(2,1)S(1)} collective-permute-done((bf16[128,128]{1,0:T(8,128)(2,1)S(1)}, bf16[128,128]{1,0:T(8,128)(2,1)S(1)}, u32[]{:S(2)}, u32[]{:S(2)}) %collective-permute-start.11) | collective-permute-done | bytes 32800 | tf_op jit(solution)/shard_map/ppermute | solution.py:534
  45.7 1.4 %loaded_attention.1 = (f32[256,128]{1,0:T(8,128)S(1)}, f32[256,128]{1,0:T(8,128)S(1)}, f32[256,128]{1,0:T(8,128)S(1)}, bf16[256,128]{1,0:T(8,128)(2,1)S(1)}) custom-call(s32[2]{0:T(128)S(1)} %pad_add_fusion.place_ref, s32[16]{0:T(128)S(1)} %copy-done.7, s32[1]{0:T(128)S(6)} %copy.15.split_ref, bf16[128,128]{1,0:T(8,128)(2,1)S(1)} %get-tuple-element.44.refs_0_, ...), custom_call_target="tpu_custom_call" | custom-call | flops 67108864 | bytes 524288 | tf_op jit(solution)/shard_map/loaded_attention/pallas_call | solution.py:634
  47.2 9.4 %collective-permute-done.9.refs_1_ = bf16[784,128]{1,0:T(8,128)(2,1)S(1)} collective-permute-done((bf16[784,128]{1,0:T(8,128)(2,1)S(1)}, bf16[784,128]{1,0:T(8,128)(2,1)S(1)}, u32[]{:S(2)}, u32[]{:S(2)}) %collective-permute-start.9) | collective-permute-done | bytes 200736 | tf_op jit(solution)/shard_map/ppermute | solution.py:534
  56.5 2.1 %front_attention.1 = (bf16[128,256]{1,0:T(8,128)(2,1)}, bf16[128,256]{1,0:T(8,128)(2,1)}, f32[256,128]{1,0:T(8,128)S(1)}, bf16[256,128]{1,0:T(8,128)(2,1)S(1)}) custom-call(s32[2]{0:T(128)S(1)} %pad_add_fusion.place_ref, s32[1]{0:T(128)S(6)} %copy.15.split_ref, bf16[784,128]{1,0:T(8,128)(2,1)S(1)} %get-tuple-element.38.own, ...), custom_call_target="tpu_custom_call" | custom-call | flops 16777216 | bytes 2097152 | tf_op jit(solution)/shard_map/front_attention/pallas_call | solution.py:653
  58.6 0.5 collective-permute-start.12
  59.2 3.7 %collective-permute-done.12.other = bf16[256,128]{1,0:T(8,128)(2,1)S(1)} collective-permute-done((bf16[256,128]{1,0:T(8,128)(2,1)S(1)}, bf16[256,128]{1,0:T(8,128)(2,1)S(1)}, u32[]{:S(2)}, u32[]{:S(2)}) %collective-permute-start.12) | collective-permute-done | bytes 65568 | tf_op jit(solution)/shard_map/ppermute | solution.py:534
  63.2 1.4 %collective-permute-start.13 = (bf16[64,128]{1,0:T(8,128)(2,1)S(1)}, bf16[64,128]{1,0:T(8,128)(2,1)S(1)}, u32[]{:S(2)}, u32[]{:S(2)}) collective-permute-start(bf16[64,128]{1,0:T(8,128)(2,1)S(1)} %get-tuple-element.54), channel_id=1, source_target_pairs={{0,12},{1,13},{2,14},{3,15},{4,8},{5,9},{6,10},{7,11},{8,4},{9,5},... | collective-permute-start | bytes 49160 | tf_op jit(solution)/shard_map/ppermute | solution.py:534
  64.6 3.0 %collective-permute-start.15 = (bf16[64,128]{1,0:T(8,128)(2,1)S(1)}, bf16[64,128]{1,0:T(8,128)(2,1)S(1)}, u32[]{:S(2)}, u32[]{:S(2)}) collective-permute-start(bf16[64,128]{1,0:T(8,128)(2,1)S(1)} %get-tuple-element.56), channel_id=1, source_target_pairs={{0,4},{1,5},{2,6},{3,7},{4,0},{5,1},{6,2},{7,3},{8,12},{9,13},{10,... | collective-permute-start | bytes 49160 | tf_op jit(solution)/shard_map/ppermute | solution.py:534
  67.7 1.1 %collective-permute-done.13.refs_0_ = bf16[64,128]{1,0:T(8,128)(2,1)S(1)} collective-permute-done((bf16[64,128]{1,0:T(8,128)(2,1)S(1)}, bf16[64,128]{1,0:T(8,128)(2,1)S(1)}, u32[]{:S(2)}, u32[]{:S(2)}) %collective-permute-start.13) | collective-permute-done | bytes 16416 | tf_op jit(solution)/shard_map/ppermute | solution.py:534
  68.8 0.4 collective-permute-done.14.refs_1_
  69.4 0.8 %finish.1 = bf16[2,2048]{1,0:T(2,128)(2,1)} custom-call(f32[64,128]{1,0:T(8,128)S(1)} %get-tuple-element.53.kept, bf16[64,128]{1,0:T(8,128)(2,1)S(1)} %collective-permute-done.13.refs_0_, bf16[64,128]{1,0:T(8,128)(2,1)S(1)} %collective-permute-done.14.refs_1_, bf16[64,128]{1,0:T(8,128)(2,1)S(1)} %collective-permute-done.15.refs_2_), custom_call_target="tpu_custom_call" | custom-call | tf_op jit(solution)/shard_map/finish/pallas_call | solution.py:683
  (36 shorter events, 1.7 us)
Async XLA Ops:
  0.6 35.3 %copy-start = (bf16[1024,256]{1,0:T(8,128)(2,1)S(1)}, bf16[1024,256]{1,0:T(8,128)(2,1)}, u32[]{:S(2)}) copy-start(bf16[1024,256]{1,0:T(8,128)(2,1)} %refs_8_.1) | copy-start | bytes 1572868
  0.6 35.3 %copy-start.1 = (bf16[1024,256]{1,0:T(8,128)(2,1)S(1)}, bf16[1024,256]{1,0:T(8,128)(2,1)}, u32[]{:S(2)}) copy-start(bf16[1024,256]{1,0:T(8,128)(2,1)} %refs_9_.1) | copy-start | bytes 1572868
  4.1 31.8 %collective-permute-start.7 = (bf16[2048,256]{1,0:T(8,128)(2,1)}, bf16[2048,256]{1,0:T(8,128)(2,1)S(1)}, u32[]{:S(2)}, u32[]{:S(2)}) collective-permute-start(bf16[2048,256]{1,0:T(8,128)(2,1)} %get-tuple-element.37), channel_id=1, source_target_pairs={{0,2},{1,3},{2,0},{3,1},{4,6},{5,7},{6,4},{7,5},{8,10},{9,11},{10,... | collective-permute-start | bytes 3145736 | tf_op jit(solution)/shard_map/ppermute | solution.py:534
  7.1 11.6 %collective-permute-start = (bf16[1072,128]{1,0:T(8,128)(2,1)}, bf16[1072,128]{1,0:T(8,128)(2,1)S(1)}, u32[]{:S(2)}, u32[]{:S(2)}) collective-permute-start(bf16[1072,128]{1,0:T(8,128)(2,1)} %get-tuple-element.30), channel_id=1, source_target_pairs={{0,12},{1,13},{2,14},{3,15},{4,8},{5,9},{6,10},{7,11},{8,4},{9,5},... | collective-permute-start | bytes 823304 | tf_op jit(solution)/shard_map/ppermute | solution.py:534
  10.7 23.8 %collective-permute-start.1 = (bf16[1072,128]{1,0:T(8,128)(2,1)}, bf16[1072,128]{1,0:T(8,128)(2,1)S(1)}, u32[]{:S(2)}, u32[]{:S(2)}) collective-permute-start(bf16[1072,128]{1,0:T(8,128)(2,1)} %get-tuple-element.33), channel_id=1, source_target_pairs={{0,1},{1,0},{2,3},{3,2},{4,5},{5,4},{6,7},{7,6},{8,9},{9,8},{10,11... | collective-permute-start | bytes 823304 | tf_op jit(solution)/shard_map/ppermute | solution.py:534
  10.7 23.3 %collective-permute-start.3 = (bf16[1072,128]{1,0:T(8,128)(2,1)}, bf16[1072,128]{1,0:T(8,128)(2,1)S(1)}, u32[]{:S(2)}, u32[]{:S(2)}) collective-permute-start(bf16[1072,128]{1,0:T(8,128)(2,1)} %get-tuple-element.35), channel_id=1, source_target_pairs={{0,8},{1,9},{2,10},{3,11},{4,12},{5,13},{6,14},{7,15},{8,0},{9,1},... | collective-permute-start | bytes 823304 | tf_op jit(solution)/shard_map/ppermute | solution.py:534
  10.7 23.3 %collective-permute-start.5 = (bf16[1072,128]{1,0:T(8,128)(2,1)}, bf16[1072,128]{1,0:T(8,128)(2,1)S(1)}, u32[]{:S(2)}, u32[]{:S(2)}) collective-permute-start(bf16[1072,128]{1,0:T(8,128)(2,1)} %get-tuple-element.36), channel_id=1, source_target_pairs={{0,4},{1,5},{2,6},{3,7},{4,0},{5,1},{6,2},{7,3},{8,12},{9,13},{10,... | collective-permute-start | bytes 823304 | tf_op jit(solution)/shard_map/ppermute | solution.py:534
  11.5 1.0 %copy-start.2 = (bf16[1072,128]{1,0:T(8,128)(2,1)S(1)}, bf16[1072,128]{1,0:T(8,128)(2,1)}, u32[]{:S(2)}) copy-start(bf16[1072,128]{1,0:T(8,128)(2,1)} %get-tuple-element.31.from_any) | copy-start | bytes 823300
  18.7 27.0 %copy-start.3 = (bf16[4,128,256]{2,1,0:T(8,128)(2,1)S(1)}, bf16[4,128,256]{2,1,0:T(8,128)(2,1)}, u32[]{:S(2)}) copy-start(bf16[4,128,256]{2,1,0:T(8,128)(2,1)} %refs_2_.1) | copy-start | bytes 786436
  18.7 27.0 %copy-start.4 = (bf16[4,128,256]{2,1,0:T(8,128)(2,1)S(1)}, bf16[4,128,256]{2,1,0:T(8,128)(2,1)}, u32[]{:S(2)}) copy-start(bf16[4,128,256]{2,1,0:T(8,128)(2,1)} %refs_3_.1) | copy-start | bytes 786436
  18.7 27.0 %copy-start.7 = (s32[16]{0:T(128)S(1)}, s32[16]{0:T(128)}, u32[]{:S(2)}) copy-start(s32[16]{0:T(128)} %table_ref.1) | copy-start | bytes 196
  18.7 37.8 %copy-start.5 = (f32[256]{0:T(256)S(1)}, f32[256]{0:T(256)}, u32[]{:S(2)}) copy-start(f32[256]{0:T(256)} %param.17) | copy-start | bytes 3076
  18.7 37.8 %copy-start.6 = (f32[256]{0:T(256)S(1)}, f32[256]{0:T(256)}, u32[]{:S(2)}) copy-start(f32[256]{0:T(256)} %param.18) | copy-start | bytes 3076
  18.7 15.8 %collective-permute-start.2 = (bf16[1072,128]{1,0:T(8,128)(2,1)S(1)}, bf16[1072,128]{1,0:T(8,128)(2,1)S(1)}, u32[]{:S(2)}, u32[]{:S(2)}) collective-permute-start(bf16[1072,128]{1,0:T(8,128)(2,1)S(1)} %collective-permute-done.refs_2_), channel_id=1, source_target_pairs={{0,1},{1,0},{2,3},{3,2},{4,5},{5,4},{6,7},{7,6},{8,9},{9,8},{10,11... | collective-permute-start | bytes 823304 | tf_op jit(solution)/shard_map/ppermute | solution.py:534
  34.0 1.6 %collective-permute-start.4 = (bf16[1072,128]{1,0:T(8,128)(2,1)S(1)}, bf16[1072,128]{1,0:T(8,128)(2,1)S(1)}, u32[]{:S(2)}, u32[]{:S(2)}) collective-permute-start(bf16[1072,128]{1,0:T(8,128)(2,1)S(1)} %collective-permute-done.3.refs_4_), channel_id=1, source_target_pairs={{0,1},{1,0},{2,3},{3,2},{4,5},{5,4},{6,7},{7,6},{8,9},{9,8},{10,11... | collective-permute-start | bytes 823304 | tf_op jit(solution)/shard_map/ppermute | solution.py:534
  34.0 1.9 %collective-permute-start.6 = (bf16[1072,128]{1,0:T(8,128)(2,1)S(1)}, bf16[1072,128]{1,0:T(8,128)(2,1)S(1)}, u32[]{:S(2)}, u32[]{:S(2)}) collective-permute-start(bf16[1072,128]{1,0:T(8,128)(2,1)S(1)} %collective-permute-done.5.refs_6_), channel_id=1, source_target_pairs={{0,1},{1,0},{2,3},{3,2},{4,5},{5,4},{6,7},{7,6},{8,9},{9,8},{10,11... | collective-permute-start | bytes 823304 | tf_op jit(solution)/shard_map/ppermute | solution.py:534
  37.3 9.8 %collective-permute-start.8 = (bf16[784,128]{1,0:T(8,128)(2,1)S(1)}, bf16[784,128]{1,0:T(8,128)(2,1)S(1)}, u32[]{:S(2)}, u32[]{:S(2)}) collective-permute-start(bf16[784,128]{1,0:T(8,128)(2,1)S(1)} %get-tuple-element.39), channel_id=1, source_target_pairs={{0,12},{1,13},{2,14},{3,15},{4,8},{5,9},{6,10},{7,11},{8,4},{9,5},... | collective-permute-start | bytes 602120 | tf_op jit(solution)/shard_map/ppermute | solution.py:534
  39.9 16.7 %collective-permute-start.9 = (bf16[784,128]{1,0:T(8,128)(2,1)S(1)}, bf16[784,128]{1,0:T(8,128)(2,1)S(1)}, u32[]{:S(2)}, u32[]{:S(2)}) collective-permute-start(bf16[784,128]{1,0:T(8,128)(2,1)S(1)} %get-tuple-element.40), channel_id=1, source_target_pairs={{0,8},{1,9},{2,10},{3,11},{4,12},{5,13},{6,14},{7,15},{8,0},{9,1},... | collective-permute-start | bytes 602120 | tf_op jit(solution)/shard_map/ppermute | solution.py:534
  39.9 16.7 %collective-permute-start.10 = (bf16[784,128]{1,0:T(8,128)(2,1)S(1)}, bf16[784,128]{1,0:T(8,128)(2,1)S(1)}, u32[]{:S(2)}, u32[]{:S(2)}) collective-permute-start(bf16[784,128]{1,0:T(8,128)(2,1)S(1)} %get-tuple-element.41), channel_id=1, source_target_pairs={{0,4},{1,5},{2,6},{3,7},{4,0},{5,1},{6,2},{7,3},{8,12},{9,13},{10,... | collective-permute-start | bytes 602120 | tf_op jit(solution)/shard_map/ppermute | solution.py:534
  41.8 3.9 %collective-permute-start.11 = (bf16[128,128]{1,0:T(8,128)(2,1)S(1)}, bf16[128,128]{1,0:T(8,128)(2,1)S(1)}, u32[]{:S(2)}, u32[]{:S(2)}) collective-permute-start(bf16[128,128]{1,0:T(8,128)(2,1)S(1)} %get-tuple-element.44.refs_0_), channel_id=1, source_target_pairs={{0,2},{1,3},{2,0},{3,1},{4,6},{5,7},{6,4},{7,5},{8,10},{9,11},{10,... | collective-permute-start | bytes 98312 | tf_op jit(solution)/shard_map/ppermute | solution.py:534
  58.6 4.3 %collective-permute-start.12 = (bf16[256,128]{1,0:T(8,128)(2,1)S(1)}, bf16[256,128]{1,0:T(8,128)(2,1)S(1)}, u32[]{:S(2)}, u32[]{:S(2)}) collective-permute-start(bf16[256,128]{1,0:T(8,128)(2,1)S(1)} %get-tuple-element.52), channel_id=1, source_target_pairs={{0,2},{1,3},{2,0},{3,1},{4,6},{5,7},{6,4},{7,5},{8,10},{9,11},{10,... | collective-permute-start | bytes 196616 | tf_op jit(solution)/shard_map/ppermute | solution.py:534
  63.2 5.6 %collective-permute-start.13 = (bf16[64,128]{1,0:T(8,128)(2,1)S(1)}, bf16[64,128]{1,0:T(8,128)(2,1)S(1)}, u32[]{:S(2)}, u32[]{:S(2)}) collective-permute-start(bf16[64,128]{1,0:T(8,128)(2,1)S(1)} %get-tuple-element.54), channel_id=1, source_target_pairs={{0,12},{1,13},{2,14},{3,15},{4,8},{5,9},{6,10},{7,11},{8,4},{9,5},... | collective-permute-start | bytes 49160 | tf_op jit(solution)/shard_map/ppermute | solution.py:534
  64.6 4.6 %collective-permute-start.14 = (bf16[64,128]{1,0:T(8,128)(2,1)S(1)}, bf16[64,128]{1,0:T(8,128)(2,1)S(1)}, u32[]{:S(2)}, u32[]{:S(2)}) collective-permute-start(bf16[64,128]{1,0:T(8,128)(2,1)S(1)} %get-tuple-element.55), channel_id=1, source_target_pairs={{0,8},{1,9},{2,10},{3,11},{4,12},{5,13},{6,14},{7,15},{8,0},{9,1},... | collective-permute-start | bytes 49160 | tf_op jit(solution)/shard_map/ppermute | solution.py:534
  64.6 4.8 %collective-permute-start.15 = (bf16[64,128]{1,0:T(8,128)(2,1)S(1)}, bf16[64,128]{1,0:T(8,128)(2,1)S(1)}, u32[]{:S(2)}, u32[]{:S(2)}) collective-permute-start(bf16[64,128]{1,0:T(8,128)(2,1)S(1)} %get-tuple-element.56), channel_id=1, source_target_pairs={{0,4},{1,5},{2,6},{3,7},{4,0},{5,1},{6,2},{7,3},{8,12},{9,13},{10,... | collective-permute-start | bytes 49160 | tf_op jit(solution)/shard_map/ppermute | solution.py:534

commit v2 on v1

--- a/solution.py
+++ b/solution.py
@@ -161,16 +161,10 @@
     return list(range(GROUPS - 1, 0, -1))
 
 
-def norm_kernel(query_any, hidden_any, suffix_any, gain_any, key_any, value_any, *rest):
-    blocks_any, packed_any, own_any = rest[:GROUPS], rest[GROUPS], rest[GROUPS + 1]
-    hidden_ref, suffix_ref, gain_ref, query_ref, packed_ref, tail_ref = rest[GROUPS + 2 : GROUPS + 8]
-    outs, (sems, out_sems) = rest[GROUPS + 8 : -2], rest[-2:]
-    depth = key_any.shape[0]
-    packing = [
-        pltpu.make_async_copy(key_any, packed_ref.at[:depth], sems.at[CHUNKS + 3]),
-        pltpu.make_async_copy(value_any, packed_ref.at[depth:], sems.at[CHUNKS + 4]),
-    ]
-    unpacking = pltpu.make_async_copy(packed_ref, packed_any, sems.at[CHUNKS + 5])
+def norm_kernel(query_any, hidden_any, suffix_any, gain_any, *rest):
+    blocks_any, own_any = rest[:GROUPS], rest[GROUPS]
+    hidden_ref, suffix_ref, gain_ref, query_ref, tail_ref = rest[GROUPS + 1 : GROUPS + 6]
+    outs, (sems, out_sems) = rest[GROUPS + 6 : -2], rest[-2:]
     core, ctx = lax.axis_index("tp"), lax.axis_index("ctx")
     z, x = ctx // PAIR, ctx % PAIR
     half_rows, features = hidden_ref.shape
@@ -190,7 +184,7 @@
                 hidden_any.at[pl.ds(start, rows)], hidden_ref.at[i * rows : (i + 1) * rows], sems.at[i]
             )
         )
-    for copy in copies + packing:
+    for copy in copies:
         copy.start()
 
     def offset(shift, side, j):
@@ -224,9 +218,6 @@
     for i in range(CHUNKS):
         copies[3 + i].wait()
         inverses.append(row_scale(hidden_ref[i * rows : (i + 1) * rows, :].astype(jnp.float32)))
-    for copy in packing:
-        copy.wait()
-    unpacking.start()
     leaving = []
     for shift in far_first() + [0]:
         for side in range(PAIR):
@@ -243,7 +234,6 @@
     leaving[-1].start()
     for copy in leaving:
         copy.wait()
-    unpacking.wait()
 
 
 def fetch_kernel(from_any, to_ref, sem):
@@ -254,9 +244,9 @@
 
 def project_kernel(*refs):
     blocks = refs[: 2 * GROUPS]
-    near_key, near_value, far = refs[2 * GROUPS : 2 * GROUPS + 3]
-    outs = refs[2 * GROUPS + 3 : 3 * GROUPS + 3]
-    query_ref, lhs_ref = refs[3 * GROUPS + 3 :]
+    near_key, near_value, far_key, far_value = refs[2 * GROUPS : 2 * GROUPS + 4]
+    outs = refs[2 * GROUPS + 4 : 3 * GROUPS + 4]
+    query_ref, lhs_ref = refs[3 * GROUPS + 4 :]
     depth = near_key.shape[0]
     pieces = 2 * depth // LANES
     half_rows = (lhs_ref.shape[0] - 16) // (2 * GROUPS)
@@ -277,13 +267,13 @@
     total = GROUPS * rows
     lhs_ref[total : total + 16, :] = jnp.concatenate(tails, 0).astype(jnp.bfloat16)
 
-    def product(near, at):
+    def product(near, far):
         return jnp.dot(
             lhs_ref[:, :depth], near[...], preferred_element_type=jnp.float32
-        ) + jnp.dot(lhs_ref[:, depth:], far[at, :], preferred_element_type=jnp.float32)
-
-    keys = product(near_key, slice(0, depth))
-    values = product(near_value, slice(depth, 2 * depth))
+        ) + jnp.dot(lhs_ref[:, depth:], far[...], preferred_element_type=jnp.float32)
+
+    keys = product(near_key, far_key)
+    values = product(near_value, far_value)
     high = keys.astype(jnp.bfloat16).astype(jnp.float32)
     low = keys - high
     columns = []
@@ -427,12 +417,10 @@
         )
         stats = (kept_stats(top[:, 0:1], total[:, 0:1]), sent_stats(top[:, 0:1], total[:, 0:1]))
         each = own_queries * sharing
-        for slot in range(GROUPS * PAIR):
-            start = (slot // PAIR * 2 * heads + head) * each
+        for slot, out in enumerate(outs):
             at = slice(slot * each, (slot + 1) * each)
-            out = outs[slot % PAIR]
-            out[start : start + each, :] = numer[at].astype(out.dtype)
-            out[start + heads * each : start + (heads + 1) * each, :] = stats[slot % PAIR][at]
+            out[head * each : (head + 1) * each, :] = numer[at].astype(out.dtype)
+            out[(heads + head) * each : (heads + head + 1) * each, :] = stats[slot > 0][at]
 
 
 def kept_stats(top, total):
@@ -469,19 +457,6 @@
     total = sum(f * t for f, t in zip(factors, totals))
     numer = sum(f * n for f, n in zip(factors, numers))
     return numer, top, total
-
-
-def merge_kernel(kept, other, keep_ref, *send_refs):
-    each = keep_ref.shape[0]
-    rows = each // 2
-    for slot in range(GROUPS):
-        numer, top, total = merged(kept, [other], slot * each, rows)
-        if slot == 0:
-            keep_ref[:rows, :] = numer
-            keep_ref[rows:, :] = kept_stats(top, total)
-        else:
-            send_refs[slot - 1][:rows, :] = numer.astype(jnp.bfloat16)
-            send_refs[slot - 1][rows:, :] = sent_stats(top, total)
 
 
 def last_kernel(kept, *refs):
@@ -533,8 +508,11 @@
                 pairs.append((c * 2 + t, to_c * 2 + to_t))
         return lax.ppermute(array, ("ctx", "tp"), pairs)
 
+    def partner(away):
+        return lambda c, t: (c ^ away, t)
+
     def along(shift):
-        return lambda c, t: ((c // PAIR ^ shift) * PAIR + c % PAIR, t)
+        return partner(shift * PAIR)
 
     def beside(c, t):
         return (c ^ 1, t)
@@ -547,26 +525,21 @@
     own_queries = suffix_query_rows.shape[0]
     lines = query_width // LANES
     block_rows = pieces * half_rows + pieces + own_queries * lines
-    *blocks, packed, own = pl.pallas_call(
+    *blocks, own = pl.pallas_call(
         norm_kernel,
-        in_specs=[hbm] * 6,
-        out_specs=[hbm] * (GROUPS + 2),
-        out_shape=[jax.ShapeDtypeStruct((block_rows, LANES), jnp.bfloat16)] * GROUPS
-        + [
-            jax.ShapeDtypeStruct((2 * key_matrix.shape[0], width), jnp.bfloat16),
-            jax.ShapeDtypeStruct((block_rows, LANES), jnp.bfloat16),
-        ],
+        in_specs=[hbm] * 4,
+        out_specs=[hbm] * (GROUPS + 1),
+        out_shape=[jax.ShapeDtypeStruct((block_rows, LANES), jnp.bfloat16)] * (GROUPS + 1),
         scratch_shapes=[
             pltpu.VMEM((half_rows, features), jnp.bfloat16),
             pltpu.VMEM(suffix_hidden.shape, jnp.bfloat16),
             pltpu.VMEM((1, features), jnp.float32),
             pltpu.VMEM(suffix_query_rows.shape, jnp.bfloat16),
-            pltpu.VMEM((2 * key_matrix.shape[0], width), jnp.bfloat16),
             pltpu.VMEM((1, features), jnp.float32),
         ]
         + [pltpu.VMEM((block_rows, LANES), jnp.bfloat16)] * GROUPS
         + [
-            pltpu.SemaphoreType.DMA((CHUNKS + 6,)),
+            pltpu.SemaphoreType.DMA((CHUNKS + 3,)),
             pltpu.SemaphoreType.DMA((GROUPS + 1,)),
         ],
         compiler_params=pltpu.CompilerParams(vmem_limit_bytes=60 * 1024 * 1024),
@@ -579,10 +552,8 @@
         hidden,
         suffix_hidden,
         norm_gain.reshape(1, features),
-        key_matrix,
-        value_matrix,
-    )
-    far = move(packed, beside)
+    )
+    far = [move(key_matrix, beside), move(value_matrix, beside)]
 
     mine = {s: move(blocks[s], along(s)) for s in far_first()}
     inverse_freq = rope_base ** (
@@ -597,6 +568,8 @@
     cosine = jnp.concatenate([cosine, cosine], 1)
     sine = jnp.concatenate([-sine, sine], 1)
 
+    first, second = far_first()[:2]
+    mine[first], own = lax.optimization_barrier((mine[first], own))
     mine[0] = pl.pallas_call(
         fetch_kernel,
         in_specs=[hbm],
@@ -604,12 +577,11 @@
         out_shape=jax.ShapeDtypeStruct(own.shape, own.dtype),
         scratch_shapes=[pltpu.SemaphoreType.DMA],
         compiler_params=params,
-        cost_estimate=pl.CostEstimate(flops=0, bytes_accessed=16 * 1024 * 1024, transcendentals=0),
+        cost_estimate=pl.CostEstimate(flops=0, bytes_accessed=64 * 1024 * 1024, transcendentals=0),
         name="fetch_own",
     )(own)
-    first = far_first()[0]
-    mine[first], mine[0], cosine, sine = lax.optimization_barrier(
-        (mine[first], mine[0], cosine, sine)
+    mine[second], mine[0], cosine, sine = lax.optimization_barrier(
+        (mine[second], mine[0], cosine, sine)
     )
     theirs = {s: move(blocks[0] if s == 0 else mine[s], sibling) for s in [0] + far_first()}
     lhs = [part[s] for s in [0] + far_first() for part in (mine, theirs)]
@@ -617,7 +589,7 @@
     part_rows = 3 * (width // LANES) * rows + 16
     *partials, own_tiles = pl.pallas_call(
         project_kernel,
-        in_specs=[vmem] * (2 * GROUPS + 3),
+        in_specs=[vmem] * (2 * GROUPS + 4),
         out_specs=[vmem] * (GROUPS + 1),
         out_shape=[jax.ShapeDtypeStruct((part_rows, LANES), jnp.bfloat16)] * GROUPS
         + [jax.ShapeDtypeStruct((GROUPS * own_queries * lines, LANES), jnp.bfloat16)],
@@ -625,7 +597,7 @@
         compiler_params=params,
         cost_estimate=pl.CostEstimate(flops=2 * GROUPS * rows * 2 * width * features // GROUPS, bytes_accessed=6 * 1024 * 1024, transcendentals=0),
         name="project",
-    )(*lhs, key_matrix, value_matrix, far)
+    )(*lhs, key_matrix, value_matrix, *far)
     received = [move(partials[1 + i], along(s)) for i, s in enumerate(far_first())]
     beside_tiles = move(own_tiles, beside)
 
@@ -646,15 +618,15 @@
     )(place, page_slot_table, split_page, own_tiles, beside_tiles, slot_keys, slot_values)
 
 
-    def payloads(size):
-        return [jax.ShapeDtypeStruct((size, LANES), kind) for kind in (jnp.float32, jnp.bfloat16)]
+    def payload(kind):
+        return jax.ShapeDtypeStruct((2 * states // n_ctx, LANES), kind)
 
     row_shape = jax.ShapeDtypeStruct((rows, width), jnp.bfloat16)
-    front_key, front_value, kept, sent = pl.pallas_call(
+    front_key, front_value, kept, *sent = pl.pallas_call(
         front_kernel,
         in_specs=[smem, smem] + [vmem] * (GROUPS + 8),
-        out_specs=[vmem] * 4,
-        out_shape=[row_shape] * 2 + payloads(states),
+        out_specs=[vmem] * (2 + n_ctx),
+        out_shape=[row_shape] * 2 + [payload(jnp.float32)] + [payload(jnp.bfloat16)] * (n_ctx - 1),
         compiler_params=params,
         cost_estimate=pl.CostEstimate(flops=4 * states * rows * HEAD_SIZE, bytes_accessed=2 * 1024 * 1024, transcendentals=states * rows),
         name="front_attention",
@@ -672,22 +644,14 @@
         total,
         numer,
     )
-    kept, *sent = pl.pallas_call(
-        merge_kernel,
-        in_specs=[vmem] * 2,
-        out_specs=[vmem] * GROUPS,
-        out_shape=payloads(states // GROUPS) + payloads(states // GROUPS)[1:] * (GROUPS - 2),
-        compiler_params=params,
-        name="merge",
-    )(kept, move(sent, beside))
     attended = pl.pallas_call(
         last_kernel,
-        in_specs=[vmem] * GROUPS,
+        in_specs=[vmem] * n_ctx,
         out_specs=vmem,
         out_shape=jax.ShapeDtypeStruct((own_queries, query_width), jnp.bfloat16),
         compiler_params=params,
         name="finish",
-    )(kept, *[move(sent[s - 1], along(s)) for s in far_first()])
+    )(kept, *[move(sent[r - 1], partner(r)) for r in range(n_ctx - 1, 0, -1)])
     return (front_key, front_value, attended)
 
 

time: 70.4 us -> 77.6 us (1.10)
  starting transfers between devices: 18 us -> 36.3 us
  waiting for transfers between devices: 39.9 us -> 29.5 us
    ppermute x16 -> x20, starting transfers between devices: 18 us -> 36.3 us  [move(): return lax.ppermute(array, ('ctx', 'tp'), pairs)]
    ppermute x16 -> x20, waiting for transfers between devices: 39.9 us -> 29.5 us  [move(): return lax.ppermute(array, ('ctx', 'tp'), pairs)]
    pallas_call x4 -> x3, Pallas kernels: 5.95 us -> 5.18 us  [the longest x1 2.97 us: exchange_plan(): pl.pallas_call(norm_kernel, in_specs=[hbm] * 4, out_specs=[hbm] * (GROUPS...]
  transfers between devices with their start and end apart: 16 -> 20, of which waited for: 11 -> 10; matrix products, arithmetic and copies ran while one was open for 1% -> 1% of each run, Pallas kernels for 2% -> 2%
where the time goes in v2:
time: 77.6 us; the launch traced here: 77.4 us
  starting transfers between devices  36.3 us (47%)
  waiting for transfers between devices  29.5 us (38%)
  Pallas kernels  8.67 us (11%)
  between operations  1.43 us (2%)
  local copies, waits for them, and re-layouts  0.98 us (1%)
    ppermute x20, starting transfers between devices, move(): return lax.ppermute(array, ('ctx', 'tp'), pairs)  36.3 us
    ppermute x20, waiting for transfers between devices, move(): return lax.ppermute(array, ('ctx', 'tp'), pairs)  29.5 us
    pallas_call x1, Pallas kernels, exchange_plan(): pl.pallas_call(norm_kernel, in_specs=[hbm] * 4, out_specs=[hbm] * (GROUPS...  2.97 us
    pallas_call x1, Pallas kernels, exchange_plan(): pl.pallas_call(front_kernel, in_specs=[smem, smem] + [vmem] * (GROUPS + 8...  2.09 us
  transfers between devices with their start and end apart: 20, of which 10 were waited for; matrix products, arithmetic and copies ran while one was open for 1% of the time, Pallas kernels for 2%

profile of v2, /device:TPU:0, one launch (start us, length us, event | category | flops | bytes accessed | tf_op | source)
XLA Modules:
  0.0 77.4 jit_solution(13318118822925179079)
XLA Ops:
  0.7 3.0 %norm_rows.1 = (bf16[1072,128]{1,0:T(8,128)(2,1)}, bf16[1072,128]{1,0:T(8,128)(2,1)}, bf16[1072,128]{1,0:T(8,128)(2,1)}, bf16[1072,128]{1,0:T(8,128)(2,1)}, bf16[1072,128]{1,0:T(8,128)(2,1)}) custom-call(bf16[2,2048]{1,0:T(2,128)(2,1)} %query_any.1, bf16[128,8192]{1,0:T(8,128)(2,1)} %hidden_any.1, bf16[2,8192]{1,0:T(2,128)(2,1)} %suffix_any.1, f32[1,8192]{1,0:T(1,128)} %bitcast.7), custom_call_target="tpu_custom_call" | custom-call | flops 2097152 | bytes 2097152 | tf_op jit(solution)/shard_map/norm_rows/pallas_call | solution.py:528
  3.6 5.1 %collective-permute-start.1 = (bf16[1072,128]{1,0:T(8,128)(2,1)}, bf16[1072,128]{1,0:T(8,128)(2,1)S(1)}, u32[]{:S(2)}, u32[]{:S(2)}) collective-permute-start(bf16[1072,128]{1,0:T(8,128)(2,1)} %get-tuple-element.34), channel_id=1, source_target_pairs={{0,12},{1,13},{2,14},{3,15},{4,8},{5,9},{6,10},{7,11},{8,4},{9,5},... | collective-permute-start | bytes 823304 | tf_op jit(solution)/shard_map/ppermute | solution.py:509
  8.7 1.5 %collective-permute-start.7 = (bf16[1024,256]{1,0:T(8,128)(2,1)S(1)}, bf16[1024,256]{1,0:T(8,128)(2,1)S(1)}, u32[]{:S(2)}, u32[]{:S(2)}) collective-permute-start(bf16[1024,256]{1,0:T(8,128)(2,1)S(1)} %copy-done), channel_id=1, source_target_pairs={{0,2},{1,3},{2,0},{3,1},{4,6},{5,7},{6,4},{7,5},{8,10},{9,11},{10,... | collective-permute-start | bytes 1572872 | tf_op jit(solution)/shard_map/ppermute | solution.py:509
  10.8 5.6 %collective-permute-done.1.refs_2_ = bf16[1072,128]{1,0:T(8,128)(2,1)S(1)} collective-permute-done((bf16[1072,128]{1,0:T(8,128)(2,1)}, bf16[1072,128]{1,0:T(8,128)(2,1)S(1)}, u32[]{:S(2)}, u32[]{:S(2)}) %collective-permute-start.1) | collective-permute-done | bytes 274464 | tf_op jit(solution)/shard_map/ppermute | solution.py:509
  16.5 11.5 %collective-permute-start.5 = (bf16[1072,128]{1,0:T(8,128)(2,1)}, bf16[1072,128]{1,0:T(8,128)(2,1)S(1)}, u32[]{:S(2)}, u32[]{:S(2)}) collective-permute-start(bf16[1072,128]{1,0:T(8,128)(2,1)} %get-tuple-element.41), channel_id=1, source_target_pairs={{0,4},{1,5},{2,6},{3,7},{4,0},{5,1},{6,2},{7,3},{8,12},{9,13},{10,... | collective-permute-start | bytes 823304 | tf_op jit(solution)/shard_map/ppermute | solution.py:509
  28.4 0.9 %copy-done.2 = bf16[1072,128]{1,0:T(8,128)(2,1)S(1)} copy-done((bf16[1072,128]{1,0:T(8,128)(2,1)S(1)}, bf16[1072,128]{1,0:T(8,128)(2,1)}, u32[]{:S(2)}) %copy-start.2) | copy-done | bytes 274456
  29.4 3.0 %collective-permute-done.refs_4_ = bf16[1072,128]{1,0:T(8,128)(2,1)S(1)} collective-permute-done((bf16[1072,128]{1,0:T(8,128)(2,1)}, bf16[1072,128]{1,0:T(8,128)(2,1)S(1)}, u32[]{:S(2)}, u32[]{:S(2)}) %collective-permute-start) | collective-permute-done | bytes 274464 | tf_op jit(solution)/shard_map/ppermute | solution.py:509
  33.0 5.1 %collective-permute-done.5.refs_6_ = bf16[1072,128]{1,0:T(8,128)(2,1)S(1)} collective-permute-done((bf16[1072,128]{1,0:T(8,128)(2,1)}, bf16[1072,128]{1,0:T(8,128)(2,1)S(1)}, u32[]{:S(2)}, u32[]{:S(2)}) %collective-permute-start.5) | collective-permute-done | bytes 274464 | tf_op jit(solution)/shard_map/ppermute | solution.py:509
  38.1 1.5 %collective-permute-done.6.refs_7_ = bf16[1072,128]{1,0:T(8,128)(2,1)S(1)} collective-permute-done((bf16[1072,128]{1,0:T(8,128)(2,1)S(1)}, bf16[1072,128]{1,0:T(8,128)(2,1)S(1)}, u32[]{:S(2)}, u32[]{:S(2)}) %collective-permute-start.6) | collective-permute-done | bytes 274464 | tf_op jit(solution)/shard_map/ppermute | solution.py:509
  39.7 1.4 %project.1 = (bf16[784,128]{1,0:T(8,128)(2,1)S(1)}, bf16[784,128]{1,0:T(8,128)(2,1)S(1)}, bf16[784,128]{1,0:T(8,128)(2,1)S(1)}, bf16[784,128]{1,0:T(8,128)(2,1)S(1)}, bf16[128,128]{1,0:T(8,128)(2,1)S(1)}) custom-call(bf16[1072,128]{1,0:T(8,128)(2,1)S(1)} %fetch_own.1.refs_0_, bf16[1072,128]{1,0:T(8,128)(2,1)S(1)} %collective-permute-done.2.refs_1_, ...), custom_call_target="tpu_custom_call" | custom-call | flops 1073741824 | bytes 6291456 | tf_op jit(solution)/shard_map/project/pallas_call | solution.py:590
  41.0 2.4 %collective-permute-start.9 = (bf16[784,128]{1,0:T(8,128)(2,1)S(1)}, bf16[784,128]{1,0:T(8,128)(2,1)S(1)}, u32[]{:S(2)}, u32[]{:S(2)}) collective-permute-start(bf16[784,128]{1,0:T(8,128)(2,1)S(1)} %get-tuple-element.43), channel_id=1, source_target_pairs={{0,12},{1,13},{2,14},{3,15},{4,8},{5,9},{6,10},{7,11},{8,4},{9,5},... | collective-permute-start | bytes 602120 | tf_op jit(solution)/shard_map/ppermute | solution.py:509
  43.4 2.1 %collective-permute-start.11 = (bf16[784,128]{1,0:T(8,128)(2,1)S(1)}, bf16[784,128]{1,0:T(8,128)(2,1)S(1)}, u32[]{:S(2)}, u32[]{:S(2)}) collective-permute-start(bf16[784,128]{1,0:T(8,128)(2,1)S(1)} %get-tuple-element.45), channel_id=1, source_target_pairs={{0,4},{1,5},{2,6},{3,7},{4,0},{5,1},{6,2},{7,3},{8,12},{9,13},{10,... | collective-permute-start | bytes 602120 | tf_op jit(solution)/shard_map/ppermute | solution.py:509
  45.5 1.5 %collective-permute-start.12 = (bf16[128,128]{1,0:T(8,128)(2,1)S(1)}, bf16[128,128]{1,0:T(8,128)(2,1)S(1)}, u32[]{:S(2)}, u32[]{:S(2)}) collective-permute-start(bf16[128,128]{1,0:T(8,128)(2,1)S(1)} %get-tuple-element.48.refs_0_), channel_id=1, source_target_pairs={{0,2},{1,3},{2,0},{3,1},{4,6},{5,7},{6,4},{7,5},{8,10},{9,11},{10,... | collective-permute-start | bytes 98312 | tf_op jit(solution)/shard_map/ppermute | solution.py:509
  47.7 1.7 %collective-permute-done.12.refs_1_ = bf16[128,128]{1,0:T(8,128)(2,1)S(1)} collective-permute-done((bf16[128,128]{1,0:T(8,128)(2,1)S(1)}, bf16[128,128]{1,0:T(8,128)(2,1)S(1)}, u32[]{:S(2)}, u32[]{:S(2)}) %collective-permute-start.12) | collective-permute-done | bytes 32800 | tf_op jit(solution)/shard_map/ppermute | solution.py:509
  49.4 1.4 %loaded_attention.1 = (f32[256,128]{1,0:T(8,128)S(1)}, f32[256,128]{1,0:T(8,128)S(1)}, f32[256,128]{1,0:T(8,128)S(1)}, bf16[256,128]{1,0:T(8,128)(2,1)S(1)}) custom-call(s32[2]{0:T(128)S(1)} %pad_add_fusion.place_ref, s32[16]{0:T(128)S(1)} %copy-done.7, s32[1]{0:T(128)S(6)} %copy.15.split_ref, bf16[128,128]{1,0:T(8,128)(2,1)S(1)} %get-tuple-element.48.refs_0_, ...), custom_call_target="tpu_custom_call" | custom-call | flops 67108864 | bytes 524288 | tf_op jit(solution)/shard_map/loaded_attention/pallas_call | solution.py:606
  50.9 9.2 %collective-permute-done.10.refs_1_ = bf16[784,128]{1,0:T(8,128)(2,1)S(1)} collective-permute-done((bf16[784,128]{1,0:T(8,128)(2,1)S(1)}, bf16[784,128]{1,0:T(8,128)(2,1)S(1)}, u32[]{:S(2)}, u32[]{:S(2)}) %collective-permute-start.10) | collective-permute-done | bytes 200736 | tf_op jit(solution)/shard_map/ppermute | solution.py:509
  60.1 2.1 %front_attention.1 = (bf16[128,256]{1,0:T(8,128)(2,1)}, bf16[128,256]{1,0:T(8,128)(2,1)}, f32[64,128]{1,0:T(8,128)S(1)}, bf16[64,128]{1,0:T(8,128)(2,1)S(1)}, bf...) custom-call(s32[2]{0:T(128)S(1)} %pad_add_fusion.place_ref, ...), custom_call_target="tpu_custom_call" | custom-call | flops 16777216 | bytes 2097152 | tf_op jit(solution)/shard_map/front_attention/pallas_call | solution.py:625
  62.2 3.2 %collective-permute-start.13 = (bf16[64,128]{1,0:T(8,128)(2,1)S(1)}, bf16[64,128]{1,0:T(8,128)(2,1)S(1)}, u32[]{:S(2)}, u32[]{:S(2)}) collective-permute-start(bf16[64,128]{1,0:T(8,128)(2,1)S(1)} %get-tuple-element.56), channel_id=1, source_target_pairs={{0,14},{1,15},{2,12},{3,13},{4,10},{5,11},{6,8},{7,9},{8,6},{9,7},... | collective-permute-start | bytes 49160 | tf_op jit(solution)/shard_map/ppermute | solution.py:509
  65.4 1.5 %collective-permute-start.14 = (bf16[64,128]{1,0:T(8,128)(2,1)S(1)}, bf16[64,128]{1,0:T(8,128)(2,1)S(1)}, u32[]{:S(2)}, u32[]{:S(2)}) collective-permute-start(bf16[64,128]{1,0:T(8,128)(2,1)S(1)} %get-tuple-element.57), channel_id=1, source_target_pairs={{0,12},{1,13},{2,14},{3,15},{4,8},{5,9},{6,10},{7,11},{8,4},{9,5},... | collective-permute-start | bytes 49160 | tf_op jit(solution)/shard_map/ppermute | solution.py:509
  67.0 2.9 %collective-permute-start.16 = (bf16[64,128]{1,0:T(8,128)(2,1)S(1)}, bf16[64,128]{1,0:T(8,128)(2,1)S(1)}, u32[]{:S(2)}, u32[]{:S(2)}) collective-permute-start(bf16[64,128]{1,0:T(8,128)(2,1)S(1)} %get-tuple-element.59), channel_id=1, source_target_pairs={{0,8},{1,9},{2,10},{3,11},{4,12},{5,13},{6,14},{7,15},{8,0},{9,1},... | collective-permute-start | bytes 49160 | tf_op jit(solution)/shard_map/ppermute | solution.py:509
  69.9 0.9 %collective-permute-start.17 = (bf16[64,128]{1,0:T(8,128)(2,1)S(1)}, bf16[64,128]{1,0:T(8,128)(2,1)S(1)}, u32[]{:S(2)}, u32[]{:S(2)}) collective-permute-start(bf16[64,128]{1,0:T(8,128)(2,1)S(1)} %get-tuple-element.60), channel_id=1, source_target_pairs={{0,6},{1,7},{2,4},{3,5},{4,2},{5,3},{6,0},{7,1},{8,14},{9,15},{10,... | collective-permute-start | bytes 49160 | tf_op jit(solution)/shard_map/ppermute | solution.py:509
  70.7 2.1 %collective-permute-start.18 = (bf16[64,128]{1,0:T(8,128)(2,1)S(1)}, bf16[64,128]{1,0:T(8,128)(2,1)S(1)}, u32[]{:S(2)}, u32[]{:S(2)}) collective-permute-start(bf16[64,128]{1,0:T(8,128)(2,1)S(1)} %get-tuple-element.61), channel_id=1, source_target_pairs={{0,4},{1,5},{2,6},{3,7},{4,0},{5,1},{6,2},{7,3},{8,12},{9,13},{10,... | collective-permute-start | bytes 49160 | tf_op jit(solution)/shard_map/ppermute | solution.py:509
  73.4 1.1 %collective-permute-done.17.refs_4_ = bf16[64,128]{1,0:T(8,128)(2,1)S(1)} collective-permute-done((bf16[64,128]{1,0:T(8,128)(2,1)S(1)}, bf16[64,128]{1,0:T(8,128)(2,1)S(1)}, u32[]{:S(2)}, u32[]{:S(2)}) %collective-permute-start.17) | collective-permute-done | bytes 16416 | tf_op jit(solution)/shard_map/ppermute | solution.py:509
  74.7 1.9 %collective-permute-done.19.refs_6_ = bf16[64,128]{1,0:T(8,128)(2,1)S(1)} collective-permute-done((bf16[64,128]{1,0:T(8,128)(2,1)S(1)}, bf16[64,128]{1,0:T(8,128)(2,1)S(1)}, u32[]{:S(2)}, u32[]{:S(2)}) %collective-permute-start.19) | collective-permute-done | bytes 16416 | tf_op jit(solution)/shard_map/ppermute | solution.py:509
  (43 shorter events, 3.4 us)
Async XLA Ops:
  3.6 12.8 %collective-permute-start.1 = (bf16[1072,128]{1,0:T(8,128)(2,1)}, bf16[1072,128]{1,0:T(8,128)(2,1)S(1)}, u32[]{:S(2)}, u32[]{:S(2)}) collective-permute-start(bf16[1072,128]{1,0:T(8,128)(2,1)} %get-tuple-element.34), channel_id=1, source_target_pairs={{0,12},{1,13},{2,14},{3,15},{4,8},{5,9},{6,10},{7,11},{8,4},{9,5},... | collective-permute-start | bytes 823304 | tf_op jit(solution)/shard_map/ppermute | solution.py:509
  8.7 29.4 %collective-permute-start.7 = (bf16[1024,256]{1,0:T(8,128)(2,1)S(1)}, bf16[1024,256]{1,0:T(8,128)(2,1)S(1)}, u32[]{:S(2)}, u32[]{:S(2)}) collective-permute-start(bf16[1024,256]{1,0:T(8,128)(2,1)S(1)} %copy-done), channel_id=1, source_target_pairs={{0,2},{1,3},{2,0},{3,1},{4,6},{5,7},{6,4},{7,5},{8,10},{9,11},{10,... | collective-permute-start | bytes 1572872 | tf_op jit(solution)/shard_map/ppermute | solution.py:509
  10.2 27.9 %collective-permute-start.8 = (bf16[1024,256]{1,0:T(8,128)(2,1)S(1)}, bf16[1024,256]{1,0:T(8,128)(2,1)S(1)}, u32[]{:S(2)}, u32[]{:S(2)}) collective-permute-start(bf16[1024,256]{1,0:T(8,128)(2,1)S(1)} %copy-done.1), channel_id=1, source_target_pairs={{0,2},{1,3},{2,0},{3,1},{4,6},{5,7},{6,4},{7,5},{8,10},{9,11},{10,... | collective-permute-start | bytes 1572872 | tf_op jit(solution)/shard_map/ppermute | solution.py:509
  10.8 21.6 %collective-permute-start = (bf16[1072,128]{1,0:T(8,128)(2,1)}, bf16[1072,128]{1,0:T(8,128)(2,1)S(1)}, u32[]{:S(2)}, u32[]{:S(2)}) collective-permute-start(bf16[1072,128]{1,0:T(8,128)(2,1)} %get-tuple-element.33), channel_id=1, source_target_pairs={{0,8},{1,9},{2,10},{3,11},{4,12},{5,13},{6,14},{7,15},{8,0},{9,1},... | collective-permute-start | bytes 823304 | tf_op jit(solution)/shard_map/ppermute | solution.py:509
  10.8 21.7 %collective-permute-start.2 = (bf16[1072,128]{1,0:T(8,128)(2,1)}, bf16[1072,128]{1,0:T(8,128)(2,1)S(1)}, u32[]{:S(2)}, u32[]{:S(2)}) collective-permute-start(bf16[1072,128]{1,0:T(8,128)(2,1)} %get-tuple-element.38), channel_id=1, source_target_pairs={{0,1},{1,0},{2,3},{3,2},{4,5},{5,4},{6,7},{7,6},{8,9},{9,8},{10,11... | collective-permute-start | bytes 823304 | tf_op jit(solution)/shard_map/ppermute | solution.py:509
  16.5 21.7 %collective-permute-start.5 = (bf16[1072,128]{1,0:T(8,128)(2,1)}, bf16[1072,128]{1,0:T(8,128)(2,1)S(1)}, u32[]{:S(2)}, u32[]{:S(2)}) collective-permute-start(bf16[1072,128]{1,0:T(8,128)(2,1)} %get-tuple-element.41), channel_id=1, source_target_pairs={{0,4},{1,5},{2,6},{3,7},{4,0},{5,1},{6,2},{7,3},{8,12},{9,13},{10,... | collective-permute-start | bytes 823304 | tf_op jit(solution)/shard_map/ppermute | solution.py:509
  32.4 17.0 %copy-start.4 = (bf16[4,128,256]{2,1,0:T(8,128)(2,1)S(1)}, bf16[4,128,256]{2,1,0:T(8,128)(2,1)}, u32[]{:S(2)}) copy-start(bf16[4,128,256]{2,1,0:T(8,128)(2,1)} %refs_3_.1) | copy-start | bytes 786436
  32.4 17.0 %copy-start.7 = (s32[16]{0:T(128)S(1)}, s32[16]{0:T(128)}, u32[]{:S(2)}) copy-start(s32[16]{0:T(128)} %table_ref.1) | copy-start | bytes 196
  32.4 27.7 %copy-start.5 = (f32[256]{0:T(256)S(1)}, f32[256]{0:T(256)}, u32[]{:S(2)}) copy-start(f32[256]{0:T(256)} %param.17) | copy-start | bytes 3076
  32.4 27.7 %copy-start.6 = (f32[256]{0:T(256)S(1)}, f32[256]{0:T(256)}, u32[]{:S(2)}) copy-start(f32[256]{0:T(256)} %param.18) | copy-start | bytes 3076
  32.4 5.7 %collective-permute-start.4 = (bf16[1072,128]{1,0:T(8,128)(2,1)S(1)}, bf16[1072,128]{1,0:T(8,128)(2,1)S(1)}, u32[]{:S(2)}, u32[]{:S(2)}) collective-permute-start(bf16[1072,128]{1,0:T(8,128)(2,1)S(1)} %collective-permute-done.refs_4_), channel_id=1, source_target_pairs={{0,1},{1,0},{2,3},{3,2},{4,5},{5,4},{6,7},{7,6},{8,9},{9,8},{10,11... | collective-permute-start | bytes 823304 | tf_op jit(solution)/shard_map/ppermute | solution.py:509
  32.5 5.6 %collective-permute-start.3 = (bf16[1072,128]{1,0:T(8,128)(2,1)S(1)}, bf16[1072,128]{1,0:T(8,128)(2,1)S(1)}, u32[]{:S(2)}, u32[]{:S(2)}) collective-permute-start(bf16[1072,128]{1,0:T(8,128)(2,1)S(1)} %collective-permute-done.1.refs_2_), channel_id=1, source_target_pairs={{0,1},{1,0},{2,3},{3,2},{4,5},{5,4},{6,7},{7,6},{8,9},{9,8},{10,11... | collective-permute-start | bytes 823304 | tf_op jit(solution)/shard_map/ppermute | solution.py:509
  38.1 1.6 %collective-permute-start.6 = (bf16[1072,128]{1,0:T(8,128)(2,1)S(1)}, bf16[1072,128]{1,0:T(8,128)(2,1)S(1)}, u32[]{:S(2)}, u32[]{:S(2)}) collective-permute-start(bf16[1072,128]{1,0:T(8,128)(2,1)S(1)} %collective-permute-done.5.refs_6_), channel_id=1, source_target_pairs={{0,1},{1,0},{2,3},{3,2},{4,5},{5,4},{6,7},{7,6},{8,9},{9,8},{10,11... | collective-permute-start | bytes 823304 | tf_op jit(solution)/shard_map/ppermute | solution.py:509
  41.0 9.8 %collective-permute-start.9 = (bf16[784,128]{1,0:T(8,128)(2,1)S(1)}, bf16[784,128]{1,0:T(8,128)(2,1)S(1)}, u32[]{:S(2)}, u32[]{:S(2)}) collective-permute-start(bf16[784,128]{1,0:T(8,128)(2,1)S(1)} %get-tuple-element.43), channel_id=1, source_target_pairs={{0,12},{1,13},{2,14},{3,15},{4,8},{5,9},{6,10},{7,11},{8,4},{9,5},... | collective-permute-start | bytes 602120 | tf_op jit(solution)/shard_map/ppermute | solution.py:509
  43.4 16.7 %collective-permute-start.10 = (bf16[784,128]{1,0:T(8,128)(2,1)S(1)}, bf16[784,128]{1,0:T(8,128)(2,1)S(1)}, u32[]{:S(2)}, u32[]{:S(2)}) collective-permute-start(bf16[784,128]{1,0:T(8,128)(2,1)S(1)} %get-tuple-element.44), channel_id=1, source_target_pairs={{0,8},{1,9},{2,10},{3,11},{4,12},{5,13},{6,14},{7,15},{8,0},{9,1},... | collective-permute-start | bytes 602120 | tf_op jit(solution)/shard_map/ppermute | solution.py:509
  43.4 16.7 %collective-permute-start.11 = (bf16[784,128]{1,0:T(8,128)(2,1)S(1)}, bf16[784,128]{1,0:T(8,128)(2,1)S(1)}, u32[]{:S(2)}, u32[]{:S(2)}) collective-permute-start(bf16[784,128]{1,0:T(8,128)(2,1)S(1)} %get-tuple-element.45), channel_id=1, source_target_pairs={{0,4},{1,5},{2,6},{3,7},{4,0},{5,1},{6,2},{7,3},{8,12},{9,13},{10,... | collective-permute-start | bytes 602120 | tf_op jit(solution)/shard_map/ppermute | solution.py:509
  45.5 3.9 %collective-permute-start.12 = (bf16[128,128]{1,0:T(8,128)(2,1)S(1)}, bf16[128,128]{1,0:T(8,128)(2,1)S(1)}, u32[]{:S(2)}, u32[]{:S(2)}) collective-permute-start(bf16[128,128]{1,0:T(8,128)(2,1)S(1)} %get-tuple-element.48.refs_0_), channel_id=1, source_target_pairs={{0,2},{1,3},{2,0},{3,1},{4,6},{5,7},{6,4},{7,5},{8,10},{9,11},{10,... | collective-permute-start | bytes 98312 | tf_op jit(solution)/shard_map/ppermute | solution.py:509
  62.2 8.5 %collective-permute-start.13 = (bf16[64,128]{1,0:T(8,128)(2,1)S(1)}, bf16[64,128]{1,0:T(8,128)(2,1)S(1)}, u32[]{:S(2)}, u32[]{:S(2)}) collective-permute-start(bf16[64,128]{1,0:T(8,128)(2,1)S(1)} %get-tuple-element.56), channel_id=1, source_target_pairs={{0,14},{1,15},{2,12},{3,13},{4,10},{5,11},{6,8},{7,9},{8,6},{9,7},... | collective-permute-start | bytes 49160 | tf_op jit(solution)/shard_map/ppermute | solution.py:509
  65.4 7.4 %collective-permute-start.14 = (bf16[64,128]{1,0:T(8,128)(2,1)S(1)}, bf16[64,128]{1,0:T(8,128)(2,1)S(1)}, u32[]{:S(2)}, u32[]{:S(2)}) collective-permute-start(bf16[64,128]{1,0:T(8,128)(2,1)S(1)} %get-tuple-element.57), channel_id=1, source_target_pairs={{0,12},{1,13},{2,14},{3,15},{4,8},{5,9},{6,10},{7,11},{8,4},{9,5},... | collective-permute-start | bytes 49160 | tf_op jit(solution)/shard_map/ppermute | solution.py:509
  67.0 6.4 %collective-permute-start.15 = (bf16[64,128]{1,0:T(8,128)(2,1)S(1)}, bf16[64,128]{1,0:T(8,128)(2,1)S(1)}, u32[]{:S(2)}, u32[]{:S(2)}) collective-permute-start(bf16[64,128]{1,0:T(8,128)(2,1)S(1)} %get-tuple-element.58), channel_id=1, source_target_pairs={{0,10},{1,11},{2,8},{3,9},{4,14},{5,15},{6,12},{7,13},{8,2},{9,3},... | collective-permute-start | bytes 49160 | tf_op jit(solution)/shard_map/ppermute | solution.py:509
  67.0 6.4 %collective-permute-start.16 = (bf16[64,128]{1,0:T(8,128)(2,1)S(1)}, bf16[64,128]{1,0:T(8,128)(2,1)S(1)}, u32[]{:S(2)}, u32[]{:S(2)}) collective-permute-start(bf16[64,128]{1,0:T(8,128)(2,1)S(1)} %get-tuple-element.59), channel_id=1, source_target_pairs={{0,8},{1,9},{2,10},{3,11},{4,12},{5,13},{6,14},{7,15},{8,0},{9,1},... | collective-permute-start | bytes 49160 | tf_op jit(solution)/shard_map/ppermute | solution.py:509
  69.9 4.6 %collective-permute-start.17 = (bf16[64,128]{1,0:T(8,128)(2,1)S(1)}, bf16[64,128]{1,0:T(8,128)(2,1)S(1)}, u32[]{:S(2)}, u32[]{:S(2)}) collective-permute-start(bf16[64,128]{1,0:T(8,128)(2,1)S(1)} %get-tuple-element.60), channel_id=1, source_target_pairs={{0,6},{1,7},{2,4},{3,5},{4,2},{5,3},{6,0},{7,1},{8,14},{9,15},{10,... | collective-permute-start | bytes 49160 | tf_op jit(solution)/shard_map/ppermute | solution.py:509
  70.7 4.0 %collective-permute-start.18 = (bf16[64,128]{1,0:T(8,128)(2,1)S(1)}, bf16[64,128]{1,0:T(8,128)(2,1)S(1)}, u32[]{:S(2)}, u32[]{:S(2)}) collective-permute-start(bf16[64,128]{1,0:T(8,128)(2,1)S(1)} %get-tuple-element.61), channel_id=1, source_target_pairs={{0,4},{1,5},{2,6},{3,7},{4,0},{5,1},{6,2},{7,3},{8,12},{9,13},{10,... | collective-permute-start | bytes 49160 | tf_op jit(solution)/shard_map/ppermute | solution.py:509
  72.8 3.7 %collective-permute-start.19 = (bf16[64,128]{1,0:T(8,128)(2,1)S(1)}, bf16[64,128]{1,0:T(8,128)(2,1)S(1)}, u32[]{:S(2)}, u32[]{:S(2)}) collective-permute-start(bf16[64,128]{1,0:T(8,128)(2,1)S(1)} %get-tuple-element.62), channel_id=1, source_target_pairs={{0,2},{1,3},{2,0},{3,1},{4,6},{5,7},{6,4},{7,5},{8,10},{9,11},{10,... | collective-permute-start | bytes 49160 | tf_op jit(solution)/shard_map/ppermute | solution.py:509
  (4 other events, 35.6 us)

commit v3 on v2

--- a/solution.py
+++ b/solution.py
@@ -417,10 +417,12 @@
         )
         stats = (kept_stats(top[:, 0:1], total[:, 0:1]), sent_stats(top[:, 0:1], total[:, 0:1]))
         each = own_queries * sharing
-        for slot, out in enumerate(outs):
+        for slot in range(GROUPS * PAIR):
+            start = (slot // PAIR * 2 * heads + head) * each
             at = slice(slot * each, (slot + 1) * each)
-            out[head * each : (head + 1) * each, :] = numer[at].astype(out.dtype)
-            out[(heads + head) * each : (heads + head + 1) * each, :] = stats[slot > 0][at]
+            out = outs[slot % PAIR]
+            out[start : start + each, :] = numer[at].astype(out.dtype)
+            out[start + heads * each : start + (heads + 1) * each, :] = stats[slot % PAIR][at]
 
 
 def kept_stats(top, total):
@@ -457,6 +459,19 @@
     total = sum(f * t for f, t in zip(factors, totals))
     numer = sum(f * n for f, n in zip(factors, numers))
     return numer, top, total
+
+
+def merge_kernel(kept, other, keep_ref, *send_refs):
+    each = keep_ref.shape[0]
+    rows = each // 2
+    for slot in range(GROUPS):
+        numer, top, total = merged(kept, [other], slot * each, rows)
+        if slot == 0:
+            keep_ref[:rows, :] = numer
+            keep_ref[rows:, :] = kept_stats(top, total)
+        else:
+            send_refs[slot - 1][:rows, :] = numer.astype(jnp.bfloat16)
+            send_refs[slot - 1][rows:, :] = sent_stats(top, total)
 
 
 def last_kernel(kept, *refs):
@@ -568,8 +583,7 @@
     cosine = jnp.concatenate([cosine, cosine], 1)
     sine = jnp.concatenate([-sine, sine], 1)
 
-    first, second = far_first()[:2]
-    mine[first], own = lax.optimization_barrier((mine[first], own))
+    first = far_first()[0]
     mine[0] = pl.pallas_call(
         fetch_kernel,
         in_specs=[hbm],
@@ -580,9 +594,10 @@
         cost_estimate=pl.CostEstimate(flops=0, bytes_accessed=64 * 1024 * 1024, transcendentals=0),
         name="fetch_own",
     )(own)
-    mine[second], mine[0], cosine, sine = lax.optimization_barrier(
-        (mine[second], mine[0], cosine, sine)
-    )
+    mine[first], mine[0], cosine, sine = lax.optimization_barrier(
+        (mine[first], mine[0], cosine, sine)
+    )
+    blocks[0], far[0] = lax.optimization_barrier((blocks[0], far[0]))
     theirs = {s: move(blocks[0] if s == 0 else mine[s], sibling) for s in [0] + far_first()}
     lhs = [part[s] for s in [0] + far_first() for part in (mine, theirs)]
 
@@ -618,15 +633,15 @@
     )(place, page_slot_table, split_page, own_tiles, beside_tiles, slot_keys, slot_values)
 
 
-    def payload(kind):
-        return jax.ShapeDtypeStruct((2 * states // n_ctx, LANES), kind)
+    def payloads(size):
+        return [jax.ShapeDtypeStruct((size, LANES), kind) for kind in (jnp.float32, jnp.bfloat16)]
 
     row_shape = jax.ShapeDtypeStruct((rows, width), jnp.bfloat16)
-    front_key, front_value, kept, *sent = pl.pallas_call(
+    front_key, front_value, kept, sent = pl.pallas_call(
         front_kernel,
         in_specs=[smem, smem] + [vmem] * (GROUPS + 8),
-        out_specs=[vmem] * (2 + n_ctx),
-        out_shape=[row_shape] * 2 + [payload(jnp.float32)] + [payload(jnp.bfloat16)] * (n_ctx - 1),
+        out_specs=[vmem] * 4,
+        out_shape=[row_shape] * 2 + payloads(states),
         compiler_params=params,
         cost_estimate=pl.CostEstimate(flops=4 * states * rows * HEAD_SIZE, bytes_accessed=2 * 1024 * 1024, transcendentals=states * rows),
         name="front_attention",
@@ -644,14 +659,22 @@
         total,
         numer,
     )
+    kept, *sent = pl.pallas_call(
+        merge_kernel,
+        in_specs=[vmem] * 2,
+        out_specs=[vmem] * GROUPS,
+        out_shape=payloads(states // GROUPS) + payloads(states // GROUPS)[1:] * (GROUPS - 2),
+        compiler_params=params,
+        name="merge",
+    )(kept, move(sent, beside))
     attended = pl.pallas_call(
         last_kernel,
-        in_specs=[vmem] * n_ctx,
+        in_specs=[vmem] * GROUPS,
         out_specs=vmem,
         out_shape=jax.ShapeDtypeStruct((own_queries, query_width), jnp.bfloat16),
         compiler_params=params,
         name="finish",
-    )(kept, *[move(sent[r - 1], partner(r)) for r in range(n_ctx - 1, 0, -1)])
+    )(kept, *[move(sent[s - 1], along(s)) for s in far_first()])
     return (front_key, front_value, attended)
 
 

time: 77.6 us -> 70.8 us (0.912)
  starting transfers between devices: 36.3 us -> 20.3 us
  waiting for transfers between devices: 29.5 us -> 38.5 us
    ppermute x20 -> x17, starting transfers between devices: 36.3 us -> 20.3 us  [move(): return lax.ppermute(array, ('ctx', 'tp'), pairs)]
    ppermute x20 -> x17, waiting for transfers between devices: 29.5 us -> 38.5 us  [move(): return lax.ppermute(array, ('ctx', 'tp'), pairs)]
  transfers between devices with their start and end apart: 20 -> 17, of which waited for: 10 -> 12; matrix products, arithmetic and copies ran while one was open for 1% -> 1% of each run, Pallas kernels for 2% -> 6%
where the time goes in v3:
time: 70.8 us; the launch traced here: 70.7 us
  waiting for transfers between devices  38.5 us (54%)
  starting transfers between devices  20.3 us (29%)
  Pallas kernels  8.9 us (13%)
  between operations  1.41 us (2%)
  local copies, waits for them, and re-layouts  0.99 us (1%)
    ppermute x17, waiting for transfers between devices, move(): return lax.ppermute(array, ('ctx', 'tp'), pairs)  38.5 us
    ppermute x17, starting transfers between devices, move(): return lax.ppermute(array, ('ctx', 'tp'), pairs)  20.3 us
    pallas_call x1, Pallas kernels, exchange_plan(): pl.pallas_call(norm_kernel, in_specs=[hbm] * 4, out_specs=[hbm] * (GROUPS...  2.89 us
    pallas_call x1, Pallas kernels, exchange_plan(): pl.pallas_call(front_kernel, in_specs=[smem, smem] + [vmem] * (GROUPS + 8...  2.08 us
  transfers between devices with their start and end apart: 17, of which 12 were waited for; matrix products, arithmetic and copies ran while one was open for 1% of the time, Pallas kernels for 6%

profile of v3, /device:TPU:0, one launch (start us, length us, event | category | flops | bytes accessed | tf_op | source)
XLA Modules:
  0.0 70.7 jit_solution(16835648906699982055)
XLA Ops:
  0.7 3.0 %collective-permute-start.1 = (bf16[1024,256]{1,0:T(8,128)(2,1)}, bf16[1024,256]{1,0:T(8,128)(2,1)S(1)}, u32[]{:S(2)}, u32[]{:S(2)}) collective-permute-start(bf16[1024,256]{1,0:T(8,128)(2,1)} %refs_8_.1), channel_id=1, source_target_pairs={{0,2},{1,3},{2,0},{3,1},{4,6},{5,7},{6,4},{7,5},{8,10},{9,11},{10,... | collective-permute-start | bytes 1572872 | tf_op jit(solution)/shard_map/ppermute | solution.py:524
  3.7 2.9 %norm_rows.1 = (bf16[1072,128]{1,0:T(8,128)(2,1)}, bf16[1072,128]{1,0:T(8,128)(2,1)}, bf16[1072,128]{1,0:T(8,128)(2,1)}, bf16[1072,128]{1,0:T(8,128)(2,1)}, bf16[1072,128]{1,0:T(8,128)(2,1)}) custom-call(bf16[2,2048]{1,0:T(2,128)(2,1)} %query_any.1, bf16[128,8192]{1,0:T(8,128)(2,1)} %hidden_any.1, bf16[2,8192]{1,0:T(2,128)(2,1)} %suffix_any.1, f32[1,8192]{1,0:T(1,128)} %bitcast.7), custom_call_target="tpu_custom_call" | custom-call | flops 2097152 | bytes 2097152 | tf_op jit(solution)/shard_map/norm_rows/pallas_call | solution.py:543
  6.6 4.1 %collective-permute-start = (bf16[1072,128]{1,0:T(8,128)(2,1)}, bf16[1072,128]{1,0:T(8,128)(2,1)S(1)}, u32[]{:S(2)}, u32[]{:S(2)}) collective-permute-start(bf16[1072,128]{1,0:T(8,128)(2,1)} %get-tuple-element.31), channel_id=1, source_target_pairs={{0,12},{1,13},{2,14},{3,15},{4,8},{5,9},{6,10},{7,11},{8,4},{9,5},... | collective-permute-start | bytes 823304 | tf_op jit(solution)/shard_map/ppermute | solution.py:524
  10.8 0.6 collective-permute-start.6
  11.4 1.0 %copy-done.2 = bf16[1072,128]{1,0:T(8,128)(2,1)S(1)} copy-done((bf16[1072,128]{1,0:T(8,128)(2,1)S(1)}, bf16[1072,128]{1,0:T(8,128)(2,1)}, u32[]{:S(2)}) %copy-start.2) | copy-done | bytes 274456
  12.9 5.6 %collective-permute-done.refs_2_ = bf16[1072,128]{1,0:T(8,128)(2,1)S(1)} collective-permute-done((bf16[1072,128]{1,0:T(8,128)(2,1)}, bf16[1072,128]{1,0:T(8,128)(2,1)S(1)}, u32[]{:S(2)}, u32[]{:S(2)}) %collective-permute-start) | collective-permute-done | bytes 274464 | tf_op jit(solution)/shard_map/ppermute | solution.py:524
  18.5 15.2 %collective-permute-done.4.refs_4_ = bf16[1072,128]{1,0:T(8,128)(2,1)S(1)} collective-permute-done((bf16[1072,128]{1,0:T(8,128)(2,1)}, bf16[1072,128]{1,0:T(8,128)(2,1)S(1)}, u32[]{:S(2)}, u32[]{:S(2)}) %collective-permute-start.4) | collective-permute-done | bytes 274464 | tf_op jit(solution)/shard_map/ppermute | solution.py:524
  33.8 0.5 collective-permute-start.7
  34.4 0.9 %collective-permute-done.5.refs_5_ = bf16[1072,128]{1,0:T(8,128)(2,1)S(1)} collective-permute-done((bf16[1072,128]{1,0:T(8,128)(2,1)S(1)}, bf16[1072,128]{1,0:T(8,128)(2,1)S(1)}, u32[]{:S(2)}, u32[]{:S(2)}) %collective-permute-start.5) | collective-permute-done | bytes 274464 | tf_op jit(solution)/shard_map/ppermute | solution.py:524
  35.7 0.6 collective-permute-done.2.refs_1_
  36.3 1.4 %project.1 = (bf16[784,128]{1,0:T(8,128)(2,1)S(1)}, bf16[784,128]{1,0:T(8,128)(2,1)S(1)}, bf16[784,128]{1,0:T(8,128)(2,1)S(1)}, bf16[784,128]{1,0:T(8,128)(2,1)S(1)}, bf16[128,128]{1,0:T(8,128)(2,1)S(1)}) custom-call(bf16[1072,128]{1,0:T(8,128)(2,1)S(1)} %fetch_own.1.refs_0_, bf16[1072,128]{1,0:T(8,128)(2,1)S(1)} %collective-permute-done.2.refs_1_, ...), custom_call_target="tpu_custom_call" | custom-call | flops 1073741824 | bytes 6291456 | tf_op jit(solution)/shard_map/project/pallas_call | solution.py:605
  37.7 2.5 %collective-permute-start.9 = (bf16[784,128]{1,0:T(8,128)(2,1)S(1)}, bf16[784,128]{1,0:T(8,128)(2,1)S(1)}, u32[]{:S(2)}, u32[]{:S(2)}) collective-permute-start(bf16[784,128]{1,0:T(8,128)(2,1)S(1)} %get-tuple-element.41), channel_id=1, source_target_pairs={{0,12},{1,13},{2,14},{3,15},{4,8},{5,9},{6,10},{7,11},{8,4},{9,5},... | collective-permute-start | bytes 602120 | tf_op jit(solution)/shard_map/ppermute | solution.py:524
  40.3 1.9 %collective-permute-start.11 = (bf16[784,128]{1,0:T(8,128)(2,1)S(1)}, bf16[784,128]{1,0:T(8,128)(2,1)S(1)}, u32[]{:S(2)}, u32[]{:S(2)}) collective-permute-start(bf16[784,128]{1,0:T(8,128)(2,1)S(1)} %get-tuple-element.43), channel_id=1, source_target_pairs={{0,4},{1,5},{2,6},{3,7},{4,0},{5,1},{6,2},{7,3},{8,12},{9,13},{10,... | collective-permute-start | bytes 602120 | tf_op jit(solution)/shard_map/ppermute | solution.py:524
  42.2 1.5 %collective-permute-start.12 = (bf16[128,128]{1,0:T(8,128)(2,1)S(1)}, bf16[128,128]{1,0:T(8,128)(2,1)S(1)}, u32[]{:S(2)}, u32[]{:S(2)}) collective-permute-start(bf16[128,128]{1,0:T(8,128)(2,1)S(1)} %get-tuple-element.46.refs_0_), channel_id=1, source_target_pairs={{0,2},{1,3},{2,0},{3,1},{4,6},{5,7},{6,4},{7,5},{8,10},{9,11},{10,... | collective-permute-start | bytes 98312 | tf_op jit(solution)/shard_map/ppermute | solution.py:524
  44.4 1.7 %collective-permute-done.12.refs_1_ = bf16[128,128]{1,0:T(8,128)(2,1)S(1)} collective-permute-done((bf16[128,128]{1,0:T(8,128)(2,1)S(1)}, bf16[128,128]{1,0:T(8,128)(2,1)S(1)}, u32[]{:S(2)}, u32[]{:S(2)}) %collective-permute-start.12) | collective-permute-done | bytes 32800 | tf_op jit(solution)/shard_map/ppermute | solution.py:524
  46.1 1.4 %loaded_attention.1 = (f32[256,128]{1,0:T(8,128)S(1)}, f32[256,128]{1,0:T(8,128)S(1)}, f32[256,128]{1,0:T(8,128)S(1)}, bf16[256,128]{1,0:T(8,128)(2,1)S(1)}) custom-call(s32[2]{0:T(128)S(1)} %pad_add_fusion.place_ref, s32[16]{0:T(128)S(1)} %copy-done.7, s32[1]{0:T(128)S(6)} %copy.15.split_ref, bf16[128,128]{1,0:T(8,128)(2,1)S(1)} %get-tuple-element.46.refs_0_, ...), custom_call_target="tpu_custom_call" | custom-call | flops 67108864 | bytes 524288 | tf_op jit(solution)/shard_map/loaded_attention/pallas_call | solution.py:621
  47.6 9.4 %collective-permute-done.10.refs_1_ = bf16[784,128]{1,0:T(8,128)(2,1)S(1)} collective-permute-done((bf16[784,128]{1,0:T(8,128)(2,1)S(1)}, bf16[784,128]{1,0:T(8,128)(2,1)S(1)}, u32[]{:S(2)}, u32[]{:S(2)}) %collective-permute-start.10) | collective-permute-done | bytes 200736 | tf_op jit(solution)/shard_map/ppermute | solution.py:524
  56.9 2.1 %front_attention.1 = (bf16[128,256]{1,0:T(8,128)(2,1)}, bf16[128,256]{1,0:T(8,128)(2,1)}, f32[256,128]{1,0:T(8,128)S(1)}, bf16[256,128]{1,0:T(8,128)(2,1)S(1)}) custom-call(s32[2]{0:T(128)S(1)} %pad_add_fusion.place_ref, s32[1]{0:T(128)S(6)} %copy.15.split_ref, bf16[784,128]{1,0:T(8,128)(2,1)S(1)} %get-tuple-element.40.own, ...), custom_call_target="tpu_custom_call" | custom-call | flops 16777216 | bytes 2097152 | tf_op jit(solution)/shard_map/front_attention/pallas_call | solution.py:640
  59.0 1.5 %collective-permute-start.13 = (bf16[256,128]{1,0:T(8,128)(2,1)S(1)}, bf16[256,128]{1,0:T(8,128)(2,1)S(1)}, u32[]{:S(2)}, u32[]{:S(2)}) collective-permute-start(bf16[256,128]{1,0:T(8,128)(2,1)S(1)} %get-tuple-element.54), channel_id=1, source_target_pairs={{0,2},{1,3},{2,0},{3,1},{4,6},{5,7},{6,4},{7,5},{8,10},{9,11},{10,... | collective-permute-start | bytes 196616 | tf_op jit(solution)/shard_map/ppermute | solution.py:524
  60.5 2.8 %collective-permute-done.13.other = bf16[256,128]{1,0:T(8,128)(2,1)S(1)} collective-permute-done((bf16[256,128]{1,0:T(8,128)(2,1)S(1)}, bf16[256,128]{1,0:T(8,128)(2,1)S(1)}, u32[]{:S(2)}, u32[]{:S(2)}) %collective-permute-start.13) | collective-permute-done | bytes 65568 | tf_op jit(solution)/shard_map/ppermute | solution.py:524
  63.6 1.4 %collective-permute-start.14 = (bf16[64,128]{1,0:T(8,128)(2,1)S(1)}, bf16[64,128]{1,0:T(8,128)(2,1)S(1)}, u32[]{:S(2)}, u32[]{:S(2)}) collective-permute-start(bf16[64,128]{1,0:T(8,128)(2,1)S(1)} %get-tuple-element.56), channel_id=1, source_target_pairs={{0,12},{1,13},{2,14},{3,15},{4,8},{5,9},{6,10},{7,11},{8,4},{9,5},... | collective-permute-start | bytes 49160 | tf_op jit(solution)/shard_map/ppermute | solution.py:524
  65.0 3.0 %collective-permute-start.16 = (bf16[64,128]{1,0:T(8,128)(2,1)S(1)}, bf16[64,128]{1,0:T(8,128)(2,1)S(1)}, u32[]{:S(2)}, u32[]{:S(2)}) collective-permute-start(bf16[64,128]{1,0:T(8,128)(2,1)S(1)} %get-tuple-element.58), channel_id=1, source_target_pairs={{0,4},{1,5},{2,6},{3,7},{4,0},{5,1},{6,2},{7,3},{8,12},{9,13},{10,... | collective-permute-start | bytes 49160 | tf_op jit(solution)/shard_map/ppermute | solution.py:524
  68.0 1.1 %collective-permute-done.14.refs_0_ = bf16[64,128]{1,0:T(8,128)(2,1)S(1)} collective-permute-done((bf16[64,128]{1,0:T(8,128)(2,1)S(1)}, bf16[64,128]{1,0:T(8,128)(2,1)S(1)}, u32[]{:S(2)}, u32[]{:S(2)}) %collective-permute-start.14) | collective-permute-done | bytes 16416 | tf_op jit(solution)/shard_map/ppermute | solution.py:524
  69.8 0.8 %finish.1 = bf16[2,2048]{1,0:T(2,128)(2,1)} custom-call(f32[64,128]{1,0:T(8,128)S(1)} %get-tuple-element.55.kept, bf16[64,128]{1,0:T(8,128)(2,1)S(1)} %collective-permute-done.14.refs_0_, bf16[64,128]{1,0:T(8,128)(2,1)S(1)} %collective-permute-done.15.refs_1_, bf16[64,128]{1,0:T(8,128)(2,1)S(1)} %collective-permute-done.16.refs_2_), custom_call_target="tpu_custom_call" | custom-call | tf_op jit(solution)/shard_map/finish/pallas_call | solution.py:670
  (38 shorter events, 2.2 us)
Async XLA Ops:
  0.6 35.7 %copy-start = (bf16[1024,256]{1,0:T(8,128)(2,1)S(1)}, bf16[1024,256]{1,0:T(8,128)(2,1)}, u32[]{:S(2)}) copy-start(bf16[1024,256]{1,0:T(8,128)(2,1)} %refs_8_.1) | copy-start | bytes 1572868
  0.6 35.7 %copy-start.1 = (bf16[1024,256]{1,0:T(8,128)(2,1)S(1)}, bf16[1024,256]{1,0:T(8,128)(2,1)}, u32[]{:S(2)}) copy-start(bf16[1024,256]{1,0:T(8,128)(2,1)} %refs_9_.1) | copy-start | bytes 1572868
  0.7 33.6 %collective-permute-start.1 = (bf16[1024,256]{1,0:T(8,128)(2,1)}, bf16[1024,256]{1,0:T(8,128)(2,1)S(1)}, u32[]{:S(2)}, u32[]{:S(2)}) collective-permute-start(bf16[1024,256]{1,0:T(8,128)(2,1)} %refs_8_.1), channel_id=1, source_target_pairs={{0,2},{1,3},{2,0},{3,1},{4,6},{5,7},{6,4},{7,5},{8,10},{9,11},{10,... | collective-permute-start | bytes 1572872 | tf_op jit(solution)/shard_map/ppermute | solution.py:524
  3.7 30.8 %collective-permute-start.8 = (bf16[1024,256]{1,0:T(8,128)(2,1)}, bf16[1024,256]{1,0:T(8,128)(2,1)S(1)}, u32[]{:S(2)}, u32[]{:S(2)}) collective-permute-start(bf16[1024,256]{1,0:T(8,128)(2,1)} %refs_9_.1), channel_id=1, source_target_pairs={{0,2},{1,3},{2,0},{3,1},{4,6},{5,7},{6,4},{7,5},{8,10},{9,11},{10,... | collective-permute-start | bytes 1572872 | tf_op jit(solution)/shard_map/ppermute | solution.py:524
  6.6 11.9 %collective-permute-start = (bf16[1072,128]{1,0:T(8,128)(2,1)}, bf16[1072,128]{1,0:T(8,128)(2,1)S(1)}, u32[]{:S(2)}, u32[]{:S(2)}) collective-permute-start(bf16[1072,128]{1,0:T(8,128)(2,1)} %get-tuple-element.31), channel_id=1, source_target_pairs={{0,12},{1,13},{2,14},{3,15},{4,8},{5,9},{6,10},{7,11},{8,4},{9,5},... | collective-permute-start | bytes 823304 | tf_op jit(solution)/shard_map/ppermute | solution.py:524
  10.8 23.0 %collective-permute-start.4 = (bf16[1072,128]{1,0:T(8,128)(2,1)}, bf16[1072,128]{1,0:T(8,128)(2,1)S(1)}, u32[]{:S(2)}, u32[]{:S(2)}) collective-permute-start(bf16[1072,128]{1,0:T(8,128)(2,1)} %get-tuple-element.37), channel_id=1, source_target_pairs={{0,8},{1,9},{2,10},{3,11},{4,12},{5,13},{6,14},{7,15},{8,0},{9,1},... | collective-permute-start | bytes 823304 | tf_op jit(solution)/shard_map/ppermute | solution.py:524
  10.8 23.0 %collective-permute-start.6 = (bf16[1072,128]{1,0:T(8,128)(2,1)}, bf16[1072,128]{1,0:T(8,128)(2,1)S(1)}, u32[]{:S(2)}, u32[]{:S(2)}) collective-permute-start(bf16[1072,128]{1,0:T(8,128)(2,1)} %get-tuple-element.38), channel_id=1, source_target_pairs={{0,4},{1,5},{2,6},{3,7},{4,0},{5,1},{6,2},{7,3},{8,12},{9,13},{10,... | collective-permute-start | bytes 823304 | tf_op jit(solution)/shard_map/ppermute | solution.py:524
  18.5 15.9 %collective-permute-start.3 = (bf16[1072,128]{1,0:T(8,128)(2,1)S(1)}, bf16[1072,128]{1,0:T(8,128)(2,1)S(1)}, u32[]{:S(2)}, u32[]{:S(2)}) collective-permute-start(bf16[1072,128]{1,0:T(8,128)(2,1)S(1)} %collective-permute-done.refs_2_), channel_id=1, source_target_pairs={{0,1},{1,0},{2,3},{3,2},{4,5},{5,4},{6,7},{7,6},{8,9},{9,8},{10,11... | collective-permute-start | bytes 823304 | tf_op jit(solution)/shard_map/ppermute | solution.py:524
  33.8 1.6 %collective-permute-start.5 = (bf16[1072,128]{1,0:T(8,128)(2,1)S(1)}, bf16[1072,128]{1,0:T(8,128)(2,1)S(1)}, u32[]{:S(2)}, u32[]{:S(2)}) collective-permute-start(bf16[1072,128]{1,0:T(8,128)(2,1)S(1)} %collective-permute-done.4.refs_4_), channel_id=1, source_target_pairs={{0,1},{1,0},{2,3},{3,2},{4,5},{5,4},{6,7},{7,6},{8,9},{9,8},{10,11... | collective-permute-start | bytes 823304 | tf_op jit(solution)/shard_map/ppermute | solution.py:524
  33.8 1.9 %collective-permute-start.7 = (bf16[1072,128]{1,0:T(8,128)(2,1)S(1)}, bf16[1072,128]{1,0:T(8,128)(2,1)S(1)}, u32[]{:S(2)}, u32[]{:S(2)}) collective-permute-start(bf16[1072,128]{1,0:T(8,128)(2,1)S(1)} %collective-permute-done.6.refs_6_), channel_id=1, source_target_pairs={{0,1},{1,0},{2,3},{3,2},{4,5},{5,4},{6,7},{7,6},{8,9},{9,8},{10,11... | collective-permute-start | bytes 823304 | tf_op jit(solution)/shard_map/ppermute | solution.py:524
  34.3 11.8 %copy-start.3 = (bf16[4,128,256]{2,1,0:T(8,128)(2,1)S(1)}, bf16[4,128,256]{2,1,0:T(8,128)(2,1)}, u32[]{:S(2)}) copy-start(bf16[4,128,256]{2,1,0:T(8,128)(2,1)} %refs_2_.1) | copy-start | bytes 786436
  34.3 11.8 %copy-start.4 = (bf16[4,128,256]{2,1,0:T(8,128)(2,1)S(1)}, bf16[4,128,256]{2,1,0:T(8,128)(2,1)}, u32[]{:S(2)}) copy-start(bf16[4,128,256]{2,1,0:T(8,128)(2,1)} %refs_3_.1) | copy-start | bytes 786436
  34.3 11.8 %copy-start.7 = (s32[16]{0:T(128)S(1)}, s32[16]{0:T(128)}, u32[]{:S(2)}) copy-start(s32[16]{0:T(128)} %table_ref.1) | copy-start | bytes 196
  34.3 22.6 %copy-start.5 = (f32[256]{0:T(256)S(1)}, f32[256]{0:T(256)}, u32[]{:S(2)}) copy-start(f32[256]{0:T(256)} %param.17) | copy-start | bytes 3076
  34.3 22.6 %copy-start.6 = (f32[256]{0:T(256)S(1)}, f32[256]{0:T(256)}, u32[]{:S(2)}) copy-start(f32[256]{0:T(256)} %param.18) | copy-start | bytes 3076
  34.3 2.0 %collective-permute-start.2 = (bf16[1072,128]{1,0:T(8,128)(2,1)}, bf16[1072,128]{1,0:T(8,128)(2,1)S(1)}, u32[]{:S(2)}, u32[]{:S(2)}) collective-permute-start(bf16[1072,128]{1,0:T(8,128)(2,1)} %get-tuple-element.35), channel_id=1, source_target_pairs={{0,1},{1,0},{2,3},{3,2},{4,5},{5,4},{6,7},{7,6},{8,9},{9,8},{10,11... | collective-permute-start | bytes 823304 | tf_op jit(solution)/shard_map/ppermute | solution.py:524
  37.7 9.8 %collective-permute-start.9 = (bf16[784,128]{1,0:T(8,128)(2,1)S(1)}, bf16[784,128]{1,0:T(8,128)(2,1)S(1)}, u32[]{:S(2)}, u32[]{:S(2)}) collective-permute-start(bf16[784,128]{1,0:T(8,128)(2,1)S(1)} %get-tuple-element.41), channel_id=1, source_target_pairs={{0,12},{1,13},{2,14},{3,15},{4,8},{5,9},{6,10},{7,11},{8,4},{9,5},... | collective-permute-start | bytes 602120 | tf_op jit(solution)/shard_map/ppermute | solution.py:524
  40.3 16.7 %collective-permute-start.10 = (bf16[784,128]{1,0:T(8,128)(2,1)S(1)}, bf16[784,128]{1,0:T(8,128)(2,1)S(1)}, u32[]{:S(2)}, u32[]{:S(2)}) collective-permute-start(bf16[784,128]{1,0:T(8,128)(2,1)S(1)} %get-tuple-element.42), channel_id=1, source_target_pairs={{0,8},{1,9},{2,10},{3,11},{4,12},{5,13},{6,14},{7,15},{8,0},{9,1},... | collective-permute-start | bytes 602120 | tf_op jit(solution)/shard_map/ppermute | solution.py:524
  40.3 16.7 %collective-permute-start.11 = (bf16[784,128]{1,0:T(8,128)(2,1)S(1)}, bf16[784,128]{1,0:T(8,128)(2,1)S(1)}, u32[]{:S(2)}, u32[]{:S(2)}) collective-permute-start(bf16[784,128]{1,0:T(8,128)(2,1)S(1)} %get-tuple-element.43), channel_id=1, source_target_pairs={{0,4},{1,5},{2,6},{3,7},{4,0},{5,1},{6,2},{7,3},{8,12},{9,13},{10,... | collective-permute-start | bytes 602120 | tf_op jit(solution)/shard_map/ppermute | solution.py:524
  42.2 3.9 %collective-permute-start.12 = (bf16[128,128]{1,0:T(8,128)(2,1)S(1)}, bf16[128,128]{1,0:T(8,128)(2,1)S(1)}, u32[]{:S(2)}, u32[]{:S(2)}) collective-permute-start(bf16[128,128]{1,0:T(8,128)(2,1)S(1)} %get-tuple-element.46.refs_0_), channel_id=1, source_target_pairs={{0,2},{1,3},{2,0},{3,1},{4,6},{5,7},{6,4},{7,5},{8,10},{9,11},{10,... | collective-permute-start | bytes 98312 | tf_op jit(solution)/shard_map/ppermute | solution.py:524
  59.0 4.3 %collective-permute-start.13 = (bf16[256,128]{1,0:T(8,128)(2,1)S(1)}, bf16[256,128]{1,0:T(8,128)(2,1)S(1)}, u32[]{:S(2)}, u32[]{:S(2)}) collective-permute-start(bf16[256,128]{1,0:T(8,128)(2,1)S(1)} %get-tuple-element.54), channel_id=1, source_target_pairs={{0,2},{1,3},{2,0},{3,1},{4,6},{5,7},{6,4},{7,5},{8,10},{9,11},{10,... | collective-permute-start | bytes 196616 | tf_op jit(solution)/shard_map/ppermute | solution.py:524
  63.6 5.6 %collective-permute-start.14 = (bf16[64,128]{1,0:T(8,128)(2,1)S(1)}, bf16[64,128]{1,0:T(8,128)(2,1)S(1)}, u32[]{:S(2)}, u32[]{:S(2)}) collective-permute-start(bf16[64,128]{1,0:T(8,128)(2,1)S(1)} %get-tuple-element.56), channel_id=1, source_target_pairs={{0,12},{1,13},{2,14},{3,15},{4,8},{5,9},{6,10},{7,11},{8,4},{9,5},... | collective-permute-start | bytes 49160 | tf_op jit(solution)/shard_map/ppermute | solution.py:524
  65.0 4.6 %collective-permute-start.15 = (bf16[64,128]{1,0:T(8,128)(2,1)S(1)}, bf16[64,128]{1,0:T(8,128)(2,1)S(1)}, u32[]{:S(2)}, u32[]{:S(2)}) collective-permute-start(bf16[64,128]{1,0:T(8,128)(2,1)S(1)} %get-tuple-element.57), channel_id=1, source_target_pairs={{0,8},{1,9},{2,10},{3,11},{4,12},{5,13},{6,14},{7,15},{8,0},{9,1},... | collective-permute-start | bytes 49160 | tf_op jit(solution)/shard_map/ppermute | solution.py:524
  65.0 4.8 %collective-permute-start.16 = (bf16[64,128]{1,0:T(8,128)(2,1)S(1)}, bf16[64,128]{1,0:T(8,128)(2,1)S(1)}, u32[]{:S(2)}, u32[]{:S(2)}) collective-permute-start(bf16[64,128]{1,0:T(8,128)(2,1)S(1)} %get-tuple-element.58), channel_id=1, source_target_pairs={{0,4},{1,5},{2,6},{3,7},{4,0},{5,1},{6,2},{7,3},{8,12},{9,13},{10,... | collective-permute-start | bytes 49160 | tf_op jit(solution)/shard_map/ppermute | solution.py:524
  (1 other events, 1.0 us)

commit v4 on v3

--- a/solution.py
+++ b/solution.py
@@ -242,29 +242,31 @@
     copy.wait()
 
 
-def project_kernel(*refs):
-    blocks = refs[: 2 * GROUPS]
-    near_key, near_value, far_key, far_value = refs[2 * GROUPS : 2 * GROUPS + 4]
-    outs = refs[2 * GROUPS + 4 : 3 * GROUPS + 4]
-    query_ref, lhs_ref = refs[3 * GROUPS + 4 :]
+def project_kernel(shifts, *refs):
+    count = len(shifts)
+    blocks, rest = refs[: 2 * count], refs[2 * count :]
+    near_key, near_value, far_key, far_value = rest[:4]
+    earlier, outs, (query_ref, lhs_ref) = rest[4 : -2 - count], rest[-2 - count : -2], rest[-2:]
     depth = near_key.shape[0]
     pieces = 2 * depth // LANES
-    half_rows = (lhs_ref.shape[0] - 16) // (2 * GROUPS)
+    half_rows = (lhs_ref.shape[0] - 16) // (2 * count)
     rows = 2 * half_rows
-    tails = [None] * len(blocks)
+    tails = []
     for i, block in enumerate(blocks):
         for j in range(pieces):
             lhs_ref[i * half_rows : (i + 1) * half_rows, j * LANES : (j + 1) * LANES] = block[
                 j * half_rows : (j + 1) * half_rows, :
             ]
         tail = block[pieces * half_rows : pieces * half_rows + pieces, :].astype(jnp.float32)
-        tails[i] = jnp.concatenate([tail[j : j + 1] for j in range(pieces)], 1)
+        tails.append(jnp.concatenate([tail[j : j + 1] for j in range(pieces)], 1))
     tails.append(jnp.zeros((16 - len(tails), 2 * depth), jnp.float32))
     lines = query_ref.shape[0] // GROUPS
-    for place, group in enumerate([0] + far_first()):
-        block = blocks[2 * place]
-        query_ref[group * lines : (group + 1) * lines, :] = block[block.shape[0] - lines :, :]
-    total = GROUPS * rows
+    if earlier:
+        query_ref[...] = earlier[0][...]
+    for i, shift in enumerate(shifts):
+        block = blocks[2 * i]
+        query_ref[shift * lines : (shift + 1) * lines, :] = block[block.shape[0] - lines :, :]
+    total = count * rows
     lhs_ref[total : total + 16, :] = jnp.concatenate(tails, 0).astype(jnp.bfloat16)
 
     def product(near, far):
@@ -280,14 +282,12 @@
     for array in (high, low, values):
         for j in range(array.shape[1] // LANES):
             columns.append(array[:, j * LANES : (j + 1) * LANES])
-    for group in range(GROUPS):
-        for t, column in enumerate(columns):
-            outs[group][t * rows : (t + 1) * rows, :] = column[
-                group * rows : (group + 1) * rows
-            ].astype(jnp.bfloat16)
-        ends = [c[total + 2 * group : total + 2 * group + 2] for c in columns]
+    for i, out in enumerate(outs):
+        for k, column in enumerate(columns):
+            out[k * rows : (k + 1) * rows, :] = column[i * rows : (i + 1) * rows].astype(jnp.bfloat16)
+        ends = [c[total + 2 * i : total + 2 * i + 2] for c in columns]
         ends.append(jnp.zeros((16 - 2 * len(columns), LANES), jnp.float32))
-        outs[group][len(columns) * rows :, :] = jnp.concatenate(ends, 0).astype(jnp.bfloat16)
+        out[len(columns) * rows :, :] = jnp.concatenate(ends, 0).astype(jnp.bfloat16)
 
 
 def head_queries(parts, head, width):
@@ -599,21 +599,37 @@
     )
     blocks[0], far[0] = lax.optimization_barrier((blocks[0], far[0]))
     theirs = {s: move(blocks[0] if s == 0 else mine[s], sibling) for s in [0] + far_first()}
-    lhs = [part[s] for s in [0] + far_first() for part in (mine, theirs)]
 
     part_rows = 3 * (width // LANES) * rows + 16
-    *partials, own_tiles = pl.pallas_call(
-        project_kernel,
-        in_specs=[vmem] * (2 * GROUPS + 4),
-        out_specs=[vmem] * (GROUPS + 1),
-        out_shape=[jax.ShapeDtypeStruct((part_rows, LANES), jnp.bfloat16)] * GROUPS
-        + [jax.ShapeDtypeStruct((GROUPS * own_queries * lines, LANES), jnp.bfloat16)],
-        scratch_shapes=[pltpu.VMEM((GROUPS * rows + 16, PAIR * features // n_ctx), jnp.bfloat16)],
-        compiler_params=params,
-        cost_estimate=pl.CostEstimate(flops=2 * GROUPS * rows * 2 * width * features // GROUPS, bytes_accessed=6 * 1024 * 1024, transcendentals=0),
-        name="project",
-    )(*lhs, key_matrix, value_matrix, *far)
-    received = [move(partials[1 + i], along(s)) for i, s in enumerate(far_first())]
+    partials, own_tiles = {}, []
+    for shifts in ((0, first), tuple(far_first()[1:])):
+        *found, tiles = pl.pallas_call(
+            functools.partial(project_kernel, shifts),
+            in_specs=[vmem] * (2 * len(shifts) + 4 + len(own_tiles)),
+            out_specs=[vmem] * (len(shifts) + 1),
+            out_shape=[jax.ShapeDtypeStruct((part_rows, LANES), jnp.bfloat16)] * len(shifts)
+            + [jax.ShapeDtypeStruct((GROUPS * own_queries * lines, LANES), jnp.bfloat16)],
+            scratch_shapes=[
+                pltpu.VMEM((len(shifts) * rows + 16, PAIR * features // n_ctx), jnp.bfloat16)
+            ],
+            compiler_params=params,
+            cost_estimate=pl.CostEstimate(
+                flops=2 * len(shifts) * rows * 2 * width * features // GROUPS,
+                bytes_accessed=6 * 1024 * 1024,
+                transcendentals=0,
+            ),
+            name="project",
+        )(
+            *[part[s] for s in shifts for part in (mine, theirs)],
+            key_matrix,
+            value_matrix,
+            *far,
+            *own_tiles,
+        )
+        partials.update(zip(shifts, found))
+        own_tiles = [tiles]
+    (own_tiles,) = own_tiles
+    received = [move(partials[s], along(s)) for s in far_first()]
     beside_tiles = move(own_tiles, beside)
 
     states = n_ctx * own_queries * query_width // HEAD_SIZE

time: 70.8 us -> 68.2 us (0.963)
  waiting for transfers between devices: 38.5 us -> 35.1 us
    ppermute x17, waiting for transfers between devices: 38.5 us -> 35.1 us  [move(): return lax.ppermute(array, ('ctx', 'tp'), pairs)]
    pallas_call x1 -> x2, Pallas kernels: 1.38 us -> 1.58 us  [exchange_plan(): pl.pallas_call(functools.partial(project_kernel, shifts), in_specs=[vmem]...]
  transfers between devices with their start and end apart: 17 -> 17, of which waited for: 12 -> 8; matrix products, arithmetic and copies ran while one was open for 1% -> 1% of each run, Pallas kernels for 6% -> 9%
where the time goes in v4:
time: 68.2 us; the launch traced here: 68 us
  waiting for transfers between devices  35.1 us (51%)
  starting transfers between devices  20.8 us (30%)
  Pallas kernels  9.09 us (13%)
  between operations  1.47 us (2%)
  local copies, waits for them, and re-layouts  0.99 us (1%)
    ppermute x17, waiting for transfers between devices, move(): return lax.ppermute(array, ('ctx', 'tp'), pairs)  35.1 us
    ppermute x17, starting transfers between devices, move(): return lax.ppermute(array, ('ctx', 'tp'), pairs)  20.8 us
    pallas_call x1, Pallas kernels, exchange_plan(): pl.pallas_call(norm_kernel, in_specs=[hbm] * 4, out_specs=[hbm] * (GROUPS...  2.89 us
    pallas_call x1, Pallas kernels, exchange_plan(): pl.pallas_call(front_kernel, in_specs=[smem, smem] + [vmem] * (GROUPS + 8...  2.09 us
    pallas_call x2, Pallas kernels, exchange_plan(): pl.pallas_call(functools.partial(project_kernel, shifts), in_specs=[vmem]...  1.58 us
  transfers between devices with their start and end apart: 17, of which 8 were waited for; matrix products, arithmetic and copies ran while one was open for 1% of the time, Pallas kernels for 9%

profile of v4, /device:TPU:0, one launch (start us, length us, event | category | flops | bytes accessed | tf_op | source)
XLA Modules:
  0.0 68.0 jit_solution(7577823438832651158)
XLA Ops:
  0.7 3.0 %collective-permute-start.1 = (bf16[1024,256]{1,0:T(8,128)(2,1)}, bf16[1024,256]{1,0:T(8,128)(2,1)S(1)}, u32[]{:S(2)}, u32[]{:S(2)}) collective-permute-start(bf16[1024,256]{1,0:T(8,128)(2,1)} %refs_4_.3), channel_id=1, source_target_pairs={{0,2},{1,3},{2,0},{3,1},{4,6},{5,7},{6,4},{7,5},{8,10},{9,11},{10,... | collective-permute-start | bytes 1572872 | tf_op jit(solution)/shard_map/ppermute | solution.py:524
  3.7 2.9 %norm_rows.1 = (bf16[1072,128]{1,0:T(8,128)(2,1)}, bf16[1072,128]{1,0:T(8,128)(2,1)}, bf16[1072,128]{1,0:T(8,128)(2,1)}, bf16[1072,128]{1,0:T(8,128)(2,1)}, bf16[1072,128]{1,0:T(8,128)(2,1)}) custom-call(bf16[2,2048]{1,0:T(2,128)(2,1)} %query_any.1, bf16[128,8192]{1,0:T(8,128)(2,1)} %hidden_any.1, bf16[2,8192]{1,0:T(2,128)(2,1)} %suffix_any.1, f32[1,8192]{1,0:T(1,128)} %bitcast.7), custom_call_target="tpu_custom_call" | custom-call | flops 2097152 | bytes 2097152 | tf_op jit(solution)/shard_map/norm_rows/pallas_call | solution.py:543
  6.6 4.1 %collective-permute-start = (bf16[1072,128]{1,0:T(8,128)(2,1)}, bf16[1072,128]{1,0:T(8,128)(2,1)S(1)}, u32[]{:S(2)}, u32[]{:S(2)}) collective-permute-start(bf16[1072,128]{1,0:T(8,128)(2,1)} %get-tuple-element.32), channel_id=1, source_target_pairs={{0,12},{1,13},{2,14},{3,15},{4,8},{5,9},{6,10},{7,11},{8,4},{9,5},... | collective-permute-start | bytes 823304 | tf_op jit(solution)/shard_map/ppermute | solution.py:524
  10.8 0.6 collective-permute-start.8
  11.8 0.9 %copy-done.2 = bf16[1072,128]{1,0:T(8,128)(2,1)S(1)} copy-done((bf16[1072,128]{1,0:T(8,128)(2,1)S(1)}, bf16[1072,128]{1,0:T(8,128)(2,1)}, u32[]{:S(2)}) %copy-start.2) | copy-done | bytes 274456
  12.9 5.7 %collective-permute-done.refs_2_ = bf16[1072,128]{1,0:T(8,128)(2,1)S(1)} collective-permute-done((bf16[1072,128]{1,0:T(8,128)(2,1)}, bf16[1072,128]{1,0:T(8,128)(2,1)S(1)}, u32[]{:S(2)}, u32[]{:S(2)}) %collective-permute-start) | collective-permute-done | bytes 274464 | tf_op jit(solution)/shard_map/ppermute | solution.py:524
  18.5 0.5 collective-permute-start.2
  19.1 14.7 %collective-permute-done.6.refs_0_ = bf16[1072,128]{1,0:T(8,128)(2,1)S(1)} collective-permute-done((bf16[1072,128]{1,0:T(8,128)(2,1)}, bf16[1072,128]{1,0:T(8,128)(2,1)S(1)}, u32[]{:S(2)}, u32[]{:S(2)}) %collective-permute-start.6) | collective-permute-done | bytes 274464 | tf_op jit(solution)/shard_map/ppermute | solution.py:524
  33.8 0.5 collective-permute-start.9
  34.3 0.8 %project.2 = (bf16[784,128]{1,0:T(8,128)(2,1)S(1)}, bf16[784,128]{1,0:T(8,128)(2,1)S(1)}, bf16[128,128]{1,0:T(8,128)(2,1)S(1)}) custom-call(bf16[1072,128]{1,0:T(8,128)(2,1)S(1)} %fetch_own.1.refs_0_, bf16[1072,128]{1,0:T(8,128)(2,1)S(1)} %collective-permute-done.2.refs_1_, bf16[1072,128]{1,0:T(8,128)(2,1)S(1)} %collective-permute-done.refs_2_, ...), custom_call_target="tpu_custom_call" | custom-call | flops 536870912 | bytes 6291456 | tf_op jit(solution)/shard_map/project/pallas_call | solution.py:606
  35.2 2.5 %collective-permute-start.5 = (bf16[784,128]{1,0:T(8,128)(2,1)S(1)}, bf16[784,128]{1,0:T(8,128)(2,1)S(1)}, u32[]{:S(2)}, u32[]{:S(2)}) collective-permute-start(bf16[784,128]{1,0:T(8,128)(2,1)S(1)} %get-tuple-element.40), channel_id=1, source_target_pairs={{0,12},{1,13},{2,14},{3,15},{4,8},{5,9},{6,10},{7,11},{8,4},{9,5},... | collective-permute-start | bytes 602120 | tf_op jit(solution)/shard_map/ppermute | solution.py:524
  37.7 0.8 %project.3 = (bf16[784,128]{1,0:T(8,128)(2,1)S(1)}, bf16[784,128]{1,0:T(8,128)(2,1)S(1)}, bf16[128,128]{1,0:T(8,128)(2,1)S(1)}) custom-call(bf16[1072,128]{1,0:T(8,128)(2,1)S(1)} %collective-permute-done.6.refs_0_, bf16[1072,128]{1,0:T(8,128)(2,1)S(1)} %collective-permute-done.7.refs_1_, bf16[1072,128]{1,0:T(8,128)(2,1)S(1)} %collective-permute-done.8.refs_2_, ...), custom_call_target="tpu_custom_call" | custom-call | flops 536870912 | bytes 6291456 | tf_op jit(solution)/shard_map/project/pallas_call | solution.py:606
  38.6 1.9 %collective-permute-start.11 = (bf16[784,128]{1,0:T(8,128)(2,1)S(1)}, bf16[784,128]{1,0:T(8,128)(2,1)S(1)}, u32[]{:S(2)}, u32[]{:S(2)}) collective-permute-start(bf16[784,128]{1,0:T(8,128)(2,1)S(1)} %get-tuple-element.45), channel_id=1, source_target_pairs={{0,4},{1,5},{2,6},{3,7},{4,0},{5,1},{6,2},{7,3},{8,12},{9,13},{10,... | collective-permute-start | bytes 602120 | tf_op jit(solution)/shard_map/ppermute | solution.py:524
  40.5 1.5 %collective-permute-start.12 = (bf16[128,128]{1,0:T(8,128)(2,1)S(1)}, bf16[128,128]{1,0:T(8,128)(2,1)S(1)}, u32[]{:S(2)}, u32[]{:S(2)}) collective-permute-start(bf16[128,128]{1,0:T(8,128)(2,1)S(1)} %get-tuple-element.48.refs_0_), channel_id=1, source_target_pairs={{0,2},{1,3},{2,0},{3,1},{4,6},{5,7},{6,4},{7,5},{8,10},{9,11},{10,... | collective-permute-start | bytes 98312 | tf_op jit(solution)/shard_map/ppermute | solution.py:524
  42.7 1.7 %collective-permute-done.12.refs_1_ = bf16[128,128]{1,0:T(8,128)(2,1)S(1)} collective-permute-done((bf16[128,128]{1,0:T(8,128)(2,1)S(1)}, bf16[128,128]{1,0:T(8,128)(2,1)S(1)}, u32[]{:S(2)}, u32[]{:S(2)}) %collective-permute-start.12) | collective-permute-done | bytes 32800 | tf_op jit(solution)/shard_map/ppermute | solution.py:524
  44.4 1.4 %loaded_attention.1 = (f32[256,128]{1,0:T(8,128)S(1)}, f32[256,128]{1,0:T(8,128)S(1)}, f32[256,128]{1,0:T(8,128)S(1)}, bf16[256,128]{1,0:T(8,128)(2,1)S(1)}) custom-call(s32[2]{0:T(128)S(1)} %pad_add_fusion.place_ref, s32[16]{0:T(128)S(1)} %copy-done.7, s32[1]{0:T(128)S(6)} %copy.15.split_ref, bf16[128,128]{1,0:T(8,128)(2,1)S(1)} %get-tuple-element.48.refs_0_, ...), custom_call_target="tpu_custom_call" | custom-call | flops 67108864 | bytes 524288 | tf_op jit(solution)/shard_map/loaded_attention/pallas_call | solution.py:637
  45.8 8.5 %collective-permute-done.10.refs_1_ = bf16[784,128]{1,0:T(8,128)(2,1)S(1)} collective-permute-done((bf16[784,128]{1,0:T(8,128)(2,1)S(1)}, bf16[784,128]{1,0:T(8,128)(2,1)S(1)}, u32[]{:S(2)}, u32[]{:S(2)}) %collective-permute-start.10) | collective-permute-done | bytes 200736 | tf_op jit(solution)/shard_map/ppermute | solution.py:524
  54.3 2.1 %front_attention.1 = (bf16[128,256]{1,0:T(8,128)(2,1)}, bf16[128,256]{1,0:T(8,128)(2,1)}, f32[256,128]{1,0:T(8,128)S(1)}, bf16[256,128]{1,0:T(8,128)(2,1)S(1)}) custom-call(s32[2]{0:T(128)S(1)} %pad_add_fusion.place_ref, s32[1]{0:T(128)S(6)} %copy.15.split_ref, bf16[784,128]{1,0:T(8,128)(2,1)S(1)} %get-tuple-element.39.own, ...), custom_call_target="tpu_custom_call" | custom-call | flops 16777216 | bytes 2097152 | tf_op jit(solution)/shard_map/front_attention/pallas_call | solution.py:656
  56.3 1.5 %collective-permute-start.13 = (bf16[256,128]{1,0:T(8,128)(2,1)S(1)}, bf16[256,128]{1,0:T(8,128)(2,1)S(1)}, u32[]{:S(2)}, u32[]{:S(2)}) collective-permute-start(bf16[256,128]{1,0:T(8,128)(2,1)S(1)} %get-tuple-element.56), channel_id=1, source_target_pairs={{0,2},{1,3},{2,0},{3,1},{4,6},{5,7},{6,4},{7,5},{8,10},{9,11},{10,... | collective-permute-start | bytes 196616 | tf_op jit(solution)/shard_map/ppermute | solution.py:524
  57.8 2.8 %collective-permute-done.13.other = bf16[256,128]{1,0:T(8,128)(2,1)S(1)} collective-permute-done((bf16[256,128]{1,0:T(8,128)(2,1)S(1)}, bf16[256,128]{1,0:T(8,128)(2,1)S(1)}, u32[]{:S(2)}, u32[]{:S(2)}) %collective-permute-start.13) | collective-permute-done | bytes 65568 | tf_op jit(solution)/shard_map/ppermute | solution.py:524
  60.9 1.4 %collective-permute-start.14 = (bf16[64,128]{1,0:T(8,128)(2,1)S(1)}, bf16[64,128]{1,0:T(8,128)(2,1)S(1)}, u32[]{:S(2)}, u32[]{:S(2)}) collective-permute-start(bf16[64,128]{1,0:T(8,128)(2,1)S(1)} %get-tuple-element.58), channel_id=1, source_target_pairs={{0,12},{1,13},{2,14},{3,15},{4,8},{5,9},{6,10},{7,11},{8,4},{9,5},... | collective-permute-start | bytes 49160 | tf_op jit(solution)/shard_map/ppermute | solution.py:524
  62.3 3.0 %collective-permute-start.16 = (bf16[64,128]{1,0:T(8,128)(2,1)S(1)}, bf16[64,128]{1,0:T(8,128)(2,1)S(1)}, u32[]{:S(2)}, u32[]{:S(2)}) collective-permute-start(bf16[64,128]{1,0:T(8,128)(2,1)S(1)} %get-tuple-element.60), channel_id=1, source_target_pairs={{0,4},{1,5},{2,6},{3,7},{4,0},{5,1},{6,2},{7,3},{8,12},{9,13},{10,... | collective-permute-start | bytes 49160 | tf_op jit(solution)/shard_map/ppermute | solution.py:524
  65.4 1.1 %collective-permute-done.14.refs_0_ = bf16[64,128]{1,0:T(8,128)(2,1)S(1)} collective-permute-done((bf16[64,128]{1,0:T(8,128)(2,1)S(1)}, bf16[64,128]{1,0:T(8,128)(2,1)S(1)}, u32[]{:S(2)}, u32[]{:S(2)}) %collective-permute-start.14) | collective-permute-done | bytes 16416 | tf_op jit(solution)/shard_map/ppermute | solution.py:524
  67.2 0.8 %finish.1 = bf16[2,2048]{1,0:T(2,128)(2,1)} custom-call(f32[64,128]{1,0:T(8,128)S(1)} %get-tuple-element.57.kept, bf16[64,128]{1,0:T(8,128)(2,1)S(1)} %collective-permute-done.14.refs_0_, bf16[64,128]{1,0:T(8,128)(2,1)S(1)} %collective-permute-done.15.refs_1_, bf16[64,128]{1,0:T(8,128)(2,1)S(1)} %collective-permute-done.16.refs_2_), custom_call_target="tpu_custom_call" | custom-call | tf_op jit(solution)/shard_map/finish/pallas_call | solution.py:686
  (39 shorter events, 1.7 us)
Async XLA Ops:
  0.6 33.7 %copy-start = (bf16[1024,256]{1,0:T(8,128)(2,1)S(1)}, bf16[1024,256]{1,0:T(8,128)(2,1)}, u32[]{:S(2)}) copy-start(bf16[1024,256]{1,0:T(8,128)(2,1)} %refs_4_.3) | copy-start | bytes 1572868
  0.6 33.7 %copy-start.1 = (bf16[1024,256]{1,0:T(8,128)(2,1)S(1)}, bf16[1024,256]{1,0:T(8,128)(2,1)}, u32[]{:S(2)}) copy-start(bf16[1024,256]{1,0:T(8,128)(2,1)} %refs_5_.3) | copy-start | bytes 1572868
  0.7 17.9 %collective-permute-start.1 = (bf16[1024,256]{1,0:T(8,128)(2,1)}, bf16[1024,256]{1,0:T(8,128)(2,1)S(1)}, u32[]{:S(2)}, u32[]{:S(2)}) collective-permute-start(bf16[1024,256]{1,0:T(8,128)(2,1)} %refs_4_.3), channel_id=1, source_target_pairs={{0,2},{1,3},{2,0},{3,1},{4,6},{5,7},{6,4},{7,5},{8,10},{9,11},{10,... | collective-permute-start | bytes 1572872 | tf_op jit(solution)/shard_map/ppermute | solution.py:524
  3.7 30.6 %collective-permute-start.4 = (bf16[1024,256]{1,0:T(8,128)(2,1)}, bf16[1024,256]{1,0:T(8,128)(2,1)S(1)}, u32[]{:S(2)}, u32[]{:S(2)}) collective-permute-start(bf16[1024,256]{1,0:T(8,128)(2,1)} %refs_5_.3), channel_id=1, source_target_pairs={{0,2},{1,3},{2,0},{3,1},{4,6},{5,7},{6,4},{7,5},{8,10},{9,11},{10,... | collective-permute-start | bytes 1572872 | tf_op jit(solution)/shard_map/ppermute | solution.py:524
  6.6 11.9 %collective-permute-start = (bf16[1072,128]{1,0:T(8,128)(2,1)}, bf16[1072,128]{1,0:T(8,128)(2,1)S(1)}, u32[]{:S(2)}, u32[]{:S(2)}) collective-permute-start(bf16[1072,128]{1,0:T(8,128)(2,1)} %get-tuple-element.32), channel_id=1, source_target_pairs={{0,12},{1,13},{2,14},{3,15},{4,8},{5,9},{6,10},{7,11},{8,4},{9,5},... | collective-permute-start | bytes 823304 | tf_op jit(solution)/shard_map/ppermute | solution.py:524
  10.8 23.0 %collective-permute-start.6 = (bf16[1072,128]{1,0:T(8,128)(2,1)}, bf16[1072,128]{1,0:T(8,128)(2,1)S(1)}, u32[]{:S(2)}, u32[]{:S(2)}) collective-permute-start(bf16[1072,128]{1,0:T(8,128)(2,1)} %get-tuple-element.41), channel_id=1, source_target_pairs={{0,8},{1,9},{2,10},{3,11},{4,12},{5,13},{6,14},{7,15},{8,0},{9,1},... | collective-permute-start | bytes 823304 | tf_op jit(solution)/shard_map/ppermute | solution.py:524
  10.8 23.0 %collective-permute-start.8 = (bf16[1072,128]{1,0:T(8,128)(2,1)}, bf16[1072,128]{1,0:T(8,128)(2,1)S(1)}, u32[]{:S(2)}, u32[]{:S(2)}) collective-permute-start(bf16[1072,128]{1,0:T(8,128)(2,1)} %get-tuple-element.42), channel_id=1, source_target_pairs={{0,4},{1,5},{2,6},{3,7},{4,0},{5,1},{6,2},{7,3},{8,12},{9,13},{10,... | collective-permute-start | bytes 823304 | tf_op jit(solution)/shard_map/ppermute | solution.py:524
  18.5 15.7 %collective-permute-start.3 = (bf16[1072,128]{1,0:T(8,128)(2,1)S(1)}, bf16[1072,128]{1,0:T(8,128)(2,1)S(1)}, u32[]{:S(2)}, u32[]{:S(2)}) collective-permute-start(bf16[1072,128]{1,0:T(8,128)(2,1)S(1)} %collective-permute-done.refs_2_), channel_id=1, source_target_pairs={{0,1},{1,0},{2,3},{3,2},{4,5},{5,4},{6,7},{7,6},{8,9},{9,8},{10,11... | collective-permute-start | bytes 823304 | tf_op jit(solution)/shard_map/ppermute | solution.py:524
  18.5 15.7 %collective-permute-start.2 = (bf16[1072,128]{1,0:T(8,128)(2,1)}, bf16[1072,128]{1,0:T(8,128)(2,1)S(1)}, u32[]{:S(2)}, u32[]{:S(2)}) collective-permute-start(bf16[1072,128]{1,0:T(8,128)(2,1)} %get-tuple-element.36), channel_id=1, source_target_pairs={{0,1},{1,0},{2,3},{3,2},{4,5},{5,4},{6,7},{7,6},{8,9},{9,8},{10,11... | collective-permute-start | bytes 823304 | tf_op jit(solution)/shard_map/ppermute | solution.py:524
  33.8 4.0 %collective-permute-start.7 = (bf16[1072,128]{1,0:T(8,128)(2,1)S(1)}, bf16[1072,128]{1,0:T(8,128)(2,1)S(1)}, u32[]{:S(2)}, u32[]{:S(2)}) collective-permute-start(bf16[1072,128]{1,0:T(8,128)(2,1)S(1)} %collective-permute-done.6.refs_0_), channel_id=1, source_target_pairs={{0,1},{1,0},{2,3},{3,2},{4,5},{5,4},{6,7},{7,6},{8,9},{9,8},{10,11... | collective-permute-start | bytes 823304 | tf_op jit(solution)/shard_map/ppermute | solution.py:524
  33.8 4.0 %collective-permute-start.9 = (bf16[1072,128]{1,0:T(8,128)(2,1)S(1)}, bf16[1072,128]{1,0:T(8,128)(2,1)S(1)}, u32[]{:S(2)}, u32[]{:S(2)}) collective-permute-start(bf16[1072,128]{1,0:T(8,128)(2,1)S(1)} %collective-permute-done.8.refs_2_), channel_id=1, source_target_pairs={{0,1},{1,0},{2,3},{3,2},{4,5},{5,4},{6,7},{7,6},{8,9},{9,8},{10,11... | collective-permute-start | bytes 823304 | tf_op jit(solution)/shard_map/ppermute | solution.py:524
  35.1 9.3 %copy-start.3 = (bf16[4,128,256]{2,1,0:T(8,128)(2,1)S(1)}, bf16[4,128,256]{2,1,0:T(8,128)(2,1)}, u32[]{:S(2)}) copy-start(bf16[4,128,256]{2,1,0:T(8,128)(2,1)} %refs_2_.1) | copy-start | bytes 786436
  35.1 9.3 %copy-start.4 = (bf16[4,128,256]{2,1,0:T(8,128)(2,1)S(1)}, bf16[4,128,256]{2,1,0:T(8,128)(2,1)}, u32[]{:S(2)}) copy-start(bf16[4,128,256]{2,1,0:T(8,128)(2,1)} %refs_3_.1) | copy-start | bytes 786436
  35.1 9.3 %copy-start.7 = (s32[16]{0:T(128)S(1)}, s32[16]{0:T(128)}, u32[]{:S(2)}) copy-start(s32[16]{0:T(128)} %table_ref.1) | copy-start | bytes 196
  35.2 19.1 %copy-start.5 = (f32[256]{0:T(256)S(1)}, f32[256]{0:T(256)}, u32[]{:S(2)}) copy-start(f32[256]{0:T(256)} %param.17) | copy-start | bytes 3076
  35.2 19.1 %copy-start.6 = (f32[256]{0:T(256)S(1)}, f32[256]{0:T(256)}, u32[]{:S(2)}) copy-start(f32[256]{0:T(256)} %param.18) | copy-start | bytes 3076
  35.2 10.6 %collective-permute-start.5 = (bf16[784,128]{1,0:T(8,128)(2,1)S(1)}, bf16[784,128]{1,0:T(8,128)(2,1)S(1)}, u32[]{:S(2)}, u32[]{:S(2)}) collective-permute-start(bf16[784,128]{1,0:T(8,128)(2,1)S(1)} %get-tuple-element.40), channel_id=1, source_target_pairs={{0,12},{1,13},{2,14},{3,15},{4,8},{5,9},{6,10},{7,11},{8,4},{9,5},... | collective-permute-start | bytes 602120 | tf_op jit(solution)/shard_map/ppermute | solution.py:524
  38.5 15.7 %collective-permute-start.10 = (bf16[784,128]{1,0:T(8,128)(2,1)S(1)}, bf16[784,128]{1,0:T(8,128)(2,1)S(1)}, u32[]{:S(2)}, u32[]{:S(2)}) collective-permute-start(bf16[784,128]{1,0:T(8,128)(2,1)S(1)} %get-tuple-element.44), channel_id=1, source_target_pairs={{0,8},{1,9},{2,10},{3,11},{4,12},{5,13},{6,14},{7,15},{8,0},{9,1},... | collective-permute-start | bytes 602120 | tf_op jit(solution)/shard_map/ppermute | solution.py:524
  38.6 15.7 %collective-permute-start.11 = (bf16[784,128]{1,0:T(8,128)(2,1)S(1)}, bf16[784,128]{1,0:T(8,128)(2,1)S(1)}, u32[]{:S(2)}, u32[]{:S(2)}) collective-permute-start(bf16[784,128]{1,0:T(8,128)(2,1)S(1)} %get-tuple-element.45), channel_id=1, source_target_pairs={{0,4},{1,5},{2,6},{3,7},{4,0},{5,1},{6,2},{7,3},{8,12},{9,13},{10,... | collective-permute-start | bytes 602120 | tf_op jit(solution)/shard_map/ppermute | solution.py:524
  40.5 3.9 %collective-permute-start.12 = (bf16[128,128]{1,0:T(8,128)(2,1)S(1)}, bf16[128,128]{1,0:T(8,128)(2,1)S(1)}, u32[]{:S(2)}, u32[]{:S(2)}) collective-permute-start(bf16[128,128]{1,0:T(8,128)(2,1)S(1)} %get-tuple-element.48.refs_0_), channel_id=1, source_target_pairs={{0,2},{1,3},{2,0},{3,1},{4,6},{5,7},{6,4},{7,5},{8,10},{9,11},{10,... | collective-permute-start | bytes 98312 | tf_op jit(solution)/shard_map/ppermute | solution.py:524
  56.3 4.3 %collective-permute-start.13 = (bf16[256,128]{1,0:T(8,128)(2,1)S(1)}, bf16[256,128]{1,0:T(8,128)(2,1)S(1)}, u32[]{:S(2)}, u32[]{:S(2)}) collective-permute-start(bf16[256,128]{1,0:T(8,128)(2,1)S(1)} %get-tuple-element.56), channel_id=1, source_target_pairs={{0,2},{1,3},{2,0},{3,1},{4,6},{5,7},{6,4},{7,5},{8,10},{9,11},{10,... | collective-permute-start | bytes 196616 | tf_op jit(solution)/shard_map/ppermute | solution.py:524
  60.9 5.6 %collective-permute-start.14 = (bf16[64,128]{1,0:T(8,128)(2,1)S(1)}, bf16[64,128]{1,0:T(8,128)(2,1)S(1)}, u32[]{:S(2)}, u32[]{:S(2)}) collective-permute-start(bf16[64,128]{1,0:T(8,128)(2,1)S(1)} %get-tuple-element.58), channel_id=1, source_target_pairs={{0,12},{1,13},{2,14},{3,15},{4,8},{5,9},{6,10},{7,11},{8,4},{9,5},... | collective-permute-start | bytes 49160 | tf_op jit(solution)/shard_map/ppermute | solution.py:524
  62.3 4.6 %collective-permute-start.15 = (bf16[64,128]{1,0:T(8,128)(2,1)S(1)}, bf16[64,128]{1,0:T(8,128)(2,1)S(1)}, u32[]{:S(2)}, u32[]{:S(2)}) collective-permute-start(bf16[64,128]{1,0:T(8,128)(2,1)S(1)} %get-tuple-element.59), channel_id=1, source_target_pairs={{0,8},{1,9},{2,10},{3,11},{4,12},{5,13},{6,14},{7,15},{8,0},{9,1},... | collective-permute-start | bytes 49160 | tf_op jit(solution)/shard_map/ppermute | solution.py:524
  62.3 4.8 %collective-permute-start.16 = (bf16[64,128]{1,0:T(8,128)(2,1)S(1)}, bf16[64,128]{1,0:T(8,128)(2,1)S(1)}, u32[]{:S(2)}, u32[]{:S(2)}) collective-permute-start(bf16[64,128]{1,0:T(8,128)(2,1)S(1)} %get-tuple-element.60), channel_id=1, source_target_pairs={{0,4},{1,5},{2,6},{3,7},{4,0},{5,1},{6,2},{7,3},{8,12},{9,13},{10,... | collective-permute-start | bytes 49160 | tf_op jit(solution)/shard_map/ppermute | solution.py:524
  (1 other events, 1.0 us)

commit v5 on v4

--- a/solution.py
+++ b/solution.py
@@ -158,7 +158,7 @@
 
 
 def far_first():
-    return list(range(GROUPS - 1, 0, -1))
+    return sorted(range(1, GROUPS), key=lambda s: s < GROUPS // 2)
 
 
 def norm_kernel(query_any, hidden_any, suffix_any, gain_any, *rest):
@@ -346,15 +346,19 @@
         numer_ref[rows, :] = numer
 
 
+def sum_kernel(one, other, out):
+    out[...] = one[...].astype(jnp.float32) + other[...].astype(jnp.float32)
+
+
 def front_kernel(
-    place_ref, split_ref, own, *refs
+    place_ref, split_ref, early, *refs
 ):
-    received = refs[: GROUPS - 1]
+    received = refs[: GROUPS - 2]
     (key_bias, value_bias, cosine_ref, sine_ref, query_ref, top_ref, total_ref, numer_ref) = refs[
-        GROUPS - 1 : GROUPS + 7
+        GROUPS - 2 : GROUPS + 6
     ]
-    front_key, front_value = refs[GROUPS + 7 : GROUPS + 9]
-    outs = refs[GROUPS + 9 :]
+    front_key, front_value = refs[GROUPS + 6 : GROUPS + 8]
+    outs = refs[GROUPS + 8 :]
     core, ctx = place_ref[0], place_ref[1]
     rows, width = front_key.shape
     half_rows = rows // 2
@@ -365,7 +369,7 @@
     visible = ctx < split_ref[0]
 
     def summed(start, size):
-        value = own[start : start + size, :].astype(jnp.float32)
+        value = early[start : start + size, :]
         for ref in received:
             value += ref[start : start + size, :].astype(jnp.float32)
         return value
@@ -568,7 +572,8 @@
         suffix_hidden,
         norm_gain.reshape(1, features),
     )
-    far = [move(key_matrix, beside), move(value_matrix, beside)]
+    *weights, blocks[1] = lax.optimization_barrier((key_matrix, value_matrix, blocks[1]))
+    far = [move(matrix, beside) for matrix in weights]
 
     mine = {s: move(blocks[s], along(s)) for s in far_first()}
     inverse_freq = rope_base ** (
@@ -630,6 +635,15 @@
         own_tiles = [tiles]
     (own_tiles,) = own_tiles
     received = [move(partials[s], along(s)) for s in far_first()]
+    early = pl.pallas_call(
+        sum_kernel,
+        in_specs=[vmem] * 2,
+        out_specs=vmem,
+        out_shape=jax.ShapeDtypeStruct((part_rows, LANES), jnp.float32),
+        compiler_params=params,
+        cost_estimate=pl.CostEstimate(flops=0, bytes_accessed=16 * 1024 * 1024, transcendentals=0),
+        name="sum_early",
+    )(partials[0], received[0])
     beside_tiles = move(own_tiles, beside)
 
     states = n_ctx * own_queries * query_width // HEAD_SIZE
@@ -655,7 +669,7 @@
     row_shape = jax.ShapeDtypeStruct((rows, width), jnp.bfloat16)
     front_key, front_value, kept, sent = pl.pallas_call(
         front_kernel,
-        in_specs=[smem, smem] + [vmem] * (GROUPS + 8),
+        in_specs=[smem, smem] + [vmem] * (GROUPS + 7),
         out_specs=[vmem] * 4,
         out_shape=[row_shape] * 2 + payloads(states),
         compiler_params=params,
@@ -664,8 +678,8 @@
     )(
         place,
         split_page,
-        partials[0],
-        *received,
+        early,
+        *received[1:],
         key_offset_bias.reshape(1, width),
         value_offset_bias.reshape(1, width),
         cosine,
@@ -690,7 +704,7 @@
         out_shape=jax.ShapeDtypeStruct((own_queries, query_width), jnp.bfloat16),
         compiler_params=params,
         name="finish",
-    )(kept, *[move(sent[s - 1], along(s)) for s in far_first()])
+    )(kept, *[move(sent[s - 1], along(s)) for s in range(GROUPS - 1, 0, -1)])
     return (front_key, front_value, attended)
 
 

time: 68.2 us -> 67.9 us (level)
  starting transfers between devices: 20.8 us -> 19.8 us
  waiting for transfers between devices: 35.1 us -> 35.8 us
    ppermute x17, starting transfers between devices: 20.8 us -> 19.8 us  [move(): return lax.ppermute(array, ('ctx', 'tp'), pairs)]
    pallas_call x1 -> x2, Pallas kernels: 2.09 us -> 2.1 us  [the longest x1 2.06 us: exchange_plan(): pl.pallas_call(front_kernel, in_specs=[smem, smem] + [vmem] * (GROUPS + 7...]
  transfers between devices with their start and end apart: 17 -> 17, of which waited for: 8 -> 11; matrix products, arithmetic and copies ran while one was open for 1% -> 1% of each run, Pallas kernels for 9% -> 4%
where the time goes in v5:
time: 67.9 us; the launch traced here: 67.7 us
  waiting for transfers between devices  35.8 us (53%)
  starting transfers between devices  19.8 us (29%)
  Pallas kernels  9.2 us (14%)
  between operations  1.44 us (2%)
  local copies, waits for them, and re-layouts  0.99 us (1%)
    ppermute x17, waiting for transfers between devices, move(): return lax.ppermute(array, ('ctx', 'tp'), pairs)  35.8 us
    ppermute x17, starting transfers between devices, move(): return lax.ppermute(array, ('ctx', 'tp'), pairs)  19.8 us
    pallas_call x1, Pallas kernels, exchange_plan(): pl.pallas_call(norm_kernel, in_specs=[hbm] * 4, out_specs=[hbm] * (GROUPS...  2.99 us
    pallas_call x1, Pallas kernels, exchange_plan(): pl.pallas_call(front_kernel, in_specs=[smem, smem] + [vmem] * (GROUPS + 7...  2.06 us
    pallas_call x2, Pallas kernels, exchange_plan(): pl.pallas_call(functools.partial(project_kernel, shifts), in_specs=[vmem]...  1.57 us
  transfers between devices with their start and end apart: 17, of which 11 were waited for; matrix products, arithmetic and copies ran while one was open for 1% of the time, Pallas kernels for 4%

profile of v5, /device:TPU:0, one launch (start us, length us, event | category | flops | bytes accessed | tf_op | source)
XLA Modules:
  0.0 67.7 jit_solution(11146201452266114641)
XLA Ops:
  0.7 3.0 %norm_rows.1 = (bf16[1072,128]{1,0:T(8,128)(2,1)}, bf16[1072,128]{1,0:T(8,128)(2,1)}, bf16[1072,128]{1,0:T(8,128)(2,1)}, bf16[1072,128]{1,0:T(8,128)(2,1)}, bf16[1072,128]{1,0:T(8,128)(2,1)}) custom-call(bf16[2,2048]{1,0:T(2,128)(2,1)} %query_any.1, bf16[128,8192]{1,0:T(8,128)(2,1)} %hidden_any.1, bf16[2,8192]{1,0:T(2,128)(2,1)} %suffix_any.1, f32[1,8192]{1,0:T(1,128)} %bitcast.7), custom_call_target="tpu_custom_call" | custom-call | flops 2097152 | bytes 2097152 | tf_op jit(solution)/shard_map/norm_rows/pallas_call | solution.py:547
  3.7 4.1 %collective-permute-start = (bf16[1072,128]{1,0:T(8,128)(2,1)}, bf16[1072,128]{1,0:T(8,128)(2,1)S(1)}, u32[]{:S(2)}, u32[]{:S(2)}) collective-permute-start(bf16[1072,128]{1,0:T(8,128)(2,1)} %get-tuple-element.35), channel_id=1, source_target_pairs={{0,8},{1,9},{2,10},{3,11},{4,12},{5,13},{6,14},{7,15},{8,0},{9,1},... | collective-permute-start | bytes 823304 | tf_op jit(solution)/shard_map/ppermute | solution.py:528
  7.8 1.5 %collective-permute-start.1 = (bf16[1024,256]{1,0:T(8,128)(2,1)S(1)}, bf16[1024,256]{1,0:T(8,128)(2,1)S(1)}, u32[]{:S(2)}, u32[]{:S(2)}) collective-permute-start(bf16[1024,256]{1,0:T(8,128)(2,1)S(1)} %copy-done), channel_id=1, source_target_pairs={{0,2},{1,3},{2,0},{3,1},{4,6},{5,7},{6,4},{7,5},{8,10},{9,11},{10,... | collective-permute-start | bytes 1572872 | tf_op jit(solution)/shard_map/ppermute | solution.py:528
  9.8 1.6 %collective-permute-start.8 = (bf16[1072,128]{1,0:T(8,128)(2,1)}, bf16[1072,128]{1,0:T(8,128)(2,1)S(1)}, u32[]{:S(2)}, u32[]{:S(2)}) collective-permute-start(bf16[1072,128]{1,0:T(8,128)(2,1)} %get-tuple-element.48), channel_id=1, source_target_pairs={{0,4},{1,5},{2,6},{3,7},{4,0},{5,1},{6,2},{7,3},{8,12},{9,13},{10,... | collective-permute-start | bytes 823304 | tf_op jit(solution)/shard_map/ppermute | solution.py:528
  11.8 0.9 %copy-done.2 = bf16[1072,128]{1,0:T(8,128)(2,1)S(1)} copy-done((bf16[1072,128]{1,0:T(8,128)(2,1)S(1)}, bf16[1072,128]{1,0:T(8,128)(2,1)}, u32[]{:S(2)}) %copy-start.2) | copy-done | bytes 274456
  12.9 9.3 %collective-permute-done.refs_2_ = bf16[1072,128]{1,0:T(8,128)(2,1)S(1)} collective-permute-done((bf16[1072,128]{1,0:T(8,128)(2,1)}, bf16[1072,128]{1,0:T(8,128)(2,1)S(1)}, u32[]{:S(2)}, u32[]{:S(2)}) %collective-permute-start) | collective-permute-done | bytes 274464 | tf_op jit(solution)/shard_map/ppermute | solution.py:528
  22.7 5.4 %collective-permute-done.8.refs_2_ = bf16[1072,128]{1,0:T(8,128)(2,1)S(1)} collective-permute-done((bf16[1072,128]{1,0:T(8,128)(2,1)}, bf16[1072,128]{1,0:T(8,128)(2,1)S(1)}, u32[]{:S(2)}, u32[]{:S(2)}) %collective-permute-start.8) | collective-permute-done | bytes 274464 | tf_op jit(solution)/shard_map/ppermute | solution.py:528
  28.6 3.8 %collective-permute-done.4.refs_7_ = bf16[1024,256]{1,0:T(8,128)(2,1)S(1)} collective-permute-done((bf16[1024,256]{1,0:T(8,128)(2,1)S(1)}, bf16[1024,256]{1,0:T(8,128)(2,1)S(1)}, u32[]{:S(2)}, u32[]{:S(2)}) %collective-permute-start.4) | collective-permute-done | bytes 524320 | tf_op jit(solution)/shard_map/ppermute | solution.py:528
  32.4 0.8 %project.2 = (bf16[784,128]{1,0:T(8,128)(2,1)S(1)}, bf16[784,128]{1,0:T(8,128)(2,1)S(1)}, bf16[128,128]{1,0:T(8,128)(2,1)S(1)}) custom-call(bf16[1072,128]{1,0:T(8,128)(2,1)S(1)} %fetch_own.1.refs_0_, bf16[1072,128]{1,0:T(8,128)(2,1)S(1)} %collective-permute-done.2.refs_1_, bf16[1072,128]{1,0:T(8,128)(2,1)S(1)} %collective-permute-done.refs_2_, ...), custom_call_target="tpu_custom_call" | custom-call | flops 536870912 | bytes 6291456 | tf_op jit(solution)/shard_map/project/pallas_call | solution.py:611
  33.2 2.6 %collective-permute-start.5 = (bf16[784,128]{1,0:T(8,128)(2,1)S(1)}, bf16[784,128]{1,0:T(8,128)(2,1)S(1)}, u32[]{:S(2)}, u32[]{:S(2)}) collective-permute-start(bf16[784,128]{1,0:T(8,128)(2,1)S(1)} %get-tuple-element.46), channel_id=1, source_target_pairs={{0,8},{1,9},{2,10},{3,11},{4,12},{5,13},{6,14},{7,15},{8,0},{9,1},... | collective-permute-start | bytes 602120 | tf_op jit(solution)/shard_map/ppermute | solution.py:528
  35.8 0.8 %project.3 = (bf16[784,128]{1,0:T(8,128)(2,1)S(1)}, bf16[784,128]{1,0:T(8,128)(2,1)S(1)}, bf16[128,128]{1,0:T(8,128)(2,1)S(1)}) custom-call(bf16[1072,128]{1,0:T(8,128)(2,1)S(1)} %collective-permute-done.6.refs_0_, bf16[1072,128]{1,0:T(8,128)(2,1)S(1)} %collective-permute-done.7.refs_1_, bf16[1072,128]{1,0:T(8,128)(2,1)S(1)} %collective-permute-done.8.refs_2_, ...), custom_call_target="tpu_custom_call" | custom-call | flops 536870912 | bytes 6291456 | tf_op jit(solution)/shard_map/project/pallas_call | solution.py:611
  36.6 1.5 %collective-permute-start.10 = (bf16[784,128]{1,0:T(8,128)(2,1)S(1)}, bf16[784,128]{1,0:T(8,128)(2,1)S(1)}, u32[]{:S(2)}, u32[]{:S(2)}) collective-permute-start(bf16[784,128]{1,0:T(8,128)(2,1)S(1)} %get-tuple-element.50), channel_id=1, source_target_pairs={{0,12},{1,13},{2,14},{3,15},{4,8},{5,9},{6,10},{7,11},{8,4},{9,5},... | collective-permute-start | bytes 602120 | tf_op jit(solution)/shard_map/ppermute | solution.py:528
  38.1 1.5 %collective-permute-start.12 = (bf16[128,128]{1,0:T(8,128)(2,1)S(1)}, bf16[128,128]{1,0:T(8,128)(2,1)S(1)}, u32[]{:S(2)}, u32[]{:S(2)}) collective-permute-start(bf16[128,128]{1,0:T(8,128)(2,1)S(1)} %get-tuple-element.54.refs_0_), channel_id=1, source_target_pairs={{0,2},{1,3},{2,0},{3,1},{4,6},{5,7},{6,4},{7,5},{8,10},{9,11},{10,... | collective-permute-start | bytes 98312 | tf_op jit(solution)/shard_map/ppermute | solution.py:528
  40.3 1.7 %collective-permute-done.12.refs_1_ = bf16[128,128]{1,0:T(8,128)(2,1)S(1)} collective-permute-done((bf16[128,128]{1,0:T(8,128)(2,1)S(1)}, bf16[128,128]{1,0:T(8,128)(2,1)S(1)}, u32[]{:S(2)}, u32[]{:S(2)}) %collective-permute-start.12) | collective-permute-done | bytes 32800 | tf_op jit(solution)/shard_map/ppermute | solution.py:528
  42.0 1.4 %loaded_attention.1 = (f32[256,128]{1,0:T(8,128)S(1)}, f32[256,128]{1,0:T(8,128)S(1)}, f32[256,128]{1,0:T(8,128)S(1)}, bf16[256,128]{1,0:T(8,128)(2,1)S(1)}) custom-call(s32[2]{0:T(128)S(1)} %pad_add_fusion.place_ref, s32[16]{0:T(128)S(1)} %copy-done.7, s32[1]{0:T(128)S(6)} %copy.15.split_ref, bf16[128,128]{1,0:T(8,128)(2,1)S(1)} %get-tuple-element.54.refs_0_, ...), custom_call_target="tpu_custom_call" | custom-call | flops 67108864 | bytes 524288 | tf_op jit(solution)/shard_map/loaded_attention/pallas_call | solution.py:651
  43.4 7.0 %collective-permute-done.5.other = bf16[784,128]{1,0:T(8,128)(2,1)S(1)} collective-permute-done((bf16[784,128]{1,0:T(8,128)(2,1)S(1)}, bf16[784,128]{1,0:T(8,128)(2,1)S(1)}, u32[]{:S(2)}, u32[]{:S(2)}) %collective-permute-start.5) | collective-permute-done | bytes 200736 | tf_op jit(solution)/shard_map/ppermute | solution.py:528
  50.4 1.8 %collective-permute-done.11.refs_1_ = bf16[784,128]{1,0:T(8,128)(2,1)S(1)} collective-permute-done((bf16[784,128]{1,0:T(8,128)(2,1)S(1)}, bf16[784,128]{1,0:T(8,128)(2,1)S(1)}, u32[]{:S(2)}, u32[]{:S(2)}) %collective-permute-start.11) | collective-permute-done | bytes 200736 | tf_op jit(solution)/shard_map/ppermute | solution.py:528
  52.3 2.1 %front_attention.1 = (bf16[128,256]{1,0:T(8,128)(2,1)}, bf16[128,256]{1,0:T(8,128)(2,1)}, f32[256,128]{1,0:T(8,128)S(1)}, bf16[256,128]{1,0:T(8,128)(2,1)S(1)}) custom-call(s32[2]{0:T(128)S(1)} %pad_add_fusion.place_ref, s32[1]{0:T(128)S(6)} %copy.15.split_ref, f32[784,128]{1,0:T(8,128)S(1)} %sum_early.1.early, ...), custom_call_target="tpu_custom_call" | custom-call | flops 16777216 | bytes 2097152 | tf_op jit(solution)/shard_map/front_attention/pallas_call | solution.py:670
  54.4 1.5 %collective-permute-start.13 = (bf16[256,128]{1,0:T(8,128)(2,1)S(1)}, bf16[256,128]{1,0:T(8,128)(2,1)S(1)}, u32[]{:S(2)}, u32[]{:S(2)}) collective-permute-start(bf16[256,128]{1,0:T(8,128)(2,1)S(1)} %get-tuple-element.62), channel_id=1, source_target_pairs={{0,2},{1,3},{2,0},{3,1},{4,6},{5,7},{6,4},{7,5},{8,10},{9,11},{10,... | collective-permute-start | bytes 196616 | tf_op jit(solution)/shard_map/ppermute | solution.py:528
  55.8 2.8 %collective-permute-done.13.other = bf16[256,128]{1,0:T(8,128)(2,1)S(1)} collective-permute-done((bf16[256,128]{1,0:T(8,128)(2,1)S(1)}, bf16[256,128]{1,0:T(8,128)(2,1)S(1)}, u32[]{:S(2)}, u32[]{:S(2)}) %collective-permute-start.13) | collective-permute-done | bytes 65568 | tf_op jit(solution)/shard_map/ppermute | solution.py:528
  59.5 3.6 %collective-permute-start.15 = (bf16[64,128]{1,0:T(8,128)(2,1)S(1)}, bf16[64,128]{1,0:T(8,128)(2,1)S(1)}, u32[]{:S(2)}, u32[]{:S(2)}) collective-permute-start(bf16[64,128]{1,0:T(8,128)(2,1)S(1)} %get-tuple-element.65), channel_id=1, source_target_pairs={{0,8},{1,9},{2,10},{3,11},{4,12},{5,13},{6,14},{7,15},{8,0},{9,1},... | collective-permute-start | bytes 49160 | tf_op jit(solution)/shard_map/ppermute | solution.py:528
  63.4 1.1 %collective-permute-done.14.refs_0_ = bf16[64,128]{1,0:T(8,128)(2,1)S(1)} collective-permute-done((bf16[64,128]{1,0:T(8,128)(2,1)S(1)}, bf16[64,128]{1,0:T(8,128)(2,1)S(1)}, u32[]{:S(2)}, u32[]{:S(2)}) %collective-permute-start.14) | collective-permute-done | bytes 16416 | tf_op jit(solution)/shard_map/ppermute | solution.py:528
  65.0 1.9 %collective-permute-done.16.refs_2_ = bf16[64,128]{1,0:T(8,128)(2,1)S(1)} collective-permute-done((bf16[64,128]{1,0:T(8,128)(2,1)S(1)}, bf16[64,128]{1,0:T(8,128)(2,1)S(1)}, u32[]{:S(2)}, u32[]{:S(2)}) %collective-permute-start.16) | collective-permute-done | bytes 16416 | tf_op jit(solution)/shard_map/ppermute | solution.py:528
  66.9 0.8 %finish.1 = bf16[2,2048]{1,0:T(2,128)(2,1)} custom-call(f32[64,128]{1,0:T(8,128)S(1)} %get-tuple-element.63.kept, bf16[64,128]{1,0:T(8,128)(2,1)S(1)} %collective-permute-done.14.refs_0_, bf16[64,128]{1,0:T(8,128)(2,1)S(1)} %collective-permute-done.15.refs_1_, bf16[64,128]{1,0:T(8,128)(2,1)S(1)} %collective-permute-done.16.refs_2_), custom_call_target="tpu_custom_call" | custom-call | tf_op jit(solution)/shard_map/finish/pallas_call | solution.py:700
  (40 shorter events, 3.9 us)
Async XLA Ops:
  0.6 7.1 %copy-start = (bf16[1024,256]{1,0:T(8,128)(2,1)S(1)}, bf16[1024,256]{1,0:T(8,128)(2,1)}, u32[]{:S(2)}) copy-start(bf16[1024,256]{1,0:T(8,128)(2,1)} %refs_4_.3) | copy-start | bytes 1572868
  0.6 8.6 %copy-start.1 = (bf16[1024,256]{1,0:T(8,128)(2,1)S(1)}, bf16[1024,256]{1,0:T(8,128)(2,1)}, u32[]{:S(2)}) copy-start(bf16[1024,256]{1,0:T(8,128)(2,1)} %refs_5_.3) | copy-start | bytes 1572868
  3.7 18.5 %collective-permute-start = (bf16[1072,128]{1,0:T(8,128)(2,1)}, bf16[1072,128]{1,0:T(8,128)(2,1)S(1)}, u32[]{:S(2)}, u32[]{:S(2)}) collective-permute-start(bf16[1072,128]{1,0:T(8,128)(2,1)} %get-tuple-element.35), channel_id=1, source_target_pairs={{0,8},{1,9},{2,10},{3,11},{4,12},{5,13},{6,14},{7,15},{8,0},{9,1},... | collective-permute-start | bytes 823304 | tf_op jit(solution)/shard_map/ppermute | solution.py:528
  7.8 14.8 %collective-permute-start.1 = (bf16[1024,256]{1,0:T(8,128)(2,1)S(1)}, bf16[1024,256]{1,0:T(8,128)(2,1)S(1)}, u32[]{:S(2)}, u32[]{:S(2)}) collective-permute-start(bf16[1024,256]{1,0:T(8,128)(2,1)S(1)} %copy-done), channel_id=1, source_target_pairs={{0,2},{1,3},{2,0},{3,1},{4,6},{5,7},{6,4},{7,5},{8,10},{9,11},{10,... | collective-permute-start | bytes 1572872 | tf_op jit(solution)/shard_map/ppermute | solution.py:528
  9.3 23.1 %collective-permute-start.4 = (bf16[1024,256]{1,0:T(8,128)(2,1)S(1)}, bf16[1024,256]{1,0:T(8,128)(2,1)S(1)}, u32[]{:S(2)}, u32[]{:S(2)}) collective-permute-start(bf16[1024,256]{1,0:T(8,128)(2,1)S(1)} %copy-done.1), channel_id=1, source_target_pairs={{0,2},{1,3},{2,0},{3,1},{4,6},{5,7},{6,4},{7,5},{8,10},{9,11},{10,... | collective-permute-start | bytes 1572872 | tf_op jit(solution)/shard_map/ppermute | solution.py:528
  9.8 18.3 %collective-permute-start.8 = (bf16[1072,128]{1,0:T(8,128)(2,1)}, bf16[1072,128]{1,0:T(8,128)(2,1)S(1)}, u32[]{:S(2)}, u32[]{:S(2)}) collective-permute-start(bf16[1072,128]{1,0:T(8,128)(2,1)} %get-tuple-element.48), channel_id=1, source_target_pairs={{0,4},{1,5},{2,6},{3,7},{4,0},{5,1},{6,2},{7,3},{8,12},{9,13},{10,... | collective-permute-start | bytes 823304 | tf_op jit(solution)/shard_map/ppermute | solution.py:528
  11.4 16.7 %collective-permute-start.6 = (bf16[1072,128]{1,0:T(8,128)(2,1)}, bf16[1072,128]{1,0:T(8,128)(2,1)S(1)}, u32[]{:S(2)}, u32[]{:S(2)}) collective-permute-start(bf16[1072,128]{1,0:T(8,128)(2,1)} %get-tuple-element.47), channel_id=1, source_target_pairs={{0,12},{1,13},{2,14},{3,15},{4,8},{5,9},{6,10},{7,11},{8,4},{9,5},... | collective-permute-start | bytes 823304 | tf_op jit(solution)/shard_map/ppermute | solution.py:528
  22.2 10.2 %collective-permute-start.3 = (bf16[1072,128]{1,0:T(8,128)(2,1)S(1)}, bf16[1072,128]{1,0:T(8,128)(2,1)S(1)}, u32[]{:S(2)}, u32[]{:S(2)}) collective-permute-start(bf16[1072,128]{1,0:T(8,128)(2,1)S(1)} %collective-permute-done.refs_2_), channel_id=1, source_target_pairs={{0,1},{1,0},{2,3},{3,2},{4,5},{5,4},{6,7},{7,6},{8,9},{9,8},{10,11... | collective-permute-start | bytes 823304 | tf_op jit(solution)/shard_map/ppermute | solution.py:528
  22.6 9.8 %collective-permute-start.2 = (bf16[1072,128]{1,0:T(8,128)(2,1)}, bf16[1072,128]{1,0:T(8,128)(2,1)S(1)}, u32[]{:S(2)}, u32[]{:S(2)}) collective-permute-start(bf16[1072,128]{1,0:T(8,128)(2,1)} %get-tuple-element.41), channel_id=1, source_target_pairs={{0,1},{1,0},{2,3},{3,2},{4,5},{5,4},{6,7},{7,6},{8,9},{9,8},{10,11... | collective-permute-start | bytes 823304 | tf_op jit(solution)/shard_map/ppermute | solution.py:528
  28.1 7.7 %collective-permute-start.9 = (bf16[1072,128]{1,0:T(8,128)(2,1)S(1)}, bf16[1072,128]{1,0:T(8,128)(2,1)S(1)}, u32[]{:S(2)}, u32[]{:S(2)}) collective-permute-start(bf16[1072,128]{1,0:T(8,128)(2,1)S(1)} %collective-permute-done.8.refs_2_), channel_id=1, source_target_pairs={{0,1},{1,0},{2,3},{3,2},{4,5},{5,4},{6,7},{7,6},{8,9},{9,8},{10,11... | collective-permute-start | bytes 823304 | tf_op jit(solution)/shard_map/ppermute | solution.py:528
  28.1 7.7 %collective-permute-start.7 = (bf16[1072,128]{1,0:T(8,128)(2,1)S(1)}, bf16[1072,128]{1,0:T(8,128)(2,1)S(1)}, u32[]{:S(2)}, u32[]{:S(2)}) collective-permute-start(bf16[1072,128]{1,0:T(8,128)(2,1)S(1)} %collective-permute-done.6.refs_0_), channel_id=1, source_target_pairs={{0,1},{1,0},{2,3},{3,2},{4,5},{5,4},{6,7},{7,6},{8,9},{9,8},{10,11... | collective-permute-start | bytes 823304 | tf_op jit(solution)/shard_map/ppermute | solution.py:528
  33.2 8.8 %copy-start.3 = (bf16[4,128,256]{2,1,0:T(8,128)(2,1)S(1)}, bf16[4,128,256]{2,1,0:T(8,128)(2,1)}, u32[]{:S(2)}) copy-start(bf16[4,128,256]{2,1,0:T(8,128)(2,1)} %refs_2_.1) | copy-start | bytes 786436
  33.2 8.8 %copy-start.4 = (bf16[4,128,256]{2,1,0:T(8,128)(2,1)S(1)}, bf16[4,128,256]{2,1,0:T(8,128)(2,1)}, u32[]{:S(2)}) copy-start(bf16[4,128,256]{2,1,0:T(8,128)(2,1)} %refs_3_.1) | copy-start | bytes 786436
  33.2 8.8 %copy-start.7 = (s32[16]{0:T(128)S(1)}, s32[16]{0:T(128)}, u32[]{:S(2)}) copy-start(s32[16]{0:T(128)} %table_ref.1) | copy-start | bytes 196
  33.2 17.2 %collective-permute-start.5 = (bf16[784,128]{1,0:T(8,128)(2,1)S(1)}, bf16[784,128]{1,0:T(8,128)(2,1)S(1)}, u32[]{:S(2)}, u32[]{:S(2)}) collective-permute-start(bf16[784,128]{1,0:T(8,128)(2,1)S(1)} %get-tuple-element.46), channel_id=1, source_target_pairs={{0,8},{1,9},{2,10},{3,11},{4,12},{5,13},{6,14},{7,15},{8,0},{9,1},... | collective-permute-start | bytes 602120 | tf_op jit(solution)/shard_map/ppermute | solution.py:528
  35.8 16.5 %copy-start.5 = (f32[256]{0:T(256)S(1)}, f32[256]{0:T(256)}, u32[]{:S(2)}) copy-start(f32[256]{0:T(256)} %param.17) | copy-start | bytes 3076
  35.8 16.5 %copy-start.6 = (f32[256]{0:T(256)S(1)}, f32[256]{0:T(256)}, u32[]{:S(2)}) copy-start(f32[256]{0:T(256)} %param.18) | copy-start | bytes 3076
  36.6 13.8 %collective-permute-start.10 = (bf16[784,128]{1,0:T(8,128)(2,1)S(1)}, bf16[784,128]{1,0:T(8,128)(2,1)S(1)}, u32[]{:S(2)}, u32[]{:S(2)}) collective-permute-start(bf16[784,128]{1,0:T(8,128)(2,1)S(1)} %get-tuple-element.50), channel_id=1, source_target_pairs={{0,12},{1,13},{2,14},{3,15},{4,8},{5,9},{6,10},{7,11},{8,4},{9,5},... | collective-permute-start | bytes 602120 | tf_op jit(solution)/shard_map/ppermute | solution.py:528
  38.1 14.2 %collective-permute-start.11 = (bf16[784,128]{1,0:T(8,128)(2,1)S(1)}, bf16[784,128]{1,0:T(8,128)(2,1)S(1)}, u32[]{:S(2)}, u32[]{:S(2)}) collective-permute-start(bf16[784,128]{1,0:T(8,128)(2,1)S(1)} %get-tuple-element.51), channel_id=1, source_target_pairs={{0,4},{1,5},{2,6},{3,7},{4,0},{5,1},{6,2},{7,3},{8,12},{9,13},{10,... | collective-permute-start | bytes 602120 | tf_op jit(solution)/shard_map/ppermute | solution.py:528
  38.1 3.9 %collective-permute-start.12 = (bf16[128,128]{1,0:T(8,128)(2,1)S(1)}, bf16[128,128]{1,0:T(8,128)(2,1)S(1)}, u32[]{:S(2)}, u32[]{:S(2)}) collective-permute-start(bf16[128,128]{1,0:T(8,128)(2,1)S(1)} %get-tuple-element.54.refs_0_), channel_id=1, source_target_pairs={{0,2},{1,3},{2,0},{3,1},{4,6},{5,7},{6,4},{7,5},{8,10},{9,11},{10,... | collective-permute-start | bytes 98312 | tf_op jit(solution)/shard_map/ppermute | solution.py:528
  54.4 4.3 %collective-permute-start.13 = (bf16[256,128]{1,0:T(8,128)(2,1)S(1)}, bf16[256,128]{1,0:T(8,128)(2,1)S(1)}, u32[]{:S(2)}, u32[]{:S(2)}) collective-permute-start(bf16[256,128]{1,0:T(8,128)(2,1)S(1)} %get-tuple-element.62), channel_id=1, source_target_pairs={{0,2},{1,3},{2,0},{3,1},{4,6},{5,7},{6,4},{7,5},{8,10},{9,11},{10,... | collective-permute-start | bytes 196616 | tf_op jit(solution)/shard_map/ppermute | solution.py:528
  58.9 5.6 %collective-permute-start.14 = (bf16[64,128]{1,0:T(8,128)(2,1)S(1)}, bf16[64,128]{1,0:T(8,128)(2,1)S(1)}, u32[]{:S(2)}, u32[]{:S(2)}) collective-permute-start(bf16[64,128]{1,0:T(8,128)(2,1)S(1)} %get-tuple-element.64), channel_id=1, source_target_pairs={{0,12},{1,13},{2,14},{3,15},{4,8},{5,9},{6,10},{7,11},{8,4},{9,5},... | collective-permute-start | bytes 49160 | tf_op jit(solution)/shard_map/ppermute | solution.py:528
  59.5 5.5 %collective-permute-start.15 = (bf16[64,128]{1,0:T(8,128)(2,1)S(1)}, bf16[64,128]{1,0:T(8,128)(2,1)S(1)}, u32[]{:S(2)}, u32[]{:S(2)}) collective-permute-start(bf16[64,128]{1,0:T(8,128)(2,1)S(1)} %get-tuple-element.65), channel_id=1, source_target_pairs={{0,8},{1,9},{2,10},{3,11},{4,12},{5,13},{6,14},{7,15},{8,0},{9,1},... | collective-permute-start | bytes 49160 | tf_op jit(solution)/shard_map/ppermute | solution.py:528
  63.1 3.7 %collective-permute-start.16 = (bf16[64,128]{1,0:T(8,128)(2,1)S(1)}, bf16[64,128]{1,0:T(8,128)(2,1)S(1)}, u32[]{:S(2)}, u32[]{:S(2)}) collective-permute-start(bf16[64,128]{1,0:T(8,128)(2,1)S(1)} %get-tuple-element.66), channel_id=1, source_target_pairs={{0,4},{1,5},{2,6},{3,7},{4,0},{5,1},{6,2},{7,3},{8,12},{9,13},{10,... | collective-permute-start | bytes 49160 | tf_op jit(solution)/shard_map/ppermute | solution.py:528
  (1 other events, 1.0 us)

commit v6 on v5

--- a/solution.py
+++ b/solution.py
@@ -298,8 +298,8 @@
     for group in range(GROUPS):
         for part in parts:
             tiles = part[group * each : (group + 1) * each, :].astype(jnp.float32)
-            for start in range(head * sharing, each, lines):
-                found.append(tiles[start : start + sharing])
+            for line in range(head * sharing, (head + 1) * sharing):
+                found += [tiles[start : start + 1] for start in range(line, each, lines)]
     return jnp.concatenate(found, 0).astype(jnp.bfloat16)
 
 
@@ -375,8 +375,8 @@
         return value
 
     ends = summed(3 * heads * rows, 16)
-    row_query = lax.broadcasted_iota(jnp.int32, (count, 16), 0) // sharing
-    query_position = (ctx ^ (row_query // own_queries)) * own_queries + row_query % own_queries
+    row = lax.broadcasted_iota(jnp.int32, (count, 16), 0)
+    query_position = (ctx ^ (row // (own_queries * sharing))) * own_queries + row % own_queries
     end_column = lax.broadcasted_iota(jnp.int32, (count, 16), 1)
     end_position = ctx * 2 + jnp.where(end_column == 0, core, 1 - core)
     end_seen = (end_column < 2) & (end_position <= query_position)
@@ -422,11 +422,11 @@
         stats = (kept_stats(top[:, 0:1], total[:, 0:1]), sent_stats(top[:, 0:1], total[:, 0:1]))
         each = own_queries * sharing
         for slot in range(GROUPS * PAIR):
-            start = (slot // PAIR * 2 * heads + head) * each
+            start = (slot % PAIR * 2 * heads + head) * each
             at = slice(slot * each, (slot + 1) * each)
-            out = outs[slot % PAIR]
+            out = outs[slot // PAIR]
             out[start : start + each, :] = numer[at].astype(out.dtype)
-            out[start + heads * each : start + (heads + 1) * each, :] = stats[slot % PAIR][at]
+            out[start + heads * each : start + (heads + 1) * each, :] = stats[slot >= PAIR][at]
 
 
 def kept_stats(top, total):
@@ -465,31 +465,25 @@
     return numer, top, total
 
 
-def merge_kernel(kept, other, keep_ref, *send_refs):
+def merge_kernel(kept, *refs):
+    others, (keep_ref, send_ref) = refs[:-2], refs[-2:]
     each = keep_ref.shape[0]
     rows = each // 2
-    for slot in range(GROUPS):
-        numer, top, total = merged(kept, [other], slot * each, rows)
-        if slot == 0:
-            keep_ref[:rows, :] = numer
-            keep_ref[rows:, :] = kept_stats(top, total)
-        else:
-            send_refs[slot - 1][:rows, :] = numer.astype(jnp.bfloat16)
-            send_refs[slot - 1][rows:, :] = sent_stats(top, total)
+    numer, top, total = merged(kept, others, 0, rows)
+    keep_ref[:rows, :] = numer
+    keep_ref[rows:, :] = kept_stats(top, total)
+    numer, top, total = merged(kept, others, each, rows)
+    send_ref[:rows, :] = numer.astype(jnp.bfloat16)
+    send_ref[rows:, :] = sent_stats(top, total)
 
 
 def last_kernel(kept, *refs):
     others, out_ref = refs[:-1], refs[-1]
     numer, _, total = merged(kept, others, 0, kept.shape[0] // 2)
     result = numer / total
-    queries, width = out_ref.shape
-    sharing = QUERY_HEADS // KEY_VALUE_HEADS
-    heads = width // HEAD_SIZE // sharing
-    lines = []
-    for i in range(queries):
-        starts = [(h * queries + i) * sharing + g for h in range(heads) for g in range(sharing)]
-        lines.append(jnp.concatenate([result[s : s + 1] for s in starts], 1))
-    out_ref[...] = jnp.concatenate(lines, 0).astype(jnp.bfloat16)
+    queries = out_ref.shape[0]
+    pieces = [result[s : s + queries] for s in range(0, result.shape[0], queries)]
+    out_ref[...] = jnp.concatenate(pieces, 1).astype(jnp.bfloat16)
 
 
 def exchange_plan(
@@ -663,15 +657,15 @@
     )(place, page_slot_table, split_page, own_tiles, beside_tiles, slot_keys, slot_values)
 
 
-    def payloads(size):
-        return [jax.ShapeDtypeStruct((size, LANES), kind) for kind in (jnp.float32, jnp.bfloat16)]
+    def payload(kind, slots):
+        return jax.ShapeDtypeStruct((2 * slots * states // n_ctx, LANES), kind)
 
     row_shape = jax.ShapeDtypeStruct((rows, width), jnp.bfloat16)
-    front_key, front_value, kept, sent = pl.pallas_call(
+    front_key, front_value, kept, *sent = pl.pallas_call(
         front_kernel,
         in_specs=[smem, smem] + [vmem] * (GROUPS + 7),
-        out_specs=[vmem] * 4,
-        out_shape=[row_shape] * 2 + payloads(states),
+        out_specs=[vmem] * (2 + GROUPS),
+        out_shape=[row_shape] * 2 + [payload(jnp.float32, PAIR)] + [payload(jnp.bfloat16, PAIR)] * (GROUPS - 1),
         compiler_params=params,
         cost_estimate=pl.CostEstimate(flops=4 * states * rows * HEAD_SIZE, bytes_accessed=2 * 1024 * 1024, transcendentals=states * rows),
         name="front_attention",
@@ -689,22 +683,22 @@
         total,
         numer,
     )
-    kept, *sent = pl.pallas_call(
+    kept, sent = pl.pallas_call(
         merge_kernel,
-        in_specs=[vmem] * 2,
-        out_specs=[vmem] * GROUPS,
-        out_shape=payloads(states // GROUPS) + payloads(states // GROUPS)[1:] * (GROUPS - 2),
+        in_specs=[vmem] * GROUPS,
+        out_specs=[vmem] * 2,
+        out_shape=[payload(jnp.float32, 1), payload(jnp.bfloat16, 1)],
         compiler_params=params,
         name="merge",
-    )(kept, move(sent, beside))
+    )(kept, *[move(sent[s - 1], along(s)) for s in range(GROUPS - 1, 0, -1)])
     attended = pl.pallas_call(
         last_kernel,
-        in_specs=[vmem] * GROUPS,
+        in_specs=[vmem] * 2,
         out_specs=vmem,
         out_shape=jax.ShapeDtypeStruct((own_queries, query_width), jnp.bfloat16),
         compiler_params=params,
         name="finish",
-    )(kept, *[move(sent[s - 1], along(s)) for s in range(GROUPS - 1, 0, -1)])
+    )(kept, move(sent, beside))
     return (front_key, front_value, attended)
 
 

time: 67.9 us -> 67.6 us (level)
  no operation moved by 1% of the time
where the time goes in v6:
time: 67.6 us; the launch traced here: 67.4 us
  waiting for transfers between devices  35.4 us (52%)
  starting transfers between devices  19.8 us (29%)
  Pallas kernels  9.22 us (14%)
  between operations  1.43 us (2%)
  local copies, waits for them, and re-layouts  0.99 us (1%)
    ppermute x17, waiting for transfers between devices, move(): return lax.ppermute(array, ('ctx', 'tp'), pairs)  35.4 us
    ppermute x17, starting transfers between devices, move(): return lax.ppermute(array, ('ctx', 'tp'), pairs)  19.8 us
    pallas_call x1, Pallas kernels, exchange_plan(): pl.pallas_call(norm_kernel, in_specs=[hbm] * 4, out_specs=[hbm] * (GROUPS...  2.99 us
    pallas_call x1, Pallas kernels, exchange_plan(): pl.pallas_call(front_kernel, in_specs=[smem, smem] + [vmem] * (GROUPS + 7...  2.16 us
    pallas_call x2, Pallas kernels, exchange_plan(): pl.pallas_call(functools.partial(project_kernel, shifts), in_specs=[vmem]...  1.57 us
    pallas_call x1, Pallas kernels, exchange_plan(): pl.pallas_call(loaded_kernel, in_specs=[smem, smem, smem] + [vmem] * (PAI...  1.35 us
  transfers between devices with their start and end apart: 17, of which 11 were waited for; matrix products, arithmetic and copies ran while one was open for 1% of the time, Pallas kernels for 4%

profile of v6, /device:TPU:0, one launch (start us, length us, event | category | flops | bytes accessed | tf_op | source)
XLA Modules:
  0.0 67.4 jit_solution(8395753335799833094)
XLA Ops:
  0.7 3.0 %norm_rows.1 = (bf16[1072,128]{1,0:T(8,128)(2,1)}, bf16[1072,128]{1,0:T(8,128)(2,1)}, bf16[1072,128]{1,0:T(8,128)(2,1)}, bf16[1072,128]{1,0:T(8,128)(2,1)}, bf16[1072,128]{1,0:T(8,128)(2,1)}) custom-call(bf16[2,2048]{1,0:T(2,128)(2,1)} %query_any.1, bf16[128,8192]{1,0:T(8,128)(2,1)} %hidden_any.1, bf16[2,8192]{1,0:T(2,128)(2,1)} %suffix_any.1, f32[1,8192]{1,0:T(1,128)} %bitcast.7), custom_call_target="tpu_custom_call" | custom-call | flops 2097152 | bytes 2097152 | tf_op jit(solution)/shard_map/norm_rows/pallas_call | solution.py:541
  3.7 4.1 %collective-permute-start = (bf16[1072,128]{1,0:T(8,128)(2,1)}, bf16[1072,128]{1,0:T(8,128)(2,1)S(1)}, u32[]{:S(2)}, u32[]{:S(2)}) collective-permute-start(bf16[1072,128]{1,0:T(8,128)(2,1)} %get-tuple-element.35), channel_id=1, source_target_pairs={{0,8},{1,9},{2,10},{3,11},{4,12},{5,13},{6,14},{7,15},{8,0},{9,1},... | collective-permute-start | bytes 823304 | tf_op jit(solution)/shard_map/ppermute | solution.py:522
  7.8 1.5 %collective-permute-start.1 = (bf16[1024,256]{1,0:T(8,128)(2,1)S(1)}, bf16[1024,256]{1,0:T(8,128)(2,1)S(1)}, u32[]{:S(2)}, u32[]{:S(2)}) collective-permute-start(bf16[1024,256]{1,0:T(8,128)(2,1)S(1)} %copy-done), channel_id=1, source_target_pairs={{0,2},{1,3},{2,0},{3,1},{4,6},{5,7},{6,4},{7,5},{8,10},{9,11},{10,... | collective-permute-start | bytes 1572872 | tf_op jit(solution)/shard_map/ppermute | solution.py:522
  9.8 1.6 %collective-permute-start.8 = (bf16[1072,128]{1,0:T(8,128)(2,1)}, bf16[1072,128]{1,0:T(8,128)(2,1)S(1)}, u32[]{:S(2)}, u32[]{:S(2)}) collective-permute-start(bf16[1072,128]{1,0:T(8,128)(2,1)} %get-tuple-element.48), channel_id=1, source_target_pairs={{0,4},{1,5},{2,6},{3,7},{4,0},{5,1},{6,2},{7,3},{8,12},{9,13},{10,... | collective-permute-start | bytes 823304 | tf_op jit(solution)/shard_map/ppermute | solution.py:522
  11.8 0.9 %copy-done.2 = bf16[1072,128]{1,0:T(8,128)(2,1)S(1)} copy-done((bf16[1072,128]{1,0:T(8,128)(2,1)S(1)}, bf16[1072,128]{1,0:T(8,128)(2,1)}, u32[]{:S(2)}) %copy-start.2) | copy-done | bytes 274456
  12.9 9.3 %collective-permute-done.refs_2_ = bf16[1072,128]{1,0:T(8,128)(2,1)S(1)} collective-permute-done((bf16[1072,128]{1,0:T(8,128)(2,1)}, bf16[1072,128]{1,0:T(8,128)(2,1)S(1)}, u32[]{:S(2)}, u32[]{:S(2)}) %collective-permute-start) | collective-permute-done | bytes 274464 | tf_op jit(solution)/shard_map/ppermute | solution.py:522
  22.7 5.4 %collective-permute-done.8.refs_2_ = bf16[1072,128]{1,0:T(8,128)(2,1)S(1)} collective-permute-done((bf16[1072,128]{1,0:T(8,128)(2,1)}, bf16[1072,128]{1,0:T(8,128)(2,1)S(1)}, u32[]{:S(2)}, u32[]{:S(2)}) %collective-permute-start.8) | collective-permute-done | bytes 274464 | tf_op jit(solution)/shard_map/ppermute | solution.py:522
  28.6 3.8 %collective-permute-done.4.refs_7_ = bf16[1024,256]{1,0:T(8,128)(2,1)S(1)} collective-permute-done((bf16[1024,256]{1,0:T(8,128)(2,1)S(1)}, bf16[1024,256]{1,0:T(8,128)(2,1)S(1)}, u32[]{:S(2)}, u32[]{:S(2)}) %collective-permute-start.4) | collective-permute-done | bytes 524320 | tf_op jit(solution)/shard_map/ppermute | solution.py:522
  32.4 0.8 %project.2 = (bf16[784,128]{1,0:T(8,128)(2,1)S(1)}, bf16[784,128]{1,0:T(8,128)(2,1)S(1)}, bf16[128,128]{1,0:T(8,128)(2,1)S(1)}) custom-call(bf16[1072,128]{1,0:T(8,128)(2,1)S(1)} %fetch_own.1.refs_0_, bf16[1072,128]{1,0:T(8,128)(2,1)S(1)} %collective-permute-done.2.refs_1_, bf16[1072,128]{1,0:T(8,128)(2,1)S(1)} %collective-permute-done.refs_2_, ...), custom_call_target="tpu_custom_call" | custom-call | flops 536870912 | bytes 6291456 | tf_op jit(solution)/shard_map/project/pallas_call | solution.py:605
  33.2 2.6 %collective-permute-start.5 = (bf16[784,128]{1,0:T(8,128)(2,1)S(1)}, bf16[784,128]{1,0:T(8,128)(2,1)S(1)}, u32[]{:S(2)}, u32[]{:S(2)}) collective-permute-start(bf16[784,128]{1,0:T(8,128)(2,1)S(1)} %get-tuple-element.46), channel_id=1, source_target_pairs={{0,8},{1,9},{2,10},{3,11},{4,12},{5,13},{6,14},{7,15},{8,0},{9,1},... | collective-permute-start | bytes 602120 | tf_op jit(solution)/shard_map/ppermute | solution.py:522
  36.6 1.5 %collective-permute-start.10 = (bf16[784,128]{1,0:T(8,128)(2,1)S(1)}, bf16[784,128]{1,0:T(8,128)(2,1)S(1)}, u32[]{:S(2)}, u32[]{:S(2)}) collective-permute-start(bf16[784,128]{1,0:T(8,128)(2,1)S(1)} %get-tuple-element.50), channel_id=1, source_target_pairs={{0,12},{1,13},{2,14},{3,15},{4,8},{5,9},{6,10},{7,11},{8,4},{9,5},... | collective-permute-start | bytes 602120 | tf_op jit(solution)/shard_map/ppermute | solution.py:522
  38.1 1.5 %collective-permute-start.12 = (bf16[128,128]{1,0:T(8,128)(2,1)S(1)}, bf16[128,128]{1,0:T(8,128)(2,1)S(1)}, u32[]{:S(2)}, u32[]{:S(2)}) collective-permute-start(bf16[128,128]{1,0:T(8,128)(2,1)S(1)} %get-tuple-element.54.refs_0_), channel_id=1, source_target_pairs={{0,2},{1,3},{2,0},{3,1},{4,6},{5,7},{6,4},{7,5},{8,10},{9,11},{10,... | collective-permute-start | bytes 98312 | tf_op jit(solution)/shard_map/ppermute | solution.py:522
  40.3 1.7 %collective-permute-done.12.refs_1_ = bf16[128,128]{1,0:T(8,128)(2,1)S(1)} collective-permute-done((bf16[128,128]{1,0:T(8,128)(2,1)S(1)}, bf16[128,128]{1,0:T(8,128)(2,1)S(1)}, u32[]{:S(2)}, u32[]{:S(2)}) %collective-permute-start.12) | collective-permute-done | bytes 32800 | tf_op jit(solution)/shard_map/ppermute | solution.py:522
  42.0 1.4 %loaded_attention.1 = (f32[256,128]{1,0:T(8,128)S(1)}, f32[256,128]{1,0:T(8,128)S(1)}, f32[256,128]{1,0:T(8,128)S(1)}, bf16[256,128]{1,0:T(8,128)(2,1)S(1)}) custom-call(s32[2]{0:T(128)S(1)} %pad_add_fusion.place_ref, s32[16]{0:T(128)S(1)} %copy-done.7, s32[1]{0:T(128)S(6)} %copy.15.split_ref, bf16[128,128]{1,0:T(8,128)(2,1)S(1)} %get-tuple-element.54.refs_0_, ...), custom_call_target="tpu_custom_call" | custom-call | flops 67108864 | bytes 524288 | tf_op jit(solution)/shard_map/loaded_attention/pallas_call | solution.py:645
  43.4 7.0 %collective-permute-done.5.other = bf16[784,128]{1,0:T(8,128)(2,1)S(1)} collective-permute-done((bf16[784,128]{1,0:T(8,128)(2,1)S(1)}, bf16[784,128]{1,0:T(8,128)(2,1)S(1)}, u32[]{:S(2)}, u32[]{:S(2)}) %collective-permute-start.5) | collective-permute-done | bytes 200736 | tf_op jit(solution)/shard_map/ppermute | solution.py:522
  50.4 1.8 %collective-permute-done.11.refs_1_ = bf16[784,128]{1,0:T(8,128)(2,1)S(1)} collective-permute-done((bf16[784,128]{1,0:T(8,128)(2,1)S(1)}, bf16[784,128]{1,0:T(8,128)(2,1)S(1)}, u32[]{:S(2)}, u32[]{:S(2)}) %collective-permute-start.11) | collective-permute-done | bytes 200736 | tf_op jit(solution)/shard_map/ppermute | solution.py:522
  52.3 2.2 %front_attention.1 = (bf16[128,256]{1,0:T(8,128)(2,1)}, bf16[128,256]{1,0:T(8,128)(2,1)}, f32[128,128]{1,0:T(8,128)S(1)}, bf16[128,128]{1,0:T(8,128)(2,1)S(1)}, ...) custom-call(s32[2]{0:T(128)S(1)} %pad_add_fusion.place_ref, s32[1]{0:T(128)S(6)} %copy.15.split_ref, ...), custom_call_target="tpu_custom_call" | custom-call | flops 16777216 | bytes 2097152 | tf_op jit(solution)/shard_map/front_attention/pallas_call | solution.py:664
  55.0 3.6 %collective-permute-start.14 = (bf16[128,128]{1,0:T(8,128)(2,1)S(1)}, bf16[128,128]{1,0:T(8,128)(2,1)S(1)}, u32[]{:S(2)}, u32[]{:S(2)}) collective-permute-start(bf16[128,128]{1,0:T(8,128)(2,1)S(1)} %get-tuple-element.63), channel_id=1, source_target_pairs={{0,8},{1,9},{2,10},{3,11},{4,12},{5,13},{6,14},{7,15},{8,0},{9,1},... | collective-permute-start | bytes 98312 | tf_op jit(solution)/shard_map/ppermute | solution.py:522
  58.8 1.6 %collective-permute-done.13.refs_0_ = bf16[128,128]{1,0:T(8,128)(2,1)S(1)} collective-permute-done((bf16[128,128]{1,0:T(8,128)(2,1)S(1)}, bf16[128,128]{1,0:T(8,128)(2,1)S(1)}, u32[]{:S(2)}, u32[]{:S(2)}) %collective-permute-start.13) | collective-permute-done | bytes 32800 | tf_op jit(solution)/shard_map/ppermute | solution.py:522
  60.5 1.1 %collective-permute-done.14.refs_1_ = bf16[128,128]{1,0:T(8,128)(2,1)S(1)} collective-permute-done((bf16[128,128]{1,0:T(8,128)(2,1)S(1)}, bf16[128,128]{1,0:T(8,128)(2,1)S(1)}, u32[]{:S(2)}, u32[]{:S(2)}) %collective-permute-start.14) | collective-permute-done | bytes 32800 | tf_op jit(solution)/shard_map/ppermute | solution.py:522
  61.6 0.9 %collective-permute-done.15.refs_2_ = bf16[128,128]{1,0:T(8,128)(2,1)S(1)} collective-permute-done((bf16[128,128]{1,0:T(8,128)(2,1)S(1)}, bf16[128,128]{1,0:T(8,128)(2,1)S(1)}, u32[]{:S(2)}, u32[]{:S(2)}) %collective-permute-start.15) | collective-permute-done | bytes 32800 | tf_op jit(solution)/shard_map/ppermute | solution.py:522
  62.8 1.6 %collective-permute-start.16 = (bf16[64,128]{1,0:T(8,128)(2,1)S(1)}, bf16[64,128]{1,0:T(8,128)(2,1)S(1)}, u32[]{:S(2)}, u32[]{:S(2)}) collective-permute-start(bf16[64,128]{1,0:T(8,128)(2,1)S(1)} %get-tuple-element.66), channel_id=1, source_target_pairs={{0,2},{1,3},{2,0},{3,1},{4,6},{5,7},{6,4},{7,5},{8,10},{9,11},{10,... | collective-permute-start | bytes 49160 | tf_op jit(solution)/shard_map/ppermute | solution.py:522
  64.3 2.2 %collective-permute-done.16.refs_0_ = bf16[64,128]{1,0:T(8,128)(2,1)S(1)} collective-permute-done((bf16[64,128]{1,0:T(8,128)(2,1)S(1)}, bf16[64,128]{1,0:T(8,128)(2,1)S(1)}, u32[]{:S(2)}, u32[]{:S(2)}) %collective-permute-start.16) | collective-permute-done | bytes 16416 | tf_op jit(solution)/shard_map/ppermute | solution.py:522
  66.6 0.8 %finish.1 = bf16[2,2048]{1,0:T(2,128)(2,1)} custom-call(f32[64,128]{1,0:T(8,128)S(1)} %get-tuple-element.65.kept, bf16[64,128]{1,0:T(8,128)(2,1)S(1)} %collective-permute-done.16.refs_0_), custom_call_target="tpu_custom_call" | custom-call | tf_op jit(solution)/shard_map/finish/pallas_call | solution.py:694
  (40 shorter events, 4.0 us)
Async XLA Ops:
  0.6 7.1 %copy-start = (bf16[1024,256]{1,0:T(8,128)(2,1)S(1)}, bf16[1024,256]{1,0:T(8,128)(2,1)}, u32[]{:S(2)}) copy-start(bf16[1024,256]{1,0:T(8,128)(2,1)} %refs_4_.3) | copy-start | bytes 1572868
  0.6 8.6 %copy-start.1 = (bf16[1024,256]{1,0:T(8,128)(2,1)S(1)}, bf16[1024,256]{1,0:T(8,128)(2,1)}, u32[]{:S(2)}) copy-start(bf16[1024,256]{1,0:T(8,128)(2,1)} %refs_5_.3) | copy-start | bytes 1572868
  3.7 18.5 %collective-permute-start = (bf16[1072,128]{1,0:T(8,128)(2,1)}, bf16[1072,128]{1,0:T(8,128)(2,1)S(1)}, u32[]{:S(2)}, u32[]{:S(2)}) collective-permute-start(bf16[1072,128]{1,0:T(8,128)(2,1)} %get-tuple-element.35), channel_id=1, source_target_pairs={{0,8},{1,9},{2,10},{3,11},{4,12},{5,13},{6,14},{7,15},{8,0},{9,1},... | collective-permute-start | bytes 823304 | tf_op jit(solution)/shard_map/ppermute | solution.py:522
  7.8 14.8 %collective-permute-start.1 = (bf16[1024,256]{1,0:T(8,128)(2,1)S(1)}, bf16[1024,256]{1,0:T(8,128)(2,1)S(1)}, u32[]{:S(2)}, u32[]{:S(2)}) collective-permute-start(bf16[1024,256]{1,0:T(8,128)(2,1)S(1)} %copy-done), channel_id=1, source_target_pairs={{0,2},{1,3},{2,0},{3,1},{4,6},{5,7},{6,4},{7,5},{8,10},{9,11},{10,... | collective-permute-start | bytes 1572872 | tf_op jit(solution)/shard_map/ppermute | solution.py:522
  9.3 23.1 %collective-permute-start.4 = (bf16[1024,256]{1,0:T(8,128)(2,1)S(1)}, bf16[1024,256]{1,0:T(8,128)(2,1)S(1)}, u32[]{:S(2)}, u32[]{:S(2)}) collective-permute-start(bf16[1024,256]{1,0:T(8,128)(2,1)S(1)} %copy-done.1), channel_id=1, source_target_pairs={{0,2},{1,3},{2,0},{3,1},{4,6},{5,7},{6,4},{7,5},{8,10},{9,11},{10,... | collective-permute-start | bytes 1572872 | tf_op jit(solution)/shard_map/ppermute | solution.py:522
  9.8 18.3 %collective-permute-start.8 = (bf16[1072,128]{1,0:T(8,128)(2,1)}, bf16[1072,128]{1,0:T(8,128)(2,1)S(1)}, u32[]{:S(2)}, u32[]{:S(2)}) collective-permute-start(bf16[1072,128]{1,0:T(8,128)(2,1)} %get-tuple-element.48), channel_id=1, source_target_pairs={{0,4},{1,5},{2,6},{3,7},{4,0},{5,1},{6,2},{7,3},{8,12},{9,13},{10,... | collective-permute-start | bytes 823304 | tf_op jit(solution)/shard_map/ppermute | solution.py:522
  11.4 16.7 %collective-permute-start.6 = (bf16[1072,128]{1,0:T(8,128)(2,1)}, bf16[1072,128]{1,0:T(8,128)(2,1)S(1)}, u32[]{:S(2)}, u32[]{:S(2)}) collective-permute-start(bf16[1072,128]{1,0:T(8,128)(2,1)} %get-tuple-element.47), channel_id=1, source_target_pairs={{0,12},{1,13},{2,14},{3,15},{4,8},{5,9},{6,10},{7,11},{8,4},{9,5},... | collective-permute-start | bytes 823304 | tf_op jit(solution)/shard_map/ppermute | solution.py:522
  22.2 10.2 %collective-permute-start.3 = (bf16[1072,128]{1,0:T(8,128)(2,1)S(1)}, bf16[1072,128]{1,0:T(8,128)(2,1)S(1)}, u32[]{:S(2)}, u32[]{:S(2)}) collective-permute-start(bf16[1072,128]{1,0:T(8,128)(2,1)S(1)} %collective-permute-done.refs_2_), channel_id=1, source_target_pairs={{0,1},{1,0},{2,3},{3,2},{4,5},{5,4},{6,7},{7,6},{8,9},{9,8},{10,11... | collective-permute-start | bytes 823304 | tf_op jit(solution)/shard_map/ppermute | solution.py:522
  22.6 9.8 %collective-permute-start.2 = (bf16[1072,128]{1,0:T(8,128)(2,1)}, bf16[1072,128]{1,0:T(8,128)(2,1)S(1)}, u32[]{:S(2)}, u32[]{:S(2)}) collective-permute-start(bf16[1072,128]{1,0:T(8,128)(2,1)} %get-tuple-element.41), channel_id=1, source_target_pairs={{0,1},{1,0},{2,3},{3,2},{4,5},{5,4},{6,7},{7,6},{8,9},{9,8},{10,11... | collective-permute-start | bytes 823304 | tf_op jit(solution)/shard_map/ppermute | solution.py:522
  28.1 7.7 %collective-permute-start.9 = (bf16[1072,128]{1,0:T(8,128)(2,1)S(1)}, bf16[1072,128]{1,0:T(8,128)(2,1)S(1)}, u32[]{:S(2)}, u32[]{:S(2)}) collective-permute-start(bf16[1072,128]{1,0:T(8,128)(2,1)S(1)} %collective-permute-done.8.refs_2_), channel_id=1, source_target_pairs={{0,1},{1,0},{2,3},{3,2},{4,5},{5,4},{6,7},{7,6},{8,9},{9,8},{10,11... | collective-permute-start | bytes 823304 | tf_op jit(solution)/shard_map/ppermute | solution.py:522
  28.1 7.7 %collective-permute-start.7 = (bf16[1072,128]{1,0:T(8,128)(2,1)S(1)}, bf16[1072,128]{1,0:T(8,128)(2,1)S(1)}, u32[]{:S(2)}, u32[]{:S(2)}) collective-permute-start(bf16[1072,128]{1,0:T(8,128)(2,1)S(1)} %collective-permute-done.6.refs_0_), channel_id=1, source_target_pairs={{0,1},{1,0},{2,3},{3,2},{4,5},{5,4},{6,7},{7,6},{8,9},{9,8},{10,11... | collective-permute-start | bytes 823304 | tf_op jit(solution)/shard_map/ppermute | solution.py:522
  33.2 8.8 %copy-start.3 = (bf16[4,128,256]{2,1,0:T(8,128)(2,1)S(1)}, bf16[4,128,256]{2,1,0:T(8,128)(2,1)}, u32[]{:S(2)}) copy-start(bf16[4,128,256]{2,1,0:T(8,128)(2,1)} %refs_2_.1) | copy-start | bytes 786436
  33.2 8.8 %copy-start.4 = (bf16[4,128,256]{2,1,0:T(8,128)(2,1)S(1)}, bf16[4,128,256]{2,1,0:T(8,128)(2,1)}, u32[]{:S(2)}) copy-start(bf16[4,128,256]{2,1,0:T(8,128)(2,1)} %refs_3_.1) | copy-start | bytes 786436
  33.2 8.8 %copy-start.7 = (s32[16]{0:T(128)S(1)}, s32[16]{0:T(128)}, u32[]{:S(2)}) copy-start(s32[16]{0:T(128)} %table_ref.1) | copy-start | bytes 196
  33.2 17.2 %collective-permute-start.5 = (bf16[784,128]{1,0:T(8,128)(2,1)S(1)}, bf16[784,128]{1,0:T(8,128)(2,1)S(1)}, u32[]{:S(2)}, u32[]{:S(2)}) collective-permute-start(bf16[784,128]{1,0:T(8,128)(2,1)S(1)} %get-tuple-element.46), channel_id=1, source_target_pairs={{0,8},{1,9},{2,10},{3,11},{4,12},{5,13},{6,14},{7,15},{8,0},{9,1},... | collective-permute-start | bytes 602120 | tf_op jit(solution)/shard_map/ppermute | solution.py:522
  35.8 16.5 %copy-start.5 = (f32[256]{0:T(256)S(1)}, f32[256]{0:T(256)}, u32[]{:S(2)}) copy-start(f32[256]{0:T(256)} %param.17) | copy-start | bytes 3076
  35.8 16.5 %copy-start.6 = (f32[256]{0:T(256)S(1)}, f32[256]{0:T(256)}, u32[]{:S(2)}) copy-start(f32[256]{0:T(256)} %param.18) | copy-start | bytes 3076
  36.6 13.8 %collective-permute-start.10 = (bf16[784,128]{1,0:T(8,128)(2,1)S(1)}, bf16[784,128]{1,0:T(8,128)(2,1)S(1)}, u32[]{:S(2)}, u32[]{:S(2)}) collective-permute-start(bf16[784,128]{1,0:T(8,128)(2,1)S(1)} %get-tuple-element.50), channel_id=1, source_target_pairs={{0,12},{1,13},{2,14},{3,15},{4,8},{5,9},{6,10},{7,11},{8,4},{9,5},... | collective-permute-start | bytes 602120 | tf_op jit(solution)/shard_map/ppermute | solution.py:522
  38.1 14.2 %collective-permute-start.11 = (bf16[784,128]{1,0:T(8,128)(2,1)S(1)}, bf16[784,128]{1,0:T(8,128)(2,1)S(1)}, u32[]{:S(2)}, u32[]{:S(2)}) collective-permute-start(bf16[784,128]{1,0:T(8,128)(2,1)S(1)} %get-tuple-element.51), channel_id=1, source_target_pairs={{0,4},{1,5},{2,6},{3,7},{4,0},{5,1},{6,2},{7,3},{8,12},{9,13},{10,... | collective-permute-start | bytes 602120 | tf_op jit(solution)/shard_map/ppermute | solution.py:522
  38.1 3.9 %collective-permute-start.12 = (bf16[128,128]{1,0:T(8,128)(2,1)S(1)}, bf16[128,128]{1,0:T(8,128)(2,1)S(1)}, u32[]{:S(2)}, u32[]{:S(2)}) collective-permute-start(bf16[128,128]{1,0:T(8,128)(2,1)S(1)} %get-tuple-element.54.refs_0_), channel_id=1, source_target_pairs={{0,2},{1,3},{2,0},{3,1},{4,6},{5,7},{6,4},{7,5},{8,10},{9,11},{10,... | collective-permute-start | bytes 98312 | tf_op jit(solution)/shard_map/ppermute | solution.py:522
  54.5 6.0 %collective-permute-start.13 = (bf16[128,128]{1,0:T(8,128)(2,1)S(1)}, bf16[128,128]{1,0:T(8,128)(2,1)S(1)}, u32[]{:S(2)}, u32[]{:S(2)}) collective-permute-start(bf16[128,128]{1,0:T(8,128)(2,1)S(1)} %get-tuple-element.62), channel_id=1, source_target_pairs={{0,12},{1,13},{2,14},{3,15},{4,8},{5,9},{6,10},{7,11},{8,4},{9,5},... | collective-permute-start | bytes 98312 | tf_op jit(solution)/shard_map/ppermute | solution.py:522
  55.0 6.6 %collective-permute-start.14 = (bf16[128,128]{1,0:T(8,128)(2,1)S(1)}, bf16[128,128]{1,0:T(8,128)(2,1)S(1)}, u32[]{:S(2)}, u32[]{:S(2)}) collective-permute-start(bf16[128,128]{1,0:T(8,128)(2,1)S(1)} %get-tuple-element.63), channel_id=1, source_target_pairs={{0,8},{1,9},{2,10},{3,11},{4,12},{5,13},{6,14},{7,15},{8,0},{9,1},... | collective-permute-start | bytes 98312 | tf_op jit(solution)/shard_map/ppermute | solution.py:522
  58.6 3.9 %collective-permute-start.15 = (bf16[128,128]{1,0:T(8,128)(2,1)S(1)}, bf16[128,128]{1,0:T(8,128)(2,1)S(1)}, u32[]{:S(2)}, u32[]{:S(2)}) collective-permute-start(bf16[128,128]{1,0:T(8,128)(2,1)S(1)} %get-tuple-element.64), channel_id=1, source_target_pairs={{0,4},{1,5},{2,6},{3,7},{4,0},{5,1},{6,2},{7,3},{8,12},{9,13},{10,... | collective-permute-start | bytes 98312 | tf_op jit(solution)/shard_map/ppermute | solution.py:522
  62.8 3.8 %collective-permute-start.16 = (bf16[64,128]{1,0:T(8,128)(2,1)S(1)}, bf16[64,128]{1,0:T(8,128)(2,1)S(1)}, u32[]{:S(2)}, u32[]{:S(2)}) collective-permute-start(bf16[64,128]{1,0:T(8,128)(2,1)S(1)} %get-tuple-element.66), channel_id=1, source_target_pairs={{0,2},{1,3},{2,0},{3,1},{4,6},{5,7},{6,4},{7,5},{8,10},{9,11},{10,... | collective-permute-start | bytes 49160 | tf_op jit(solution)/shard_map/ppermute | solution.py:522
  (1 other events, 1.0 us)

commit v7 on v6

--- a/solution.py
+++ b/solution.py
@@ -357,8 +357,8 @@
     (key_bias, value_bias, cosine_ref, sine_ref, query_ref, top_ref, total_ref, numer_ref) = refs[
         GROUPS - 2 : GROUPS + 6
     ]
-    front_key, front_value = refs[GROUPS + 6 : GROUPS + 8]
-    outs = refs[GROUPS + 8 :]
+    key_any, value_any, *outs = refs[GROUPS + 6 : -3]
+    front_key, front_value, sems = refs[-3:]
     core, ctx = place_ref[0], place_ref[1]
     rows, width = front_key.shape
     half_rows = rows // 2
@@ -381,6 +381,7 @@
     end_position = ctx * 2 + jnp.where(end_column == 0, core, 1 - core)
     end_seen = (end_column < 2) & (end_position <= query_position)
     pad = jnp.zeros((14, HEAD_SIZE), jnp.float32)
+    end_pairs = []
     for head in range(heads):
         columns = slice(head * HEAD_SIZE, (head + 1) * HEAD_SIZE)
         raw = summed(head * rows, rows) + summed((heads + head) * rows, rows)
@@ -401,6 +402,14 @@
             to = pl.ds(pl.multiple_of(lax.rem(core + half, 2) * half_rows, half_rows), half_rows)
             front_key[to, columns] = key[half * half_rows : (half + 1) * half_rows]
             front_value[to, columns] = value[half * half_rows : (half + 1) * half_rows]
+        end_pairs.append((key, value, end_key, end_value))
+    leaving = [
+        pltpu.make_async_copy(front_key, key_any, sems.at[0]),
+        pltpu.make_async_copy(front_value, value_any, sems.at[1]),
+    ]
+    for copy in leaving:
+        copy.start()
+    for head, (key, value, end_key, end_value) in enumerate(end_pairs):
         part = slice(head * count, (head + 1) * count)
         queries = query_ref[part, :]
         scores = jnp.where(visible, times_transposed(queries, key) * SCALE, masked_score)
@@ -419,14 +428,23 @@
             + jnp.dot(expos.astype(jnp.bfloat16), value, preferred_element_type=jnp.float32)
             + jnp.dot(end_expos.astype(jnp.bfloat16), end_value, preferred_element_type=jnp.float32)
         )
-        stats = (kept_stats(top[:, 0:1], total[:, 0:1]), sent_stats(top[:, 0:1], total[:, 0:1]))
         each = own_queries * sharing
+        split = PAIR * each
+        stats = jnp.concatenate(
+            [
+                kept_stats(top[:split, 0:1], total[:split, 0:1]),
+                sent_stats(top[split:, 0:1], total[split:, 0:1]).astype(jnp.float32),
+            ],
+            0,
+        )
         for slot in range(GROUPS * PAIR):
             start = (slot % PAIR * 2 * heads + head) * each
             at = slice(slot * each, (slot + 1) * each)
             out = outs[slot // PAIR]
             out[start : start + each, :] = numer[at].astype(out.dtype)
-            out[start + heads * each : start + (heads + 1) * each, :] = stats[slot >= PAIR][at]
+            out[start + heads * each : start + (heads + 1) * each, :] = stats[at].astype(out.dtype)
+    for copy in leaving:
+        copy.wait()
 
 
 def kept_stats(top, total):
@@ -664,7 +682,8 @@
     front_key, front_value, kept, *sent = pl.pallas_call(
         front_kernel,
         in_specs=[smem, smem] + [vmem] * (GROUPS + 7),
-        out_specs=[vmem] * (2 + GROUPS),
+        out_specs=[hbm] * 2 + [vmem] * GROUPS,
+        scratch_shapes=[pltpu.VMEM((rows, width), jnp.bfloat16)] * 2 + [pltpu.SemaphoreType.DMA((2,))],
         out_shape=[row_shape] * 2 + [payload(jnp.float32, PAIR)] + [payload(jnp.bfloat16, PAIR)] * (GROUPS - 1),
         compiler_params=params,
         cost_estimate=pl.CostEstimate(flops=4 * states * rows * HEAD_SIZE, bytes_accessed=2 * 1024 * 1024, transcendentals=states * rows),

time: 67.6 us -> 67.6 us (level)
  no operation moved by 1% of the time
where the time goes in v7:
time: 67.6 us; the launch traced here: 67.4 us
  waiting for transfers between devices  35.4 us (52%)
  starting transfers between devices  19.9 us (29%)
  Pallas kernels  9.15 us (14%)
  between operations  1.44 us (2%)
  local copies, waits for them, and re-layouts  0.99 us (1%)
    ppermute x17, waiting for transfers between devices, move(): return lax.ppermute(array, ('ctx', 'tp'), pairs)  35.4 us
    ppermute x17, starting transfers between devices, move(): return lax.ppermute(array, ('ctx', 'tp'), pairs)  19.9 us
    pallas_call x1, Pallas kernels, exchange_plan(): pl.pallas_call(norm_kernel, in_specs=[hbm] * 4, out_specs=[hbm] * (GROUPS...  2.99 us
    pallas_call x1, Pallas kernels, exchange_plan(): pl.pallas_call(front_kernel, in_specs=[smem, smem] + [vmem] * (GROUPS + 7...  2.09 us
    pallas_call x2, Pallas kernels, exchange_plan(): pl.pallas_call(functools.partial(project_kernel, shifts), in_specs=[vmem]...  1.57 us
    pallas_call x1, Pallas kernels, exchange_plan(): pl.pallas_call(loaded_kernel, in_specs=[smem, smem, smem] + [vmem] * (PAI...  1.35 us
  transfers between devices with their start and end apart: 17, of which 11 were waited for; matrix products, arithmetic and copies ran while one was open for 1% of the time, Pallas kernels for 4%

profile of v7, /device:TPU:0, one launch (start us, length us, event | category | flops | bytes accessed | tf_op | source)
XLA Modules:
  0.0 67.4 jit_solution(8328194490237309144)
XLA Ops:
  0.7 3.0 %norm_rows.1 = (bf16[1072,128]{1,0:T(8,128)(2,1)}, bf16[1072,128]{1,0:T(8,128)(2,1)}, bf16[1072,128]{1,0:T(8,128)(2,1)}, bf16[1072,128]{1,0:T(8,128)(2,1)}, bf16[1072,128]{1,0:T(8,128)(2,1)}) custom-call(bf16[2,2048]{1,0:T(2,128)(2,1)} %query_any.1, bf16[128,8192]{1,0:T(8,128)(2,1)} %hidden_any.1, bf16[2,8192]{1,0:T(2,128)(2,1)} %suffix_any.1, f32[1,8192]{1,0:T(1,128)} %bitcast.7), custom_call_target="tpu_custom_call" | custom-call | flops 2097152 | bytes 2097152 | tf_op jit(solution)/shard_map/norm_rows/pallas_call | solution.py:559
  3.7 4.1 %collective-permute-start = (bf16[1072,128]{1,0:T(8,128)(2,1)}, bf16[1072,128]{1,0:T(8,128)(2,1)S(1)}, u32[]{:S(2)}, u32[]{:S(2)}) collective-permute-start(bf16[1072,128]{1,0:T(8,128)(2,1)} %get-tuple-element.35), channel_id=1, source_target_pairs={{0,8},{1,9},{2,10},{3,11},{4,12},{5,13},{6,14},{7,15},{8,0},{9,1},... | collective-permute-start | bytes 823304 | tf_op jit(solution)/shard_map/ppermute | solution.py:540
  7.8 1.5 %collective-permute-start.1 = (bf16[1024,256]{1,0:T(8,128)(2,1)S(1)}, bf16[1024,256]{1,0:T(8,128)(2,1)S(1)}, u32[]{:S(2)}, u32[]{:S(2)}) collective-permute-start(bf16[1024,256]{1,0:T(8,128)(2,1)S(1)} %copy-done), channel_id=1, source_target_pairs={{0,2},{1,3},{2,0},{3,1},{4,6},{5,7},{6,4},{7,5},{8,10},{9,11},{10,... | collective-permute-start | bytes 1572872 | tf_op jit(solution)/shard_map/ppermute | solution.py:540
  9.8 1.6 %collective-permute-start.8 = (bf16[1072,128]{1,0:T(8,128)(2,1)}, bf16[1072,128]{1,0:T(8,128)(2,1)S(1)}, u32[]{:S(2)}, u32[]{:S(2)}) collective-permute-start(bf16[1072,128]{1,0:T(8,128)(2,1)} %get-tuple-element.48), channel_id=1, source_target_pairs={{0,4},{1,5},{2,6},{3,7},{4,0},{5,1},{6,2},{7,3},{8,12},{9,13},{10,... | collective-permute-start | bytes 823304 | tf_op jit(solution)/shard_map/ppermute | solution.py:540
  11.8 0.9 %copy-done.2 = bf16[1072,128]{1,0:T(8,128)(2,1)S(1)} copy-done((bf16[1072,128]{1,0:T(8,128)(2,1)S(1)}, bf16[1072,128]{1,0:T(8,128)(2,1)}, u32[]{:S(2)}) %copy-start.2) | copy-done | bytes 274456
  12.9 9.3 %collective-permute-done.refs_2_ = bf16[1072,128]{1,0:T(8,128)(2,1)S(1)} collective-permute-done((bf16[1072,128]{1,0:T(8,128)(2,1)}, bf16[1072,128]{1,0:T(8,128)(2,1)S(1)}, u32[]{:S(2)}, u32[]{:S(2)}) %collective-permute-start) | collective-permute-done | bytes 274464 | tf_op jit(solution)/shard_map/ppermute | solution.py:540
  22.7 5.4 %collective-permute-done.8.refs_2_ = bf16[1072,128]{1,0:T(8,128)(2,1)S(1)} collective-permute-done((bf16[1072,128]{1,0:T(8,128)(2,1)}, bf16[1072,128]{1,0:T(8,128)(2,1)S(1)}, u32[]{:S(2)}, u32[]{:S(2)}) %collective-permute-start.8) | collective-permute-done | bytes 274464 | tf_op jit(solution)/shard_map/ppermute | solution.py:540
  28.6 3.8 %collective-permute-done.4.refs_7_ = bf16[1024,256]{1,0:T(8,128)(2,1)S(1)} collective-permute-done((bf16[1024,256]{1,0:T(8,128)(2,1)S(1)}, bf16[1024,256]{1,0:T(8,128)(2,1)S(1)}, u32[]{:S(2)}, u32[]{:S(2)}) %collective-permute-start.4) | collective-permute-done | bytes 524320 | tf_op jit(solution)/shard_map/ppermute | solution.py:540
  32.4 0.8 %project.2 = (bf16[784,128]{1,0:T(8,128)(2,1)S(1)}, bf16[784,128]{1,0:T(8,128)(2,1)S(1)}, bf16[128,128]{1,0:T(8,128)(2,1)S(1)}) custom-call(bf16[1072,128]{1,0:T(8,128)(2,1)S(1)} %fetch_own.1.refs_0_, bf16[1072,128]{1,0:T(8,128)(2,1)S(1)} %collective-permute-done.2.refs_1_, bf16[1072,128]{1,0:T(8,128)(2,1)S(1)} %collective-permute-done.refs_2_, ...), custom_call_target="tpu_custom_call" | custom-call | flops 536870912 | bytes 6291456 | tf_op jit(solution)/shard_map/project/pallas_call | solution.py:623
  33.2 2.6 %collective-permute-start.5 = (bf16[784,128]{1,0:T(8,128)(2,1)S(1)}, bf16[784,128]{1,0:T(8,128)(2,1)S(1)}, u32[]{:S(2)}, u32[]{:S(2)}) collective-permute-start(bf16[784,128]{1,0:T(8,128)(2,1)S(1)} %get-tuple-element.46), channel_id=1, source_target_pairs={{0,8},{1,9},{2,10},{3,11},{4,12},{5,13},{6,14},{7,15},{8,0},{9,1},... | collective-permute-start | bytes 602120 | tf_op jit(solution)/shard_map/ppermute | solution.py:540
  36.6 1.5 %collective-permute-start.10 = (bf16[784,128]{1,0:T(8,128)(2,1)S(1)}, bf16[784,128]{1,0:T(8,128)(2,1)S(1)}, u32[]{:S(2)}, u32[]{:S(2)}) collective-permute-start(bf16[784,128]{1,0:T(8,128)(2,1)S(1)} %get-tuple-element.50), channel_id=1, source_target_pairs={{0,12},{1,13},{2,14},{3,15},{4,8},{5,9},{6,10},{7,11},{8,4},{9,5},... | collective-permute-start | bytes 602120 | tf_op jit(solution)/shard_map/ppermute | solution.py:540
  38.1 1.5 %collective-permute-start.12 = (bf16[128,128]{1,0:T(8,128)(2,1)S(1)}, bf16[128,128]{1,0:T(8,128)(2,1)S(1)}, u32[]{:S(2)}, u32[]{:S(2)}) collective-permute-start(bf16[128,128]{1,0:T(8,128)(2,1)S(1)} %get-tuple-element.54.refs_0_), channel_id=1, source_target_pairs={{0,2},{1,3},{2,0},{3,1},{4,6},{5,7},{6,4},{7,5},{8,10},{9,11},{10,... | collective-permute-start | bytes 98312 | tf_op jit(solution)/shard_map/ppermute | solution.py:540
  40.3 1.7 %collective-permute-done.12.refs_1_ = bf16[128,128]{1,0:T(8,128)(2,1)S(1)} collective-permute-done((bf16[128,128]{1,0:T(8,128)(2,1)S(1)}, bf16[128,128]{1,0:T(8,128)(2,1)S(1)}, u32[]{:S(2)}, u32[]{:S(2)}) %collective-permute-start.12) | collective-permute-done | bytes 32800 | tf_op jit(solution)/shard_map/ppermute | solution.py:540
  42.0 1.4 %loaded_attention.1 = (f32[256,128]{1,0:T(8,128)S(1)}, f32[256,128]{1,0:T(8,128)S(1)}, f32[256,128]{1,0:T(8,128)S(1)}, bf16[256,128]{1,0:T(8,128)(2,1)S(1)}) custom-call(s32[2]{0:T(128)S(1)} %pad_add_fusion.place_ref, s32[16]{0:T(128)S(1)} %copy-done.7, s32[1]{0:T(128)S(6)} %copy.15.split_ref, bf16[128,128]{1,0:T(8,128)(2,1)S(1)} %get-tuple-element.54.refs_0_, ...), custom_call_target="tpu_custom_call" | custom-call | flops 67108864 | bytes 524288 | tf_op jit(solution)/shard_map/loaded_attention/pallas_call | solution.py:663
  43.4 7.0 %collective-permute-done.5.other = bf16[784,128]{1,0:T(8,128)(2,1)S(1)} collective-permute-done((bf16[784,128]{1,0:T(8,128)(2,1)S(1)}, bf16[784,128]{1,0:T(8,128)(2,1)S(1)}, u32[]{:S(2)}, u32[]{:S(2)}) %collective-permute-start.5) | collective-permute-done | bytes 200736 | tf_op jit(solution)/shard_map/ppermute | solution.py:540
  50.4 1.8 %collective-permute-done.11.refs_1_ = bf16[784,128]{1,0:T(8,128)(2,1)S(1)} collective-permute-done((bf16[784,128]{1,0:T(8,128)(2,1)S(1)}, bf16[784,128]{1,0:T(8,128)(2,1)S(1)}, u32[]{:S(2)}, u32[]{:S(2)}) %collective-permute-start.11) | collective-permute-done | bytes 200736 | tf_op jit(solution)/shard_map/ppermute | solution.py:540
  52.3 2.1 %front_attention.1 = (bf16[128,256]{1,0:T(8,128)(2,1)}, bf16[128,256]{1,0:T(8,128)(2,1)}, f32[128,128]{1,0:T(8,128)S(1)}, bf16[128,128]{1,0:T(8,128)(2,1)S(1)}, ...) custom-call(s32[2]{0:T(128)S(1)} %pad_add_fusion.place_ref, s32[1]{0:T(128)S(6)} %copy.15.split_ref, ...), custom_call_target="tpu_custom_call" | custom-call | flops 16777216 | bytes 2097152 | tf_op jit(solution)/shard_map/front_attention/pallas_call | solution.py:682
  55.0 3.6 %collective-permute-start.14 = (bf16[128,128]{1,0:T(8,128)(2,1)S(1)}, bf16[128,128]{1,0:T(8,128)(2,1)S(1)}, u32[]{:S(2)}, u32[]{:S(2)}) collective-permute-start(bf16[128,128]{1,0:T(8,128)(2,1)S(1)} %get-tuple-element.63), channel_id=1, source_target_pairs={{0,8},{1,9},{2,10},{3,11},{4,12},{5,13},{6,14},{7,15},{8,0},{9,1},... | collective-permute-start | bytes 98312 | tf_op jit(solution)/shard_map/ppermute | solution.py:540
  58.9 1.5 %collective-permute-done.13.refs_0_ = bf16[128,128]{1,0:T(8,128)(2,1)S(1)} collective-permute-done((bf16[128,128]{1,0:T(8,128)(2,1)S(1)}, bf16[128,128]{1,0:T(8,128)(2,1)S(1)}, u32[]{:S(2)}, u32[]{:S(2)}) %collective-permute-start.13) | collective-permute-done | bytes 32800 | tf_op jit(solution)/shard_map/ppermute | solution.py:540
  60.4 0.8 %collective-permute-done.14.refs_1_ = bf16[128,128]{1,0:T(8,128)(2,1)S(1)} collective-permute-done((bf16[128,128]{1,0:T(8,128)(2,1)S(1)}, bf16[128,128]{1,0:T(8,128)(2,1)S(1)}, u32[]{:S(2)}, u32[]{:S(2)}) %collective-permute-start.14) | collective-permute-done | bytes 32800 | tf_op jit(solution)/shard_map/ppermute | solution.py:540
  61.2 1.3 %collective-permute-done.15.refs_2_ = bf16[128,128]{1,0:T(8,128)(2,1)S(1)} collective-permute-done((bf16[128,128]{1,0:T(8,128)(2,1)S(1)}, bf16[128,128]{1,0:T(8,128)(2,1)S(1)}, u32[]{:S(2)}, u32[]{:S(2)}) %collective-permute-start.15) | collective-permute-done | bytes 32800 | tf_op jit(solution)/shard_map/ppermute | solution.py:540
  62.8 1.6 %collective-permute-start.16 = (bf16[64,128]{1,0:T(8,128)(2,1)S(1)}, bf16[64,128]{1,0:T(8,128)(2,1)S(1)}, u32[]{:S(2)}, u32[]{:S(2)}) collective-permute-start(bf16[64,128]{1,0:T(8,128)(2,1)S(1)} %get-tuple-element.66), channel_id=1, source_target_pairs={{0,2},{1,3},{2,0},{3,1},{4,6},{5,7},{6,4},{7,5},{8,10},{9,11},{10,... | collective-permute-start | bytes 49160 | tf_op jit(solution)/shard_map/ppermute | solution.py:540
  64.3 2.2 %collective-permute-done.16.refs_0_ = bf16[64,128]{1,0:T(8,128)(2,1)S(1)} collective-permute-done((bf16[64,128]{1,0:T(8,128)(2,1)S(1)}, bf16[64,128]{1,0:T(8,128)(2,1)S(1)}, u32[]{:S(2)}, u32[]{:S(2)}) %collective-permute-start.16) | collective-permute-done | bytes 16416 | tf_op jit(solution)/shard_map/ppermute | solution.py:540
  66.6 0.8 %finish.1 = bf16[2,2048]{1,0:T(2,128)(2,1)} custom-call(f32[64,128]{1,0:T(8,128)S(1)} %get-tuple-element.65.kept, bf16[64,128]{1,0:T(8,128)(2,1)S(1)} %collective-permute-done.16.refs_0_), custom_call_target="tpu_custom_call" | custom-call | tf_op jit(solution)/shard_map/finish/pallas_call | solution.py:713
  (40 shorter events, 4.1 us)
Async XLA Ops:
  0.6 7.1 %copy-start = (bf16[1024,256]{1,0:T(8,128)(2,1)S(1)}, bf16[1024,256]{1,0:T(8,128)(2,1)}, u32[]{:S(2)}) copy-start(bf16[1024,256]{1,0:T(8,128)(2,1)} %refs_4_.3) | copy-start | bytes 1572868
  0.6 8.6 %copy-start.1 = (bf16[1024,256]{1,0:T(8,128)(2,1)S(1)}, bf16[1024,256]{1,0:T(8,128)(2,1)}, u32[]{:S(2)}) copy-start(bf16[1024,256]{1,0:T(8,128)(2,1)} %refs_5_.3) | copy-start | bytes 1572868
  3.7 18.5 %collective-permute-start = (bf16[1072,128]{1,0:T(8,128)(2,1)}, bf16[1072,128]{1,0:T(8,128)(2,1)S(1)}, u32[]{:S(2)}, u32[]{:S(2)}) collective-permute-start(bf16[1072,128]{1,0:T(8,128)(2,1)} %get-tuple-element.35), channel_id=1, source_target_pairs={{0,8},{1,9},{2,10},{3,11},{4,12},{5,13},{6,14},{7,15},{8,0},{9,1},... | collective-permute-start | bytes 823304 | tf_op jit(solution)/shard_map/ppermute | solution.py:540
  7.8 14.8 %collective-permute-start.1 = (bf16[1024,256]{1,0:T(8,128)(2,1)S(1)}, bf16[1024,256]{1,0:T(8,128)(2,1)S(1)}, u32[]{:S(2)}, u32[]{:S(2)}) collective-permute-start(bf16[1024,256]{1,0:T(8,128)(2,1)S(1)} %copy-done), channel_id=1, source_target_pairs={{0,2},{1,3},{2,0},{3,1},{4,6},{5,7},{6,4},{7,5},{8,10},{9,11},{10,... | collective-permute-start | bytes 1572872 | tf_op jit(solution)/shard_map/ppermute | solution.py:540
  9.3 23.1 %collective-permute-start.4 = (bf16[1024,256]{1,0:T(8,128)(2,1)S(1)}, bf16[1024,256]{1,0:T(8,128)(2,1)S(1)}, u32[]{:S(2)}, u32[]{:S(2)}) collective-permute-start(bf16[1024,256]{1,0:T(8,128)(2,1)S(1)} %copy-done.1), channel_id=1, source_target_pairs={{0,2},{1,3},{2,0},{3,1},{4,6},{5,7},{6,4},{7,5},{8,10},{9,11},{10,... | collective-permute-start | bytes 1572872 | tf_op jit(solution)/shard_map/ppermute | solution.py:540
  9.8 18.3 %collective-permute-start.8 = (bf16[1072,128]{1,0:T(8,128)(2,1)}, bf16[1072,128]{1,0:T(8,128)(2,1)S(1)}, u32[]{:S(2)}, u32[]{:S(2)}) collective-permute-start(bf16[1072,128]{1,0:T(8,128)(2,1)} %get-tuple-element.48), channel_id=1, source_target_pairs={{0,4},{1,5},{2,6},{3,7},{4,0},{5,1},{6,2},{7,3},{8,12},{9,13},{10,... | collective-permute-start | bytes 823304 | tf_op jit(solution)/shard_map/ppermute | solution.py:540
  11.4 16.7 %collective-permute-start.6 = (bf16[1072,128]{1,0:T(8,128)(2,1)}, bf16[1072,128]{1,0:T(8,128)(2,1)S(1)}, u32[]{:S(2)}, u32[]{:S(2)}) collective-permute-start(bf16[1072,128]{1,0:T(8,128)(2,1)} %get-tuple-element.47), channel_id=1, source_target_pairs={{0,12},{1,13},{2,14},{3,15},{4,8},{5,9},{6,10},{7,11},{8,4},{9,5},... | collective-permute-start | bytes 823304 | tf_op jit(solution)/shard_map/ppermute | solution.py:540
  22.2 10.2 %collective-permute-start.3 = (bf16[1072,128]{1,0:T(8,128)(2,1)S(1)}, bf16[1072,128]{1,0:T(8,128)(2,1)S(1)}, u32[]{:S(2)}, u32[]{:S(2)}) collective-permute-start(bf16[1072,128]{1,0:T(8,128)(2,1)S(1)} %collective-permute-done.refs_2_), channel_id=1, source_target_pairs={{0,1},{1,0},{2,3},{3,2},{4,5},{5,4},{6,7},{7,6},{8,9},{9,8},{10,11... | collective-permute-start | bytes 823304 | tf_op jit(solution)/shard_map/ppermute | solution.py:540
  22.6 9.8 %collective-permute-start.2 = (bf16[1072,128]{1,0:T(8,128)(2,1)}, bf16[1072,128]{1,0:T(8,128)(2,1)S(1)}, u32[]{:S(2)}, u32[]{:S(2)}) collective-permute-start(bf16[1072,128]{1,0:T(8,128)(2,1)} %get-tuple-element.41), channel_id=1, source_target_pairs={{0,1},{1,0},{2,3},{3,2},{4,5},{5,4},{6,7},{7,6},{8,9},{9,8},{10,11... | collective-permute-start | bytes 823304 | tf_op jit(solution)/shard_map/ppermute | solution.py:540
  28.1 7.7 %collective-permute-start.9 = (bf16[1072,128]{1,0:T(8,128)(2,1)S(1)}, bf16[1072,128]{1,0:T(8,128)(2,1)S(1)}, u32[]{:S(2)}, u32[]{:S(2)}) collective-permute-start(bf16[1072,128]{1,0:T(8,128)(2,1)S(1)} %collective-permute-done.8.refs_2_), channel_id=1, source_target_pairs={{0,1},{1,0},{2,3},{3,2},{4,5},{5,4},{6,7},{7,6},{8,9},{9,8},{10,11... | collective-permute-start | bytes 823304 | tf_op jit(solution)/shard_map/ppermute | solution.py:540
  28.1 7.7 %collective-permute-start.7 = (bf16[1072,128]{1,0:T(8,128)(2,1)S(1)}, bf16[1072,128]{1,0:T(8,128)(2,1)S(1)}, u32[]{:S(2)}, u32[]{:S(2)}) collective-permute-start(bf16[1072,128]{1,0:T(8,128)(2,1)S(1)} %collective-permute-done.6.refs_0_), channel_id=1, source_target_pairs={{0,1},{1,0},{2,3},{3,2},{4,5},{5,4},{6,7},{7,6},{8,9},{9,8},{10,11... | collective-permute-start | bytes 823304 | tf_op jit(solution)/shard_map/ppermute | solution.py:540
  33.2 8.8 %copy-start.3 = (bf16[4,128,256]{2,1,0:T(8,128)(2,1)S(1)}, bf16[4,128,256]{2,1,0:T(8,128)(2,1)}, u32[]{:S(2)}) copy-start(bf16[4,128,256]{2,1,0:T(8,128)(2,1)} %refs_2_.1) | copy-start | bytes 786436
  33.2 8.8 %copy-start.4 = (bf16[4,128,256]{2,1,0:T(8,128)(2,1)S(1)}, bf16[4,128,256]{2,1,0:T(8,128)(2,1)}, u32[]{:S(2)}) copy-start(bf16[4,128,256]{2,1,0:T(8,128)(2,1)} %refs_3_.1) | copy-start | bytes 786436
  33.2 8.8 %copy-start.7 = (s32[16]{0:T(128)S(1)}, s32[16]{0:T(128)}, u32[]{:S(2)}) copy-start(s32[16]{0:T(128)} %table_ref.1) | copy-start | bytes 196
  33.2 17.2 %collective-permute-start.5 = (bf16[784,128]{1,0:T(8,128)(2,1)S(1)}, bf16[784,128]{1,0:T(8,128)(2,1)S(1)}, u32[]{:S(2)}, u32[]{:S(2)}) collective-permute-start(bf16[784,128]{1,0:T(8,128)(2,1)S(1)} %get-tuple-element.46), channel_id=1, source_target_pairs={{0,8},{1,9},{2,10},{3,11},{4,12},{5,13},{6,14},{7,15},{8,0},{9,1},... | collective-permute-start | bytes 602120 | tf_op jit(solution)/shard_map/ppermute | solution.py:540
  35.8 16.5 %copy-start.5 = (f32[256]{0:T(256)S(1)}, f32[256]{0:T(256)}, u32[]{:S(2)}) copy-start(f32[256]{0:T(256)} %param.17) | copy-start | bytes 3076
  35.8 16.5 %copy-start.6 = (f32[256]{0:T(256)S(1)}, f32[256]{0:T(256)}, u32[]{:S(2)}) copy-start(f32[256]{0:T(256)} %param.18) | copy-start | bytes 3076
  36.6 13.8 %collective-permute-start.10 = (bf16[784,128]{1,0:T(8,128)(2,1)S(1)}, bf16[784,128]{1,0:T(8,128)(2,1)S(1)}, u32[]{:S(2)}, u32[]{:S(2)}) collective-permute-start(bf16[784,128]{1,0:T(8,128)(2,1)S(1)} %get-tuple-element.50), channel_id=1, source_target_pairs={{0,12},{1,13},{2,14},{3,15},{4,8},{5,9},{6,10},{7,11},{8,4},{9,5},... | collective-permute-start | bytes 602120 | tf_op jit(solution)/shard_map/ppermute | solution.py:540
  38.1 14.2 %collective-permute-start.11 = (bf16[784,128]{1,0:T(8,128)(2,1)S(1)}, bf16[784,128]{1,0:T(8,128)(2,1)S(1)}, u32[]{:S(2)}, u32[]{:S(2)}) collective-permute-start(bf16[784,128]{1,0:T(8,128)(2,1)S(1)} %get-tuple-element.51), channel_id=1, source_target_pairs={{0,4},{1,5},{2,6},{3,7},{4,0},{5,1},{6,2},{7,3},{8,12},{9,13},{10,... | collective-permute-start | bytes 602120 | tf_op jit(solution)/shard_map/ppermute | solution.py:540
  38.1 3.9 %collective-permute-start.12 = (bf16[128,128]{1,0:T(8,128)(2,1)S(1)}, bf16[128,128]{1,0:T(8,128)(2,1)S(1)}, u32[]{:S(2)}, u32[]{:S(2)}) collective-permute-start(bf16[128,128]{1,0:T(8,128)(2,1)S(1)} %get-tuple-element.54.refs_0_), channel_id=1, source_target_pairs={{0,2},{1,3},{2,0},{3,1},{4,6},{5,7},{6,4},{7,5},{8,10},{9,11},{10,... | collective-permute-start | bytes 98312 | tf_op jit(solution)/shard_map/ppermute | solution.py:540
  54.4 6.0 %collective-permute-start.13 = (bf16[128,128]{1,0:T(8,128)(2,1)S(1)}, bf16[128,128]{1,0:T(8,128)(2,1)S(1)}, u32[]{:S(2)}, u32[]{:S(2)}) collective-permute-start(bf16[128,128]{1,0:T(8,128)(2,1)S(1)} %get-tuple-element.62), channel_id=1, source_target_pairs={{0,12},{1,13},{2,14},{3,15},{4,8},{5,9},{6,10},{7,11},{8,4},{9,5},... | collective-permute-start | bytes 98312 | tf_op jit(solution)/shard_map/ppermute | solution.py:540
  55.0 6.2 %collective-permute-start.14 = (bf16[128,128]{1,0:T(8,128)(2,1)S(1)}, bf16[128,128]{1,0:T(8,128)(2,1)S(1)}, u32[]{:S(2)}, u32[]{:S(2)}) collective-permute-start(bf16[128,128]{1,0:T(8,128)(2,1)S(1)} %get-tuple-element.63), channel_id=1, source_target_pairs={{0,8},{1,9},{2,10},{3,11},{4,12},{5,13},{6,14},{7,15},{8,0},{9,1},... | collective-permute-start | bytes 98312 | tf_op jit(solution)/shard_map/ppermute | solution.py:540
  58.6 3.9 %collective-permute-start.15 = (bf16[128,128]{1,0:T(8,128)(2,1)S(1)}, bf16[128,128]{1,0:T(8,128)(2,1)S(1)}, u32[]{:S(2)}, u32[]{:S(2)}) collective-permute-start(bf16[128,128]{1,0:T(8,128)(2,1)S(1)} %get-tuple-element.64), channel_id=1, source_target_pairs={{0,4},{1,5},{2,6},{3,7},{4,0},{5,1},{6,2},{7,3},{8,12},{9,13},{10,... | collective-permute-start | bytes 98312 | tf_op jit(solution)/shard_map/ppermute | solution.py:540
  62.8 3.8 %collective-permute-start.16 = (bf16[64,128]{1,0:T(8,128)(2,1)S(1)}, bf16[64,128]{1,0:T(8,128)(2,1)S(1)}, u32[]{:S(2)}, u32[]{:S(2)}) collective-permute-start(bf16[64,128]{1,0:T(8,128)(2,1)S(1)} %get-tuple-element.66), channel_id=1, source_target_pairs={{0,2},{1,3},{2,0},{3,1},{4,6},{5,7},{6,4},{7,5},{8,10},{9,11},{10,... | collective-permute-start | bytes 49160 | tf_op jit(solution)/shard_map/ppermute | solution.py:540
  (1 other events, 1.0 us)

commit v8 on v7

--- a/solution.py
+++ b/solution.py
@@ -161,10 +161,11 @@
     return sorted(range(1, GROUPS), key=lambda s: s < GROUPS // 2)
 
 
-def norm_kernel(query_any, hidden_any, suffix_any, gain_any, *rest):
-    blocks_any, own_any = rest[:GROUPS], rest[GROUPS]
-    hidden_ref, suffix_ref, gain_ref, query_ref, tail_ref = rest[GROUPS + 1 : GROUPS + 6]
-    outs, (sems, out_sems) = rest[GROUPS + 6 : -2], rest[-2:]
+def norm_kernel(shifts, query_any, hidden_any, suffix_any, gain_any, *rest):
+    count = len(shifts)
+    blocks_any, rest = rest[:count], rest[count:]
+    (hidden_ref, suffix_ref, gain_ref, query_ref, tail_ref), rest = rest[:5], rest[5:]
+    outs, (sems, out_sems) = rest[:count], rest[count:]
     core, ctx = lax.axis_index("tp"), lax.axis_index("ctx")
     z, x = ctx // PAIR, ctx % PAIR
     half_rows, features = hidden_ref.shape
@@ -206,20 +207,20 @@
     both = suffix_ref[...].astype(jnp.float32)
     normed = both * row_scale(both) * gain_ref[...]
     tail_ref[...] = jnp.where(core == 0, normed[0:1], normed[1:2])
-    for shift in range(GROUPS):
+    for shift, out in zip(shifts, outs):
         ends = [
             tail_ref[:, pl.ds(offset(shift, side, j), LANES)]
             for side in range(PAIR)
             for j in range(per_block)
         ]
         start = pieces * half_rows
-        outs[shift][start : start + pieces, :] = jnp.concatenate(ends, 0).astype(jnp.bfloat16)
+        out[start : start + pieces, :] = jnp.concatenate(ends, 0).astype(jnp.bfloat16)
     inverses = []
     for i in range(CHUNKS):
         copies[3 + i].wait()
         inverses.append(row_scale(hidden_ref[i * rows : (i + 1) * rows, :].astype(jnp.float32)))
     leaving = []
-    for shift in far_first() + [0]:
+    for place, (shift, out) in enumerate(zip(shifts, outs)):
         for side in range(PAIR):
             for j in range(per_block):
                 columns = pl.ds(offset(shift, side, j), LANES)
@@ -227,11 +228,9 @@
                     piece = hidden_ref[i * rows : (i + 1) * rows, columns].astype(jnp.float32)
                     piece = piece * inverses[i] * gain_ref[:, columns]
                     start = (side * per_block + j) * half_rows + i * rows
-                    outs[shift][start : start + rows, :] = piece.astype(jnp.bfloat16)
-        leaving.append(pltpu.make_async_copy(outs[shift], blocks_any[shift], out_sems.at[shift]))
+                    out[start : start + rows, :] = piece.astype(jnp.bfloat16)
+        leaving.append(pltpu.make_async_copy(out, blocks_any[place], out_sems.at[place]))
         leaving[-1].start()
-    leaving.append(pltpu.make_async_copy(outs[0], own_any, out_sems.at[GROUPS]))
-    leaving[-1].start()
     for copy in leaving:
         copy.wait()
 
@@ -556,35 +555,33 @@
     own_queries = suffix_query_rows.shape[0]
     lines = query_width // LANES
     block_rows = pieces * half_rows + pieces + own_queries * lines
-    *blocks, own = pl.pallas_call(
-        norm_kernel,
-        in_specs=[hbm] * 4,
-        out_specs=[hbm] * (GROUPS + 1),
-        out_shape=[jax.ShapeDtypeStruct((block_rows, LANES), jnp.bfloat16)] * (GROUPS + 1),
-        scratch_shapes=[
-            pltpu.VMEM((half_rows, features), jnp.bfloat16),
-            pltpu.VMEM(suffix_hidden.shape, jnp.bfloat16),
-            pltpu.VMEM((1, features), jnp.float32),
-            pltpu.VMEM(suffix_query_rows.shape, jnp.bfloat16),
-            pltpu.VMEM((1, features), jnp.float32),
-        ]
-        + [pltpu.VMEM((block_rows, LANES), jnp.bfloat16)] * GROUPS
-        + [
-            pltpu.SemaphoreType.DMA((CHUNKS + 3,)),
-            pltpu.SemaphoreType.DMA((GROUPS + 1,)),
-        ],
-        compiler_params=pltpu.CompilerParams(vmem_limit_bytes=60 * 1024 * 1024),
-        cost_estimate=pl.CostEstimate(
-            flops=4 * half_rows * features, bytes_accessed=4 * half_rows * features, transcendentals=0
-        ),
-        name="norm_rows",
-    )(
-        suffix_query_rows,
-        hidden,
-        suffix_hidden,
-        norm_gain.reshape(1, features),
-    )
-    *weights, blocks[1] = lax.optimization_barrier((key_matrix, value_matrix, blocks[1]))
+    blocks = {}
+    for shifts in (tuple(far_first()[:1]), tuple(far_first()[1:]) + (0,)):
+        found = pl.pallas_call(
+            functools.partial(norm_kernel, shifts),
+            in_specs=[hbm] * 4,
+            out_specs=[hbm] * len(shifts),
+            out_shape=[jax.ShapeDtypeStruct((block_rows, LANES), jnp.bfloat16)] * len(shifts),
+            scratch_shapes=[
+                pltpu.VMEM((half_rows, features), jnp.bfloat16),
+                pltpu.VMEM(suffix_hidden.shape, jnp.bfloat16),
+                pltpu.VMEM((1, features), jnp.float32),
+                pltpu.VMEM(suffix_query_rows.shape, jnp.bfloat16),
+                pltpu.VMEM((1, features), jnp.float32),
+            ]
+            + [pltpu.VMEM((block_rows, LANES), jnp.bfloat16)] * len(shifts)
+            + [pltpu.SemaphoreType.DMA((CHUNKS + 3,)), pltpu.SemaphoreType.DMA((len(shifts),))],
+            compiler_params=pltpu.CompilerParams(vmem_limit_bytes=60 * 1024 * 1024),
+            cost_estimate=pl.CostEstimate(
+                flops=4 * half_rows * features,
+                bytes_accessed=4 * half_rows * features,
+                transcendentals=0,
+            ),
+            name="norm_rows",
+        )(suffix_query_rows, hidden, suffix_hidden, norm_gain.reshape(1, features))
+        blocks.update(zip(shifts, found))
+    own = blocks[0]
+    *weights, blocks[2] = lax.optimization_barrier((key_matrix, value_matrix, blocks[2]))
     far = [move(matrix, beside) for matrix in weights]
 
     mine = {s: move(blocks[s], along(s)) for s in far_first()}

time: 67.6 us -> 67.4 us (level)
  Pallas kernels: 9.15 us -> 12.3 us
  waiting for transfers between devices: 35.4 us -> 32.5 us
  local copies, waits for them, and re-layouts: 0.99 us -> 0.04 us
    ppermute x17, waiting for transfers between devices: 35.4 us -> 32.5 us  [move(): return lax.ppermute(array, ('ctx', 'tp'), pairs)]
    pallas_call x1 -> x2, Pallas kernels: 2.99 us -> 5.22 us  [exchange_plan(): pl.pallas_call(functools.partial(norm_kernel, shifts), in_specs=[hbm] * 4...]
    unnamed x16 -> x14, local copies, waits for them, and re-layouts: 0.99 us -> 0.04 us
    pallas_call x1, Pallas kernels: 0.04 us -> 0.96 us  [exchange_plan(): pl.pallas_call(fetch_kernel, in_specs=[hbm], out_specs=vmem, out_shape=ja...]
  transfers between devices with their start and end apart: 17 -> 17, of which waited for: 11 -> 10; matrix products, arithmetic and copies ran while one was open for 1% -> 1% of each run, Pallas kernels for 4% -> 10%
where the time goes in v8:
time: 67.4 us; the launch traced here: 67.2 us
  waiting for transfers between devices  32.5 us (48%)
  starting transfers between devices  20.3 us (30%)
  Pallas kernels  12.3 us (18%)
  between operations  1.44 us (2%)
    ppermute x17, waiting for transfers between devices, move(): return lax.ppermute(array, ('ctx', 'tp'), pairs)  32.5 us
    ppermute x17, starting transfers between devices, move(): return lax.ppermute(array, ('ctx', 'tp'), pairs)  20.3 us
    pallas_call x2, Pallas kernels, exchange_plan(): pl.pallas_call(functools.partial(norm_kernel, shifts), in_specs=[hbm] * 4...  5.22 us
    pallas_call x1, Pallas kernels, exchange_plan(): pl.pallas_call(front_kernel, in_specs=[smem, smem] + [vmem] * (GROUPS + 7...  2.1 us
    pallas_call x2, Pallas kernels, exchange_plan(): pl.pallas_call(functools.partial(project_kernel, shifts), in_specs=[vmem]...  1.57 us
    pallas_call x1, Pallas kernels, exchange_plan(): pl.pallas_call(loaded_kernel, in_specs=[smem, smem, smem] + [vmem] * (PAI...  1.35 us
  transfers between devices with their start and end apart: 17, of which 10 were waited for; matrix products, arithmetic and copies ran while one was open for 1% of the time, Pallas kernels for 10%

profile of v8, /device:TPU:0, one launch (start us, length us, event | category | flops | bytes accessed | tf_op | source)
XLA Modules:
  0.0 67.2 jit_solution(13767946964139510077)
XLA Ops:
  0.7 2.5 %norm_rows.2 = bf16[1072,128]{1,0:T(8,128)(2,1)} custom-call(bf16[2,2048]{1,0:T(2,128)(2,1)} %query_any.3, bf16[128,8192]{1,0:T(8,128)(2,1)} %hidden_any.3, bf16[2,8192]{1,0:T(2,128)(2,1)} %suffix_any.3, f32[1,8192]{1,0:T(1,128)} %bitcast.7), custom_call_target="tpu_custom_call" | custom-call | flops 2097152 | bytes 2097152 | tf_op jit(solution)/shard_map/norm_rows/pallas_call | solution.py:560
  3.2 4.1 %collective-permute-start = (bf16[1072,128]{1,0:T(8,128)(2,1)}, bf16[1072,128]{1,0:T(8,128)(2,1)S(1)}, u32[]{:S(2)}, u32[]{:S(2)}) collective-permute-start(bf16[1072,128]{1,0:T(8,128)(2,1)} %norm_rows.2), channel_id=1, source_target_pairs={{0,8},{1,9},{2,10},{3,11},{4,12},{5,13},{6,14},{7,15},{8,0},{9,1},... | collective-permute-start | bytes 823304 | tf_op jit(solution)/shard_map/ppermute | solution.py:539
  7.3 1.5 %collective-permute-start.1 = (bf16[1024,256]{1,0:T(8,128)(2,1)S(1)}, bf16[1024,256]{1,0:T(8,128)(2,1)S(1)}, u32[]{:S(2)}, u32[]{:S(2)}) collective-permute-start(bf16[1024,256]{1,0:T(8,128)(2,1)S(1)} %copy-done), channel_id=1, source_target_pairs={{0,2},{1,3},{2,0},{3,1},{4,6},{5,7},{6,4},{7,5},{8,10},{9,11},{10,... | collective-permute-start | bytes 1572872 | tf_op jit(solution)/shard_map/ppermute | solution.py:539
  9.3 2.7 %norm_rows.3 = (bf16[1072,128]{1,0:T(8,128)(2,1)}, bf16[1072,128]{1,0:T(8,128)(2,1)}, bf16[1072,128]{1,0:T(8,128)(2,1)}) custom-call(bf16[2,2048]{1,0:T(2,128)(2,1)} %query_any.3, bf16[128,8192]{1,0:T(8,128)(2,1)} %hidden_any.3, bf16[2,8192]{1,0:T(2,128)(2,1)} %suffix_any.3, f32[1,8192]{1,0:T(1,128)} %bitcast.8), custom_call_target="tpu_custom_call" | custom-call | flops 2097152 | bytes 2097152 | tf_op jit(solution)/shard_map/norm_rows/pallas_call | solution.py:560
  12.0 1.4 %collective-permute-start.6 = (bf16[1072,128]{1,0:T(8,128)(2,1)}, bf16[1072,128]{1,0:T(8,128)(2,1)S(1)}, u32[]{:S(2)}, u32[]{:S(2)}) collective-permute-start(bf16[1072,128]{1,0:T(8,128)(2,1)} %get-tuple-element.43), channel_id=1, source_target_pairs={{0,12},{1,13},{2,14},{3,15},{4,8},{5,9},{6,10},{7,11},{8,4},{9,5},... | collective-permute-start | bytes 823304 | tf_op jit(solution)/shard_map/ppermute | solution.py:539
  14.1 1.0 %fetch_own.1.refs_0_ = bf16[1072,128]{1,0:T(8,128)(2,1)S(1)} custom-call(bf16[1072,128]{1,0:T(8,128)(2,1)} %get-tuple-element.37.from_any), custom_call_target="tpu_custom_call" | custom-call | bytes 67108864 | tf_op jit(solution)/shard_map/fetch_own/pallas_call | solution.py:601
  15.2 11.5 %collective-permute-done.refs_2_ = bf16[1072,128]{1,0:T(8,128)(2,1)S(1)} collective-permute-done((bf16[1072,128]{1,0:T(8,128)(2,1)}, bf16[1072,128]{1,0:T(8,128)(2,1)S(1)}, u32[]{:S(2)}, u32[]{:S(2)}) %collective-permute-start) | collective-permute-done | bytes 274464 | tf_op jit(solution)/shard_map/ppermute | solution.py:539
  27.3 4.2 %collective-permute-done.8.refs_2_ = bf16[1072,128]{1,0:T(8,128)(2,1)S(1)} collective-permute-done((bf16[1072,128]{1,0:T(8,128)(2,1)}, bf16[1072,128]{1,0:T(8,128)(2,1)S(1)}, u32[]{:S(2)}, u32[]{:S(2)}) %collective-permute-start.8) | collective-permute-done | bytes 274464 | tf_op jit(solution)/shard_map/ppermute | solution.py:539
  31.9 0.8 %project.2 = (bf16[784,128]{1,0:T(8,128)(2,1)S(1)}, bf16[784,128]{1,0:T(8,128)(2,1)S(1)}, bf16[128,128]{1,0:T(8,128)(2,1)S(1)}) custom-call(bf16[1072,128]{1,0:T(8,128)(2,1)S(1)} %fetch_own.1.refs_0_, bf16[1072,128]{1,0:T(8,128)(2,1)S(1)} %collective-permute-done.2.refs_1_, bf16[1072,128]{1,0:T(8,128)(2,1)S(1)} %collective-permute-done.refs_2_, ...), custom_call_target="tpu_custom_call" | custom-call | flops 536870912 | bytes 6291456 | tf_op jit(solution)/shard_map/project/pallas_call | solution.py:620
  32.8 3.1 %collective-permute-start.5 = (bf16[784,128]{1,0:T(8,128)(2,1)S(1)}, bf16[784,128]{1,0:T(8,128)(2,1)S(1)}, u32[]{:S(2)}, u32[]{:S(2)}) collective-permute-start(bf16[784,128]{1,0:T(8,128)(2,1)S(1)} %get-tuple-element.42), channel_id=1, source_target_pairs={{0,8},{1,9},{2,10},{3,11},{4,12},{5,13},{6,14},{7,15},{8,0},{9,1},... | collective-permute-start | bytes 602120 | tf_op jit(solution)/shard_map/ppermute | solution.py:539
  36.6 1.0 %collective-permute-start.10 = (bf16[784,128]{1,0:T(8,128)(2,1)S(1)}, bf16[784,128]{1,0:T(8,128)(2,1)S(1)}, u32[]{:S(2)}, u32[]{:S(2)}) collective-permute-start(bf16[784,128]{1,0:T(8,128)(2,1)S(1)} %get-tuple-element.46), channel_id=1, source_target_pairs={{0,12},{1,13},{2,14},{3,15},{4,8},{5,9},{6,10},{7,11},{8,4},{9,5},... | collective-permute-start | bytes 602120 | tf_op jit(solution)/shard_map/ppermute | solution.py:539
  37.8 1.5 %collective-permute-start.12 = (bf16[128,128]{1,0:T(8,128)(2,1)S(1)}, bf16[128,128]{1,0:T(8,128)(2,1)S(1)}, u32[]{:S(2)}, u32[]{:S(2)}) collective-permute-start(bf16[128,128]{1,0:T(8,128)(2,1)S(1)} %get-tuple-element.50.refs_0_), channel_id=1, source_target_pairs={{0,2},{1,3},{2,0},{3,1},{4,6},{5,7},{6,4},{7,5},{8,10},{9,11},{10,... | collective-permute-start | bytes 98312 | tf_op jit(solution)/shard_map/ppermute | solution.py:539
  40.0 1.7 %collective-permute-done.12.refs_1_ = bf16[128,128]{1,0:T(8,128)(2,1)S(1)} collective-permute-done((bf16[128,128]{1,0:T(8,128)(2,1)S(1)}, bf16[128,128]{1,0:T(8,128)(2,1)S(1)}, u32[]{:S(2)}, u32[]{:S(2)}) %collective-permute-start.12) | collective-permute-done | bytes 32800 | tf_op jit(solution)/shard_map/ppermute | solution.py:539
  41.7 1.4 %loaded_attention.1 = (f32[256,128]{1,0:T(8,128)S(1)}, f32[256,128]{1,0:T(8,128)S(1)}, f32[256,128]{1,0:T(8,128)S(1)}, bf16[256,128]{1,0:T(8,128)(2,1)S(1)}) custom-call(s32[2]{0:T(128)S(1)} %pad_add_fusion.place_ref, s32[16]{0:T(128)S(1)} %copy-done.6, s32[1]{0:T(128)S(6)} %copy.15.split_ref, bf16[128,128]{1,0:T(8,128)(2,1)S(1)} %get-tuple-element.50.refs_0_, ...), custom_call_target="tpu_custom_call" | custom-call | flops 67108864 | bytes 524288 | tf_op jit(solution)/shard_map/loaded_attention/pallas_call | solution.py:660
  43.0 7.1 %collective-permute-done.5.other = bf16[784,128]{1,0:T(8,128)(2,1)S(1)} collective-permute-done((bf16[784,128]{1,0:T(8,128)(2,1)S(1)}, bf16[784,128]{1,0:T(8,128)(2,1)S(1)}, u32[]{:S(2)}, u32[]{:S(2)}) %collective-permute-start.5) | collective-permute-done | bytes 200736 | tf_op jit(solution)/shard_map/ppermute | solution.py:539
  50.2 1.9 %collective-permute-done.11.refs_1_ = bf16[784,128]{1,0:T(8,128)(2,1)S(1)} collective-permute-done((bf16[784,128]{1,0:T(8,128)(2,1)S(1)}, bf16[784,128]{1,0:T(8,128)(2,1)S(1)}, u32[]{:S(2)}, u32[]{:S(2)}) %collective-permute-start.11) | collective-permute-done | bytes 200736 | tf_op jit(solution)/shard_map/ppermute | solution.py:539
  52.1 2.1 %front_attention.1 = (bf16[128,256]{1,0:T(8,128)(2,1)}, bf16[128,256]{1,0:T(8,128)(2,1)}, f32[128,128]{1,0:T(8,128)S(1)}, bf16[128,128]{1,0:T(8,128)(2,1)S(1)}, ...) custom-call(s32[2]{0:T(128)S(1)} %pad_add_fusion.place_ref, s32[1]{0:T(128)S(6)} %copy.15.split_ref, ...), custom_call_target="tpu_custom_call" | custom-call | flops 16777216 | bytes 2097152 | tf_op jit(solution)/shard_map/front_attention/pallas_call | solution.py:679
  54.2 2.9 %collective-permute-start.13 = (bf16[128,128]{1,0:T(8,128)(2,1)S(1)}, bf16[128,128]{1,0:T(8,128)(2,1)S(1)}, u32[]{:S(2)}, u32[]{:S(2)}) collective-permute-start(bf16[128,128]{1,0:T(8,128)(2,1)S(1)} %get-tuple-element.58), channel_id=1, source_target_pairs={{0,12},{1,13},{2,14},{3,15},{4,8},{5,9},{6,10},{7,11},{8,4},{9,5},... | collective-permute-start | bytes 98312 | tf_op jit(solution)/shard_map/ppermute | solution.py:539
  57.1 1.3 %collective-permute-start.14 = (bf16[128,128]{1,0:T(8,128)(2,1)S(1)}, bf16[128,128]{1,0:T(8,128)(2,1)S(1)}, u32[]{:S(2)}, u32[]{:S(2)}) collective-permute-start(bf16[128,128]{1,0:T(8,128)(2,1)S(1)} %get-tuple-element.59), channel_id=1, source_target_pairs={{0,8},{1,9},{2,10},{3,11},{4,12},{5,13},{6,14},{7,15},{8,0},{9,1},... | collective-permute-start | bytes 98312 | tf_op jit(solution)/shard_map/ppermute | solution.py:539
  58.9 1.1 %collective-permute-done.13.refs_0_ = bf16[128,128]{1,0:T(8,128)(2,1)S(1)} collective-permute-done((bf16[128,128]{1,0:T(8,128)(2,1)S(1)}, bf16[128,128]{1,0:T(8,128)(2,1)S(1)}, u32[]{:S(2)}, u32[]{:S(2)}) %collective-permute-start.13) | collective-permute-done | bytes 32800 | tf_op jit(solution)/shard_map/ppermute | solution.py:539
  60.0 2.0 %collective-permute-done.14.refs_1_ = bf16[128,128]{1,0:T(8,128)(2,1)S(1)} collective-permute-done((bf16[128,128]{1,0:T(8,128)(2,1)S(1)}, bf16[128,128]{1,0:T(8,128)(2,1)S(1)}, u32[]{:S(2)}, u32[]{:S(2)}) %collective-permute-start.14) | collective-permute-done | bytes 32800 | tf_op jit(solution)/shard_map/ppermute | solution.py:539
  62.5 1.5 %collective-permute-start.16 = (bf16[64,128]{1,0:T(8,128)(2,1)S(1)}, bf16[64,128]{1,0:T(8,128)(2,1)S(1)}, u32[]{:S(2)}, u32[]{:S(2)}) collective-permute-start(bf16[64,128]{1,0:T(8,128)(2,1)S(1)} %get-tuple-element.62), channel_id=1, source_target_pairs={{0,2},{1,3},{2,0},{3,1},{4,6},{5,7},{6,4},{7,5},{8,10},{9,11},{10,... | collective-permute-start | bytes 49160 | tf_op jit(solution)/shard_map/ppermute | solution.py:539
  64.1 2.2 %collective-permute-done.16.refs_0_ = bf16[64,128]{1,0:T(8,128)(2,1)S(1)} collective-permute-done((bf16[64,128]{1,0:T(8,128)(2,1)S(1)}, bf16[64,128]{1,0:T(8,128)(2,1)S(1)}, u32[]{:S(2)}, u32[]{:S(2)}) %collective-permute-start.16) | collective-permute-done | bytes 16416 | tf_op jit(solution)/shard_map/ppermute | solution.py:539
  66.3 0.8 %finish.1 = bf16[2,2048]{1,0:T(2,128)(2,1)} custom-call(f32[64,128]{1,0:T(8,128)S(1)} %get-tuple-element.61.kept, bf16[64,128]{1,0:T(8,128)(2,1)S(1)} %collective-permute-done.16.refs_0_), custom_call_target="tpu_custom_call" | custom-call | tf_op jit(solution)/shard_map/finish/pallas_call | solution.py:710
  (39 shorter events, 4.5 us)
Async XLA Ops:
  0.6 8.2 %copy-start.1 = (bf16[1024,256]{1,0:T(8,128)(2,1)S(1)}, bf16[1024,256]{1,0:T(8,128)(2,1)}, u32[]{:S(2)}) copy-start(bf16[1024,256]{1,0:T(8,128)(2,1)} %refs_5_.3) | copy-start | bytes 1572868
  0.6 6.7 %copy-start = (bf16[1024,256]{1,0:T(8,128)(2,1)S(1)}, bf16[1024,256]{1,0:T(8,128)(2,1)}, u32[]{:S(2)}) copy-start(bf16[1024,256]{1,0:T(8,128)(2,1)} %refs_4_.3) | copy-start | bytes 1572868
  3.2 23.5 %collective-permute-start = (bf16[1072,128]{1,0:T(8,128)(2,1)}, bf16[1072,128]{1,0:T(8,128)(2,1)S(1)}, u32[]{:S(2)}, u32[]{:S(2)}) collective-permute-start(bf16[1072,128]{1,0:T(8,128)(2,1)} %norm_rows.2), channel_id=1, source_target_pairs={{0,8},{1,9},{2,10},{3,11},{4,12},{5,13},{6,14},{7,15},{8,0},{9,1},... | collective-permute-start | bytes 823304 | tf_op jit(solution)/shard_map/ppermute | solution.py:539
  7.3 19.4 %collective-permute-start.1 = (bf16[1024,256]{1,0:T(8,128)(2,1)S(1)}, bf16[1024,256]{1,0:T(8,128)(2,1)S(1)}, u32[]{:S(2)}, u32[]{:S(2)}) collective-permute-start(bf16[1024,256]{1,0:T(8,128)(2,1)S(1)} %copy-done), channel_id=1, source_target_pairs={{0,2},{1,3},{2,0},{3,1},{4,6},{5,7},{6,4},{7,5},{8,10},{9,11},{10,... | collective-permute-start | bytes 1572872 | tf_op jit(solution)/shard_map/ppermute | solution.py:539
  8.8 23.1 %collective-permute-start.4 = (bf16[1024,256]{1,0:T(8,128)(2,1)S(1)}, bf16[1024,256]{1,0:T(8,128)(2,1)S(1)}, u32[]{:S(2)}, u32[]{:S(2)}) collective-permute-start(bf16[1024,256]{1,0:T(8,128)(2,1)S(1)} %copy-done.1), channel_id=1, source_target_pairs={{0,2},{1,3},{2,0},{3,1},{4,6},{5,7},{6,4},{7,5},{8,10},{9,11},{10,... | collective-permute-start | bytes 1572872 | tf_op jit(solution)/shard_map/ppermute | solution.py:539
  12.0 15.2 %collective-permute-start.6 = (bf16[1072,128]{1,0:T(8,128)(2,1)}, bf16[1072,128]{1,0:T(8,128)(2,1)S(1)}, u32[]{:S(2)}, u32[]{:S(2)}) collective-permute-start(bf16[1072,128]{1,0:T(8,128)(2,1)} %get-tuple-element.43), channel_id=1, source_target_pairs={{0,12},{1,13},{2,14},{3,15},{4,8},{5,9},{6,10},{7,11},{8,4},{9,5},... | collective-permute-start | bytes 823304 | tf_op jit(solution)/shard_map/ppermute | solution.py:539
  13.4 18.0 %collective-permute-start.8 = (bf16[1072,128]{1,0:T(8,128)(2,1)}, bf16[1072,128]{1,0:T(8,128)(2,1)S(1)}, u32[]{:S(2)}, u32[]{:S(2)}) collective-permute-start(bf16[1072,128]{1,0:T(8,128)(2,1)} %get-tuple-element.44), channel_id=1, source_target_pairs={{0,4},{1,5},{2,6},{3,7},{4,0},{5,1},{6,2},{7,3},{8,12},{9,13},{10,... | collective-permute-start | bytes 823304 | tf_op jit(solution)/shard_map/ppermute | solution.py:539
  26.7 5.2 %collective-permute-start.3 = (bf16[1072,128]{1,0:T(8,128)(2,1)S(1)}, bf16[1072,128]{1,0:T(8,128)(2,1)S(1)}, u32[]{:S(2)}, u32[]{:S(2)}) collective-permute-start(bf16[1072,128]{1,0:T(8,128)(2,1)S(1)} %collective-permute-done.refs_2_), channel_id=1, source_target_pairs={{0,1},{1,0},{2,3},{3,2},{4,5},{5,4},{6,7},{7,6},{8,9},{9,8},{10,11... | collective-permute-start | bytes 823304 | tf_op jit(solution)/shard_map/ppermute | solution.py:539
  26.7 5.2 %collective-permute-start.2 = (bf16[1072,128]{1,0:T(8,128)(2,1)}, bf16[1072,128]{1,0:T(8,128)(2,1)S(1)}, u32[]{:S(2)}, u32[]{:S(2)}) collective-permute-start(bf16[1072,128]{1,0:T(8,128)(2,1)} %get-tuple-element.37.from_any), channel_id=1, source_target_pairs={{0,1},{1,0},{2,3},{3,2},{4,5},{5,4},{6,7},{7,6},{8,9},{9,8},{10,11... | collective-permute-start | bytes 823304 | tf_op jit(solution)/shard_map/ppermute | solution.py:539
  27.2 8.6 %collective-permute-start.7 = (bf16[1072,128]{1,0:T(8,128)(2,1)S(1)}, bf16[1072,128]{1,0:T(8,128)(2,1)S(1)}, u32[]{:S(2)}, u32[]{:S(2)}) collective-permute-start(bf16[1072,128]{1,0:T(8,128)(2,1)S(1)} %collective-permute-done.6.refs_0_), channel_id=1, source_target_pairs={{0,1},{1,0},{2,3},{3,2},{4,5},{5,4},{6,7},{7,6},{8,9},{9,8},{10,11... | collective-permute-start | bytes 823304 | tf_op jit(solution)/shard_map/ppermute | solution.py:539
  31.5 4.4 %collective-permute-start.9 = (bf16[1072,128]{1,0:T(8,128)(2,1)S(1)}, bf16[1072,128]{1,0:T(8,128)(2,1)S(1)}, u32[]{:S(2)}, u32[]{:S(2)}) collective-permute-start(bf16[1072,128]{1,0:T(8,128)(2,1)S(1)} %collective-permute-done.8.refs_2_), channel_id=1, source_target_pairs={{0,1},{1,0},{2,3},{3,2},{4,5},{5,4},{6,7},{7,6},{8,9},{9,8},{10,11... | collective-permute-start | bytes 823304 | tf_op jit(solution)/shard_map/ppermute | solution.py:539
  32.7 9.0 %copy-start.2 = (bf16[4,128,256]{2,1,0:T(8,128)(2,1)S(1)}, bf16[4,128,256]{2,1,0:T(8,128)(2,1)}, u32[]{:S(2)}) copy-start(bf16[4,128,256]{2,1,0:T(8,128)(2,1)} %refs_2_.1) | copy-start | bytes 786436
  32.7 8.9 %copy-start.3 = (bf16[4,128,256]{2,1,0:T(8,128)(2,1)S(1)}, bf16[4,128,256]{2,1,0:T(8,128)(2,1)}, u32[]{:S(2)}) copy-start(bf16[4,128,256]{2,1,0:T(8,128)(2,1)} %refs_3_.1) | copy-start | bytes 786436
  32.7 8.9 %copy-start.6 = (s32[16]{0:T(128)S(1)}, s32[16]{0:T(128)}, u32[]{:S(2)}) copy-start(s32[16]{0:T(128)} %table_ref.1) | copy-start | bytes 196
  32.8 17.4 %collective-permute-start.5 = (bf16[784,128]{1,0:T(8,128)(2,1)S(1)}, bf16[784,128]{1,0:T(8,128)(2,1)S(1)}, u32[]{:S(2)}, u32[]{:S(2)}) collective-permute-start(bf16[784,128]{1,0:T(8,128)(2,1)S(1)} %get-tuple-element.42), channel_id=1, source_target_pairs={{0,8},{1,9},{2,10},{3,11},{4,12},{5,13},{6,14},{7,15},{8,0},{9,1},... | collective-permute-start | bytes 602120 | tf_op jit(solution)/shard_map/ppermute | solution.py:539
  35.8 16.2 %copy-start.4 = (f32[256]{0:T(256)S(1)}, f32[256]{0:T(256)}, u32[]{:S(2)}) copy-start(f32[256]{0:T(256)} %param.17) | copy-start | bytes 3076
  35.8 16.2 %copy-start.5 = (f32[256]{0:T(256)S(1)}, f32[256]{0:T(256)}, u32[]{:S(2)}) copy-start(f32[256]{0:T(256)} %param.18) | copy-start | bytes 3076
  36.6 13.5 %collective-permute-start.10 = (bf16[784,128]{1,0:T(8,128)(2,1)S(1)}, bf16[784,128]{1,0:T(8,128)(2,1)S(1)}, u32[]{:S(2)}, u32[]{:S(2)}) collective-permute-start(bf16[784,128]{1,0:T(8,128)(2,1)S(1)} %get-tuple-element.46), channel_id=1, source_target_pairs={{0,12},{1,13},{2,14},{3,15},{4,8},{5,9},{6,10},{7,11},{8,4},{9,5},... | collective-permute-start | bytes 602120 | tf_op jit(solution)/shard_map/ppermute | solution.py:539
  37.6 14.4 %collective-permute-start.11 = (bf16[784,128]{1,0:T(8,128)(2,1)S(1)}, bf16[784,128]{1,0:T(8,128)(2,1)S(1)}, u32[]{:S(2)}, u32[]{:S(2)}) collective-permute-start(bf16[784,128]{1,0:T(8,128)(2,1)S(1)} %get-tuple-element.47), channel_id=1, source_target_pairs={{0,4},{1,5},{2,6},{3,7},{4,0},{5,1},{6,2},{7,3},{8,12},{9,13},{10,... | collective-permute-start | bytes 602120 | tf_op jit(solution)/shard_map/ppermute | solution.py:539
  37.8 3.9 %collective-permute-start.12 = (bf16[128,128]{1,0:T(8,128)(2,1)S(1)}, bf16[128,128]{1,0:T(8,128)(2,1)S(1)}, u32[]{:S(2)}, u32[]{:S(2)}) collective-permute-start(bf16[128,128]{1,0:T(8,128)(2,1)S(1)} %get-tuple-element.50.refs_0_), channel_id=1, source_target_pairs={{0,2},{1,3},{2,0},{3,1},{4,6},{5,7},{6,4},{7,5},{8,10},{9,11},{10,... | collective-permute-start | bytes 98312 | tf_op jit(solution)/shard_map/ppermute | solution.py:539
  54.2 5.8 %collective-permute-start.13 = (bf16[128,128]{1,0:T(8,128)(2,1)S(1)}, bf16[128,128]{1,0:T(8,128)(2,1)S(1)}, u32[]{:S(2)}, u32[]{:S(2)}) collective-permute-start(bf16[128,128]{1,0:T(8,128)(2,1)S(1)} %get-tuple-element.58), channel_id=1, source_target_pairs={{0,12},{1,13},{2,14},{3,15},{4,8},{5,9},{6,10},{7,11},{8,4},{9,5},... | collective-permute-start | bytes 98312 | tf_op jit(solution)/shard_map/ppermute | solution.py:539
  57.1 4.9 %collective-permute-start.14 = (bf16[128,128]{1,0:T(8,128)(2,1)S(1)}, bf16[128,128]{1,0:T(8,128)(2,1)S(1)}, u32[]{:S(2)}, u32[]{:S(2)}) collective-permute-start(bf16[128,128]{1,0:T(8,128)(2,1)S(1)} %get-tuple-element.59), channel_id=1, source_target_pairs={{0,8},{1,9},{2,10},{3,11},{4,12},{5,13},{6,14},{7,15},{8,0},{9,1},... | collective-permute-start | bytes 98312 | tf_op jit(solution)/shard_map/ppermute | solution.py:539
  58.4 3.9 %collective-permute-start.15 = (bf16[128,128]{1,0:T(8,128)(2,1)S(1)}, bf16[128,128]{1,0:T(8,128)(2,1)S(1)}, u32[]{:S(2)}, u32[]{:S(2)}) collective-permute-start(bf16[128,128]{1,0:T(8,128)(2,1)S(1)} %get-tuple-element.60), channel_id=1, source_target_pairs={{0,4},{1,5},{2,6},{3,7},{4,0},{5,1},{6,2},{7,3},{8,12},{9,13},{10,... | collective-permute-start | bytes 98312 | tf_op jit(solution)/shard_map/ppermute | solution.py:539
  62.5 3.8 %collective-permute-start.16 = (bf16[64,128]{1,0:T(8,128)(2,1)S(1)}, bf16[64,128]{1,0:T(8,128)(2,1)S(1)}, u32[]{:S(2)}, u32[]{:S(2)}) collective-permute-start(bf16[64,128]{1,0:T(8,128)(2,1)S(1)} %get-tuple-element.62), channel_id=1, source_target_pairs={{0,2},{1,3},{2,0},{3,1},{4,6},{5,7},{6,4},{7,5},{8,10},{9,11},{10,... | collective-permute-start | bytes 49160 | tf_op jit(solution)/shard_map/ppermute | solution.py:539

commit v9 on v8

--- a/solution.py
+++ b/solution.py
@@ -306,10 +306,10 @@
     return lax.dot_general(a, b, (((1,), (1,)), ((), ())), preferred_element_type=jnp.float32)
 
 
-def loaded_kernel(place_ref, table_ref, split_ref, *refs):
+def loaded_kernel(table_ref, split_ref, *refs):
     parts = refs[:PAIR]
     key_ref, value_ref, top_ref, total_ref, numer_ref, query_ref = refs[PAIR:]
-    ctx = place_ref[1]
+    ctx = lax.axis_index("ctx")
     slots, page, width = key_ref.shape
     heads = width // HEAD_SIZE
     split = split_ref[0]
@@ -349,16 +349,14 @@
     out[...] = one[...].astype(jnp.float32) + other[...].astype(jnp.float32)
 
 
-def front_kernel(
-    place_ref, split_ref, early, *refs
-):
+def front_kernel(split_ref, early, *refs):
     received = refs[: GROUPS - 2]
     (key_bias, value_bias, cosine_ref, sine_ref, query_ref, top_ref, total_ref, numer_ref) = refs[
         GROUPS - 2 : GROUPS + 6
     ]
     key_any, value_any, *outs = refs[GROUPS + 6 : -3]
     front_key, front_value, sems = refs[-3:]
-    core, ctx = place_ref[0], place_ref[1]
+    core, ctx = lax.axis_index("tp"), lax.axis_index("ctx")
     rows, width = front_key.shape
     half_rows = rows // 2
     heads = width // HEAD_SIZE
@@ -520,7 +518,6 @@
     n_ctx = GROUPS * PAIR
     ctx = lax.axis_index("ctx").astype(jnp.int32)
     core = lax.axis_index("tp").astype(jnp.int32)
-    place = jnp.stack([core, ctx])
     rows, features = hidden.shape
     half_rows = rows // 2
     width = key_matrix.shape[1]
@@ -659,7 +656,7 @@
     state = jax.ShapeDtypeStruct((states, LANES), jnp.float32)
     top, total, numer, queries = pl.pallas_call(
         loaded_kernel,
-        in_specs=[smem, smem, smem] + [vmem] * (PAIR + 2),
+        in_specs=[smem, smem] + [vmem] * (PAIR + 2),
         out_specs=[vmem] * 4,
         out_shape=[state] * 3 + [jax.ShapeDtypeStruct((states, LANES), jnp.bfloat16)],
         compiler_params=params,
@@ -669,7 +666,7 @@
             transcendentals=states * slot_keys.shape[0] * slot_keys.shape[1],
         ),
         name="loaded_attention",
-    )(place, page_slot_table, split_page, own_tiles, beside_tiles, slot_keys, slot_values)
+    )(page_slot_table, split_page, own_tiles, beside_tiles, slot_keys, slot_values)
 
 
     def payload(kind, slots):
@@ -678,7 +675,7 @@
     row_shape = jax.ShapeDtypeStruct((rows, width), jnp.bfloat16)
     front_key, front_value, kept, *sent = pl.pallas_call(
         front_kernel,
-        in_specs=[smem, smem] + [vmem] * (GROUPS + 7),
+        in_specs=[smem] + [vmem] * (GROUPS + 7),
         out_specs=[hbm] * 2 + [vmem] * GROUPS,
         scratch_shapes=[pltpu.VMEM((rows, width), jnp.bfloat16)] * 2 + [pltpu.SemaphoreType.DMA((2,))],
         out_shape=[row_shape] * 2 + [payload(jnp.float32, PAIR)] + [payload(jnp.bfloat16, PAIR)] * (GROUPS - 1),
@@ -686,7 +683,6 @@
         cost_estimate=pl.CostEstimate(flops=4 * states * rows * HEAD_SIZE, bytes_accessed=2 * 1024 * 1024, transcendentals=states * rows),
         name="front_attention",
     )(
-        place,
         split_page,
         early,
         *received[1:],

time: 67.4 us -> 66.8 us (level)
  no operation moved by 1% of the time
where the time goes in v9:
time: 66.8 us; the launch traced here: 66.6 us
  waiting for transfers between devices  32.6 us (49%)
  starting transfers between devices  20.3 us (30%)
  Pallas kernels  11.8 us (18%)
  between operations  1.44 us (2%)
    ppermute x17, waiting for transfers between devices, move(): return lax.ppermute(array, ('ctx', 'tp'), pairs)  32.6 us
    ppermute x17, starting transfers between devices, move(): return lax.ppermute(array, ('ctx', 'tp'), pairs)  20.3 us
    pallas_call x2, Pallas kernels, exchange_plan(): pl.pallas_call(functools.partial(norm_kernel, shifts), in_specs=[hbm] * 4...  5.22 us
    pallas_call x2, Pallas kernels, exchange_plan(): pl.pallas_call(functools.partial(project_kernel, shifts), in_specs=[vmem]...  1.57 us
    pallas_call x1, Pallas kernels, exchange_plan(): pl.pallas_call(front_kernel, in_specs=[smem] + [vmem] * (GROUPS + 7), out...  1.55 us
    pallas_call x1, Pallas kernels, exchange_plan(): pl.pallas_call(loaded_kernel, in_specs=[smem, smem] + [vmem] * (PAIR + 2)...  1.35 us
  transfers between devices with their start and end apart: 17, of which 10 were waited for; matrix products, arithmetic and copies ran while one was open for 1% of the time, Pallas kernels for 10%

profile of v9, /device:TPU:0, one launch (start us, length us, event | category | flops | bytes accessed | tf_op | source)
XLA Modules:
  0.0 66.6 jit_solution(13754041026627598659)
XLA Ops:
  0.7 2.5 %norm_rows.2 = bf16[1072,128]{1,0:T(8,128)(2,1)} custom-call(bf16[2,2048]{1,0:T(2,128)(2,1)} %query_any.3, bf16[128,8192]{1,0:T(8,128)(2,1)} %hidden_any.3, bf16[2,8192]{1,0:T(2,128)(2,1)} %suffix_any.3, f32[1,8192]{1,0:T(1,128)} %bitcast.5), custom_call_target="tpu_custom_call" | custom-call | flops 2097152 | bytes 2097152 | tf_op jit(solution)/shard_map/norm_rows/pallas_call | solution.py:557
  3.2 4.1 %collective-permute-start = (bf16[1072,128]{1,0:T(8,128)(2,1)}, bf16[1072,128]{1,0:T(8,128)(2,1)S(1)}, u32[]{:S(2)}, u32[]{:S(2)}) collective-permute-start(bf16[1072,128]{1,0:T(8,128)(2,1)} %norm_rows.2), channel_id=1, source_target_pairs={{0,8},{1,9},{2,10},{3,11},{4,12},{5,13},{6,14},{7,15},{8,0},{9,1},... | collective-permute-start | bytes 823304 | tf_op jit(solution)/shard_map/ppermute | solution.py:536
  7.3 1.5 %collective-permute-start.1 = (bf16[1024,256]{1,0:T(8,128)(2,1)S(1)}, bf16[1024,256]{1,0:T(8,128)(2,1)S(1)}, u32[]{:S(2)}, u32[]{:S(2)}) collective-permute-start(bf16[1024,256]{1,0:T(8,128)(2,1)S(1)} %copy-done), channel_id=1, source_target_pairs={{0,2},{1,3},{2,0},{3,1},{4,6},{5,7},{6,4},{7,5},{8,10},{9,11},{10,... | collective-permute-start | bytes 1572872 | tf_op jit(solution)/shard_map/ppermute | solution.py:536
  9.3 2.7 %norm_rows.3 = (bf16[1072,128]{1,0:T(8,128)(2,1)}, bf16[1072,128]{1,0:T(8,128)(2,1)}, bf16[1072,128]{1,0:T(8,128)(2,1)}) custom-call(bf16[2,2048]{1,0:T(2,128)(2,1)} %query_any.3, bf16[128,8192]{1,0:T(8,128)(2,1)} %hidden_any.3, bf16[2,8192]{1,0:T(2,128)(2,1)} %suffix_any.3, f32[1,8192]{1,0:T(1,128)} %bitcast.6), custom_call_target="tpu_custom_call" | custom-call | flops 2097152 | bytes 2097152 | tf_op jit(solution)/shard_map/norm_rows/pallas_call | solution.py:557
  12.0 1.4 %collective-permute-start.6 = (bf16[1072,128]{1,0:T(8,128)(2,1)}, bf16[1072,128]{1,0:T(8,128)(2,1)S(1)}, u32[]{:S(2)}, u32[]{:S(2)}) collective-permute-start(bf16[1072,128]{1,0:T(8,128)(2,1)} %get-tuple-element.43), channel_id=1, source_target_pairs={{0,12},{1,13},{2,14},{3,15},{4,8},{5,9},{6,10},{7,11},{8,4},{9,5},... | collective-permute-start | bytes 823304 | tf_op jit(solution)/shard_map/ppermute | solution.py:536
  14.1 1.0 %fetch_own.1.refs_0_ = bf16[1072,128]{1,0:T(8,128)(2,1)S(1)} custom-call(bf16[1072,128]{1,0:T(8,128)(2,1)} %get-tuple-element.37.from_any), custom_call_target="tpu_custom_call" | custom-call | bytes 67108864 | tf_op jit(solution)/shard_map/fetch_own/pallas_call | solution.py:598
  15.2 11.5 %collective-permute-done.refs_2_ = bf16[1072,128]{1,0:T(8,128)(2,1)S(1)} collective-permute-done((bf16[1072,128]{1,0:T(8,128)(2,1)}, bf16[1072,128]{1,0:T(8,128)(2,1)S(1)}, u32[]{:S(2)}, u32[]{:S(2)}) %collective-permute-start) | collective-permute-done | bytes 274464 | tf_op jit(solution)/shard_map/ppermute | solution.py:536
  27.3 4.2 %collective-permute-done.8.refs_2_ = bf16[1072,128]{1,0:T(8,128)(2,1)S(1)} collective-permute-done((bf16[1072,128]{1,0:T(8,128)(2,1)}, bf16[1072,128]{1,0:T(8,128)(2,1)S(1)}, u32[]{:S(2)}, u32[]{:S(2)}) %collective-permute-start.8) | collective-permute-done | bytes 274464 | tf_op jit(solution)/shard_map/ppermute | solution.py:536
  32.8 3.1 %collective-permute-start.5 = (bf16[784,128]{1,0:T(8,128)(2,1)S(1)}, bf16[784,128]{1,0:T(8,128)(2,1)S(1)}, u32[]{:S(2)}, u32[]{:S(2)}) collective-permute-start(bf16[784,128]{1,0:T(8,128)(2,1)S(1)} %get-tuple-element.42), channel_id=1, source_target_pairs={{0,8},{1,9},{2,10},{3,11},{4,12},{5,13},{6,14},{7,15},{8,0},{9,1},... | collective-permute-start | bytes 602120 | tf_op jit(solution)/shard_map/ppermute | solution.py:536
  35.8 0.8 %project.3 = (bf16[784,128]{1,0:T(8,128)(2,1)S(1)}, bf16[784,128]{1,0:T(8,128)(2,1)S(1)}, bf16[128,128]{1,0:T(8,128)(2,1)S(1)}) custom-call(bf16[1072,128]{1,0:T(8,128)(2,1)S(1)} %collective-permute-done.6.refs_0_, bf16[1072,128]{1,0:T(8,128)(2,1)S(1)} %collective-permute-done.7.refs_1_, bf16[1072,128]{1,0:T(8,128)(2,1)S(1)} %collective-permute-done.8.refs_2_, ...), custom_call_target="tpu_custom_call" | custom-call | flops 536870912 | bytes 6291456 | tf_op jit(solution)/shard_map/project/pallas_call | solution.py:617
  36.6 1.0 %collective-permute-start.10 = (bf16[784,128]{1,0:T(8,128)(2,1)S(1)}, bf16[784,128]{1,0:T(8,128)(2,1)S(1)}, u32[]{:S(2)}, u32[]{:S(2)}) collective-permute-start(bf16[784,128]{1,0:T(8,128)(2,1)S(1)} %get-tuple-element.46), channel_id=1, source_target_pairs={{0,12},{1,13},{2,14},{3,15},{4,8},{5,9},{6,10},{7,11},{8,4},{9,5},... | collective-permute-start | bytes 602120 | tf_op jit(solution)/shard_map/ppermute | solution.py:536
  37.8 1.5 %collective-permute-start.12 = (bf16[128,128]{1,0:T(8,128)(2,1)S(1)}, bf16[128,128]{1,0:T(8,128)(2,1)S(1)}, u32[]{:S(2)}, u32[]{:S(2)}) collective-permute-start(bf16[128,128]{1,0:T(8,128)(2,1)S(1)} %get-tuple-element.50.refs_0_), channel_id=1, source_target_pairs={{0,2},{1,3},{2,0},{3,1},{4,6},{5,7},{6,4},{7,5},{8,10},{9,11},{10,... | collective-permute-start | bytes 98312 | tf_op jit(solution)/shard_map/ppermute | solution.py:536
  39.9 1.8 %collective-permute-done.12.refs_1_ = bf16[128,128]{1,0:T(8,128)(2,1)S(1)} collective-permute-done((bf16[128,128]{1,0:T(8,128)(2,1)S(1)}, bf16[128,128]{1,0:T(8,128)(2,1)S(1)}, u32[]{:S(2)}, u32[]{:S(2)}) %collective-permute-start.12) | collective-permute-done | bytes 32800 | tf_op jit(solution)/shard_map/ppermute | solution.py:536
  41.7 1.4 %loaded_attention.1 = (f32[256,128]{1,0:T(8,128)S(1)}, f32[256,128]{1,0:T(8,128)S(1)}, f32[256,128]{1,0:T(8,128)S(1)}, bf16[256,128]{1,0:T(8,128)(2,1)S(1)}) custom-call(s32[16]{0:T(128)S(1)} %copy-done.6, s32[1]{0:T(128)S(6)} %copy.15.split_ref, bf16[128,128]{1,0:T(8,128)(2,1)S(1)} %get-tuple-element.50.refs_0_, ...), custom_call_target="tpu_custom_call" | custom-call | flops 67108864 | bytes 524288 | tf_op jit(solution)/shard_map/loaded_attention/pallas_call | solution.py:657
  43.1 7.1 %collective-permute-done.5.other = bf16[784,128]{1,0:T(8,128)(2,1)S(1)} collective-permute-done((bf16[784,128]{1,0:T(8,128)(2,1)S(1)}, bf16[784,128]{1,0:T(8,128)(2,1)S(1)}, u32[]{:S(2)}, u32[]{:S(2)}) %collective-permute-start.5) | collective-permute-done | bytes 200736 | tf_op jit(solution)/shard_map/ppermute | solution.py:536
  50.2 1.9 %collective-permute-done.11.refs_1_ = bf16[784,128]{1,0:T(8,128)(2,1)S(1)} collective-permute-done((bf16[784,128]{1,0:T(8,128)(2,1)S(1)}, bf16[784,128]{1,0:T(8,128)(2,1)S(1)}, u32[]{:S(2)}, u32[]{:S(2)}) %collective-permute-start.11) | collective-permute-done | bytes 200736 | tf_op jit(solution)/shard_map/ppermute | solution.py:536
  52.1 1.6 %front_attention.1 = (bf16[128,256]{1,0:T(8,128)(2,1)}, bf16[128,256]{1,0:T(8,128)(2,1)}, f32[128,128]{1,0:T(8,128)S(1)}, bf16[128,128]{1,0:T(8,128)(2,1)S(1)}, ...) custom-call(s32[1]{0:T(128)S(6)} %copy.15.split_ref, f32[784,128]{1,0:T(8,128)S(1)} %sum_early.1.early, ...), custom_call_target="tpu_custom_call" | custom-call | flops 16777216 | bytes 2097152 | tf_op jit(solution)/shard_map/front_attention/pallas_call | solution.py:676
  53.7 2.9 %collective-permute-start.13 = (bf16[128,128]{1,0:T(8,128)(2,1)S(1)}, bf16[128,128]{1,0:T(8,128)(2,1)S(1)}, u32[]{:S(2)}, u32[]{:S(2)}) collective-permute-start(bf16[128,128]{1,0:T(8,128)(2,1)S(1)} %get-tuple-element.58), channel_id=1, source_target_pairs={{0,12},{1,13},{2,14},{3,15},{4,8},{5,9},{6,10},{7,11},{8,4},{9,5},... | collective-permute-start | bytes 98312 | tf_op jit(solution)/shard_map/ppermute | solution.py:536
  56.5 1.3 %collective-permute-start.14 = (bf16[128,128]{1,0:T(8,128)(2,1)S(1)}, bf16[128,128]{1,0:T(8,128)(2,1)S(1)}, u32[]{:S(2)}, u32[]{:S(2)}) collective-permute-start(bf16[128,128]{1,0:T(8,128)(2,1)S(1)} %get-tuple-element.59), channel_id=1, source_target_pairs={{0,8},{1,9},{2,10},{3,11},{4,12},{5,13},{6,14},{7,15},{8,0},{9,1},... | collective-permute-start | bytes 98312 | tf_op jit(solution)/shard_map/ppermute | solution.py:536
  58.3 1.1 %collective-permute-done.13.refs_0_ = bf16[128,128]{1,0:T(8,128)(2,1)S(1)} collective-permute-done((bf16[128,128]{1,0:T(8,128)(2,1)S(1)}, bf16[128,128]{1,0:T(8,128)(2,1)S(1)}, u32[]{:S(2)}, u32[]{:S(2)}) %collective-permute-start.13) | collective-permute-done | bytes 32800 | tf_op jit(solution)/shard_map/ppermute | solution.py:536
  59.4 1.9 %collective-permute-done.14.refs_1_ = bf16[128,128]{1,0:T(8,128)(2,1)S(1)} collective-permute-done((bf16[128,128]{1,0:T(8,128)(2,1)S(1)}, bf16[128,128]{1,0:T(8,128)(2,1)S(1)}, u32[]{:S(2)}, u32[]{:S(2)}) %collective-permute-start.14) | collective-permute-done | bytes 32800 | tf_op jit(solution)/shard_map/ppermute | solution.py:536
  62.0 1.5 %collective-permute-start.16 = (bf16[64,128]{1,0:T(8,128)(2,1)S(1)}, bf16[64,128]{1,0:T(8,128)(2,1)S(1)}, u32[]{:S(2)}, u32[]{:S(2)}) collective-permute-start(bf16[64,128]{1,0:T(8,128)(2,1)S(1)} %get-tuple-element.62), channel_id=1, source_target_pairs={{0,2},{1,3},{2,0},{3,1},{4,6},{5,7},{6,4},{7,5},{8,10},{9,11},{10,... | collective-permute-start | bytes 49160 | tf_op jit(solution)/shard_map/ppermute | solution.py:536
  63.5 2.2 %collective-permute-done.16.refs_0_ = bf16[64,128]{1,0:T(8,128)(2,1)S(1)} collective-permute-done((bf16[64,128]{1,0:T(8,128)(2,1)S(1)}, bf16[64,128]{1,0:T(8,128)(2,1)S(1)}, u32[]{:S(2)}, u32[]{:S(2)}) %collective-permute-start.16) | collective-permute-done | bytes 16416 | tf_op jit(solution)/shard_map/ppermute | solution.py:536
  65.8 0.8 %finish.1 = bf16[2,2048]{1,0:T(2,128)(2,1)} custom-call(f32[64,128]{1,0:T(8,128)S(1)} %get-tuple-element.61.kept, bf16[64,128]{1,0:T(8,128)(2,1)S(1)} %collective-permute-done.16.refs_0_), custom_call_target="tpu_custom_call" | custom-call | tf_op jit(solution)/shard_map/finish/pallas_call | solution.py:706
  (38 shorter events, 4.4 us)
Async XLA Ops:
  0.6 6.7 %copy-start = (bf16[1024,256]{1,0:T(8,128)(2,1)S(1)}, bf16[1024,256]{1,0:T(8,128)(2,1)}, u32[]{:S(2)}) copy-start(bf16[1024,256]{1,0:T(8,128)(2,1)} %refs_4_.3) | copy-start | bytes 1572868
  0.6 8.2 %copy-start.1 = (bf16[1024,256]{1,0:T(8,128)(2,1)S(1)}, bf16[1024,256]{1,0:T(8,128)(2,1)}, u32[]{:S(2)}) copy-start(bf16[1024,256]{1,0:T(8,128)(2,1)} %refs_5_.3) | copy-start | bytes 1572868
  3.2 23.5 %collective-permute-start = (bf16[1072,128]{1,0:T(8,128)(2,1)}, bf16[1072,128]{1,0:T(8,128)(2,1)S(1)}, u32[]{:S(2)}, u32[]{:S(2)}) collective-permute-start(bf16[1072,128]{1,0:T(8,128)(2,1)} %norm_rows.2), channel_id=1, source_target_pairs={{0,8},{1,9},{2,10},{3,11},{4,12},{5,13},{6,14},{7,15},{8,0},{9,1},... | collective-permute-start | bytes 823304 | tf_op jit(solution)/shard_map/ppermute | solution.py:536
  7.3 19.4 %collective-permute-start.1 = (bf16[1024,256]{1,0:T(8,128)(2,1)S(1)}, bf16[1024,256]{1,0:T(8,128)(2,1)S(1)}, u32[]{:S(2)}, u32[]{:S(2)}) collective-permute-start(bf16[1024,256]{1,0:T(8,128)(2,1)S(1)} %copy-done), channel_id=1, source_target_pairs={{0,2},{1,3},{2,0},{3,1},{4,6},{5,7},{6,4},{7,5},{8,10},{9,11},{10,... | collective-permute-start | bytes 1572872 | tf_op jit(solution)/shard_map/ppermute | solution.py:536
  8.8 23.1 %collective-permute-start.4 = (bf16[1024,256]{1,0:T(8,128)(2,1)S(1)}, bf16[1024,256]{1,0:T(8,128)(2,1)S(1)}, u32[]{:S(2)}, u32[]{:S(2)}) collective-permute-start(bf16[1024,256]{1,0:T(8,128)(2,1)S(1)} %copy-done.1), channel_id=1, source_target_pairs={{0,2},{1,3},{2,0},{3,1},{4,6},{5,7},{6,4},{7,5},{8,10},{9,11},{10,... | collective-permute-start | bytes 1572872 | tf_op jit(solution)/shard_map/ppermute | solution.py:536
  12.0 15.2 %collective-permute-start.6 = (bf16[1072,128]{1,0:T(8,128)(2,1)}, bf16[1072,128]{1,0:T(8,128)(2,1)S(1)}, u32[]{:S(2)}, u32[]{:S(2)}) collective-permute-start(bf16[1072,128]{1,0:T(8,128)(2,1)} %get-tuple-element.43), channel_id=1, source_target_pairs={{0,12},{1,13},{2,14},{3,15},{4,8},{5,9},{6,10},{7,11},{8,4},{9,5},... | collective-permute-start | bytes 823304 | tf_op jit(solution)/shard_map/ppermute | solution.py:536
  13.4 18.0 %collective-permute-start.8 = (bf16[1072,128]{1,0:T(8,128)(2,1)}, bf16[1072,128]{1,0:T(8,128)(2,1)S(1)}, u32[]{:S(2)}, u32[]{:S(2)}) collective-permute-start(bf16[1072,128]{1,0:T(8,128)(2,1)} %get-tuple-element.44), channel_id=1, source_target_pairs={{0,4},{1,5},{2,6},{3,7},{4,0},{5,1},{6,2},{7,3},{8,12},{9,13},{10,... | collective-permute-start | bytes 823304 | tf_op jit(solution)/shard_map/ppermute | solution.py:536
  26.7 5.2 %collective-permute-start.3 = (bf16[1072,128]{1,0:T(8,128)(2,1)S(1)}, bf16[1072,128]{1,0:T(8,128)(2,1)S(1)}, u32[]{:S(2)}, u32[]{:S(2)}) collective-permute-start(bf16[1072,128]{1,0:T(8,128)(2,1)S(1)} %collective-permute-done.refs_2_), channel_id=1, source_target_pairs={{0,1},{1,0},{2,3},{3,2},{4,5},{5,4},{6,7},{7,6},{8,9},{9,8},{10,11... | collective-permute-start | bytes 823304 | tf_op jit(solution)/shard_map/ppermute | solution.py:536
  26.7 5.2 %collective-permute-start.2 = (bf16[1072,128]{1,0:T(8,128)(2,1)}, bf16[1072,128]{1,0:T(8,128)(2,1)S(1)}, u32[]{:S(2)}, u32[]{:S(2)}) collective-permute-start(bf16[1072,128]{1,0:T(8,128)(2,1)} %get-tuple-element.37.from_any), channel_id=1, source_target_pairs={{0,1},{1,0},{2,3},{3,2},{4,5},{5,4},{6,7},{7,6},{8,9},{9,8},{10,11... | collective-permute-start | bytes 823304 | tf_op jit(solution)/shard_map/ppermute | solution.py:536
  27.2 8.6 %collective-permute-start.7 = (bf16[1072,128]{1,0:T(8,128)(2,1)S(1)}, bf16[1072,128]{1,0:T(8,128)(2,1)S(1)}, u32[]{:S(2)}, u32[]{:S(2)}) collective-permute-start(bf16[1072,128]{1,0:T(8,128)(2,1)S(1)} %collective-permute-done.6.refs_0_), channel_id=1, source_target_pairs={{0,1},{1,0},{2,3},{3,2},{4,5},{5,4},{6,7},{7,6},{8,9},{9,8},{10,11... | collective-permute-start | bytes 823304 | tf_op jit(solution)/shard_map/ppermute | solution.py:536
  31.5 4.4 %collective-permute-start.9 = (bf16[1072,128]{1,0:T(8,128)(2,1)S(1)}, bf16[1072,128]{1,0:T(8,128)(2,1)S(1)}, u32[]{:S(2)}, u32[]{:S(2)}) collective-permute-start(bf16[1072,128]{1,0:T(8,128)(2,1)S(1)} %collective-permute-done.8.refs_2_), channel_id=1, source_target_pairs={{0,1},{1,0},{2,3},{3,2},{4,5},{5,4},{6,7},{7,6},{8,9},{9,8},{10,11... | collective-permute-start | bytes 823304 | tf_op jit(solution)/shard_map/ppermute | solution.py:536
  32.7 9.0 %copy-start.2 = (bf16[4,128,256]{2,1,0:T(8,128)(2,1)S(1)}, bf16[4,128,256]{2,1,0:T(8,128)(2,1)}, u32[]{:S(2)}) copy-start(bf16[4,128,256]{2,1,0:T(8,128)(2,1)} %refs_2_.1) | copy-start | bytes 786436
  32.7 9.0 %copy-start.3 = (bf16[4,128,256]{2,1,0:T(8,128)(2,1)S(1)}, bf16[4,128,256]{2,1,0:T(8,128)(2,1)}, u32[]{:S(2)}) copy-start(bf16[4,128,256]{2,1,0:T(8,128)(2,1)} %refs_3_.1) | copy-start | bytes 786436
  32.7 9.0 %copy-start.6 = (s32[16]{0:T(128)S(1)}, s32[16]{0:T(128)}, u32[]{:S(2)}) copy-start(s32[16]{0:T(128)} %table_ref.1) | copy-start | bytes 196
  32.8 17.4 %collective-permute-start.5 = (bf16[784,128]{1,0:T(8,128)(2,1)S(1)}, bf16[784,128]{1,0:T(8,128)(2,1)S(1)}, u32[]{:S(2)}, u32[]{:S(2)}) collective-permute-start(bf16[784,128]{1,0:T(8,128)(2,1)S(1)} %get-tuple-element.42), channel_id=1, source_target_pairs={{0,8},{1,9},{2,10},{3,11},{4,12},{5,13},{6,14},{7,15},{8,0},{9,1},... | collective-permute-start | bytes 602120 | tf_op jit(solution)/shard_map/ppermute | solution.py:536
  35.8 16.3 %copy-start.4 = (f32[256]{0:T(256)S(1)}, f32[256]{0:T(256)}, u32[]{:S(2)}) copy-start(f32[256]{0:T(256)} %param.17) | copy-start | bytes 3076
  35.8 16.3 %copy-start.5 = (f32[256]{0:T(256)S(1)}, f32[256]{0:T(256)}, u32[]{:S(2)}) copy-start(f32[256]{0:T(256)} %param.18) | copy-start | bytes 3076
  36.6 13.5 %collective-permute-start.10 = (bf16[784,128]{1,0:T(8,128)(2,1)S(1)}, bf16[784,128]{1,0:T(8,128)(2,1)S(1)}, u32[]{:S(2)}, u32[]{:S(2)}) collective-permute-start(bf16[784,128]{1,0:T(8,128)(2,1)S(1)} %get-tuple-element.46), channel_id=1, source_target_pairs={{0,12},{1,13},{2,14},{3,15},{4,8},{5,9},{6,10},{7,11},{8,4},{9,5},... | collective-permute-start | bytes 602120 | tf_op jit(solution)/shard_map/ppermute | solution.py:536
  37.6 14.5 %collective-permute-start.11 = (bf16[784,128]{1,0:T(8,128)(2,1)S(1)}, bf16[784,128]{1,0:T(8,128)(2,1)S(1)}, u32[]{:S(2)}, u32[]{:S(2)}) collective-permute-start(bf16[784,128]{1,0:T(8,128)(2,1)S(1)} %get-tuple-element.47), channel_id=1, source_target_pairs={{0,4},{1,5},{2,6},{3,7},{4,0},{5,1},{6,2},{7,3},{8,12},{9,13},{10,... | collective-permute-start | bytes 602120 | tf_op jit(solution)/shard_map/ppermute | solution.py:536
  37.8 3.9 %collective-permute-start.12 = (bf16[128,128]{1,0:T(8,128)(2,1)S(1)}, bf16[128,128]{1,0:T(8,128)(2,1)S(1)}, u32[]{:S(2)}, u32[]{:S(2)}) collective-permute-start(bf16[128,128]{1,0:T(8,128)(2,1)S(1)} %get-tuple-element.50.refs_0_), channel_id=1, source_target_pairs={{0,2},{1,3},{2,0},{3,1},{4,6},{5,7},{6,4},{7,5},{8,10},{9,11},{10,... | collective-permute-start | bytes 98312 | tf_op jit(solution)/shard_map/ppermute | solution.py:536
  53.7 5.8 %collective-permute-start.13 = (bf16[128,128]{1,0:T(8,128)(2,1)S(1)}, bf16[128,128]{1,0:T(8,128)(2,1)S(1)}, u32[]{:S(2)}, u32[]{:S(2)}) collective-permute-start(bf16[128,128]{1,0:T(8,128)(2,1)S(1)} %get-tuple-element.58), channel_id=1, source_target_pairs={{0,12},{1,13},{2,14},{3,15},{4,8},{5,9},{6,10},{7,11},{8,4},{9,5},... | collective-permute-start | bytes 98312 | tf_op jit(solution)/shard_map/ppermute | solution.py:536
  56.5 4.8 %collective-permute-start.14 = (bf16[128,128]{1,0:T(8,128)(2,1)S(1)}, bf16[128,128]{1,0:T(8,128)(2,1)S(1)}, u32[]{:S(2)}, u32[]{:S(2)}) collective-permute-start(bf16[128,128]{1,0:T(8,128)(2,1)S(1)} %get-tuple-element.59), channel_id=1, source_target_pairs={{0,8},{1,9},{2,10},{3,11},{4,12},{5,13},{6,14},{7,15},{8,0},{9,1},... | collective-permute-start | bytes 98312 | tf_op jit(solution)/shard_map/ppermute | solution.py:536
  57.8 3.9 %collective-permute-start.15 = (bf16[128,128]{1,0:T(8,128)(2,1)S(1)}, bf16[128,128]{1,0:T(8,128)(2,1)S(1)}, u32[]{:S(2)}, u32[]{:S(2)}) collective-permute-start(bf16[128,128]{1,0:T(8,128)(2,1)S(1)} %get-tuple-element.60), channel_id=1, source_target_pairs={{0,4},{1,5},{2,6},{3,7},{4,0},{5,1},{6,2},{7,3},{8,12},{9,13},{10,... | collective-permute-start | bytes 98312 | tf_op jit(solution)/shard_map/ppermute | solution.py:536
  62.0 3.8 %collective-permute-start.16 = (bf16[64,128]{1,0:T(8,128)(2,1)S(1)}, bf16[64,128]{1,0:T(8,128)(2,1)S(1)}, u32[]{:S(2)}, u32[]{:S(2)}) collective-permute-start(bf16[64,128]{1,0:T(8,128)(2,1)S(1)} %get-tuple-element.62), channel_id=1, source_target_pairs={{0,2},{1,3},{2,0},{3,1},{4,6},{5,7},{6,4},{7,5},{8,10},{9,11},{10,... | collective-permute-start | bytes 49160 | tf_op jit(solution)/shard_map/ppermute | solution.py:536

commit v10 on v9

--- a/solution.py
+++ b/solution.py
@@ -345,8 +345,22 @@
         numer_ref[rows, :] = numer
 
 
-def sum_kernel(one, other, out):
-    out[...] = one[...].astype(jnp.float32) + other[...].astype(jnp.float32)
+def sum_kernel(one, other, key_bias, value_bias, out):
+    heads = key_bias.shape[1] // HEAD_SIZE
+    rows = (one.shape[0] - 16) // (3 * heads)
+
+    def summed(start, size):
+        at = slice(start, start + size)
+        return one[at, :].astype(jnp.float32) + other[at, :].astype(jnp.float32)
+
+    for head in range(heads):
+        columns = slice(head * HEAD_SIZE, (head + 1) * HEAD_SIZE)
+        keys = summed(head * rows, rows) + summed((heads + head) * rows, rows)
+        out[head * rows : (head + 1) * rows, :] = keys + key_bias[:, columns]
+        out[(heads + head) * rows : (heads + head + 1) * rows, :] = (
+            summed((2 * heads + head) * rows, rows) + value_bias[:, columns]
+        )
+    out[2 * heads * rows :, :] = summed(3 * heads * rows, 16)
 
 
 def front_kernel(split_ref, early, *refs):
@@ -365,13 +379,15 @@
     own_queries = count // sharing // (GROUPS * PAIR)
     visible = ctx < split_ref[0]
 
-    def summed(start, size):
+    def summed(start, *places):
+        size = rows if start < 2 * heads * rows else 16
         value = early[start : start + size, :]
         for ref in received:
-            value += ref[start : start + size, :].astype(jnp.float32)
+            for place in places:
+                value += ref[place : place + size, :].astype(jnp.float32)
         return value
 
-    ends = summed(3 * heads * rows, 16)
+    ends = summed(2 * heads * rows, 3 * heads * rows)
     row = lax.broadcasted_iota(jnp.int32, (count, 16), 0)
     query_position = (ctx ^ (row // (own_queries * sharing))) * own_queries + row % own_queries
     end_column = lax.broadcasted_iota(jnp.int32, (count, 16), 1)
@@ -381,13 +397,12 @@
     end_pairs = []
     for head in range(heads):
         columns = slice(head * HEAD_SIZE, (head + 1) * HEAD_SIZE)
-        raw = summed(head * rows, rows) + summed((heads + head) * rows, rows)
-        value = (summed((2 * heads + head) * rows, rows) + value_bias[:, columns]).astype(jnp.bfloat16)
+        raw = summed(head * rows, head * rows, (heads + head) * rows)
+        value = summed((heads + head) * rows, (2 * heads + head) * rows).astype(jnp.bfloat16)
         end_raw = ends[2 * head : 2 * head + 2] + ends[2 * (heads + head) : 2 * (heads + head) + 2]
         end_value = ends[2 * (2 * heads + head) : 2 * (2 * heads + head) + 2] + value_bias[:, columns]
         end_raw = jnp.concatenate([end_raw + key_bias[:, columns], pad], 0)
         end_value = jnp.concatenate([end_value, pad], 0).astype(jnp.bfloat16)
-        raw = raw + key_bias[:, columns]
 
         def rotated(k, part):
             turned = pltpu.roll(k, HEAD_SIZE // 2, 1)
@@ -641,15 +656,16 @@
         own_tiles = [tiles]
     (own_tiles,) = own_tiles
     received = [move(partials[s], along(s)) for s in far_first()]
+    biases = [bias.reshape(1, width) for bias in (key_offset_bias, value_offset_bias)]
     early = pl.pallas_call(
         sum_kernel,
-        in_specs=[vmem] * 2,
+        in_specs=[vmem] * 4,
         out_specs=vmem,
-        out_shape=jax.ShapeDtypeStruct((part_rows, LANES), jnp.float32),
+        out_shape=jax.ShapeDtypeStruct((2 * (width // LANES) * rows + 16, LANES), jnp.float32),
         compiler_params=params,
         cost_estimate=pl.CostEstimate(flops=0, bytes_accessed=16 * 1024 * 1024, transcendentals=0),
         name="sum_early",
-    )(partials[0], received[0])
+    )(partials[0], received[0], *biases)
     beside_tiles = move(own_tiles, beside)
 
     states = n_ctx * own_queries * query_width // HEAD_SIZE
@@ -686,8 +702,7 @@
         split_page,
         early,
         *received[1:],
-        key_offset_bias.reshape(1, width),
-        value_offset_bias.reshape(1, width),
+        *biases,
         cosine,
         sine,
         queries,

time: 66.8 us -> 66.8 us (level)
  no operation moved by 1% of the time
where the time goes in v10:
time: 66.8 us; the launch traced here: 66.6 us
  waiting for transfers between devices  32.5 us (49%)
  starting transfers between devices  20.3 us (30%)
  Pallas kernels  11.8 us (18%)
  between operations  1.44 us (2%)
    ppermute x17, waiting for transfers between devices, move(): return lax.ppermute(array, ('ctx', 'tp'), pairs)  32.5 us
    ppermute x17, starting transfers between devices, move(): return lax.ppermute(array, ('ctx', 'tp'), pairs)  20.3 us
    pallas_call x2, Pallas kernels, exchange_plan(): pl.pallas_call(functools.partial(norm_kernel, shifts), in_specs=[hbm] * 4...  5.22 us
    pallas_call x2, Pallas kernels, exchange_plan(): pl.pallas_call(functools.partial(project_kernel, shifts), in_specs=[vmem]...  1.57 us
    pallas_call x1, Pallas kernels, exchange_plan(): pl.pallas_call(front_kernel, in_specs=[smem] + [vmem] * (GROUPS + 7), out...  1.56 us
    pallas_call x1, Pallas kernels, exchange_plan(): pl.pallas_call(loaded_kernel, in_specs=[smem, smem] + [vmem] * (PAIR + 2)...  1.36 us
  transfers between devices with their start and end apart: 17, of which 10 were waited for; matrix products, arithmetic and copies ran while one was open for 1% of the time, Pallas kernels for 10%

profile of v10, /device:TPU:0, one launch (start us, length us, event | category | flops | bytes accessed | tf_op | source)
XLA Modules:
  0.0 66.6 jit_solution(8150434219648062083)
XLA Ops:
  0.7 2.5 %norm_rows.2 = bf16[1072,128]{1,0:T(8,128)(2,1)} custom-call(bf16[2,2048]{1,0:T(2,128)(2,1)} %query_any.3, bf16[128,8192]{1,0:T(8,128)(2,1)} %hidden_any.3, bf16[2,8192]{1,0:T(2,128)(2,1)} %suffix_any.3, f32[1,8192]{1,0:T(1,128)} %bitcast.7), custom_call_target="tpu_custom_call" | custom-call | flops 2097152 | bytes 2097152 | tf_op jit(solution)/shard_map/norm_rows/pallas_call | solution.py:572
  3.2 4.1 %collective-permute-start = (bf16[1072,128]{1,0:T(8,128)(2,1)}, bf16[1072,128]{1,0:T(8,128)(2,1)S(1)}, u32[]{:S(2)}, u32[]{:S(2)}) collective-permute-start(bf16[1072,128]{1,0:T(8,128)(2,1)} %norm_rows.2), channel_id=1, source_target_pairs={{0,8},{1,9},{2,10},{3,11},{4,12},{5,13},{6,14},{7,15},{8,0},{9,1},... | collective-permute-start | bytes 823304 | tf_op jit(solution)/shard_map/ppermute | solution.py:551
  7.3 1.5 %collective-permute-start.1 = (bf16[1024,256]{1,0:T(8,128)(2,1)S(1)}, bf16[1024,256]{1,0:T(8,128)(2,1)S(1)}, u32[]{:S(2)}, u32[]{:S(2)}) collective-permute-start(bf16[1024,256]{1,0:T(8,128)(2,1)S(1)} %copy-done), channel_id=1, source_target_pairs={{0,2},{1,3},{2,0},{3,1},{4,6},{5,7},{6,4},{7,5},{8,10},{9,11},{10,... | collective-permute-start | bytes 1572872 | tf_op jit(solution)/shard_map/ppermute | solution.py:551
  9.3 2.7 %norm_rows.3 = (bf16[1072,128]{1,0:T(8,128)(2,1)}, bf16[1072,128]{1,0:T(8,128)(2,1)}, bf16[1072,128]{1,0:T(8,128)(2,1)}) custom-call(bf16[2,2048]{1,0:T(2,128)(2,1)} %query_any.3, bf16[128,8192]{1,0:T(8,128)(2,1)} %hidden_any.3, bf16[2,8192]{1,0:T(2,128)(2,1)} %suffix_any.3, f32[1,8192]{1,0:T(1,128)} %bitcast.8), custom_call_target="tpu_custom_call" | custom-call | flops 2097152 | bytes 2097152 | tf_op jit(solution)/shard_map/norm_rows/pallas_call | solution.py:572
  12.0 1.4 %collective-permute-start.6 = (bf16[1072,128]{1,0:T(8,128)(2,1)}, bf16[1072,128]{1,0:T(8,128)(2,1)S(1)}, u32[]{:S(2)}, u32[]{:S(2)}) collective-permute-start(bf16[1072,128]{1,0:T(8,128)(2,1)} %get-tuple-element.43), channel_id=1, source_target_pairs={{0,12},{1,13},{2,14},{3,15},{4,8},{5,9},{6,10},{7,11},{8,4},{9,5},... | collective-permute-start | bytes 823304 | tf_op jit(solution)/shard_map/ppermute | solution.py:551
  14.1 1.0 %fetch_own.1.refs_0_ = bf16[1072,128]{1,0:T(8,128)(2,1)S(1)} custom-call(bf16[1072,128]{1,0:T(8,128)(2,1)} %get-tuple-element.37.from_any), custom_call_target="tpu_custom_call" | custom-call | bytes 67108864 | tf_op jit(solution)/shard_map/fetch_own/pallas_call | solution.py:613
  15.2 11.5 %collective-permute-done.refs_2_ = bf16[1072,128]{1,0:T(8,128)(2,1)S(1)} collective-permute-done((bf16[1072,128]{1,0:T(8,128)(2,1)}, bf16[1072,128]{1,0:T(8,128)(2,1)S(1)}, u32[]{:S(2)}, u32[]{:S(2)}) %collective-permute-start) | collective-permute-done | bytes 274464 | tf_op jit(solution)/shard_map/ppermute | solution.py:551
  27.3 4.2 %collective-permute-done.8.refs_2_ = bf16[1072,128]{1,0:T(8,128)(2,1)S(1)} collective-permute-done((bf16[1072,128]{1,0:T(8,128)(2,1)}, bf16[1072,128]{1,0:T(8,128)(2,1)S(1)}, u32[]{:S(2)}, u32[]{:S(2)}) %collective-permute-start.8) | collective-permute-done | bytes 274464 | tf_op jit(solution)/shard_map/ppermute | solution.py:551
  32.8 3.1 %collective-permute-start.5 = (bf16[784,128]{1,0:T(8,128)(2,1)S(1)}, bf16[784,128]{1,0:T(8,128)(2,1)S(1)}, u32[]{:S(2)}, u32[]{:S(2)}) collective-permute-start(bf16[784,128]{1,0:T(8,128)(2,1)S(1)} %get-tuple-element.42), channel_id=1, source_target_pairs={{0,8},{1,9},{2,10},{3,11},{4,12},{5,13},{6,14},{7,15},{8,0},{9,1},... | collective-permute-start | bytes 602120 | tf_op jit(solution)/shard_map/ppermute | solution.py:551
  35.8 0.8 %project.3 = (bf16[784,128]{1,0:T(8,128)(2,1)S(1)}, bf16[784,128]{1,0:T(8,128)(2,1)S(1)}, bf16[128,128]{1,0:T(8,128)(2,1)S(1)}) custom-call(bf16[1072,128]{1,0:T(8,128)(2,1)S(1)} %collective-permute-done.6.refs_0_, bf16[1072,128]{1,0:T(8,128)(2,1)S(1)} %collective-permute-done.7.refs_1_, bf16[1072,128]{1,0:T(8,128)(2,1)S(1)} %collective-permute-done.8.refs_2_, ...), custom_call_target="tpu_custom_call" | custom-call | flops 536870912 | bytes 6291456 | tf_op jit(solution)/shard_map/project/pallas_call | solution.py:632
  36.6 1.0 %collective-permute-start.10 = (bf16[784,128]{1,0:T(8,128)(2,1)S(1)}, bf16[784,128]{1,0:T(8,128)(2,1)S(1)}, u32[]{:S(2)}, u32[]{:S(2)}) collective-permute-start(bf16[784,128]{1,0:T(8,128)(2,1)S(1)} %get-tuple-element.46), channel_id=1, source_target_pairs={{0,12},{1,13},{2,14},{3,15},{4,8},{5,9},{6,10},{7,11},{8,4},{9,5},... | collective-permute-start | bytes 602120 | tf_op jit(solution)/shard_map/ppermute | solution.py:551
  37.8 1.5 %collective-permute-start.12 = (bf16[128,128]{1,0:T(8,128)(2,1)S(1)}, bf16[128,128]{1,0:T(8,128)(2,1)S(1)}, u32[]{:S(2)}, u32[]{:S(2)}) collective-permute-start(bf16[128,128]{1,0:T(8,128)(2,1)S(1)} %get-tuple-element.50.refs_0_), channel_id=1, source_target_pairs={{0,2},{1,3},{2,0},{3,1},{4,6},{5,7},{6,4},{7,5},{8,10},{9,11},{10,... | collective-permute-start | bytes 98312 | tf_op jit(solution)/shard_map/ppermute | solution.py:551
  39.9 1.8 %collective-permute-done.12.refs_1_ = bf16[128,128]{1,0:T(8,128)(2,1)S(1)} collective-permute-done((bf16[128,128]{1,0:T(8,128)(2,1)S(1)}, bf16[128,128]{1,0:T(8,128)(2,1)S(1)}, u32[]{:S(2)}, u32[]{:S(2)}) %collective-permute-start.12) | collective-permute-done | bytes 32800 | tf_op jit(solution)/shard_map/ppermute | solution.py:551
  41.7 1.4 %loaded_attention.1 = (f32[256,128]{1,0:T(8,128)S(1)}, f32[256,128]{1,0:T(8,128)S(1)}, f32[256,128]{1,0:T(8,128)S(1)}, bf16[256,128]{1,0:T(8,128)(2,1)S(1)}) custom-call(s32[16]{0:T(128)S(1)} %copy-done.6, s32[1]{0:T(128)S(6)} %copy.15.split_ref, bf16[128,128]{1,0:T(8,128)(2,1)S(1)} %get-tuple-element.50.refs_0_, ...), custom_call_target="tpu_custom_call" | custom-call | flops 67108864 | bytes 524288 | tf_op jit(solution)/shard_map/loaded_attention/pallas_call | solution.py:673
  43.0 7.1 %collective-permute-done.5.other = bf16[784,128]{1,0:T(8,128)(2,1)S(1)} collective-permute-done((bf16[784,128]{1,0:T(8,128)(2,1)S(1)}, bf16[784,128]{1,0:T(8,128)(2,1)S(1)}, u32[]{:S(2)}, u32[]{:S(2)}) %collective-permute-start.5) | collective-permute-done | bytes 200736 | tf_op jit(solution)/shard_map/ppermute | solution.py:551
  50.2 1.9 %collective-permute-done.11.refs_1_ = bf16[784,128]{1,0:T(8,128)(2,1)S(1)} collective-permute-done((bf16[784,128]{1,0:T(8,128)(2,1)S(1)}, bf16[784,128]{1,0:T(8,128)(2,1)S(1)}, u32[]{:S(2)}, u32[]{:S(2)}) %collective-permute-start.11) | collective-permute-done | bytes 200736 | tf_op jit(solution)/shard_map/ppermute | solution.py:551
  52.1 1.6 %front_attention.1 = (bf16[128,256]{1,0:T(8,128)(2,1)}, bf16[128,256]{1,0:T(8,128)(2,1)}, f32[128,128]{1,0:T(8,128)S(1)}, bf16[128,128]{1,0:T(8,128)(2,1)S(1)}, ...) custom-call(s32[1]{0:T(128)S(6)} %copy.15.split_ref, f32[528,128]{1,0:T(8,128)S(1)} %sum_early.1.early, ...), custom_call_target="tpu_custom_call" | custom-call | flops 16777216 | bytes 2097152 | tf_op jit(solution)/shard_map/front_attention/pallas_call | solution.py:692
  53.7 2.9 %collective-permute-start.13 = (bf16[128,128]{1,0:T(8,128)(2,1)S(1)}, bf16[128,128]{1,0:T(8,128)(2,1)S(1)}, u32[]{:S(2)}, u32[]{:S(2)}) collective-permute-start(bf16[128,128]{1,0:T(8,128)(2,1)S(1)} %get-tuple-element.58), channel_id=1, source_target_pairs={{0,12},{1,13},{2,14},{3,15},{4,8},{5,9},{6,10},{7,11},{8,4},{9,5},... | collective-permute-start | bytes 98312 | tf_op jit(solution)/shard_map/ppermute | solution.py:551
  56.5 1.3 %collective-permute-start.14 = (bf16[128,128]{1,0:T(8,128)(2,1)S(1)}, bf16[128,128]{1,0:T(8,128)(2,1)S(1)}, u32[]{:S(2)}, u32[]{:S(2)}) collective-permute-start(bf16[128,128]{1,0:T(8,128)(2,1)S(1)} %get-tuple-element.59), channel_id=1, source_target_pairs={{0,8},{1,9},{2,10},{3,11},{4,12},{5,13},{6,14},{7,15},{8,0},{9,1},... | collective-permute-start | bytes 98312 | tf_op jit(solution)/shard_map/ppermute | solution.py:551
  58.3 1.1 %collective-permute-done.13.refs_0_ = bf16[128,128]{1,0:T(8,128)(2,1)S(1)} collective-permute-done((bf16[128,128]{1,0:T(8,128)(2,1)S(1)}, bf16[128,128]{1,0:T(8,128)(2,1)S(1)}, u32[]{:S(2)}, u32[]{:S(2)}) %collective-permute-start.13) | collective-permute-done | bytes 32800 | tf_op jit(solution)/shard_map/ppermute | solution.py:551
  59.4 2.0 %collective-permute-done.14.refs_1_ = bf16[128,128]{1,0:T(8,128)(2,1)S(1)} collective-permute-done((bf16[128,128]{1,0:T(8,128)(2,1)S(1)}, bf16[128,128]{1,0:T(8,128)(2,1)S(1)}, u32[]{:S(2)}, u32[]{:S(2)}) %collective-permute-start.14) | collective-permute-done | bytes 32800 | tf_op jit(solution)/shard_map/ppermute | solution.py:551
  62.0 1.5 %collective-permute-start.16 = (bf16[64,128]{1,0:T(8,128)(2,1)S(1)}, bf16[64,128]{1,0:T(8,128)(2,1)S(1)}, u32[]{:S(2)}, u32[]{:S(2)}) collective-permute-start(bf16[64,128]{1,0:T(8,128)(2,1)S(1)} %get-tuple-element.62), channel_id=1, source_target_pairs={{0,2},{1,3},{2,0},{3,1},{4,6},{5,7},{6,4},{7,5},{8,10},{9,11},{10,... | collective-permute-start | bytes 49160 | tf_op jit(solution)/shard_map/ppermute | solution.py:551
  63.6 2.2 %collective-permute-done.16.refs_0_ = bf16[64,128]{1,0:T(8,128)(2,1)S(1)} collective-permute-done((bf16[64,128]{1,0:T(8,128)(2,1)S(1)}, bf16[64,128]{1,0:T(8,128)(2,1)S(1)}, u32[]{:S(2)}, u32[]{:S(2)}) %collective-permute-start.16) | collective-permute-done | bytes 16416 | tf_op jit(solution)/shard_map/ppermute | solution.py:551
  65.8 0.8 %finish.1 = bf16[2,2048]{1,0:T(2,128)(2,1)} custom-call(f32[64,128]{1,0:T(8,128)S(1)} %get-tuple-element.61.kept, bf16[64,128]{1,0:T(8,128)(2,1)S(1)} %collective-permute-done.16.refs_0_), custom_call_target="tpu_custom_call" | custom-call | tf_op jit(solution)/shard_map/finish/pallas_call | solution.py:721
  (38 shorter events, 4.4 us)
Async XLA Ops:
  0.6 6.7 %copy-start = (bf16[1024,256]{1,0:T(8,128)(2,1)S(1)}, bf16[1024,256]{1,0:T(8,128)(2,1)}, u32[]{:S(2)}) copy-start(bf16[1024,256]{1,0:T(8,128)(2,1)} %refs_4_.3) | copy-start | bytes 1572868
  0.6 8.2 %copy-start.1 = (bf16[1024,256]{1,0:T(8,128)(2,1)S(1)}, bf16[1024,256]{1,0:T(8,128)(2,1)}, u32[]{:S(2)}) copy-start(bf16[1024,256]{1,0:T(8,128)(2,1)} %refs_5_.3) | copy-start | bytes 1572868
  3.2 23.5 %collective-permute-start = (bf16[1072,128]{1,0:T(8,128)(2,1)}, bf16[1072,128]{1,0:T(8,128)(2,1)S(1)}, u32[]{:S(2)}, u32[]{:S(2)}) collective-permute-start(bf16[1072,128]{1,0:T(8,128)(2,1)} %norm_rows.2), channel_id=1, source_target_pairs={{0,8},{1,9},{2,10},{3,11},{4,12},{5,13},{6,14},{7,15},{8,0},{9,1},... | collective-permute-start | bytes 823304 | tf_op jit(solution)/shard_map/ppermute | solution.py:551
  7.3 19.4 %collective-permute-start.1 = (bf16[1024,256]{1,0:T(8,128)(2,1)S(1)}, bf16[1024,256]{1,0:T(8,128)(2,1)S(1)}, u32[]{:S(2)}, u32[]{:S(2)}) collective-permute-start(bf16[1024,256]{1,0:T(8,128)(2,1)S(1)} %copy-done), channel_id=1, source_target_pairs={{0,2},{1,3},{2,0},{3,1},{4,6},{5,7},{6,4},{7,5},{8,10},{9,11},{10,... | collective-permute-start | bytes 1572872 | tf_op jit(solution)/shard_map/ppermute | solution.py:551
  8.8 23.1 %collective-permute-start.4 = (bf16[1024,256]{1,0:T(8,128)(2,1)S(1)}, bf16[1024,256]{1,0:T(8,128)(2,1)S(1)}, u32[]{:S(2)}, u32[]{:S(2)}) collective-permute-start(bf16[1024,256]{1,0:T(8,128)(2,1)S(1)} %copy-done.1), channel_id=1, source_target_pairs={{0,2},{1,3},{2,0},{3,1},{4,6},{5,7},{6,4},{7,5},{8,10},{9,11},{10,... | collective-permute-start | bytes 1572872 | tf_op jit(solution)/shard_map/ppermute | solution.py:551
  12.0 15.2 %collective-permute-start.6 = (bf16[1072,128]{1,0:T(8,128)(2,1)}, bf16[1072,128]{1,0:T(8,128)(2,1)S(1)}, u32[]{:S(2)}, u32[]{:S(2)}) collective-permute-start(bf16[1072,128]{1,0:T(8,128)(2,1)} %get-tuple-element.43), channel_id=1, source_target_pairs={{0,12},{1,13},{2,14},{3,15},{4,8},{5,9},{6,10},{7,11},{8,4},{9,5},... | collective-permute-start | bytes 823304 | tf_op jit(solution)/shard_map/ppermute | solution.py:551
  13.4 18.0 %collective-permute-start.8 = (bf16[1072,128]{1,0:T(8,128)(2,1)}, bf16[1072,128]{1,0:T(8,128)(2,1)S(1)}, u32[]{:S(2)}, u32[]{:S(2)}) collective-permute-start(bf16[1072,128]{1,0:T(8,128)(2,1)} %get-tuple-element.44), channel_id=1, source_target_pairs={{0,4},{1,5},{2,6},{3,7},{4,0},{5,1},{6,2},{7,3},{8,12},{9,13},{10,... | collective-permute-start | bytes 823304 | tf_op jit(solution)/shard_map/ppermute | solution.py:551
  26.7 5.2 %collective-permute-start.3 = (bf16[1072,128]{1,0:T(8,128)(2,1)S(1)}, bf16[1072,128]{1,0:T(8,128)(2,1)S(1)}, u32[]{:S(2)}, u32[]{:S(2)}) collective-permute-start(bf16[1072,128]{1,0:T(8,128)(2,1)S(1)} %collective-permute-done.refs_2_), channel_id=1, source_target_pairs={{0,1},{1,0},{2,3},{3,2},{4,5},{5,4},{6,7},{7,6},{8,9},{9,8},{10,11... | collective-permute-start | bytes 823304 | tf_op jit(solution)/shard_map/ppermute | solution.py:551
  26.7 5.2 %collective-permute-start.2 = (bf16[1072,128]{1,0:T(8,128)(2,1)}, bf16[1072,128]{1,0:T(8,128)(2,1)S(1)}, u32[]{:S(2)}, u32[]{:S(2)}) collective-permute-start(bf16[1072,128]{1,0:T(8,128)(2,1)} %get-tuple-element.37.from_any), channel_id=1, source_target_pairs={{0,1},{1,0},{2,3},{3,2},{4,5},{5,4},{6,7},{7,6},{8,9},{9,8},{10,11... | collective-permute-start | bytes 823304 | tf_op jit(solution)/shard_map/ppermute | solution.py:551
  27.2 8.6 %collective-permute-start.7 = (bf16[1072,128]{1,0:T(8,128)(2,1)S(1)}, bf16[1072,128]{1,0:T(8,128)(2,1)S(1)}, u32[]{:S(2)}, u32[]{:S(2)}) collective-permute-start(bf16[1072,128]{1,0:T(8,128)(2,1)S(1)} %collective-permute-done.6.refs_0_), channel_id=1, source_target_pairs={{0,1},{1,0},{2,3},{3,2},{4,5},{5,4},{6,7},{7,6},{8,9},{9,8},{10,11... | collective-permute-start | bytes 823304 | tf_op jit(solution)/shard_map/ppermute | solution.py:551
  31.5 4.4 %collective-permute-start.9 = (bf16[1072,128]{1,0:T(8,128)(2,1)S(1)}, bf16[1072,128]{1,0:T(8,128)(2,1)S(1)}, u32[]{:S(2)}, u32[]{:S(2)}) collective-permute-start(bf16[1072,128]{1,0:T(8,128)(2,1)S(1)} %collective-permute-done.8.refs_2_), channel_id=1, source_target_pairs={{0,1},{1,0},{2,3},{3,2},{4,5},{5,4},{6,7},{7,6},{8,9},{9,8},{10,11... | collective-permute-start | bytes 823304 | tf_op jit(solution)/shard_map/ppermute | solution.py:551
  32.7 9.0 %copy-start.2 = (bf16[4,128,256]{2,1,0:T(8,128)(2,1)S(1)}, bf16[4,128,256]{2,1,0:T(8,128)(2,1)}, u32[]{:S(2)}) copy-start(bf16[4,128,256]{2,1,0:T(8,128)(2,1)} %refs_2_.1) | copy-start | bytes 786436
  32.7 9.0 %copy-start.3 = (bf16[4,128,256]{2,1,0:T(8,128)(2,1)S(1)}, bf16[4,128,256]{2,1,0:T(8,128)(2,1)}, u32[]{:S(2)}) copy-start(bf16[4,128,256]{2,1,0:T(8,128)(2,1)} %refs_3_.1) | copy-start | bytes 786436
  32.7 8.9 %copy-start.6 = (s32[16]{0:T(128)S(1)}, s32[16]{0:T(128)}, u32[]{:S(2)}) copy-start(s32[16]{0:T(128)} %table_ref.1) | copy-start | bytes 196
  32.8 17.4 %copy-start.4 = (f32[256]{0:T(256)S(1)}, f32[256]{0:T(256)}, u32[]{:S(2)}) copy-start(f32[256]{0:T(256)} %param.17) | copy-start | bytes 3076
  32.8 17.4 %copy-start.5 = (f32[256]{0:T(256)S(1)}, f32[256]{0:T(256)}, u32[]{:S(2)}) copy-start(f32[256]{0:T(256)} %param.18) | copy-start | bytes 3076
  32.8 17.4 %collective-permute-start.5 = (bf16[784,128]{1,0:T(8,128)(2,1)S(1)}, bf16[784,128]{1,0:T(8,128)(2,1)S(1)}, u32[]{:S(2)}, u32[]{:S(2)}) collective-permute-start(bf16[784,128]{1,0:T(8,128)(2,1)S(1)} %get-tuple-element.42), channel_id=1, source_target_pairs={{0,8},{1,9},{2,10},{3,11},{4,12},{5,13},{6,14},{7,15},{8,0},{9,1},... | collective-permute-start | bytes 602120 | tf_op jit(solution)/shard_map/ppermute | solution.py:551
  36.6 13.6 %collective-permute-start.10 = (bf16[784,128]{1,0:T(8,128)(2,1)S(1)}, bf16[784,128]{1,0:T(8,128)(2,1)S(1)}, u32[]{:S(2)}, u32[]{:S(2)}) collective-permute-start(bf16[784,128]{1,0:T(8,128)(2,1)S(1)} %get-tuple-element.46), channel_id=1, source_target_pairs={{0,12},{1,13},{2,14},{3,15},{4,8},{5,9},{6,10},{7,11},{8,4},{9,5},... | collective-permute-start | bytes 602120 | tf_op jit(solution)/shard_map/ppermute | solution.py:551
  37.6 14.5 %collective-permute-start.11 = (bf16[784,128]{1,0:T(8,128)(2,1)S(1)}, bf16[784,128]{1,0:T(8,128)(2,1)S(1)}, u32[]{:S(2)}, u32[]{:S(2)}) collective-permute-start(bf16[784,128]{1,0:T(8,128)(2,1)S(1)} %get-tuple-element.47), channel_id=1, source_target_pairs={{0,4},{1,5},{2,6},{3,7},{4,0},{5,1},{6,2},{7,3},{8,12},{9,13},{10,... | collective-permute-start | bytes 602120 | tf_op jit(solution)/shard_map/ppermute | solution.py:551
  37.8 3.9 %collective-permute-start.12 = (bf16[128,128]{1,0:T(8,128)(2,1)S(1)}, bf16[128,128]{1,0:T(8,128)(2,1)S(1)}, u32[]{:S(2)}, u32[]{:S(2)}) collective-permute-start(bf16[128,128]{1,0:T(8,128)(2,1)S(1)} %get-tuple-element.50.refs_0_), channel_id=1, source_target_pairs={{0,2},{1,3},{2,0},{3,1},{4,6},{5,7},{6,4},{7,5},{8,10},{9,11},{10,... | collective-permute-start | bytes 98312 | tf_op jit(solution)/shard_map/ppermute | solution.py:551
  53.7 5.8 %collective-permute-start.13 = (bf16[128,128]{1,0:T(8,128)(2,1)S(1)}, bf16[128,128]{1,0:T(8,128)(2,1)S(1)}, u32[]{:S(2)}, u32[]{:S(2)}) collective-permute-start(bf16[128,128]{1,0:T(8,128)(2,1)S(1)} %get-tuple-element.58), channel_id=1, source_target_pairs={{0,12},{1,13},{2,14},{3,15},{4,8},{5,9},{6,10},{7,11},{8,4},{9,5},... | collective-permute-start | bytes 98312 | tf_op jit(solution)/shard_map/ppermute | solution.py:551
  56.5 4.9 %collective-permute-start.14 = (bf16[128,128]{1,0:T(8,128)(2,1)S(1)}, bf16[128,128]{1,0:T(8,128)(2,1)S(1)}, u32[]{:S(2)}, u32[]{:S(2)}) collective-permute-start(bf16[128,128]{1,0:T(8,128)(2,1)S(1)} %get-tuple-element.59), channel_id=1, source_target_pairs={{0,8},{1,9},{2,10},{3,11},{4,12},{5,13},{6,14},{7,15},{8,0},{9,1},... | collective-permute-start | bytes 98312 | tf_op jit(solution)/shard_map/ppermute | solution.py:551
  57.8 3.9 %collective-permute-start.15 = (bf16[128,128]{1,0:T(8,128)(2,1)S(1)}, bf16[128,128]{1,0:T(8,128)(2,1)S(1)}, u32[]{:S(2)}, u32[]{:S(2)}) collective-permute-start(bf16[128,128]{1,0:T(8,128)(2,1)S(1)} %get-tuple-element.60), channel_id=1, source_target_pairs={{0,4},{1,5},{2,6},{3,7},{4,0},{5,1},{6,2},{7,3},{8,12},{9,13},{10,... | collective-permute-start | bytes 98312 | tf_op jit(solution)/shard_map/ppermute | solution.py:551
  62.0 3.8 %collective-permute-start.16 = (bf16[64,128]{1,0:T(8,128)(2,1)S(1)}, bf16[64,128]{1,0:T(8,128)(2,1)S(1)}, u32[]{:S(2)}, u32[]{:S(2)}) collective-permute-start(bf16[64,128]{1,0:T(8,128)(2,1)S(1)} %get-tuple-element.62), channel_id=1, source_target_pairs={{0,2},{1,3},{2,0},{3,1},{4,6},{5,7},{6,4},{7,5},{8,10},{9,11},{10,... | collective-permute-start | bytes 49160 | tf_op jit(solution)/shard_map/ppermute | solution.py:551

commit v11 on v9

--- a/solution.py
+++ b/solution.py
@@ -578,7 +578,8 @@
         )(suffix_query_rows, hidden, suffix_hidden, norm_gain.reshape(1, features))
         blocks.update(zip(shifts, found))
     own = blocks[0]
-    *weights, blocks[2] = lax.optimization_barrier((key_matrix, value_matrix, blocks[2]))
+    late, blocks[2] = lax.optimization_barrier((value_matrix, blocks[2]))
+    weights = (key_matrix, late)
     far = [move(matrix, beside) for matrix in weights]
 
     mine = {s: move(blocks[s], along(s)) for s in far_first()}

time: 66.8 us -> 66.8 us (level)
  no operation moved by 1% of the time
where the time goes in v11:
time: 66.8 us; the launch traced here: 66.6 us
  waiting for transfers between devices  32.6 us (49%)
  starting transfers between devices  20.3 us (30%)
  Pallas kernels  11.8 us (18%)
  between operations  1.44 us (2%)
    ppermute x17, waiting for transfers between devices, move(): return lax.ppermute(array, ('ctx', 'tp'), pairs)  32.6 us
    ppermute x17, starting transfers between devices, move(): return lax.ppermute(array, ('ctx', 'tp'), pairs)  20.3 us
    pallas_call x2, Pallas kernels, exchange_plan(): pl.pallas_call(functools.partial(norm_kernel, shifts), in_specs=[hbm] * 4...  5.22 us
    pallas_call x2, Pallas kernels, exchange_plan(): pl.pallas_call(functools.partial(project_kernel, shifts), in_specs=[vmem]...  1.57 us
    pallas_call x1, Pallas kernels, exchange_plan(): pl.pallas_call(front_kernel, in_specs=[smem] + [vmem] * (GROUPS + 7), out...  1.55 us
    pallas_call x1, Pallas kernels, exchange_plan(): pl.pallas_call(loaded_kernel, in_specs=[smem, smem] + [vmem] * (PAIR + 2)...  1.35 us
  transfers between devices with their start and end apart: 17, of which 10 were waited for; matrix products, arithmetic and copies ran while one was open for 1% of the time, Pallas kernels for 10%

profile of v11, /device:TPU:0, one launch (start us, length us, event | category | flops | bytes accessed | tf_op | source)
XLA Modules:
  0.0 66.6 jit_solution(10090983955570938731)
XLA Ops:
  0.7 2.5 %norm_rows.2 = bf16[1072,128]{1,0:T(8,128)(2,1)} custom-call(bf16[2,2048]{1,0:T(2,128)(2,1)} %query_any.3, bf16[128,8192]{1,0:T(8,128)(2,1)} %hidden_any.3, bf16[2,8192]{1,0:T(2,128)(2,1)} %suffix_any.3, f32[1,8192]{1,0:T(1,128)} %bitcast.5), custom_call_target="tpu_custom_call" | custom-call | flops 2097152 | bytes 2097152 | tf_op jit(solution)/shard_map/norm_rows/pallas_call | solution.py:557
  3.2 4.1 %collective-permute-start = (bf16[1072,128]{1,0:T(8,128)(2,1)}, bf16[1072,128]{1,0:T(8,128)(2,1)S(1)}, u32[]{:S(2)}, u32[]{:S(2)}) collective-permute-start(bf16[1072,128]{1,0:T(8,128)(2,1)} %norm_rows.2), channel_id=1, source_target_pairs={{0,8},{1,9},{2,10},{3,11},{4,12},{5,13},{6,14},{7,15},{8,0},{9,1},... | collective-permute-start | bytes 823304 | tf_op jit(solution)/shard_map/ppermute | solution.py:536
  7.3 1.5 %collective-permute-start.1 = (bf16[1024,256]{1,0:T(8,128)(2,1)S(1)}, bf16[1024,256]{1,0:T(8,128)(2,1)S(1)}, u32[]{:S(2)}, u32[]{:S(2)}) collective-permute-start(bf16[1024,256]{1,0:T(8,128)(2,1)S(1)} %copy-done), channel_id=1, source_target_pairs={{0,2},{1,3},{2,0},{3,1},{4,6},{5,7},{6,4},{7,5},{8,10},{9,11},{10,... | collective-permute-start | bytes 1572872 | tf_op jit(solution)/shard_map/ppermute | solution.py:536
  9.3 2.7 %norm_rows.3 = (bf16[1072,128]{1,0:T(8,128)(2,1)}, bf16[1072,128]{1,0:T(8,128)(2,1)}, bf16[1072,128]{1,0:T(8,128)(2,1)}) custom-call(bf16[2,2048]{1,0:T(2,128)(2,1)} %query_any.3, bf16[128,8192]{1,0:T(8,128)(2,1)} %hidden_any.3, bf16[2,8192]{1,0:T(2,128)(2,1)} %suffix_any.3, f32[1,8192]{1,0:T(1,128)} %bitcast.6), custom_call_target="tpu_custom_call" | custom-call | flops 2097152 | bytes 2097152 | tf_op jit(solution)/shard_map/norm_rows/pallas_call | solution.py:557
  12.0 1.4 %collective-permute-start.6 = (bf16[1072,128]{1,0:T(8,128)(2,1)}, bf16[1072,128]{1,0:T(8,128)(2,1)S(1)}, u32[]{:S(2)}, u32[]{:S(2)}) collective-permute-start(bf16[1072,128]{1,0:T(8,128)(2,1)} %get-tuple-element.41), channel_id=1, source_target_pairs={{0,12},{1,13},{2,14},{3,15},{4,8},{5,9},{6,10},{7,11},{8,4},{9,5},... | collective-permute-start | bytes 823304 | tf_op jit(solution)/shard_map/ppermute | solution.py:536
  14.1 1.0 %fetch_own.1.refs_0_ = bf16[1072,128]{1,0:T(8,128)(2,1)S(1)} custom-call(bf16[1072,128]{1,0:T(8,128)(2,1)} %get-tuple-element.35.from_any), custom_call_target="tpu_custom_call" | custom-call | bytes 67108864 | tf_op jit(solution)/shard_map/fetch_own/pallas_call | solution.py:599
  15.2 11.5 %collective-permute-done.refs_2_ = bf16[1072,128]{1,0:T(8,128)(2,1)S(1)} collective-permute-done((bf16[1072,128]{1,0:T(8,128)(2,1)}, bf16[1072,128]{1,0:T(8,128)(2,1)S(1)}, u32[]{:S(2)}, u32[]{:S(2)}) %collective-permute-start) | collective-permute-done | bytes 274464 | tf_op jit(solution)/shard_map/ppermute | solution.py:536
  27.3 4.2 %collective-permute-done.8.refs_2_ = bf16[1072,128]{1,0:T(8,128)(2,1)S(1)} collective-permute-done((bf16[1072,128]{1,0:T(8,128)(2,1)}, bf16[1072,128]{1,0:T(8,128)(2,1)S(1)}, u32[]{:S(2)}, u32[]{:S(2)}) %collective-permute-start.8) | collective-permute-done | bytes 274464 | tf_op jit(solution)/shard_map/ppermute | solution.py:536
  32.8 3.1 %collective-permute-start.5 = (bf16[784,128]{1,0:T(8,128)(2,1)S(1)}, bf16[784,128]{1,0:T(8,128)(2,1)S(1)}, u32[]{:S(2)}, u32[]{:S(2)}) collective-permute-start(bf16[784,128]{1,0:T(8,128)(2,1)S(1)} %get-tuple-element.40), channel_id=1, source_target_pairs={{0,8},{1,9},{2,10},{3,11},{4,12},{5,13},{6,14},{7,15},{8,0},{9,1},... | collective-permute-start | bytes 602120 | tf_op jit(solution)/shard_map/ppermute | solution.py:536
  35.8 0.8 %project.3 = (bf16[784,128]{1,0:T(8,128)(2,1)S(1)}, bf16[784,128]{1,0:T(8,128)(2,1)S(1)}, bf16[128,128]{1,0:T(8,128)(2,1)S(1)}) custom-call(bf16[1072,128]{1,0:T(8,128)(2,1)S(1)} %collective-permute-done.6.refs_0_, bf16[1072,128]{1,0:T(8,128)(2,1)S(1)} %collective-permute-done.7.refs_1_, bf16[1072,128]{1,0:T(8,128)(2,1)S(1)} %collective-permute-done.8.refs_2_, ...), custom_call_target="tpu_custom_call" | custom-call | flops 536870912 | bytes 6291456 | tf_op jit(solution)/shard_map/project/pallas_call | solution.py:618
  36.6 1.0 %collective-permute-start.10 = (bf16[784,128]{1,0:T(8,128)(2,1)S(1)}, bf16[784,128]{1,0:T(8,128)(2,1)S(1)}, u32[]{:S(2)}, u32[]{:S(2)}) collective-permute-start(bf16[784,128]{1,0:T(8,128)(2,1)S(1)} %get-tuple-element.44), channel_id=1, source_target_pairs={{0,12},{1,13},{2,14},{3,15},{4,8},{5,9},{6,10},{7,11},{8,4},{9,5},... | collective-permute-start | bytes 602120 | tf_op jit(solution)/shard_map/ppermute | solution.py:536
  37.8 1.5 %collective-permute-start.12 = (bf16[128,128]{1,0:T(8,128)(2,1)S(1)}, bf16[128,128]{1,0:T(8,128)(2,1)S(1)}, u32[]{:S(2)}, u32[]{:S(2)}) collective-permute-start(bf16[128,128]{1,0:T(8,128)(2,1)S(1)} %get-tuple-element.48.refs_0_), channel_id=1, source_target_pairs={{0,2},{1,3},{2,0},{3,1},{4,6},{5,7},{6,4},{7,5},{8,10},{9,11},{10,... | collective-permute-start | bytes 98312 | tf_op jit(solution)/shard_map/ppermute | solution.py:536
  39.9 1.8 %collective-permute-done.12.refs_1_ = bf16[128,128]{1,0:T(8,128)(2,1)S(1)} collective-permute-done((bf16[128,128]{1,0:T(8,128)(2,1)S(1)}, bf16[128,128]{1,0:T(8,128)(2,1)S(1)}, u32[]{:S(2)}, u32[]{:S(2)}) %collective-permute-start.12) | collective-permute-done | bytes 32800 | tf_op jit(solution)/shard_map/ppermute | solution.py:536
  41.7 1.4 %loaded_attention.1 = (f32[256,128]{1,0:T(8,128)S(1)}, f32[256,128]{1,0:T(8,128)S(1)}, f32[256,128]{1,0:T(8,128)S(1)}, bf16[256,128]{1,0:T(8,128)(2,1)S(1)}) custom-call(s32[16]{0:T(128)S(1)} %copy-done.6, s32[1]{0:T(128)S(6)} %copy.15.split_ref, bf16[128,128]{1,0:T(8,128)(2,1)S(1)} %get-tuple-element.48.refs_0_, ...), custom_call_target="tpu_custom_call" | custom-call | flops 67108864 | bytes 524288 | tf_op jit(solution)/shard_map/loaded_attention/pallas_call | solution.py:658
  43.1 7.1 %collective-permute-done.5.other = bf16[784,128]{1,0:T(8,128)(2,1)S(1)} collective-permute-done((bf16[784,128]{1,0:T(8,128)(2,1)S(1)}, bf16[784,128]{1,0:T(8,128)(2,1)S(1)}, u32[]{:S(2)}, u32[]{:S(2)}) %collective-permute-start.5) | collective-permute-done | bytes 200736 | tf_op jit(solution)/shard_map/ppermute | solution.py:536
  50.2 1.9 %collective-permute-done.11.refs_1_ = bf16[784,128]{1,0:T(8,128)(2,1)S(1)} collective-permute-done((bf16[784,128]{1,0:T(8,128)(2,1)S(1)}, bf16[784,128]{1,0:T(8,128)(2,1)S(1)}, u32[]{:S(2)}, u32[]{:S(2)}) %collective-permute-start.11) | collective-permute-done | bytes 200736 | tf_op jit(solution)/shard_map/ppermute | solution.py:536
  52.1 1.6 %front_attention.1 = (bf16[128,256]{1,0:T(8,128)(2,1)}, bf16[128,256]{1,0:T(8,128)(2,1)}, f32[128,128]{1,0:T(8,128)S(1)}, bf16[128,128]{1,0:T(8,128)(2,1)S(1)}, ...) custom-call(s32[1]{0:T(128)S(6)} %copy.15.split_ref, f32[784,128]{1,0:T(8,128)S(1)} %sum_early.1.early, ...), custom_call_target="tpu_custom_call" | custom-call | flops 16777216 | bytes 2097152 | tf_op jit(solution)/shard_map/front_attention/pallas_call | solution.py:677
  53.7 2.9 %collective-permute-start.13 = (bf16[128,128]{1,0:T(8,128)(2,1)S(1)}, bf16[128,128]{1,0:T(8,128)(2,1)S(1)}, u32[]{:S(2)}, u32[]{:S(2)}) collective-permute-start(bf16[128,128]{1,0:T(8,128)(2,1)S(1)} %get-tuple-element.56), channel_id=1, source_target_pairs={{0,12},{1,13},{2,14},{3,15},{4,8},{5,9},{6,10},{7,11},{8,4},{9,5},... | collective-permute-start | bytes 98312 | tf_op jit(solution)/shard_map/ppermute | solution.py:536
  56.5 1.3 %collective-permute-start.14 = (bf16[128,128]{1,0:T(8,128)(2,1)S(1)}, bf16[128,128]{1,0:T(8,128)(2,1)S(1)}, u32[]{:S(2)}, u32[]{:S(2)}) collective-permute-start(bf16[128,128]{1,0:T(8,128)(2,1)S(1)} %get-tuple-element.57), channel_id=1, source_target_pairs={{0,8},{1,9},{2,10},{3,11},{4,12},{5,13},{6,14},{7,15},{8,0},{9,1},... | collective-permute-start | bytes 98312 | tf_op jit(solution)/shard_map/ppermute | solution.py:536
  58.3 1.1 %collective-permute-done.13.refs_0_ = bf16[128,128]{1,0:T(8,128)(2,1)S(1)} collective-permute-done((bf16[128,128]{1,0:T(8,128)(2,1)S(1)}, bf16[128,128]{1,0:T(8,128)(2,1)S(1)}, u32[]{:S(2)}, u32[]{:S(2)}) %collective-permute-start.13) | collective-permute-done | bytes 32800 | tf_op jit(solution)/shard_map/ppermute | solution.py:536
  59.4 1.9 %collective-permute-done.14.refs_1_ = bf16[128,128]{1,0:T(8,128)(2,1)S(1)} collective-permute-done((bf16[128,128]{1,0:T(8,128)(2,1)S(1)}, bf16[128,128]{1,0:T(8,128)(2,1)S(1)}, u32[]{:S(2)}, u32[]{:S(2)}) %collective-permute-start.14) | collective-permute-done | bytes 32800 | tf_op jit(solution)/shard_map/ppermute | solution.py:536
  62.0 1.5 %collective-permute-start.16 = (bf16[64,128]{1,0:T(8,128)(2,1)S(1)}, bf16[64,128]{1,0:T(8,128)(2,1)S(1)}, u32[]{:S(2)}, u32[]{:S(2)}) collective-permute-start(bf16[64,128]{1,0:T(8,128)(2,1)S(1)} %get-tuple-element.60), channel_id=1, source_target_pairs={{0,2},{1,3},{2,0},{3,1},{4,6},{5,7},{6,4},{7,5},{8,10},{9,11},{10,... | collective-permute-start | bytes 49160 | tf_op jit(solution)/shard_map/ppermute | solution.py:536
  63.5 2.2 %collective-permute-done.16.refs_0_ = bf16[64,128]{1,0:T(8,128)(2,1)S(1)} collective-permute-done((bf16[64,128]{1,0:T(8,128)(2,1)S(1)}, bf16[64,128]{1,0:T(8,128)(2,1)S(1)}, u32[]{:S(2)}, u32[]{:S(2)}) %collective-permute-start.16) | collective-permute-done | bytes 16416 | tf_op jit(solution)/shard_map/ppermute | solution.py:536
  65.8 0.8 %finish.1 = bf16[2,2048]{1,0:T(2,128)(2,1)} custom-call(f32[64,128]{1,0:T(8,128)S(1)} %get-tuple-element.59.kept, bf16[64,128]{1,0:T(8,128)(2,1)S(1)} %collective-permute-done.16.refs_0_), custom_call_target="tpu_custom_call" | custom-call | tf_op jit(solution)/shard_map/finish/pallas_call | solution.py:707
  (38 shorter events, 4.4 us)
Async XLA Ops:
  0.6 8.2 %copy-start.1 = (bf16[1024,256]{1,0:T(8,128)(2,1)S(1)}, bf16[1024,256]{1,0:T(8,128)(2,1)}, u32[]{:S(2)}) copy-start(bf16[1024,256]{1,0:T(8,128)(2,1)} %refs_5_.3) | copy-start | bytes 1572868
  0.6 6.7 %copy-start = (bf16[1024,256]{1,0:T(8,128)(2,1)S(1)}, bf16[1024,256]{1,0:T(8,128)(2,1)}, u32[]{:S(2)}) copy-start(bf16[1024,256]{1,0:T(8,128)(2,1)} %refs_4_.3) | copy-start | bytes 1572868
  3.2 23.5 %collective-permute-start = (bf16[1072,128]{1,0:T(8,128)(2,1)}, bf16[1072,128]{1,0:T(8,128)(2,1)S(1)}, u32[]{:S(2)}, u32[]{:S(2)}) collective-permute-start(bf16[1072,128]{1,0:T(8,128)(2,1)} %norm_rows.2), channel_id=1, source_target_pairs={{0,8},{1,9},{2,10},{3,11},{4,12},{5,13},{6,14},{7,15},{8,0},{9,1},... | collective-permute-start | bytes 823304 | tf_op jit(solution)/shard_map/ppermute | solution.py:536
  7.3 19.4 %collective-permute-start.1 = (bf16[1024,256]{1,0:T(8,128)(2,1)S(1)}, bf16[1024,256]{1,0:T(8,128)(2,1)S(1)}, u32[]{:S(2)}, u32[]{:S(2)}) collective-permute-start(bf16[1024,256]{1,0:T(8,128)(2,1)S(1)} %copy-done), channel_id=1, source_target_pairs={{0,2},{1,3},{2,0},{3,1},{4,6},{5,7},{6,4},{7,5},{8,10},{9,11},{10,... | collective-permute-start | bytes 1572872 | tf_op jit(solution)/shard_map/ppermute | solution.py:536
  8.8 23.1 %collective-permute-start.4 = (bf16[1024,256]{1,0:T(8,128)(2,1)S(1)}, bf16[1024,256]{1,0:T(8,128)(2,1)S(1)}, u32[]{:S(2)}, u32[]{:S(2)}) collective-permute-start(bf16[1024,256]{1,0:T(8,128)(2,1)S(1)} %copy-done.1), channel_id=1, source_target_pairs={{0,2},{1,3},{2,0},{3,1},{4,6},{5,7},{6,4},{7,5},{8,10},{9,11},{10,... | collective-permute-start | bytes 1572872 | tf_op jit(solution)/shard_map/ppermute | solution.py:536
  12.0 15.2 %collective-permute-start.6 = (bf16[1072,128]{1,0:T(8,128)(2,1)}, bf16[1072,128]{1,0:T(8,128)(2,1)S(1)}, u32[]{:S(2)}, u32[]{:S(2)}) collective-permute-start(bf16[1072,128]{1,0:T(8,128)(2,1)} %get-tuple-element.41), channel_id=1, source_target_pairs={{0,12},{1,13},{2,14},{3,15},{4,8},{5,9},{6,10},{7,11},{8,4},{9,5},... | collective-permute-start | bytes 823304 | tf_op jit(solution)/shard_map/ppermute | solution.py:536
  13.4 18.0 %collective-permute-start.8 = (bf16[1072,128]{1,0:T(8,128)(2,1)}, bf16[1072,128]{1,0:T(8,128)(2,1)S(1)}, u32[]{:S(2)}, u32[]{:S(2)}) collective-permute-start(bf16[1072,128]{1,0:T(8,128)(2,1)} %get-tuple-element.42), channel_id=1, source_target_pairs={{0,4},{1,5},{2,6},{3,7},{4,0},{5,1},{6,2},{7,3},{8,12},{9,13},{10,... | collective-permute-start | bytes 823304 | tf_op jit(solution)/shard_map/ppermute | solution.py:536
  26.7 5.2 %collective-permute-start.3 = (bf16[1072,128]{1,0:T(8,128)(2,1)S(1)}, bf16[1072,128]{1,0:T(8,128)(2,1)S(1)}, u32[]{:S(2)}, u32[]{:S(2)}) collective-permute-start(bf16[1072,128]{1,0:T(8,128)(2,1)S(1)} %collective-permute-done.refs_2_), channel_id=1, source_target_pairs={{0,1},{1,0},{2,3},{3,2},{4,5},{5,4},{6,7},{7,6},{8,9},{9,8},{10,11... | collective-permute-start | bytes 823304 | tf_op jit(solution)/shard_map/ppermute | solution.py:536
  26.7 5.2 %collective-permute-start.2 = (bf16[1072,128]{1,0:T(8,128)(2,1)}, bf16[1072,128]{1,0:T(8,128)(2,1)S(1)}, u32[]{:S(2)}, u32[]{:S(2)}) collective-permute-start(bf16[1072,128]{1,0:T(8,128)(2,1)} %get-tuple-element.35.from_any), channel_id=1, source_target_pairs={{0,1},{1,0},{2,3},{3,2},{4,5},{5,4},{6,7},{7,6},{8,9},{9,8},{10,11... | collective-permute-start | bytes 823304 | tf_op jit(solution)/shard_map/ppermute | solution.py:536
  27.2 8.6 %collective-permute-start.7 = (bf16[1072,128]{1,0:T(8,128)(2,1)S(1)}, bf16[1072,128]{1,0:T(8,128)(2,1)S(1)}, u32[]{:S(2)}, u32[]{:S(2)}) collective-permute-start(bf16[1072,128]{1,0:T(8,128)(2,1)S(1)} %collective-permute-done.6.refs_0_), channel_id=1, source_target_pairs={{0,1},{1,0},{2,3},{3,2},{4,5},{5,4},{6,7},{7,6},{8,9},{9,8},{10,11... | collective-permute-start | bytes 823304 | tf_op jit(solution)/shard_map/ppermute | solution.py:536
  31.5 4.4 %collective-permute-start.9 = (bf16[1072,128]{1,0:T(8,128)(2,1)S(1)}, bf16[1072,128]{1,0:T(8,128)(2,1)S(1)}, u32[]{:S(2)}, u32[]{:S(2)}) collective-permute-start(bf16[1072,128]{1,0:T(8,128)(2,1)S(1)} %collective-permute-done.8.refs_2_), channel_id=1, source_target_pairs={{0,1},{1,0},{2,3},{3,2},{4,5},{5,4},{6,7},{7,6},{8,9},{9,8},{10,11... | collective-permute-start | bytes 823304 | tf_op jit(solution)/shard_map/ppermute | solution.py:536
  32.7 9.0 %copy-start.2 = (bf16[4,128,256]{2,1,0:T(8,128)(2,1)S(1)}, bf16[4,128,256]{2,1,0:T(8,128)(2,1)}, u32[]{:S(2)}) copy-start(bf16[4,128,256]{2,1,0:T(8,128)(2,1)} %refs_2_.1) | copy-start | bytes 786436
  32.7 9.0 %copy-start.3 = (bf16[4,128,256]{2,1,0:T(8,128)(2,1)S(1)}, bf16[4,128,256]{2,1,0:T(8,128)(2,1)}, u32[]{:S(2)}) copy-start(bf16[4,128,256]{2,1,0:T(8,128)(2,1)} %refs_3_.1) | copy-start | bytes 786436
  32.7 9.0 %copy-start.6 = (s32[16]{0:T(128)S(1)}, s32[16]{0:T(128)}, u32[]{:S(2)}) copy-start(s32[16]{0:T(128)} %table_ref.1) | copy-start | bytes 196
  32.8 17.4 %collective-permute-start.5 = (bf16[784,128]{1,0:T(8,128)(2,1)S(1)}, bf16[784,128]{1,0:T(8,128)(2,1)S(1)}, u32[]{:S(2)}, u32[]{:S(2)}) collective-permute-start(bf16[784,128]{1,0:T(8,128)(2,1)S(1)} %get-tuple-element.40), channel_id=1, source_target_pairs={{0,8},{1,9},{2,10},{3,11},{4,12},{5,13},{6,14},{7,15},{8,0},{9,1},... | collective-permute-start | bytes 602120 | tf_op jit(solution)/shard_map/ppermute | solution.py:536
  35.8 16.3 %copy-start.4 = (f32[256]{0:T(256)S(1)}, f32[256]{0:T(256)}, u32[]{:S(2)}) copy-start(f32[256]{0:T(256)} %param.17) | copy-start | bytes 3076
  35.8 16.3 %copy-start.5 = (f32[256]{0:T(256)S(1)}, f32[256]{0:T(256)}, u32[]{:S(2)}) copy-start(f32[256]{0:T(256)} %param.18) | copy-start | bytes 3076
  36.6 13.5 %collective-permute-start.10 = (bf16[784,128]{1,0:T(8,128)(2,1)S(1)}, bf16[784,128]{1,0:T(8,128)(2,1)S(1)}, u32[]{:S(2)}, u32[]{:S(2)}) collective-permute-start(bf16[784,128]{1,0:T(8,128)(2,1)S(1)} %get-tuple-element.44), channel_id=1, source_target_pairs={{0,12},{1,13},{2,14},{3,15},{4,8},{5,9},{6,10},{7,11},{8,4},{9,5},... | collective-permute-start | bytes 602120 | tf_op jit(solution)/shard_map/ppermute | solution.py:536
  37.6 14.5 %collective-permute-start.11 = (bf16[784,128]{1,0:T(8,128)(2,1)S(1)}, bf16[784,128]{1,0:T(8,128)(2,1)S(1)}, u32[]{:S(2)}, u32[]{:S(2)}) collective-permute-start(bf16[784,128]{1,0:T(8,128)(2,1)S(1)} %get-tuple-element.45), channel_id=1, source_target_pairs={{0,4},{1,5},{2,6},{3,7},{4,0},{5,1},{6,2},{7,3},{8,12},{9,13},{10,... | collective-permute-start | bytes 602120 | tf_op jit(solution)/shard_map/ppermute | solution.py:536
  37.8 3.9 %collective-permute-start.12 = (bf16[128,128]{1,0:T(8,128)(2,1)S(1)}, bf16[128,128]{1,0:T(8,128)(2,1)S(1)}, u32[]{:S(2)}, u32[]{:S(2)}) collective-permute-start(bf16[128,128]{1,0:T(8,128)(2,1)S(1)} %get-tuple-element.48.refs_0_), channel_id=1, source_target_pairs={{0,2},{1,3},{2,0},{3,1},{4,6},{5,7},{6,4},{7,5},{8,10},{9,11},{10,... | collective-permute-start | bytes 98312 | tf_op jit(solution)/shard_map/ppermute | solution.py:536
  53.7 5.8 %collective-permute-start.13 = (bf16[128,128]{1,0:T(8,128)(2,1)S(1)}, bf16[128,128]{1,0:T(8,128)(2,1)S(1)}, u32[]{:S(2)}, u32[]{:S(2)}) collective-permute-start(bf16[128,128]{1,0:T(8,128)(2,1)S(1)} %get-tuple-element.56), channel_id=1, source_target_pairs={{0,12},{1,13},{2,14},{3,15},{4,8},{5,9},{6,10},{7,11},{8,4},{9,5},... | collective-permute-start | bytes 98312 | tf_op jit(solution)/shard_map/ppermute | solution.py:536
  56.5 4.8 %collective-permute-start.14 = (bf16[128,128]{1,0:T(8,128)(2,1)S(1)}, bf16[128,128]{1,0:T(8,128)(2,1)S(1)}, u32[]{:S(2)}, u32[]{:S(2)}) collective-permute-start(bf16[128,128]{1,0:T(8,128)(2,1)S(1)} %get-tuple-element.57), channel_id=1, source_target_pairs={{0,8},{1,9},{2,10},{3,11},{4,12},{5,13},{6,14},{7,15},{8,0},{9,1},... | collective-permute-start | bytes 98312 | tf_op jit(solution)/shard_map/ppermute | solution.py:536
  57.8 3.9 %collective-permute-start.15 = (bf16[128,128]{1,0:T(8,128)(2,1)S(1)}, bf16[128,128]{1,0:T(8,128)(2,1)S(1)}, u32[]{:S(2)}, u32[]{:S(2)}) collective-permute-start(bf16[128,128]{1,0:T(8,128)(2,1)S(1)} %get-tuple-element.58), channel_id=1, source_target_pairs={{0,4},{1,5},{2,6},{3,7},{4,0},{5,1},{6,2},{7,3},{8,12},{9,13},{10,... | collective-permute-start | bytes 98312 | tf_op jit(solution)/shard_map/ppermute | solution.py:536
  62.0 3.8 %collective-permute-start.16 = (bf16[64,128]{1,0:T(8,128)(2,1)S(1)}, bf16[64,128]{1,0:T(8,128)(2,1)S(1)}, u32[]{:S(2)}, u32[]{:S(2)}) collective-permute-start(bf16[64,128]{1,0:T(8,128)(2,1)S(1)} %get-tuple-element.60), channel_id=1, source_target_pairs={{0,2},{1,3},{2,0},{3,1},{4,6},{5,7},{6,4},{7,5},{8,10},{9,11},{10,... | collective-permute-start | bytes 49160 | tf_op jit(solution)/shard_map/ppermute | solution.py:536
